TPU v7x, 32 devices: a whole 2x2x4 slice. The times are simulated.
32 devices in a mesh: row: 8 (over z, y), col: 4 (over x, core).
Axes of the slice: x: 2, y: 2, z: 4, core: 2. Of those that a mesh axis runs over, the one named last changes fastest.
Arguments:
- amplitudes: bfloat16 [24576, 3072], P('row', 'col'), may hold values from -6 to 6
- pair_mask: int32 [96, 12], P('row', 'col'), may hold values 0 or 1
- integrals: bfloat16 [8, 4, 2, 256, 256], P('row', 'col'), may hold values from -0.25 to 0.25
- tile_list: int32 [8, 4, 2], P('row', 'col'), may hold values from 0 to 2, as said below
- tile_count: int32 [8, 4], P('row', 'col'), may hold values from 1 to 2, as said below
- owner: int32 [4, 4], P(None, 'col'), may hold values from 0 to 7, as said below
Outputs:
- ladder: bfloat16 [24576, 1024], P('row', 'col')
Inputs may be any that keep to these rules, and one draw needn't show every extreme that they name: `owner`: within a column the 4 owners differ. `tile_count`: some panel that serves a step has all 2 slots live. `tile_list`: the live slots of a panel name distinct cd tile pairs; entries past the count are in range and unused.
All inputs are finite; a program needn't handle non-finite values. No bound on the sum of `pair_mask` on one device may be relied on, other than what follows from the above.
Results may differ from a plain program's by a relative error of at most 0.001.
Values may be sent and summed in bfloat16 or wider, within the bound.
No kernel may reach another device: no remote copies, remote signals or barrier semaphores. Data moves between devices by JAX's collectives and lax.ppermute only.
A program may use at most 128 MiB of HBM per device.

v0:
```python
from functools import partial

import jax
import jax.numpy as jnp
from jax import lax
from jax.sharding import PartitionSpec as P

STEPS = 4


def passed_along(value, axis, by):
    peers = lax.axis_size(axis)
    return lax.ppermute(value, axis, [(i, (i + by) % peers) for i in range(peers)])


def broadcast(value, axis, source):
    kept = jnp.where(lax.axis_index(axis) == source, value, 0).astype(value.dtype)
    return lax.psum(kept, axis)


def slot_product(current, panel_tiles, slot_tiles, slot_index, tile_width):
    start = slot_tiles[slot_index] * tile_width
    tile_block = lax.dynamic_slice_in_dim(current, start, tile_width, 1)
    weights = lax.dynamic_index_in_dim(panel_tiles, slot_index, 0, keepdims=False)
    return jnp.dot(tile_block, weights, preferred_element_type=jnp.float32)


def live_update(current, panel_tiles, slot_tiles, tile_width, slot_index, running):
    return running + slot_product(current, panel_tiles, slot_tiles, slot_index, tile_width)


def shards(amplitudes, pair_mask, integrals, tile_list, tile_count, owner):
    row_count, full_width = amplitudes.shape
    tile_width = integrals.shape[-1]
    block_count, local_tiles = pair_mask.shape
    shaped = amplitudes.reshape(block_count, row_count // block_count, local_tiles, tile_width)
    masked = (shaped * pair_mask.astype(jnp.bfloat16)[:, None, :, None]).reshape(
        row_count, full_width
    )
    running = jnp.zeros((row_count, tile_width), jnp.float32)
    current = masked
    for grid_step in range(STEPS):
        if grid_step > 0:
            current = passed_along(current, "col", 1)
        panel_tiles, slot_tiles, live_count = (
            broadcast(integrals[0, 0], "row", owner[grid_step, 0]),
            broadcast(tile_list[0, 0], "row", owner[grid_step, 0]),
            broadcast(tile_count[0, 0], "row", owner[grid_step, 0]),
        )
        running = lax.fori_loop(
            0,
            live_count,
            partial(live_update, current, panel_tiles, slot_tiles, tile_width),
            running,
        )
    return running.astype(jnp.bfloat16)


def solution(mesh):
    return jax.shard_map(
        shards,
        mesh=mesh,
        in_specs=(
            P("row", "col"),
            P("row", "col"),
            P("row", "col", None, None, None),
            P("row", "col", None),
            P("row", "col"),
            P(None, "col"),
        ),
        out_specs=P("row", "col"),
        check_vma=False,
    )
```

profile of v0, /device:TPU:0, one launch (start us, length us, event | category | flops | bytes accessed | tf_op | source)
XLA Modules:
  0.0 207.3 jit_solution(18338017915776126792)
XLA Ops:
  6.5 0.0 all-reduce.4.cloned.1.call-start
  6.5 0.7 convert_element_type.11
  7.2 0.5 mul.35
  7.7 5.3 %copy.17 = bf16[96,8,12,256]{3,1,2,0:T(8,128)(2,1)} copy(bf16[96,8,12,256]{3,2,1,0:T(8,128)(2,1)S(1)} %bitcast.62) | data formatting | bytes 9437184
  13.0 6.6 %copy.8 = bf16[3072,768]{0,1:T(8,128)(2,1)} copy(bf16[3072,768]{1,0:T(8,128)(2,1)} %param.14) | data formatting | bytes 9437184 | tf_op args[0]
  19.7 0.0 copy-start.4
  19.7 0.0 copy-start.3
  19.7 0.0 copy-start.5
  19.7 5.7 %mul.37 = bf16[3072,768]{0,1:T(8,128)(2,1)S(1)} multiply(bf16[3072,768]{0,1:T(8,128)(2,1)} %copy.8, bf16[3072,768]{0,1:T(8,128)(2,1)} %bitcast.63) | non-fusion elementwise | flops 2359296 | bytes 14155776 | tf_op jit(solution)/shard_map/mul | solution.py:37
  25.4 0.0 copy-start
  25.4 2.1 %copy-done = bf16[3072,768]{0,1:T(8,128)(2,1)} copy-done((bf16[3072,768]{0,1:T(8,128)(2,1)}, bf16[3072,768]{0,1:T(8,128)(2,1)S(1)}, u32[]{:S(2)}) %copy-start) | copy-done | bytes 4718616
  27.5 0.5 collective-permute-start
  28.0 53.8 %collective-permute-done = bf16[3072,768]{0,1:T(8,128)(2,1)} collective-permute-done((bf16[3072,768]{0,1:T(8,128)(2,1)S(1)}, bf16[3072,768]{0,1:T(8,128)(2,1)}, u32[]{:S(2)}, u32[]{:S(2)}) %collective-permute-start) | collective-permute-done | bytes 4718624 | tf_op jit(solution)/shard_map/ppermute | solution.py:13
  81.8 0.0 collective-permute-start.1
  81.8 0.0 copy-done.4
  81.8 0.6 fusion.20
  84.9 0.0 copy-done.3
  84.9 1.0 select_bitcast_fusion
  85.9 0.0 all-reduce.4.cloned.1.call-update
  85.9 49.8 %collective-permute-done.1 = bf16[3072,768]{0,1:T(8,128)(2,1)} collective-permute-done((bf16[3072,768]{0,1:T(8,128)(2,1)}, bf16[3072,768]{0,1:T(8,128)(2,1)}, u32[]{:S(2)}, u32[]{:S(2)}) %collective-permute-start.1) | collective-permute-done | bytes 4718624 | tf_op jit(solution)/shard_map/ppermute | solution.py:13
  135.7 0.0 collective-permute-start.2
  135.7 0.0 copy-done.5
  136.4 13.0 %all-reduce = (s32[]{:T(128)}, s32[2]{0:T(128)S(1)}, s32[]{:T(128)}, s32[2]{0:T(128)S(1)}, s32[]{:T(128)}, /*index=5*/s32[2]{0:T(128)S(1)}, s32[]{:T(128)}, s32[2]{0:T(128)S(1)}) all-reduce(s32[]{:T(128)S(6)} %select_n.118, s32[2]{0:T(128)S(1)} %get-tuple-element.231, s32[]{:T(128)S(6)} %select_n.125, ...), channel_id=1, replica_groups=mesh['row'=8,'col'=4] {'row'}, use_global_device_ids=true, to_apply=%region_0.1 | all-reduce | flops 12 | bytes 96 | tf_op jit(solution)/shard_map/psum | solution.py:18
  149.4 18.1 %all-reduce.4.cloned.1.call-done = (bf16[2,256,256]{2,1,0:T(8,128)(2,1)}, bf16[2,256,256]{2,1,0:T(8,128)(2,1)}, bf16[2,256,256]{2,1,0:T(8,128)(2,1)}, bf16[2,256,256]{2,1,0:T(8,128)(2,1)}) async-done(((bf16[2,256,256]{2,1,0:T(8,128)(2,1)}, bf16[2,256,256]{2,1,0:T(8,128)(2,1)}, bf16[2,256,256]{2,1,0:T(8,128)(2,1)}, bf16[2,256,256]{2,1,0:T(8,128)(2,1)}), (bf16[2,256,256]{2,1,0:T(8,128)(2,1)}, ...) | async-done | bytes 1048592 | tf_op jit(solution)/shard_map/psum | solution.py:18
  167.5 0.2 broadcast_in_dim.18
  167.7 0.0 copy-start.2
  167.7 9.6 %while.40 = (s32[]{:T(128)}, f32[3072,256]{1,0:T(8,128)S(1)}, s32[]{:T(128)}, s32[2]{0:T(128)S(1)}, bf16[3072,768]{0,1:T(8,128)(2,1)}, /*index=5*/bf16[2,256,256...) while((s32[]{:T(128)}, f32[3072,256]{1,0:T(8,128)S(1)}, ...), condition=%wide.region_4.5_spmd, body=%wide.region_3.4_spmd.sunk | while | flops 403439616 | bytes 7995601 | solution.py:50
  168.4 0.6 dynamic_slice.75
  169.6 2.6 %convolution_add_fusion.8 = f32[3072,256]{1,0:T(8,128)S(1)} fusion(f32[3072,256]{1,0:T(8,128)S(1)} %get-tuple-element.401, bf16[3072,768]{0,1:T(8,128)(2,1)} %get-tuple-element.415, s32[]{:T(128)S(6)} %select_n.187, bf16[2,256,256]{2,1,0:T(8,128)(2,1)} %get-tuple-element.416, s32[]{:T(128)S(6)} %select_n.186), kind=kOutput, calls=%fused_computation.clone.1 | convolution fusion | flops 403439616 | bytes 7995400 | tf_op jit(solution)/shard_map/while/body/dot_general | solution.py:25
  172.9 0.6 dynamic_slice.75
  174.1 2.6 %convolution_add_fusion.8 = f32[3072,256]{1,0:T(8,128)S(1)} fusion(f32[3072,256]{1,0:T(8,128)S(1)} %get-tuple-element.401, bf16[3072,768]{0,1:T(8,128)(2,1)} %get-tuple-element.415, s32[]{:T(128)S(6)} %select_n.187, bf16[2,256,256]{2,1,0:T(8,128)(2,1)} %get-tuple-element.416, s32[]{:T(128)S(6)} %select_n.186), kind=kOutput, calls=%fused_computation.clone.1 | convolution fusion | flops 403439616 | bytes 7995400 | tf_op jit(solution)/shard_map/while/body/dot_general | solution.py:25
  177.4 0.0 copy-done.2
  177.4 5.2 %while.41 = (s32[]{:T(128)}, f32[3072,256]{1,0:T(8,128)S(1)}, s32[]{:T(128)}, s32[2]{0:T(128)S(1)}, bf16[3072,768]{0,1:T(8,128)(2,1)}, /*index=5*/bf16[2,256,256...) while((s32[]{:T(128)}, f32[3072,256]{1,0:T(8,128)S(1)}, ...), condition=%wide.region_9.10_spmd, body=%wide.region_8.9_spmd.sunk | while | flops 403439616 | bytes 7995601 | solution.py:50
  178.1 0.6 dynamic_slice.78
  179.3 2.6 %convolution_add_fusion.9 = f32[3072,256]{1,0:T(8,128)S(1)} fusion(f32[3072,256]{1,0:T(8,128)S(1)} %get-tuple-element.434, bf16[3072,768]{0,1:T(8,128)(2,1)} %get-tuple-element.448, s32[]{:T(128)S(6)} %select_n.189, bf16[2,256,256]{2,1,0:T(8,128)(2,1)S(1)} %get-tuple-element.449, s32[]{:T(128)S(6)} %select_n.188), kind=kOutput, calls=%fused_computation.5.clone.1 | convolution fusion | flops 403439616 | bytes 7995400 | tf_op jit(solution)/shard_map/while/body/dot_general | solution.py:25
  182.6 0.0 copy-start.1
  182.6 5.3 %while.42 = (s32[]{:T(128)}, f32[3072,256]{1,0:T(8,128)S(1)}, s32[]{:T(128)}, s32[2]{0:T(128)S(1)}, bf16[3072,768]{0,1:T(8,128)(2,1)}, /*index=5*/bf16[2,256,256...) while((s32[]{:T(128)}, f32[3072,256]{1,0:T(8,128)S(1)}, ...), condition=%wide.region_14.15_spmd, body=%wide.region_13.14_spmd.sunk | while | flops 403439616 | bytes 7995601 | solution.py:50
  183.4 0.6 dynamic_slice.81
  184.6 2.6 %convolution_add_fusion.10 = f32[3072,256]{1,0:T(8,128)S(1)} fusion(f32[3072,256]{1,0:T(8,128)S(1)} %get-tuple-element.467, bf16[3072,768]{0,1:T(8,128)(2,1)} %get-tuple-element.481, s32[]{:T(128)S(6)} %select_n.191, bf16[2,256,256]{2,1,0:T(8,128)(2,1)} %get-tuple-element.482, s32[]{:T(128)S(6)} %select_n.190), kind=kOutput, calls=%fused_computation.10.clone.1 | convolution fusion | flops 403439616 | bytes 7995400 | tf_op jit(solution)/shard_map/while/body/dot_general | solution.py:25
  187.9 1.6 collective-permute-done.2
  189.5 0.0 copy-done.1
  189.6 9.6 %while.43 = (s32[]{:T(128)}, f32[3072,256]{1,0:T(8,128)S(1)}, s32[]{:T(128)}, s32[2]{0:T(128)S(1)}, bf16[3072,768]{0,1:T(8,128)(2,1)}, /*index=5*/bf16[2,256,256...) while((s32[]{:T(128)}, f32[3072,256]{1,0:T(8,128)S(1)}, ...), condition=%wide.region_19.20_spmd, body=%wide.region_18.19_spmd.sunk | while | flops 403439616 | bytes 7995601 | solution.py:50
  190.2 0.6 dynamic_slice.84
  191.4 2.6 %convolution_add_fusion.11 = f32[3072,256]{1,0:T(8,128)S(1)} fusion(f32[3072,256]{1,0:T(8,128)S(1)} %get-tuple-element.500, bf16[3072,768]{0,1:T(8,128)(2,1)} %get-tuple-element.514, s32[]{:T(128)S(6)} %select_n.193, bf16[2,256,256]{2,1,0:T(8,128)(2,1)S(1)} %get-tuple-element.515, s32[]{:T(128)S(6)} %select_n.192), kind=kOutput, calls=%fused_computation.15.clone.1 | convolution fusion | flops 403439616 | bytes 7995400 | tf_op jit(solution)/shard_map/while/body/dot_general | solution.py:25
  194.7 0.6 dynamic_slice.84
  195.9 2.6 %convolution_add_fusion.11 = f32[3072,256]{1,0:T(8,128)S(1)} fusion(f32[3072,256]{1,0:T(8,128)S(1)} %get-tuple-element.500, bf16[3072,768]{0,1:T(8,128)(2,1)} %get-tuple-element.514, s32[]{:T(128)S(6)} %select_n.193, bf16[2,256,256]{2,1,0:T(8,128)(2,1)S(1)} %get-tuple-element.515, s32[]{:T(128)S(6)} %select_n.192), kind=kOutput, calls=%fused_computation.15.clone.1 | convolution fusion | flops 403439616 | bytes 7995400 | tf_op jit(solution)/shard_map/while/body/dot_general | solution.py:25
  199.2 1.3 convert_element_type.12
  (1 shorter events, 0.0 us)
Async XLA Ops:
  6.5 161.0 %all-reduce.4.cloned.1.call-start = ((), (), s32[]{:S(2)}) async-start(), calls=%async_computation | async-start | bytes 2097152 | tf_op jit(solution)/shard_map/psum | solution.py:18
  19.7 62.2 %copy-start.4 = (s32[4,1]{0,1:T(1,128)S(1)}, s32[4,1]{0,1:T(1,128)}, u32[]{:S(2)}) copy-start(s32[4,1]{0,1:T(1,128)} %param.19) | copy-start | bytes 52
  19.7 65.2 %copy-start.3 = (bf16[1,1,2,256,256]{4,3,2,1,0:T(8,128)(2,1)S(1)}, bf16[1,1,2,256,256]{4,3,2,1,0:T(8,128)(2,1)}, u32[]{:S(2)}) copy-start(bf16[1,1,2,256,256]{4,3,2,1,0:T(8,128)(2,1)} %param.16) | copy-start | bytes 786436
  19.7 116.0 %copy-start.5 = (s32[1,1,2]{2,1,0:T(1,128)S(1)}, s32[1,1,2]{2,1,0:T(1,128)}, u32[]{:S(2)}) copy-start(s32[1,1,2]{2,1,0:T(1,128)} %param.17) | copy-start | bytes 28
  25.4 2.1 %copy-start = (bf16[3072,768]{0,1:T(8,128)(2,1)}, bf16[3072,768]{0,1:T(8,128)(2,1)S(1)}, u32[]{:S(2)}) copy-start(bf16[3072,768]{0,1:T(8,128)(2,1)S(1)} %mul.37) | copy-start | bytes 14155780
  27.5 54.3 %collective-permute-start = (bf16[3072,768]{0,1:T(8,128)(2,1)S(1)}, bf16[3072,768]{0,1:T(8,128)(2,1)}, u32[]{:S(2)}, u32[]{:S(2)}) collective-permute-start(bf16[3072,768]{0,1:T(8,128)(2,1)S(1)} %mul.37), channel_id=1, source_target_pairs={{0,1},{1,2},{2,3},{3,0},{4,5},{5,6},{6,7},{7,4},{8,9},{9,10},{10,1... | collective-permute-start | bytes 14155784 | tf_op jit(solution)/shard_map/ppermute | solution.py:13
  81.8 53.9 %collective-permute-start.1 = (bf16[3072,768]{0,1:T(8,128)(2,1)}, bf16[3072,768]{0,1:T(8,128)(2,1)}, u32[]{:S(2)}, u32[]{:S(2)}) collective-permute-start(bf16[3072,768]{0,1:T(8,128)(2,1)} %collective-permute-done), channel_id=1, source_target_pairs={{0,1},{1,2},{2,3},{3,0},{4,5},{5,6},{6,7},{7,4},{8,9},{9,10},{10,1... | collective-permute-start | bytes 14155784 | tf_op jit(solution)/shard_map/ppermute | solution.py:13
  135.7 53.9 %collective-permute-start.2 = (bf16[3072,768]{0,1:T(8,128)(2,1)}, bf16[3072,768]{0,1:T(8,128)(2,1)}, u32[]{:S(2)}, u32[]{:S(2)}) collective-permute-start(bf16[3072,768]{0,1:T(8,128)(2,1)} %collective-permute-done.1), channel_id=1, source_target_pairs={{0,1},{1,2},{2,3},{3,0},{4,5},{5,6},{6,7},{7,4},{8,9},{9,10},{10,1... | collective-permute-start | bytes 14155784 | tf_op jit(solution)/shard_map/ppermute | solution.py:13
  167.7 9.6 %copy-start.2 = (bf16[2,256,256]{2,1,0:T(8,128)(2,1)S(1)}, bf16[2,256,256]{2,1,0:T(8,128)(2,1)}, u32[]{:S(2)}) copy-start(bf16[2,256,256]{2,1,0:T(8,128)(2,1)} %get-tuple-element.427) | copy-start | bytes 786436
  182.6 6.9 %copy-start.1 = (bf16[2,256,256]{2,1,0:T(8,128)(2,1)S(1)}, bf16[2,256,256]{2,1,0:T(8,128)(2,1)}, u32[]{:S(2)}) copy-start(bf16[2,256,256]{2,1,0:T(8,128)(2,1)} %get-tuple-element.493) | copy-start | bytes 786436
Sparse Core Ops, SparseCore 0:
  86.0 81.4 all-reduce.3
where the time goes:
time: 206 us; the launch traced here: 207 us
  waiting for transfers between devices  123 us (60%)
  local copies, waits for them, and re-layouts  18.9 us (9%)
  between operations  16.6 us (8%)
  matrix products  15.7 us (8%)
  blocking collectives  13 us (6%)
  loops' own time  10.6 us (5%)
  other arithmetic  8.71 us (4%)
    ppermute x3, waiting for transfers between devices, passed_along(): lax.ppermute(value, axis, [(i, (i + by) % peers) for i in range(peers)])  105 us
    psum x1, waiting for transfers between devices, broadcast(): return lax.psum(kept, axis)  18.1 us
    dot_general x6, matrix products, slot_product(): return jnp.dot(tile_block, weights, preferred_element_type=jnp.float32)  15.7 us
    unnamed x14, local copies, waits for them, and re-layouts  14.1 us
    psum x1, blocking collectives, broadcast(): return lax.psum(kept, axis)  13 us
    another operation x4, loops' own time, shards(): lax.fori_loop(0, live_count, partial(live_update, current, panel_tiles, s...  10.6 us
    mul x1, other arithmetic, shards(): shaped * pair_mask.astype(jnp.bfloat16)[:, None, :, None]  5.74 us
  transfers between devices with their start and end apart: 4, of which 4 were waited for; matrix products, arithmetic and copies ran while one was open for 7% of the time, Pallas kernels for 0%

commit v1 on v0

v1 whole, which is shorter than its diff:
```python
from functools import partial

import jax
import jax.numpy as jnp
from jax import lax
from jax.experimental import pallas as pl
from jax.experimental.pallas import tpu as pltpu
from jax.sharding import PartitionSpec as P

STEPS = 4
CORES = 2
CHUNKS = 4
CODE_TOP = 32767.0
META_ROWS = 16


def pair_offsets(col_count):
    pairs = col_count // CORES
    offsets = set()
    for core in range(CORES):
        for step in range(STEPS):
            offsets.add(((core - step) // CORES * -1) % pairs)
    return sorted(offsets)


def fill_weights(info_ref, panels_ref, dense_ref, tile_width):
    pieces, groups, stored, _ = panels_ref.shape
    depth = tile_width // pieces
    slots = stored // depth
    width = dense_ref.shape[0] // groups
    dense_ref[...] = jnp.zeros_like(dense_ref)
    for group in range(groups):
        for slot in range(slots):

            @pl.when(slot < info_ref[group, slots])
            def _():
                start = pl.multiple_of(group * width + info_ref[group, slot] * tile_width, tile_width)
                for piece in range(pieces):
                    dense_ref[pl.ds(start + piece * depth, depth), :] = panels_ref[
                        piece, group, pl.ds(slot * depth, depth), :
                    ]


def block_product(mask_ref, row_block, own_ref, other_ref, dense_ref, tile_width):
    tiles = own_ref.shape[1] // tile_width
    total = None
    for group, source in enumerate((own_ref, other_ref)):
        for tile in range(tiles):
            live = mask_ref[row_block, group * tiles + tile].astype(jnp.float32).astype(jnp.bfloat16)
            screened = source[:, pl.ds(tile * tile_width, tile_width)] * live
            weights = dense_ref[pl.ds((group * tiles + tile) * tile_width, tile_width), :]
            term = jnp.dot(screened, weights, preferred_element_type=jnp.float32)
            total = term if total is None else total + term
    return total


def send_kernel(first, tile_width, info_ref, mask_ref, own_ref, other_ref, panels_ref, code_ref, scale_ref, dense_ref):
    step = pl.program_id(0)

    @pl.when(step == 0)
    def _():
        fill_weights(info_ref, panels_ref, dense_ref, tile_width)

    total = block_product(mask_ref, first + step, own_ref, other_ref, dense_ref, tile_width)
    top = jnp.max(jnp.abs(total), axis=0, keepdims=True)
    safe = jnp.where(top > 0, top, 1.0)
    code_ref[...] = jnp.round(total * (CODE_TOP / safe)).astype(jnp.int32).astype(jnp.int16)
    scale_ref[pl.ds(step, 1), :] = safe * (1.0 / CODE_TOP)


def join_kernel(first, tile_width, arrivals, *refs):
    info_ref, mask_ref, own_ref, other_ref, panels_ref = refs[:5]
    codes, scales = refs[5 : 5 + arrivals], refs[5 + arrivals : 5 + 2 * arrivals]
    out_ref, dense_ref = refs[-2:]
    step = pl.program_id(0)

    @pl.when(step == 0)
    def _():
        fill_weights(info_ref, panels_ref, dense_ref, tile_width)

    total = block_product(mask_ref, first + step, own_ref, other_ref, dense_ref, tile_width)
    for code_ref, scale_ref in zip(codes, scales):
        total = total + code_ref[...].astype(jnp.int32).astype(jnp.float32) * scale_ref[pl.ds(step, 1), :]
    out_ref[...] = total.astype(out_ref.dtype)


def shards(amplitudes, pair_mask, integrals, tile_list, tile_count, owner):
    row_count, full_width = amplitudes.shape
    slots, tile_width = integrals.shape[2], integrals.shape[-1]
    block_count, tiles = pair_mask.shape
    block_rows = row_count // block_count
    row_peers, col_peers = lax.axis_size("row"), lax.axis_size("col")
    depth = tile_width // row_peers
    core = lax.axis_index("col") % CORES
    offsets = pair_offsets(col_peers)

    swap = [(c, c ^ 1) for c in range(col_peers)]
    other = lax.ppermute(amplitudes, "col", swap)
    other_mask = lax.ppermute(pair_mask, "col", swap)
    masks = jnp.concatenate([pair_mask, other_mask], axis=1)

    pieces = integrals[0, 0].reshape(slots, row_peers, depth, tile_width)
    pieces = jnp.transpose(pieces, (1, 0, 2, 3)).reshape(row_peers, slots * depth, tile_width)
    info = jnp.concatenate([tile_list[0, 0], tile_count[0, 0][None]]).astype(integrals.dtype)
    info = jnp.pad(info[None, :], ((0, META_ROWS - 1), (0, tile_width - slots - 1)))
    pieces = jnp.concatenate([pieces, jnp.broadcast_to(info, (row_peers, META_ROWS, tile_width))], axis=1)
    pieces = lax.all_to_all(pieces, "row", 0, 0)

    def wanted(offset):
        chosen = []
        for group_shift in (0, 1 - 2 * core):
            step = (CORES * offset - group_shift) % col_peers
            holder = owner[jnp.minimum(step, STEPS - 1), 0]
            piece = lax.dynamic_index_in_dim(pieces, holder, 0, keepdims=False)
            chosen.append(jnp.where(step < STEPS, piece, jnp.zeros_like(piece)))
        chosen = jnp.stack(chosen)
        if offset % (col_peers // CORES):
            chosen = lax.ppermute(chosen, "col", [(c, (c - CORES * offset) % col_peers) for c in range(col_peers)])
        info = chosen[:, slots * depth, : slots + 1].astype(jnp.int32)
        return info, lax.all_gather(chosen[:, : slots * depth], "row")

    plans = {offset: wanted(offset) for offset in sorted(offsets, reverse=True)}

    chunks = CHUNKS if block_count % CHUNKS == 0 else 1
    span = block_count // chunks
    smem = pl.BlockSpec(memory_space=pltpu.SMEM)

    def inputs(first):
        rows = pl.BlockSpec((block_rows, full_width), lambda i: (first + i, 0))
        panels = pl.BlockSpec((row_peers, CORES, slots * depth, tile_width), lambda i: (0, 0, 0, 0))
        return [smem, smem, rows, rows, panels]

    codes = pl.BlockSpec((block_rows, tile_width), lambda i: (i, 0))
    scale_rows = -(-span // 8) * 8
    scales = pl.BlockSpec((scale_rows, tile_width), lambda i: (0, 0))
    dense = pltpu.VMEM((CORES * full_width, tile_width), jnp.bfloat16)
    cost = pl.CostEstimate(
        flops=2 * span * block_rows * CORES * full_width * tile_width,
        bytes_accessed=span * block_rows * (CORES * full_width + tile_width) * 2,
        transcendentals=0,
    )
    limit = pltpu.CompilerParams(vmem_limit_bytes=32 * 1024 * 1024)

    arrived = []
    for chunk in range(chunks):
        first = chunk * span
        received = []
        for offset in offsets:
            if offset == 0:
                continue
            code, scale = pl.pallas_call(
                partial(send_kernel, first, tile_width),
                grid=(span,),
                in_specs=inputs(first),
                out_specs=[codes, scales],
                out_shape=[
                    jax.ShapeDtypeStruct((span * block_rows, tile_width), jnp.int16),
                    jax.ShapeDtypeStruct((scale_rows, tile_width), jnp.float32),
                ],
                scratch_shapes=[dense],
                compiler_params=limit,
                cost_estimate=cost,
                name="send_part",
            )(plans[offset][0], masks, amplitudes, other, plans[offset][1])
            up = [(c, (c + CORES * offset) % col_peers) for c in range(col_peers)]
            received.append((lax.ppermute(code, "col", up), lax.ppermute(scale, "col", up)))
        arrived.append(received)

    out = None
    for chunk in range(chunks):
        first = chunk * span
        arrivals = len(arrived[chunk])
        operands = [plans[0][0], masks, amplitudes, other, plans[0][1]]
        operands += [code for code, _ in arrived[chunk]] + [scale for _, scale in arrived[chunk]]
        specs = inputs(first) + [codes] * arrivals + [scales] * arrivals
        body = partial(join_kernel, first, tile_width, arrivals)
        aliases = {}
        if out is not None:
            body = partial(skip_operand, len(operands), body)
            aliases = {len(operands): 0}
            operands.append(out)
            specs.append(pl.BlockSpec(memory_space=pl.ANY))
        out = pl.pallas_call(
            body,
            grid=(span,),
            in_specs=specs,
            out_specs=pl.BlockSpec((block_rows, tile_width), lambda i, first=first: (first + i, 0)),
            out_shape=jax.ShapeDtypeStruct((row_count, tile_width), jnp.bfloat16),
            scratch_shapes=[dense],
            input_output_aliases=aliases,
            compiler_params=limit,
            cost_estimate=cost,
            name="join_part",
        )(*operands)
    return out


def skip_operand(position, body, *refs):
    body(*refs[:position], *refs[position + 1 :])


def solution(mesh):
    return jax.shard_map(
        shards,
        mesh=mesh,
        in_specs=(
            P("row", "col"),
            P("row", "col"),
            P("row", "col", None, None, None),
            P("row", "col", None),
            P("row", "col"),
            P(None, "col"),
        ),
        out_specs=P("row", "col"),
        check_vma=False,
    )
```

time: 206 us -> 130 us (0.63); the launches traced: 207 us -> 129 us
  waiting for transfers between devices: 123 us -> 7.95 us
  blocking collectives: 13 us -> 62.9 us
  Pallas kernels: 0 us -> 26.5 us
  starting transfers between devices: 0.46 us -> 17.4 us
  matrix products: 15.7 us -> 0 us
  local copies, waits for them, and re-layouts: 18.9 us -> 4.09 us
  loops' own time: 10.6 us -> 0 us
  between operations: 16.6 us -> 8.42 us
  other arithmetic: 8.71 us -> 1.6 us
    ppermute x3 -> x11, waiting for transfers between devices: 105 us -> 5.75 us  [the longest x1 2.94 us: wanted(): lax.ppermute(chosen, 'col', [(c, (c - CORES * offset) % col_peers) for c...]
    all_gather x0 -> x2, blocking collectives: none -> 62.9 us  [wanted(): return (info, lax.all_gather(chosen[:, :slots * depth], 'row'))]
    pallas_call x0 -> x8, Pallas kernels: none -> 26.5 us  [the longest x4 14.6 us: shards(): pl.pallas_call(body, grid=(span,), in_specs=specs, out_specs=pl.BlockSpec...]
    psum x1 -> x0, waiting for transfers between devices: 18.1 us -> none  [broadcast(): return lax.psum(kept, axis)]
    dot_general x6 -> x0, matrix products: 15.7 us -> none  [slot_product(): return jnp.dot(tile_block, weights, preferred_element_type=jnp.float32)]
    psum x1 -> x0, blocking collectives: 13 us -> none  [broadcast(): return lax.psum(kept, axis)]
    unnamed x14 -> x11, local copies, waits for them, and re-layouts: 14.1 us -> 2.45 us
    another operation x4 -> x0, loops' own time: 10.6 us -> none  [shards(): lax.fori_loop(0, live_count, partial(live_update, current, panel_tiles, s...]
  transfers between devices with their start and end apart: 4 -> 12, of which waited for: 4 -> 3; matrix products, arithmetic and copies ran while one was open for 7% -> 3% of each run, Pallas kernels for 0% -> 15%
where the time goes in v1:
time: 130 us; the launch traced here: 129 us
  blocking collectives  62.9 us (48%)
  Pallas kernels  26.5 us (20%)
  starting transfers between devices  17.4 us (13%)
  between operations  8.42 us (6%)
  waiting for transfers between devices  7.95 us (6%)
  local copies, waits for them, and re-layouts  4.09 us (3%)
  other arithmetic  1.6 us (1%)
    all_gather x2, blocking collectives, wanted(): return (info, lax.all_gather(chosen[:, :slots * depth], 'row'))  62.9 us
    pallas_call x4, Pallas kernels, shards(): pl.pallas_call(body, grid=(span,), in_specs=specs, out_specs=pl.BlockSpec...  14.6 us
    pallas_call x4, Pallas kernels, shards(): pl.pallas_call(partial(send_kernel, first, tile_width), grid=(span,), in_...  11.9 us
    all_to_all x1, starting transfers between devices, shards(): pieces = lax.all_to_all(pieces, 'row', 0, 0)  6.86 us
    ppermute x4, starting transfers between devices, shards(): lax.ppermute(code, 'col', up)  4.61 us
    ppermute x4, starting transfers between devices, shards(): lax.ppermute(scale, 'col', up)  3.73 us
    ppermute x1, waiting for transfers between devices, wanted(): lax.ppermute(chosen, 'col', [(c, (c - CORES * offset) % col_peers) for c...  2.94 us
    ppermute x4, waiting for transfers between devices, shards(): lax.ppermute(scale, 'col', up)  2.79 us
  transfers between devices with their start and end apart: 12, of which 3 were waited for; matrix products, arithmetic and copies ran while one was open for 3% of the time, Pallas kernels for 15%

profile of v1, /device:TPU:0, one launch (start us, length us, event | category | flops | bytes accessed | tf_op | source)
XLA Modules:
  0.0 128.8 jit_solution(17227079223783370713)
XLA Ops:
  0.0 0.5 collective-permute-start.1
  0.5 1.0 copy.15
  2.1 0.7 convert_bitcast_fusion
  2.7 0.1 fusion.5
  2.8 0.7 pad_maximum_fusion
  3.6 6.9 %all-to-all-start = ((bf16[8,80,256]{2,1,0:T(8,128)(2,1)}), bf16[8,80,256]{2,1,0:T(8,128)(2,1)S(1)}, u32[]{:S(2)}, u32[]{:S(2)}) async-start(bf16[8,80,256]{2,1,0:T(8,128)(2,1)} %pad_maximum_fusion), calls=%async_computation | async-start | bytes 655360 | tf_op jit(solution)/shard_map/all_to_all | solution.py:107
  10.4 0.0 copy-done.2
  10.4 0.1 copy.17
  10.5 0.2 collective-permute-start
  10.7 0.0 copy-done.1
  10.7 0.7 fusion.6
  19.1 0.0 collective-permute-done
  19.1 0.1 pad_add_fusion.mask_ref.refs_1_
  19.1 2.2 %all-to-all-done = bf16[8,80,256]{2,1,0:T(8,128)(2,1)S(1)} async-done(((bf16[8,80,256]{2,1,0:T(8,128)(2,1)}), bf16[8,80,256]{2,1,0:T(8,128)(2,1)S(1)}, u32[]{:S(2)}, u32[]{:S(2)}) %all-to-all-start) | async-done | bytes 327712 | tf_op jit(solution)/shard_map/all_to_all | solution.py:107
  21.4 1.6 %collective-permute-start.2 = (bf16[2,80,256]{2,1,0:T(8,128)(2,1)S(1)}, bf16[2,80,256]{2,1,0:T(8,128)(2,1)S(1)}, u32[]{:S(2)}, u32[]{:S(2)}) collective-permute-start(bf16[2,80,256]{2,1,0:T(8,128)(2,1)S(1)} %pad_maximum_fusion.1), channel_id=1, source_target_pairs={{0,2},{1,3},{2,0},{3,1},{4,6},{5,7},{6,4},{7,5},{8,10},{9,11},{10,... | collective-permute-start | bytes 245768 | tf_op jit(solution)/shard_map/ppermute | solution.py:118
  23.0 2.9 %collective-permute-done.2 = bf16[2,80,256]{2,1,0:T(8,128)(2,1)S(1)} collective-permute-done((bf16[2,80,256]{2,1,0:T(8,128)(2,1)S(1)}, bf16[2,80,256]{2,1,0:T(8,128)(2,1)S(1)}, u32[]{:S(2)}, u32[]{:S(2)}) %collective-permute-start.2) | collective-permute-done | bytes 81952 | tf_op jit(solution)/shard_map/ppermute | solution.py:118
  25.9 31.3 %all-gather.1 = bf16[16,64,256]{2,1,0:T(8,128)(2,1)S(1)} all-gather(bf16[2,64,256]{2,1,0:T(8,128)(2,1)S(1)} %slice.17), channel_id=3, replica_groups=mesh['row'=8,'col'=4] {'row'}, dimensions={0}, use_global_device_ids=true | all-gather | bytes 589824 | tf_op jit(solution)/shard_map/all_gather | solution.py:120
  57.2 0.0 collective-permute-done.1.other_ref.refs_3_
  57.2 2.3 %copy-done = bf16[3072,768]{1,0:T(8,128)(2,1)S(1)} copy-done((bf16[3072,768]{1,0:T(8,128)(2,1)S(1)}, bf16[3072,768]{1,0:T(8,128)(2,1)}, u32[]{:S(2)}) %copy-start) | copy-done | bytes 4718616
  59.6 3.0 %send_part.7 = (s16[768,256]{1,0:T(8,128)(2,1)S(1)}, f32[8,256]{1,0:T(8,128)S(1)}) custom-call(s32[2,3]{1,0:T(2,128)S(1)} %bitcast.24, s32[12,6]{1,0:T(8,128)S(1)} %pad_add_fusion.mask_ref.refs_1_, bf16[3072,768]{1,0:T(8,128)(2,1)S(1)} %copy-done, bf16[3072,768]{1,0:T(8,128)(2,1)} %collective-permute-done.1.other_ref.refs_3_, ...), custom_call_target="tpu_custom_call" | custom-call | flops 603979776 | bytes 2752512 | tf_op jit(solution)/shard_map/send_part/pallas_call | solution.py:151
  62.6 1.6 %collective-permute-start.9 = (s16[768,256]{1,0:T(8,128)(2,1)S(1)}, s16[768,256]{1,0:T(8,128)(2,1)S(1)}, u32[]{:S(2)}, u32[]{:S(2)}) collective-permute-start(s16[768,256]{1,0:T(8,128)(2,1)S(1)} %get-tuple-element.19), channel_id=1, source_target_pairs={{0,2},{1,3},{2,0},{3,1},{4,6},{5,7},{6,4},{7,5},{8,10},{9,11},{10,... | collective-permute-start | bytes 1179656 | tf_op jit(solution)/shard_map/ppermute | solution.py:166
  64.1 3.0 %send_part.6 = (s16[768,256]{1,0:T(8,128)(2,1)S(1)}, f32[8,256]{1,0:T(8,128)S(1)}) custom-call(s32[2,3]{1,0:T(2,128)S(1)} %bitcast.25, s32[12,6]{1,0:T(8,128)S(1)} %pad_add_fusion.mask_ref.refs_1_, bf16[3072,768]{1,0:T(8,128)(2,1)S(1)} %copy-done, bf16[3072,768]{1,0:T(8,128)(2,1)} %collective-permute-done.1.other_ref.refs_3_, ...), custom_call_target="tpu_custom_call" | custom-call | flops 603979776 | bytes 2752512 | tf_op jit(solution)/shard_map/send_part/pallas_call | solution.py:151
  67.1 0.6 collective-permute-start.7
  67.7 3.0 %send_part.5 = (s16[768,256]{1,0:T(8,128)(2,1)S(1)}, f32[8,256]{1,0:T(8,128)S(1)}) custom-call(s32[2,3]{1,0:T(2,128)S(1)} %bitcast.26, s32[12,6]{1,0:T(8,128)S(1)} %pad_add_fusion.mask_ref.refs_1_, bf16[3072,768]{1,0:T(8,128)(2,1)S(1)} %copy-done, bf16[3072,768]{1,0:T(8,128)(2,1)} %collective-permute-done.1.other_ref.refs_3_, ...), custom_call_target="tpu_custom_call" | custom-call | flops 603979776 | bytes 2752512 | tf_op jit(solution)/shard_map/send_part/pallas_call | solution.py:151
  70.7 0.0 slice-start
  70.7 0.0 slice-start.1
  70.7 1.6 %collective-permute-start.5 = (s16[768,256]{1,0:T(8,128)(2,1)S(1)}, s16[768,256]{1,0:T(8,128)(2,1)S(1)}, u32[]{:S(2)}, u32[]{:S(2)}) collective-permute-start(s16[768,256]{1,0:T(8,128)(2,1)S(1)} %get-tuple-element.15), channel_id=1, source_target_pairs={{0,2},{1,3},{2,0},{3,1},{4,6},{5,7},{6,4},{7,5},{8,10},{9,11},{10,... | collective-permute-start | bytes 1179656 | tf_op jit(solution)/shard_map/ppermute | solution.py:166
  72.3 3.0 %send_part.4 = (s16[768,256]{1,0:T(8,128)(2,1)S(1)}, f32[8,256]{1,0:T(8,128)S(1)}) custom-call(s32[2,3]{1,0:T(2,128)S(1)} %bitcast.27, s32[12,6]{1,0:T(8,128)S(1)} %pad_add_fusion.mask_ref.refs_1_, bf16[3072,768]{1,0:T(8,128)(2,1)S(1)} %copy-done, bf16[3072,768]{1,0:T(8,128)(2,1)} %collective-permute-done.1.other_ref.refs_3_, ...), custom_call_target="tpu_custom_call" | custom-call | flops 603979776 | bytes 2752512 | tf_op jit(solution)/shard_map/send_part/pallas_call | solution.py:151
  75.3 0.9 collective-permute-start.3
  76.2 31.5 %all-gather = bf16[16,64,256]{2,1,0:T(8,128)(2,1)S(1)} all-gather(bf16[2,64,256]{2,1,0:T(8,128)(2,1)S(1)} %pad_maximum_fusion.2), channel_id=2, replica_groups=mesh['row'=8,'col'=4] {'row'}, dimensions={0}, use_global_device_ids=true | all-gather | bytes 589824 | tf_op jit(solution)/shard_map/all_gather | solution.py:120
  107.7 0.9 collective-permute-start.10
  108.6 2.8 %collective-permute-done.10.refs_6_ = f32[8,256]{1,0:T(8,128)S(1)} collective-permute-done((f32[8,256]{1,0:T(8,128)S(1)}, f32[8,256]{1,0:T(8,128)S(1)}, u32[]{:S(2)}, u32[]{:S(2)}) %collective-permute-start.10) | collective-permute-done | bytes 8224 | tf_op jit(solution)/shard_map/ppermute | solution.py:166
  111.3 0.9 collective-permute-start.8
  112.2 0.0 collective-permute-done.9.refs_5_
  112.2 1.2 collective-permute-start.6
  113.4 0.0 slice-done
  113.4 0.0 slice-done.1
  113.4 3.6 %join_part.4.refs_7_ = bf16[3072,256]{1,0:T(8,128)(2,1)} custom-call(s32[2,3]{1,0:T(2,128)S(1)} %bitcast.28, s32[12,6]{1,0:T(8,128)S(1)} %pad_add_fusion.mask_ref.refs_1_, bf16[3072,768]{1,0:T(8,128)(2,1)S(1)} %bitcast.15, bf16[3072,768]{1,0:T(8,128)(2,1)} %collective-permute-done.1.other_ref.refs_3_, bf16[8,2,64,256]{3,2,1,0:T(8,128)(2,1)S(1)} %bitcast.20, ...), custom_call_target="tpu_custom_call" | custom-call | flops 603979776 | bytes 2752512 | tf_op jit(solution)/shard_map/join_part/pallas_call | solution.py:183
  117.0 0.0 collective-permute-done.8.refs_6_
  117.0 0.8 collective-permute-start.4
  117.9 0.0 collective-permute-done.7.refs_5_
  117.9 3.6 %join_part.5.refs_7_ = bf16[3072,256]{1,0:T(8,128)(2,1)} custom-call(s32[2,3]{1,0:T(2,128)S(1)} %bitcast.29, s32[12,6]{1,0:T(8,128)S(1)} %pad_add_fusion.mask_ref.refs_1_, bf16[3072,768]{1,0:T(8,128)(2,1)S(1)} %bitcast.15, bf16[3072,768]{1,0:T(8,128)(2,1)} %collective-permute-done.1.other_ref.refs_3_, ...), custom_call_target="tpu_custom_call", output_to_operand_aliasing={{}: (7, {})} | custom-call | flops 603979776 | bytes 2752512 | tf_op jit(solution)/shard_map/join_part/pallas_call | solution.py:183
  121.5 0.0 collective-permute-done.6.refs_6_
  121.5 0.0 collective-permute-done.5.refs_5_
  121.5 3.6 %join_part.6.refs_7_ = bf16[3072,256]{1,0:T(8,128)(2,1)} custom-call(s32[2,3]{1,0:T(2,128)S(1)} %bitcast.30, s32[12,6]{1,0:T(8,128)S(1)} %pad_add_fusion.mask_ref.refs_1_, bf16[3072,768]{1,0:T(8,128)(2,1)S(1)} %bitcast.15, bf16[3072,768]{1,0:T(8,128)(2,1)} %collective-permute-done.1.other_ref.refs_3_, ...), custom_call_target="tpu_custom_call", output_to_operand_aliasing={{}: (7, {})} | custom-call | flops 603979776 | bytes 2752512 | tf_op jit(solution)/shard_map/join_part/pallas_call | solution.py:183
  125.1 0.0 collective-permute-done.4.refs_6_
  125.2 0.0 collective-permute-done.3.refs_5_
  125.2 3.6 %join_part.7 = bf16[3072,256]{1,0:T(8,128)(2,1)} custom-call(s32[2,3]{1,0:T(2,128)S(1)} %bitcast.31, s32[12,6]{1,0:T(8,128)S(1)} %pad_add_fusion.mask_ref.refs_1_, bf16[3072,768]{1,0:T(8,128)(2,1)S(1)} %bitcast.15, bf16[3072,768]{1,0:T(8,128)(2,1)} %collective-permute-done.1.other_ref.refs_3_, ...), custom_call_target="tpu_custom_call", output_to_operand_aliasing={{}: (7, {})} | custom-call | flops 603979776 | bytes 2752512 | tf_op jit(solution)/shard_map/join_part/pallas_call | solution.py:183
  (11 shorter events, 0.1 us)
Async XLA Ops:
  0.0 10.4 %copy-start.2 = (s32[12,3]{0,1:T(4,128)S(1)}, s32[12,3]{0,1:T(4,128)}, u32[]{:S(2)}) copy-start(s32[12,3]{0,1:T(4,128)} %param.7) | copy-start | bytes 436
  0.0 10.7 %copy-start.1 = (s32[4,1]{0,1:T(1,128)S(1)}, s32[4,1]{0,1:T(1,128)}, u32[]{:S(2)}) copy-start(s32[4,1]{0,1:T(1,128)} %param.11) | copy-start | bytes 52
  0.0 57.2 %collective-permute-start.1 = (bf16[3072,768]{1,0:T(8,128)(2,1)}, bf16[3072,768]{1,0:T(8,128)(2,1)}, u32[]{:S(2)}, u32[]{:S(2)}) collective-permute-start(bf16[3072,768]{1,0:T(8,128)(2,1)} %refs_2_.7), channel_id=1, source_target_pairs={{0,1},{1,0},{2,3},{3,2},{4,5},{5,4},{6,7},{7,6},{8,9},{9,8},{10,11... | collective-permute-start | bytes 14155784 | tf_op jit(solution)/shard_map/ppermute | solution.py:98
  3.6 17.8 %all-to-all-start = ((bf16[8,80,256]{2,1,0:T(8,128)(2,1)}), bf16[8,80,256]{2,1,0:T(8,128)(2,1)S(1)}, u32[]{:S(2)}, u32[]{:S(2)}) async-start(bf16[8,80,256]{2,1,0:T(8,128)(2,1)} %pad_maximum_fusion), calls=%async_computation | async-start | bytes 655360 | tf_op jit(solution)/shard_map/all_to_all | solution.py:107
  10.5 8.5 %collective-permute-start = (s32[12,3]{1,0:T(8,128)S(1)}, s32[12,3]{1,0:T(8,128)S(1)}, u32[]{:S(2)}, u32[]{:S(2)}) collective-permute-start(s32[12,3]{1,0:T(8,128)S(1)} %copy.17), channel_id=1, source_target_pairs={{0,1},{1,0},{2,3},{3,2},{4,5},{5,4},{6,7},{7,6},{8,9},{9,8},{10,11... | collective-permute-start | bytes 440 | tf_op jit(solution)/shard_map/ppermute | solution.py:99
  21.4 4.5 %collective-permute-start.2 = (bf16[2,80,256]{2,1,0:T(8,128)(2,1)S(1)}, bf16[2,80,256]{2,1,0:T(8,128)(2,1)S(1)}, u32[]{:S(2)}, u32[]{:S(2)}) collective-permute-start(bf16[2,80,256]{2,1,0:T(8,128)(2,1)S(1)} %pad_maximum_fusion.1), channel_id=1, source_target_pairs={{0,2},{1,3},{2,0},{3,1},{4,6},{5,7},{6,4},{7,5},{8,10},{9,11},{10,... | collective-permute-start | bytes 245768 | tf_op jit(solution)/shard_map/ppermute | solution.py:118
  57.2 2.3 %copy-start = (bf16[3072,768]{1,0:T(8,128)(2,1)S(1)}, bf16[3072,768]{1,0:T(8,128)(2,1)}, u32[]{:S(2)}) copy-start(bf16[3072,768]{1,0:T(8,128)(2,1)} %refs_2_.7) | copy-start | bytes 14155780
  62.6 49.6 %collective-permute-start.9 = (s16[768,256]{1,0:T(8,128)(2,1)S(1)}, s16[768,256]{1,0:T(8,128)(2,1)S(1)}, u32[]{:S(2)}, u32[]{:S(2)}) collective-permute-start(s16[768,256]{1,0:T(8,128)(2,1)S(1)} %get-tuple-element.19), channel_id=1, source_target_pairs={{0,2},{1,3},{2,0},{3,1},{4,6},{5,7},{6,4},{7,5},{8,10},{9,11},{10,... | collective-permute-start | bytes 1179656 | tf_op jit(solution)/shard_map/ppermute | solution.py:166
  67.1 50.8 %collective-permute-start.7 = (s16[768,256]{1,0:T(8,128)(2,1)S(1)}, s16[768,256]{1,0:T(8,128)(2,1)S(1)}, u32[]{:S(2)}, u32[]{:S(2)}) collective-permute-start(s16[768,256]{1,0:T(8,128)(2,1)S(1)} %get-tuple-element.17), channel_id=1, source_target_pairs={{0,2},{1,3},{2,0},{3,1},{4,6},{5,7},{6,4},{7,5},{8,10},{9,11},{10,... | collective-permute-start | bytes 1179656 | tf_op jit(solution)/shard_map/ppermute | solution.py:166
  70.7 42.7 %slice-start = ((s8[4718592]{0:T(1024)(128)(4,1)}), s8[4194304]{0:T(1024)(128)(4,1)S(1)}, s32[]{:S(2)}) async-start(s8[4718592]{0:T(1024)(128)(4,1)} %bitcast.14), calls=%async_computation.1 | async-start | bytes 8388608
  70.7 42.7 %slice-start.1 = ((s8[4718592]{0:T(1024)(128)(4,1)}), s8[524288]{0:T(1024)(128)(4,1)S(1)}, s32[]{:S(2)}) async-start(s8[4718592]{0:T(1024)(128)(4,1)} %bitcast.14), calls=%async_computation.2 | async-start | bytes 1048576
  70.7 50.8 %collective-permute-start.5 = (s16[768,256]{1,0:T(8,128)(2,1)S(1)}, s16[768,256]{1,0:T(8,128)(2,1)S(1)}, u32[]{:S(2)}, u32[]{:S(2)}) collective-permute-start(s16[768,256]{1,0:T(8,128)(2,1)S(1)} %get-tuple-element.15), channel_id=1, source_target_pairs={{0,2},{1,3},{2,0},{3,1},{4,6},{5,7},{6,4},{7,5},{8,10},{9,11},{10,... | collective-permute-start | bytes 1179656 | tf_op jit(solution)/shard_map/ppermute | solution.py:166
  75.3 49.9 %collective-permute-start.3 = (s16[768,256]{1,0:T(8,128)(2,1)S(1)}, s16[768,256]{1,0:T(8,128)(2,1)S(1)}, u32[]{:S(2)}, u32[]{:S(2)}) collective-permute-start(s16[768,256]{1,0:T(8,128)(2,1)S(1)} %get-tuple-element.13), channel_id=1, source_target_pairs={{0,2},{1,3},{2,0},{3,1},{4,6},{5,7},{6,4},{7,5},{8,10},{9,11},{10,... | collective-permute-start | bytes 1179656 | tf_op jit(solution)/shard_map/ppermute | solution.py:166
  107.7 3.7 %collective-permute-start.10 = (f32[8,256]{1,0:T(8,128)S(1)}, f32[8,256]{1,0:T(8,128)S(1)}, u32[]{:S(2)}, u32[]{:S(2)}) collective-permute-start(f32[8,256]{1,0:T(8,128)S(1)} %get-tuple-element.20), channel_id=1, source_target_pairs={{0,2},{1,3},{2,0},{3,1},{4,6},{5,7},{6,4},{7,5},{8,10},{9,11},{10,... | collective-permute-start | bytes 24584 | tf_op jit(solution)/shard_map/ppermute | solution.py:166
  111.3 5.7 %collective-permute-start.8 = (f32[8,256]{1,0:T(8,128)S(1)}, f32[8,256]{1,0:T(8,128)S(1)}, u32[]{:S(2)}, u32[]{:S(2)}) collective-permute-start(f32[8,256]{1,0:T(8,128)S(1)} %get-tuple-element.18), channel_id=1, source_target_pairs={{0,2},{1,3},{2,0},{3,1},{4,6},{5,7},{6,4},{7,5},{8,10},{9,11},{10,... | collective-permute-start | bytes 24584 | tf_op jit(solution)/shard_map/ppermute | solution.py:166
  112.2 9.3 %collective-permute-start.6 = (f32[8,256]{1,0:T(8,128)S(1)}, f32[8,256]{1,0:T(8,128)S(1)}, u32[]{:S(2)}, u32[]{:S(2)}) collective-permute-start(f32[8,256]{1,0:T(8,128)S(1)} %get-tuple-element.16), channel_id=1, source_target_pairs={{0,2},{1,3},{2,0},{3,1},{4,6},{5,7},{6,4},{7,5},{8,10},{9,11},{10,... | collective-permute-start | bytes 24584 | tf_op jit(solution)/shard_map/ppermute | solution.py:166
  117.0 8.1 %collective-permute-start.4 = (f32[8,256]{1,0:T(8,128)S(1)}, f32[8,256]{1,0:T(8,128)S(1)}, u32[]{:S(2)}, u32[]{:S(2)}) collective-permute-start(f32[8,256]{1,0:T(8,128)S(1)} %get-tuple-element.14), channel_id=1, source_target_pairs={{0,2},{1,3},{2,0},{3,1},{4,6},{5,7},{6,4},{7,5},{8,10},{9,11},{10,... | collective-permute-start | bytes 24584 | tf_op jit(solution)/shard_map/ppermute | solution.py:166

commit v2 on v1

v2 whole, which is shorter than its diff:
```python
from functools import partial

import jax
import jax.numpy as jnp
from jax import lax
from jax.experimental import pallas as pl
from jax.experimental.pallas import tpu as pltpu
from jax.sharding import PartitionSpec as P

STEPS = 4
CORES = 2
CHUNKS = 4
CODE_TOP = 32767.0
META_ROWS = 16
META_TILE = (8, 128)
PARAMS = pltpu.CompilerParams(vmem_limit_bytes=56 * 1024 * 1024)
SMEM = pl.BlockSpec(memory_space=pltpu.SMEM)
VMEM = pl.BlockSpec(memory_space=pltpu.VMEM)


def pair_offsets(col_count):
    pairs = col_count // CORES
    offsets = set()
    for core in range(CORES):
        for step in range(STEPS):
            offsets.add(-((core - step) // CORES) % pairs)
    return sorted(offsets)


def pack_kernel(list_ref, count_ref, panel_ref, pieces_ref):
    peers, height, _ = pieces_ref.shape
    slots, tile_width = panel_ref.shape[2:4]
    share = height - META_ROWS
    lane = lax.broadcasted_iota(jnp.int32, (META_ROWS, pieces_ref.shape[2]), 1)
    info = jnp.where(lane == slots, count_ref[0, 0], 0)
    for slot in range(slots):
        info = jnp.where(lane == slot, list_ref[0, 0, slot], info)
    info = info.astype(jnp.float32).astype(pieces_ref.dtype)
    for peer in range(peers):
        slot, start = divmod(peer * share, tile_width)
        pieces_ref[peer, pl.ds(0, share), :] = panel_ref[0, 0, slot, pl.ds(start, share), :]
        pieces_ref[peer, pl.ds(share, META_ROWS), :] = info


def choose_kernel(col_peers, offsets, owner_ref, place_ref, pieces_ref, *out_refs):
    share = pieces_ref.shape[1] - META_ROWS
    core = lax.rem(place_ref[0], CORES)
    sign = 1 - 2 * core
    for number, offset in enumerate(offsets):
        data_ref, info_ref = out_refs[2 * number : 2 * number + 2]
        rows = []
        for group, shift in enumerate((0, sign)):
            step = lax.rem(CORES * offset - shift + col_peers, col_peers)
            used = step < STEPS
            holder = owner_ref[jnp.minimum(step, STEPS - 1), 0]
            data_ref[pl.ds(group * share, share), :] = pieces_ref[holder, pl.ds(0, share), :]
            info = pieces_ref[holder, pl.ds(share, META_ROWS), :].astype(jnp.float32).astype(jnp.int32)
            rows.append(jnp.where(used, info[: META_TILE[0], : META_TILE[1]], 0))
        line = lax.broadcasted_iota(jnp.int32, META_TILE, 0)
        info_ref[...] = jnp.where(line == 0, rows[0], rows[1])


def fill_weights(row_place, info_ref, piece_refs, dense_ref, tile_width, slots):
    peers = len(piece_refs)
    share = piece_refs[0].shape[0] // CORES
    width = dense_ref.shape[0] // CORES
    dense_ref[...] = jnp.zeros_like(dense_ref)
    for shift, piece_ref in enumerate(piece_refs):
        first = lax.rem(row_place - shift + peers, peers) * share
        slot = first // tile_width
        for group in range(CORES):

            @pl.when(slot < info_ref[group, slots])
            def _():
                start = group * width + info_ref[group, slot] * tile_width + lax.rem(first, tile_width)
                dense_ref[pl.ds(pl.multiple_of(start, 16), share), :] = piece_ref[pl.ds(group * share, share), :]


def block_product(mask_refs, row_block, own_ref, other_ref, dense_ref, tile_width):
    tiles = own_ref.shape[1] // tile_width
    width = tiles * tile_width
    total = None
    for group, source in enumerate((own_ref, other_ref)):
        screened = []
        for tile in range(tiles):
            live = mask_refs[group][row_block, tile].astype(jnp.float32).astype(jnp.bfloat16)
            screened.append(source[:, pl.ds(tile * tile_width, tile_width)] * live)
        term = jnp.dot(
            jnp.concatenate(screened, axis=1),
            dense_ref[pl.ds(group * width, width), :],
            preferred_element_type=jnp.float32,
        )
        total = term if total is None else total + term
    return total


def send_kernel(first, tile_width, slots, peers, *refs):
    place_ref, info_ref, mask_ref, other_mask_ref, own_ref, other_ref = refs[:6]
    piece_refs = refs[6 : 6 + peers]
    code_ref, scale_ref, dense_ref = refs[6 + peers :]
    step = pl.program_id(0)

    @pl.when(step == 0)
    def _():
        fill_weights(place_ref[0], info_ref, piece_refs, dense_ref, tile_width, slots)

    total = block_product((mask_ref, other_mask_ref), first + step, own_ref, other_ref, dense_ref, tile_width)
    top = jnp.max(jnp.abs(total), axis=0, keepdims=True)
    safe = jnp.where(top > 0, top, 1.0)
    code_ref[...] = jnp.round(total * (CODE_TOP / safe)).astype(jnp.int32).astype(jnp.int16)
    scale_ref[pl.ds(step, 1), :] = safe * (1.0 / CODE_TOP)


def join_kernel(first, tile_width, slots, peers, arrivals, *refs):
    place_ref, info_ref, mask_ref, other_mask_ref, own_ref, other_ref = refs[:6]
    piece_refs = refs[6 : 6 + peers]
    code_refs = refs[6 + peers : 6 + peers + arrivals]
    scale_refs = refs[6 + peers + arrivals : 6 + peers + 2 * arrivals]
    out_ref, dense_ref = refs[-2:]
    step = pl.program_id(0)

    @pl.when(step == 0)
    def _():
        fill_weights(place_ref[0], info_ref, piece_refs, dense_ref, tile_width, slots)

    total = block_product((mask_ref, other_mask_ref), first + step, own_ref, other_ref, dense_ref, tile_width)
    for code_ref, scale_ref in zip(code_refs, scale_refs):
        total = total + code_ref[...].astype(jnp.int32).astype(jnp.float32) * scale_ref[pl.ds(step, 1), :]
    out_ref[...] = total.astype(out_ref.dtype)


def shards(amplitudes, pair_mask, integrals, tile_list, tile_count, owner):
    row_count, full_width = amplitudes.shape
    slots, tile_width = integrals.shape[2], integrals.shape[-1]
    block_count = pair_mask.shape[0]
    block_rows = row_count // block_count
    row_peers, col_peers = lax.axis_size("row"), lax.axis_size("col")
    share = slots * tile_width // row_peers
    offsets = pair_offsets(col_peers)
    row_place = lax.axis_index("row").reshape(1)
    col_place = lax.axis_index("col").reshape(1)

    swap = [(c, c ^ 1) for c in range(col_peers)]
    other = lax.ppermute(amplitudes, "col", swap)
    other_mask = lax.ppermute(pair_mask, "col", swap)

    pieces = pl.pallas_call(
        pack_kernel,
        in_specs=[SMEM, SMEM, VMEM],
        out_specs=VMEM,
        out_shape=jax.ShapeDtypeStruct((row_peers, share + META_ROWS, tile_width), integrals.dtype),
        compiler_params=PARAMS,
        name="pack",
    )(tile_list, tile_count, integrals)
    pieces = lax.all_to_all(pieces, "row", 0, 0)
    chosen = pl.pallas_call(
        partial(choose_kernel, col_peers, offsets),
        in_specs=[SMEM, SMEM, VMEM],
        out_specs=[VMEM] * (2 * len(offsets)),
        out_shape=[
            jax.ShapeDtypeStruct((CORES * share, tile_width), integrals.dtype),
            jax.ShapeDtypeStruct(META_TILE, jnp.int32),
        ]
        * len(offsets),
        compiler_params=PARAMS,
        name="choose",
    )(owner, col_place, pieces)

    plans = {}
    for number, offset in reversed(list(enumerate(offsets))):
        data, info = chosen[2 * number : 2 * number + 2]
        if offset:
            down = [(c, (c - CORES * offset) % col_peers) for c in range(col_peers)]
            data, info = lax.ppermute(data, "col", down), lax.ppermute(info, "col", down)
        spread = [data]
        for shift in range(1, row_peers):
            spread.append(lax.ppermute(data, "row", [(r, (r + shift) % row_peers) for r in range(row_peers)]))
        plans[offset] = (info, spread)

    chunks = CHUNKS if block_count % CHUNKS == 0 else 1
    span = block_count // chunks

    def inputs(first):
        rows = pl.BlockSpec((block_rows, full_width), lambda i: (first + i, 0))
        piece = pl.BlockSpec((CORES * share, tile_width), lambda i: (0, 0))
        return [SMEM, SMEM, SMEM, SMEM, rows, rows] + [piece] * row_peers

    codes = pl.BlockSpec((block_rows, tile_width), lambda i: (i, 0))
    scale_rows = -(-span // 8) * 8
    scales = pl.BlockSpec((scale_rows, tile_width), lambda i: (0, 0))
    dense = pltpu.VMEM((CORES * full_width, tile_width), jnp.bfloat16)
    cost = pl.CostEstimate(
        flops=2 * span * block_rows * CORES * full_width * tile_width,
        bytes_accessed=span * block_rows * (CORES * full_width + tile_width) * 2,
        transcendentals=0,
    )

    arrived = []
    for chunk in range(chunks):
        first = chunk * span
        received = []
        for offset in offsets:
            if offset == 0:
                continue
            info, spread = plans[offset]
            code, scale = pl.pallas_call(
                partial(send_kernel, first, tile_width, slots, row_peers),
                grid=(span,),
                in_specs=inputs(first),
                out_specs=[codes, scales],
                out_shape=[
                    jax.ShapeDtypeStruct((span * block_rows, tile_width), jnp.int16),
                    jax.ShapeDtypeStruct((scale_rows, tile_width), jnp.float32),
                ],
                scratch_shapes=[dense],
                compiler_params=PARAMS,
                cost_estimate=cost,
                name="send_part",
            )(row_place, info, pair_mask, other_mask, amplitudes, other, *spread)
            up = [(c, (c + CORES * offset) % col_peers) for c in range(col_peers)]
            received.append((lax.ppermute(code, "col", up), lax.ppermute(scale, "col", up)))
        arrived.append(received)

    out = None
    info, spread = plans[0]
    for chunk in range(chunks):
        first = chunk * span
        arrivals = len(arrived[chunk])
        operands = [row_place, info, pair_mask, other_mask, amplitudes, other, *spread]
        operands += [code for code, _ in arrived[chunk]] + [scale for _, scale in arrived[chunk]]
        specs = inputs(first) + [codes] * arrivals + [scales] * arrivals
        body = partial(join_kernel, first, tile_width, slots, row_peers, arrivals)
        aliases = {}
        if out is not None:
            body = partial(skip_operand, len(operands), body)
            aliases = {len(operands): 0}
            operands.append(out)
            specs.append(pl.BlockSpec(memory_space=pl.ANY))
        out = pl.pallas_call(
            body,
            grid=(span,),
            in_specs=specs,
            out_specs=pl.BlockSpec((block_rows, tile_width), lambda i, first=first: (first + i, 0)),
            out_shape=jax.ShapeDtypeStruct((row_count, tile_width), jnp.bfloat16),
            scratch_shapes=[dense],
            input_output_aliases=aliases,
            compiler_params=PARAMS,
            cost_estimate=cost,
            name="join_part",
        )(*operands)
    return out


def skip_operand(position, body, *refs):
    body(*refs[:position], *refs[position + 1 :])


def solution(mesh):
    return jax.shard_map(
        shards,
        mesh=mesh,
        in_specs=(
            P("row", "col"),
            P("row", "col"),
            P("row", "col", None, None, None),
            P("row", "col", None),
            P("row", "col"),
            P(None, "col"),
        ),
        out_specs=P("row", "col"),
        check_vma=False,
    )
```

time: 130 us -> 119 us (0.915)
  blocking collectives: 62.9 us -> 0 us
  starting transfers between devices: 17.4 us -> 44.4 us
  waiting for transfers between devices: 7.95 us -> 29.3 us
  Pallas kernels: 26.5 us -> 37.5 us
  between operations: 8.42 us -> 0.92 us
  local copies, waits for them, and re-layouts: 4.09 us -> 6.31 us
  other arithmetic: 1.6 us -> 0 us
    all_gather x2 -> x0, blocking collectives: 62.9 us -> none  [wanted(): return (info, lax.all_gather(chosen[:, :slots * depth], 'row'))]
    ppermute x1 -> x16, starting transfers between devices: 1.56 us -> 27.9 us  [the longest x14 24.9 us: shards(): lax.ppermute(data, 'row', [(r, (r + shift) % row_peers) for r in range(ro...]
    ppermute x1 -> x16, waiting for transfers between devices: 2.94 us -> 16.3 us  [the longest x14 11 us: shards(): lax.ppermute(data, 'row', [(r, (r + shift) % row_peers) for r in range(ro...]
    pallas_call x4 -> x6, Pallas kernels: 11.9 us -> 20.2 us  [the longest x4 16.9 us: shards(): pl.pallas_call(partial(send_kernel, first, tile_width, slots, row_peers),...]
    all_to_all x1, waiting for transfers between devices: 2.21 us -> 9.63 us  [shards(): pieces = lax.all_to_all(pieces, 'row', 0, 0)]
    unnamed x11 -> x68, local copies, waits for them, and re-layouts: 2.45 us -> 6.31 us
    pallas_call x4, Pallas kernels: 14.6 us -> 17.2 us  [shards(): pl.pallas_call(body, grid=(span,), in_specs=specs, out_specs=pl.BlockSpec...]
    concatenate x4 -> x0, other arithmetic: 1.56 us -> none  [the longest x1 0.75 us: shards(): jnp.concatenate([pieces, jnp.broadcast_to(info, (row_peers, META_ROWS, ti...]
  transfers between devices with their start and end apart: 12 -> 27, of which waited for: 3 -> 11; matrix products, arithmetic and copies ran while one was open for 3% -> 1% of each run, Pallas kernels for 15% -> 28%
where the time goes in v2:
time: 119 us; the launch traced here: 118 us
  starting transfers between devices  44.4 us (37%)
  Pallas kernels  37.5 us (32%)
  waiting for transfers between devices  29.3 us (25%)
  local copies, waits for them, and re-layouts  6.31 us (5%)
    ppermute x14, starting transfers between devices, shards(): lax.ppermute(data, 'row', [(r, (r + shift) % row_peers) for r in range(ro...  24.9 us
    pallas_call x4, Pallas kernels, shards(): pl.pallas_call(body, grid=(span,), in_specs=specs, out_specs=pl.BlockSpec...  17.2 us
    pallas_call x4, Pallas kernels, shards(): pl.pallas_call(partial(send_kernel, first, tile_width, slots, row_peers),...  16.9 us
    ppermute x14, waiting for transfers between devices, shards(): lax.ppermute(data, 'row', [(r, (r + shift) % row_peers) for r in range(ro...  11 us
    all_to_all x1, waiting for transfers between devices, shards(): pieces = lax.all_to_all(pieces, 'row', 0, 0)  9.63 us
    all_to_all x1, starting transfers between devices, shards(): pieces = lax.all_to_all(pieces, 'row', 0, 0)  6.84 us
    unnamed x68, local copies, waits for them, and re-layouts  6.31 us
    ppermute x4, starting transfers between devices, shards(): lax.ppermute(scale, 'col', up)  5.05 us
  transfers between devices with their start and end apart: 27, of which 11 were waited for; matrix products, arithmetic and copies ran while one was open for 1% of the time, Pallas kernels for 28%

profile of v2, /device:TPU:0, one launch (start us, length us, event | category | flops | bytes accessed | tf_op | source)
XLA Modules:
  0.0 118.4 jit_solution(984064688188237951)
XLA Ops:
  1.1 1.7 %pack.1 = bf16[8,80,256]{2,1,0:T(8,128)(2,1)} custom-call(s32[1,1,2]{2,1,0:T(1,128)} %list_ref.1, s32[1,1]{1,0:T(1,128)S(6)} %copy.23.count_ref, bf16[1,1,2,256,256]{4,3,2,1,0:T(8,128)(2,1)} %panel_ref.1), custom_call_target="tpu_custom_call" | custom-call | tf_op jit(solution)/shard_map/pack/pallas_call | solution.py:147
  2.8 6.8 %all-to-all-start = ((bf16[8,80,256]{2,1,0:T(8,128)(2,1)}), bf16[8,80,256]{2,1,0:T(8,128)(2,1)S(1)}, u32[]{:S(2)}, u32[]{:S(2)}) async-start(bf16[8,80,256]{2,1,0:T(8,128)(2,1)} %pack.1), calls=%async_computation | async-start | bytes 655360 | tf_op jit(solution)/shard_map/all_to_all | solution.py:155
  9.7 1.3 %copy.10.owner_ref = s32[4,1]{1,0:T(4,128)} copy(s32[4,1]{0,1:T(1,128)} %param.11) | data formatting | bytes 32 | tf_op args[5]
  11.0 9.6 %all-to-all-done.pieces_ref = bf16[8,80,256]{2,1,0:T(8,128)(2,1)S(1)} async-done(((bf16[8,80,256]{2,1,0:T(8,128)(2,1)}), bf16[8,80,256]{2,1,0:T(8,128)(2,1)S(1)}, u32[]{:S(2)}, u32[]{:S(2)}) %all-to-all-start) | async-done | bytes 327712 | tf_op jit(solution)/shard_map/all_to_all | solution.py:155
  20.6 0.7 copy-done
  21.3 1.7 %choose.1 = (bf16[128,256]{1,0:T(8,128)(2,1)}, s32[8,128]{1,0:T(8,128)}, bf16[128,256]{1,0:T(8,128)(2,1)}, s32[8,128]{1,0:T(8,128)}) custom-call(s32[4,1]{1,0:T(4,128)} %copy.10.owner_ref, s32[1]{0:T(128)} %bitcast.1.place_ref, bf16[8,80,256]{2,1,0:T(8,128)(2,1)} %copy-done), custom_call_target="tpu_custom_call" | custom-call | tf_op jit(solution)/shard_map/choose/pallas_call | solution.py:156
  23.0 1.5 %collective-permute-start.10 = (bf16[128,256]{1,0:T(8,128)(2,1)}, bf16[128,256]{1,0:T(8,128)(2,1)S(1)}, u32[]{:S(2)}, u32[]{:S(2)}) collective-permute-start(bf16[128,256]{1,0:T(8,128)(2,1)} %get-tuple-element.20), channel_id=1, source_target_pairs={{0,2},{1,3},{2,0},{3,1},{4,6},{5,7},{6,4},{7,5},{8,10},{9,11},{10,... | collective-permute-start | bytes 196616 | tf_op jit(solution)/shard_map/ppermute | solution.py:174
  24.5 3.0 %collective-permute-done.10.refs_6_ = bf16[128,256]{1,0:T(8,128)(2,1)S(1)} collective-permute-done((bf16[128,256]{1,0:T(8,128)(2,1)}, bf16[128,256]{1,0:T(8,128)(2,1)S(1)}, u32[]{:S(2)}, u32[]{:S(2)}) %collective-permute-start.10) | collective-permute-done | bytes 65568 | tf_op jit(solution)/shard_map/ppermute | solution.py:174
  27.4 1.5 %collective-permute-start.11 = (bf16[128,256]{1,0:T(8,128)(2,1)S(1)}, bf16[128,256]{1,0:T(8,128)(2,1)S(1)}, u32[]{:S(2)}, u32[]{:S(2)}) collective-permute-start(bf16[128,256]{1,0:T(8,128)(2,1)S(1)} %collective-permute-done.10.refs_6_), channel_id=1, source_target_pairs={{0,4},{4,8},{8,12},{12,16},{16,20},{20,24},{24,28},{28,0},{1,5},{5... | collective-permute-start | bytes 196616 | tf_op jit(solution)/shard_map/ppermute | solution.py:177
  28.9 1.7 %collective-permute-start.13 = (bf16[128,256]{1,0:T(8,128)(2,1)S(1)}, bf16[128,256]{1,0:T(8,128)(2,1)S(1)}, u32[]{:S(2)}, u32[]{:S(2)}) collective-permute-start(bf16[128,256]{1,0:T(8,128)(2,1)S(1)} %collective-permute-done.10.refs_6_), channel_id=1, source_target_pairs={{0,12},{4,16},{8,20},{12,24},{16,28},{20,0},{24,4},{28,8},{1,13},{... | collective-permute-start | bytes 196616 | tf_op jit(solution)/shard_map/ppermute | solution.py:177
  30.8 1.2 collective-permute-done.refs_3_
  31.9 1.5 %collective-permute-start.9 = (s32[8,128]{1,0:T(8,128)}, s32[8,128]{1,0:T(8,128)S(1)}, u32[]{:S(2)}, u32[]{:S(2)}) collective-permute-start(s32[8,128]{1,0:T(8,128)} %get-tuple-element.19), channel_id=1, source_target_pairs={{0,2},{1,3},{2,0},{3,1},{4,6},{5,7},{6,4},{7,5},{8,10},{9,11},{10,... | collective-permute-start | bytes 12296 | tf_op jit(solution)/shard_map/ppermute | solution.py:174
  33.4 2.3 %collective-permute-done.9.refs_1_ = s32[8,128]{1,0:T(8,128)S(1)} collective-permute-done((s32[8,128]{1,0:T(8,128)}, s32[8,128]{1,0:T(8,128)S(1)}, u32[]{:S(2)}, u32[]{:S(2)}) %collective-permute-start.9) | collective-permute-done | bytes 4128 | tf_op jit(solution)/shard_map/ppermute | solution.py:174
  35.8 3.1 %collective-permute-start.14 = (bf16[128,256]{1,0:T(8,128)(2,1)S(1)}, bf16[128,256]{1,0:T(8,128)(2,1)S(1)}, u32[]{:S(2)}, u32[]{:S(2)}) collective-permute-start(bf16[128,256]{1,0:T(8,128)(2,1)S(1)} %collective-permute-done.10.refs_6_), channel_id=1, source_target_pairs={{0,16},{4,20},{8,24},{12,28},{16,0},{20,4},{24,8},{28,12},{1,17},{... | collective-permute-start | bytes 196616 | tf_op jit(solution)/shard_map/ppermute | solution.py:177
  38.9 1.0 collective-permute-start.15
  39.9 1.9 %collective-permute-start.16 = (bf16[128,256]{1,0:T(8,128)(2,1)S(1)}, bf16[128,256]{1,0:T(8,128)(2,1)S(1)}, u32[]{:S(2)}, u32[]{:S(2)}) collective-permute-start(bf16[128,256]{1,0:T(8,128)(2,1)S(1)} %collective-permute-done.10.refs_6_), channel_id=1, source_target_pairs={{0,24},{4,28},{8,0},{12,4},{16,8},{20,12},{24,16},{28,20},{1,25},{... | collective-permute-start | bytes 196616 | tf_op jit(solution)/shard_map/ppermute | solution.py:177
  41.7 1.1 collective-permute-start.17
  42.9 1.6 %collective-permute-done.14.refs_10_ = bf16[128,256]{1,0:T(8,128)(2,1)S(1)} collective-permute-done((bf16[128,256]{1,0:T(8,128)(2,1)S(1)}, bf16[128,256]{1,0:T(8,128)(2,1)S(1)}, u32[]{:S(2)}, u32[]{:S(2)}) %collective-permute-start.14) | collective-permute-done | bytes 65568 | tf_op jit(solution)/shard_map/ppermute | solution.py:177
  44.7 1.3 %collective-permute-done.17.refs_13_ = bf16[128,256]{1,0:T(8,128)(2,1)S(1)} collective-permute-done((bf16[128,256]{1,0:T(8,128)(2,1)S(1)}, bf16[128,256]{1,0:T(8,128)(2,1)S(1)}, u32[]{:S(2)}, u32[]{:S(2)}) %collective-permute-start.17) | collective-permute-done | bytes 65568 | tf_op jit(solution)/shard_map/ppermute | solution.py:177
  46.6 4.2 %send_part.7 = (s16[768,256]{1,0:T(8,128)(2,1)}, f32[8,256]{1,0:T(8,128)}) custom-call(s32[1]{0:T(128)} %bitcast.refs_0_, s32[8,128]{1,0:T(8,128)} %copy-done.23, s32[12,3]{1,0:T(8,128)} %copy-done.17, s32[12,3]{1,0:T(8,128)} %copy-done.18, bf16[3072,768]{1,0:T(8,128)(2,1)} %refs_4_.15, bf16[3072,768]{1,0:T(8,128)(2,1)} %collective-permute-done.1.refs_5_, ...), custom_call_target="tpu_custom_call" | custom-call | flops 603979776 | bytes 2752512 | tf_op jit(solution)/shard_map/send_part/pallas_call | solution.py:206
  50.9 1.5 %collective-permute-start.24 = (s16[768,256]{1,0:T(8,128)(2,1)}, s16[768,256]{1,0:T(8,128)(2,1)S(1)}, u32[]{:S(2)}, u32[]{:S(2)}) collective-permute-start(s16[768,256]{1,0:T(8,128)(2,1)} %get-tuple-element.27), channel_id=1, source_target_pairs={{0,2},{1,3},{2,0},{3,1},{4,6},{5,7},{6,4},{7,5},{8,10},{9,11},{10,... | collective-permute-start | bytes 1179656 | tf_op jit(solution)/shard_map/ppermute | solution.py:221
  52.4 1.7 %collective-permute-start.3 = (bf16[128,256]{1,0:T(8,128)(2,1)S(1)}, bf16[128,256]{1,0:T(8,128)(2,1)S(1)}, u32[]{:S(2)}, u32[]{:S(2)}) collective-permute-start(bf16[128,256]{1,0:T(8,128)(2,1)S(1)} %copy-done.1), channel_id=1, source_target_pairs={{0,8},{4,12},{8,16},{12,20},{16,24},{20,28},{24,0},{28,4},{1,9},{5... | collective-permute-start | bytes 196616 | tf_op jit(solution)/shard_map/ppermute | solution.py:177
  54.1 2.7 %collective-permute-start.4 = (bf16[128,256]{1,0:T(8,128)(2,1)S(1)}, bf16[128,256]{1,0:T(8,128)(2,1)S(1)}, u32[]{:S(2)}, u32[]{:S(2)}) collective-permute-start(bf16[128,256]{1,0:T(8,128)(2,1)S(1)} %copy-done.1), channel_id=1, source_target_pairs={{0,12},{4,16},{8,20},{12,24},{16,28},{20,0},{24,4},{28,8},{1,13},{... | collective-permute-start | bytes 196616 | tf_op jit(solution)/shard_map/ppermute | solution.py:177
  56.7 4.2 %send_part.6 = (s16[768,256]{1,0:T(8,128)(2,1)}, f32[8,256]{1,0:T(8,128)}) custom-call(s32[1]{0:T(128)} %bitcast.refs_0_, s32[8,128]{1,0:T(8,128)} %copy-done.23, s32[12,3]{1,0:T(8,128)} %copy-done.17, s32[12,3]{1,0:T(8,128)} %copy-done.18, bf16[3072,768]{1,0:T(8,128)(2,1)} %refs_4_.15, bf16[3072,768]{1,0:T(8,128)(2,1)} %collective-permute-done.1.refs_5_, ...), custom_call_target="tpu_custom_call" | custom-call | flops 603979776 | bytes 2752512 | tf_op jit(solution)/shard_map/send_part/pallas_call | solution.py:206
  61.5 4.2 %send_part.5 = (s16[768,256]{1,0:T(8,128)(2,1)}, f32[8,256]{1,0:T(8,128)}) custom-call(s32[1]{0:T(128)} %bitcast.refs_0_, s32[8,128]{1,0:T(8,128)} %copy-done.23, s32[12,3]{1,0:T(8,128)} %copy-done.17, s32[12,3]{1,0:T(8,128)} %copy-done.18, bf16[3072,768]{1,0:T(8,128)(2,1)} %refs_4_.15, bf16[3072,768]{1,0:T(8,128)(2,1)} %collective-permute-done.1.refs_5_, ...), custom_call_target="tpu_custom_call" | custom-call | flops 603979776 | bytes 2752512 | tf_op jit(solution)/shard_map/send_part/pallas_call | solution.py:206
  65.7 1.4 %collective-permute-start.5 = (bf16[128,256]{1,0:T(8,128)(2,1)S(1)}, bf16[128,256]{1,0:T(8,128)(2,1)S(1)}, u32[]{:S(2)}, u32[]{:S(2)}) collective-permute-start(bf16[128,256]{1,0:T(8,128)(2,1)S(1)} %copy-done.1), channel_id=1, source_target_pairs={{0,16},{4,20},{8,24},{12,28},{16,0},{20,4},{24,8},{28,12},{1,17},{... | collective-permute-start | bytes 196616 | tf_op jit(solution)/shard_map/ppermute | solution.py:177
  67.1 1.5 %collective-permute-start.20 = (s16[768,256]{1,0:T(8,128)(2,1)}, s16[768,256]{1,0:T(8,128)(2,1)S(1)}, u32[]{:S(2)}, u32[]{:S(2)}) collective-permute-start(s16[768,256]{1,0:T(8,128)(2,1)} %get-tuple-element.23), channel_id=1, source_target_pairs={{0,2},{1,3},{2,0},{3,1},{4,6},{5,7},{6,4},{7,5},{8,10},{9,11},{10,... | collective-permute-start | bytes 1179656 | tf_op jit(solution)/shard_map/ppermute | solution.py:221
  68.6 4.2 %send_part.4 = (s16[768,256]{1,0:T(8,128)(2,1)}, f32[8,256]{1,0:T(8,128)}) custom-call(s32[1]{0:T(128)} %bitcast.refs_0_, s32[8,128]{1,0:T(8,128)} %copy-done.23, s32[12,3]{1,0:T(8,128)} %copy-done.17, s32[12,3]{1,0:T(8,128)} %copy-done.18, bf16[3072,768]{1,0:T(8,128)(2,1)} %refs_4_.15, bf16[3072,768]{1,0:T(8,128)(2,1)} %collective-permute-done.1.refs_5_, ...), custom_call_target="tpu_custom_call" | custom-call | flops 603979776 | bytes 2752512 | tf_op jit(solution)/shard_map/send_part/pallas_call | solution.py:206
  72.9 0.6 collective-permute-start.18
  73.5 1.1 collective-permute-start.6
  74.6 4.1 %collective-permute-done.6.refs_11_ = bf16[128,256]{1,0:T(8,128)(2,1)S(1)} collective-permute-done((bf16[128,256]{1,0:T(8,128)(2,1)S(1)}, bf16[128,256]{1,0:T(8,128)(2,1)S(1)}, u32[]{:S(2)}, u32[]{:S(2)}) %collective-permute-start.6) | collective-permute-done | bytes 65568 | tf_op jit(solution)/shard_map/ppermute | solution.py:177
  78.7 4.6 %collective-permute-start.7 = (bf16[128,256]{1,0:T(8,128)(2,1)S(1)}, bf16[128,256]{1,0:T(8,128)(2,1)S(1)}, u32[]{:S(2)}, u32[]{:S(2)}) collective-permute-start(bf16[128,256]{1,0:T(8,128)(2,1)S(1)} %copy-done.1), channel_id=1, source_target_pairs={{0,24},{4,28},{8,0},{12,4},{16,8},{20,12},{24,16},{28,20},{1,25},{... | collective-permute-start | bytes 196616 | tf_op jit(solution)/shard_map/ppermute | solution.py:177
  83.2 1.9 %collective-permute-done.7.refs_12_ = bf16[128,256]{1,0:T(8,128)(2,1)S(1)} collective-permute-done((bf16[128,256]{1,0:T(8,128)(2,1)S(1)}, bf16[128,256]{1,0:T(8,128)(2,1)S(1)}, u32[]{:S(2)}, u32[]{:S(2)}) %collective-permute-start.7) | collective-permute-done | bytes 65568 | tf_op jit(solution)/shard_map/ppermute | solution.py:177
  85.1 3.2 %collective-permute-start.8 = (bf16[128,256]{1,0:T(8,128)(2,1)S(1)}, bf16[128,256]{1,0:T(8,128)(2,1)S(1)}, u32[]{:S(2)}, u32[]{:S(2)}) collective-permute-start(bf16[128,256]{1,0:T(8,128)(2,1)S(1)} %copy-done.1), channel_id=1, source_target_pairs={{0,28},{4,0},{8,4},{12,8},{16,12},{20,16},{24,20},{28,24},{1,29},{... | collective-permute-start | bytes 196616 | tf_op jit(solution)/shard_map/ppermute | solution.py:177
  88.3 1.9 %collective-permute-done.8.refs_13_ = bf16[128,256]{1,0:T(8,128)(2,1)S(1)} collective-permute-done((bf16[128,256]{1,0:T(8,128)(2,1)S(1)}, bf16[128,256]{1,0:T(8,128)(2,1)S(1)}, u32[]{:S(2)}, u32[]{:S(2)}) %collective-permute-start.8) | collective-permute-done | bytes 65568 | tf_op jit(solution)/shard_map/ppermute | solution.py:177
  90.2 1.5 %collective-permute-start.25 = (f32[8,256]{1,0:T(8,128)S(1)}, f32[8,256]{1,0:T(8,128)S(1)}, u32[]{:S(2)}, u32[]{:S(2)}) collective-permute-start(f32[8,256]{1,0:T(8,128)S(1)} %copy-done.32), channel_id=1, source_target_pairs={{0,2},{1,3},{2,0},{3,1},{4,6},{5,7},{6,4},{7,5},{8,10},{9,11},{10,... | collective-permute-start | bytes 24584 | tf_op jit(solution)/shard_map/ppermute | solution.py:221
  91.7 2.2 %collective-permute-done.25.refs_15_ = f32[8,256]{1,0:T(8,128)S(1)} collective-permute-done((f32[8,256]{1,0:T(8,128)S(1)}, f32[8,256]{1,0:T(8,128)S(1)}, u32[]{:S(2)}, u32[]{:S(2)}) %collective-permute-start.25) | collective-permute-done | bytes 8224 | tf_op jit(solution)/shard_map/ppermute | solution.py:221
  93.9 1.5 %collective-permute-start.23 = (f32[8,256]{1,0:T(8,128)S(1)}, f32[8,256]{1,0:T(8,128)S(1)}, u32[]{:S(2)}, u32[]{:S(2)}) collective-permute-start(f32[8,256]{1,0:T(8,128)S(1)} %copy-done.31), channel_id=1, source_target_pairs={{0,2},{1,3},{2,0},{3,1},{4,6},{5,7},{6,4},{7,5},{8,10},{9,11},{10,... | collective-permute-start | bytes 24584 | tf_op jit(solution)/shard_map/ppermute | solution.py:221
  95.4 0.6 collective-permute-start.21
  96.1 4.4 %join_part.4.refs_16_ = bf16[3072,256]{1,0:T(8,128)(2,1)} custom-call(s32[1]{0:T(128)} %bitcast.refs_0_, s32[8,128]{1,0:T(8,128)} %get-tuple-element.17.refs_1_, s32[12,3]{1,0:T(8,128)} %copy-done.17, s32[12,3]{1,0:T(8,128)} %copy-done.18, bf16[3072,768]{1,0:T(8,128)(2,1)} %refs_4_.15, bf16[3072,768]{1,0:T(8,128)(2,1)} %collective-permute-done.1.refs_5_, ...), custom_call_target="tpu_custom_call" | custom-call | flops 603979776 | bytes 2752512 | tf_op jit(solution)/shard_map/join_part/pallas_call | solution.py:239
  100.5 1.5 %collective-permute-start.19 = (f32[8,256]{1,0:T(8,128)S(1)}, f32[8,256]{1,0:T(8,128)S(1)}, u32[]{:S(2)}, u32[]{:S(2)}) collective-permute-start(f32[8,256]{1,0:T(8,128)S(1)} %copy-done.30), channel_id=1, source_target_pairs={{0,2},{1,3},{2,0},{3,1},{4,6},{5,7},{6,4},{7,5},{8,10},{9,11},{10,... | collective-permute-start | bytes 24584 | tf_op jit(solution)/shard_map/ppermute | solution.py:221
  102.0 0.8 copy-done.19
  102.8 4.3 %join_part.5.refs_16_ = bf16[3072,256]{1,0:T(8,128)(2,1)} custom-call(s32[1]{0:T(128)} %bitcast.refs_0_, s32[8,128]{1,0:T(8,128)} %get-tuple-element.17.refs_1_, s32[12,3]{1,0:T(8,128)} %copy-done.17, s32[12,3]{1,0:T(8,128)} %copy-done.18, bf16[3072,768]{1,0:T(8,128)(2,1)} %refs_4_.15, ...), custom_call_target="tpu_custom_call", output_to_operand_aliasing={{}: (16, {})} | custom-call | flops 603979776 | bytes 2752512 | tf_op jit(solution)/shard_map/join_part/pallas_call | solution.py:239
  107.7 0.8 copy-done.22
  108.4 4.3 %join_part.6.refs_16_ = bf16[3072,256]{1,0:T(8,128)(2,1)} custom-call(s32[1]{0:T(128)} %bitcast.refs_0_, s32[8,128]{1,0:T(8,128)} %get-tuple-element.17.refs_1_, s32[12,3]{1,0:T(8,128)} %copy-done.17, s32[12,3]{1,0:T(8,128)} %copy-done.18, bf16[3072,768]{1,0:T(8,128)(2,1)} %refs_4_.15, ...), custom_call_target="tpu_custom_call", output_to_operand_aliasing={{}: (16, {})} | custom-call | flops 603979776 | bytes 2752512 | tf_op jit(solution)/shard_map/join_part/pallas_call | solution.py:239
  112.8 0.6 copy-done.25
  113.3 0.7 copy-done.21
  114.1 4.3 %join_part.7 = bf16[3072,256]{1,0:T(8,128)(2,1)} custom-call(s32[1]{0:T(128)} %bitcast.refs_0_, s32[8,128]{1,0:T(8,128)} %get-tuple-element.17.refs_1_, s32[12,3]{1,0:T(8,128)} %copy-done.17, s32[12,3]{1,0:T(8,128)} %copy-done.18, bf16[3072,768]{1,0:T(8,128)(2,1)} %refs_4_.15, ...), custom_call_target="tpu_custom_call", output_to_operand_aliasing={{}: (16, {})} | custom-call | flops 603979776 | bytes 2752512 | tf_op jit(solution)/shard_map/join_part/pallas_call | solution.py:239
  (84 shorter events, 2.7 us)
Async XLA Ops:
  0.0 30.7 %copy-start.28 = (s32[12,3]{0,1:T(4,128)S(1)}, s32[12,3]{0,1:T(4,128)}, u32[]{:S(2)}) copy-start(s32[12,3]{0,1:T(4,128)} %param.7) | copy-start | bytes 436
  0.0 46.0 %collective-permute-start.1 = (bf16[3072,768]{1,0:T(8,128)(2,1)}, bf16[3072,768]{1,0:T(8,128)(2,1)}, u32[]{:S(2)}, u32[]{:S(2)}) collective-permute-start(bf16[3072,768]{1,0:T(8,128)(2,1)} %refs_4_.15), channel_id=1, source_target_pairs={{0,1},{1,0},{2,3},{3,2},{4,5},{5,4},{6,7},{7,6},{8,9},{9,8},{10,11... | collective-permute-start | bytes 14155784 | tf_op jit(solution)/shard_map/ppermute | solution.py:144
  2.8 17.8 %all-to-all-start = ((bf16[8,80,256]{2,1,0:T(8,128)(2,1)}), bf16[8,80,256]{2,1,0:T(8,128)(2,1)S(1)}, u32[]{:S(2)}, u32[]{:S(2)}) async-start(bf16[8,80,256]{2,1,0:T(8,128)(2,1)} %pack.1), calls=%async_computation | async-start | bytes 655360 | tf_op jit(solution)/shard_map/all_to_all | solution.py:155
  23.0 4.5 %collective-permute-start.10 = (bf16[128,256]{1,0:T(8,128)(2,1)}, bf16[128,256]{1,0:T(8,128)(2,1)S(1)}, u32[]{:S(2)}, u32[]{:S(2)}) collective-permute-start(bf16[128,256]{1,0:T(8,128)(2,1)} %get-tuple-element.20), channel_id=1, source_target_pairs={{0,2},{1,3},{2,0},{3,1},{4,6},{5,7},{6,4},{7,5},{8,10},{9,11},{10,... | collective-permute-start | bytes 196616 | tf_op jit(solution)/shard_map/ppermute | solution.py:174
  27.4 18.6 %copy-start.5 = (bf16[128,256]{1,0:T(8,128)(2,1)}, bf16[128,256]{1,0:T(8,128)(2,1)S(1)}, u32[]{:S(2)}) copy-start(bf16[128,256]{1,0:T(8,128)(2,1)S(1)} %collective-permute-done.10.refs_6_) | copy-start | bytes 196612
  27.4 11.4 %collective-permute-start.11 = (bf16[128,256]{1,0:T(8,128)(2,1)S(1)}, bf16[128,256]{1,0:T(8,128)(2,1)S(1)}, u32[]{:S(2)}, u32[]{:S(2)}) collective-permute-start(bf16[128,256]{1,0:T(8,128)(2,1)S(1)} %collective-permute-done.10.refs_6_), channel_id=1, source_target_pairs={{0,4},{4,8},{8,12},{12,16},{16,20},{20,24},{24,28},{28,0},{1,5},{5... | collective-permute-start | bytes 196616 | tf_op jit(solution)/shard_map/ppermute | solution.py:177
  28.9 11.0 %collective-permute-start.12 = (bf16[128,256]{1,0:T(8,128)(2,1)S(1)}, bf16[128,256]{1,0:T(8,128)(2,1)S(1)}, u32[]{:S(2)}, u32[]{:S(2)}) collective-permute-start(bf16[128,256]{1,0:T(8,128)(2,1)S(1)} %collective-permute-done.10.refs_6_), channel_id=1, source_target_pairs={{0,8},{4,12},{8,16},{12,20},{16,24},{20,28},{24,0},{28,4},{1,9},{5... | collective-permute-start | bytes 196616 | tf_op jit(solution)/shard_map/ppermute | solution.py:177
  28.9 12.8 %collective-permute-start.13 = (bf16[128,256]{1,0:T(8,128)(2,1)S(1)}, bf16[128,256]{1,0:T(8,128)(2,1)S(1)}, u32[]{:S(2)}, u32[]{:S(2)}) collective-permute-start(bf16[128,256]{1,0:T(8,128)(2,1)S(1)} %collective-permute-done.10.refs_6_), channel_id=1, source_target_pairs={{0,12},{4,16},{8,20},{12,24},{16,28},{20,0},{24,4},{28,8},{1,13},{... | collective-permute-start | bytes 196616 | tf_op jit(solution)/shard_map/ppermute | solution.py:177
  30.8 15.3 %copy-start.17 = (s32[12,3]{1,0:T(8,128)}, s32[12,3]{1,0:T(8,128)S(1)}, u32[]{:S(2)}) copy-start(s32[12,3]{1,0:T(8,128)S(1)} %copy.19.refs_2_) | copy-start | bytes 436
  30.8 1.2 collective-permute-start
  31.9 14.1 %copy-start.18 = (s32[12,3]{1,0:T(8,128)}, s32[12,3]{1,0:T(8,128)S(1)}, u32[]{:S(2)}) copy-start(s32[12,3]{1,0:T(8,128)S(1)} %collective-permute-done.refs_3_) | copy-start | bytes 436
  31.9 3.8 %collective-permute-start.9 = (s32[8,128]{1,0:T(8,128)}, s32[8,128]{1,0:T(8,128)S(1)}, u32[]{:S(2)}, u32[]{:S(2)}) collective-permute-start(s32[8,128]{1,0:T(8,128)} %get-tuple-element.19), channel_id=1, source_target_pairs={{0,2},{1,3},{2,0},{3,1},{4,6},{5,7},{6,4},{7,5},{8,10},{9,11},{10,... | collective-permute-start | bytes 12296 | tf_op jit(solution)/shard_map/ppermute | solution.py:174
  35.8 10.3 %copy-start.23 = (s32[8,128]{1,0:T(8,128)}, s32[8,128]{1,0:T(8,128)S(1)}, u32[]{:S(2)}) copy-start(s32[8,128]{1,0:T(8,128)S(1)} %collective-permute-done.9.refs_1_) | copy-start | bytes 12292
  35.8 8.7 %collective-permute-start.14 = (bf16[128,256]{1,0:T(8,128)(2,1)S(1)}, bf16[128,256]{1,0:T(8,128)(2,1)S(1)}, u32[]{:S(2)}, u32[]{:S(2)}) collective-permute-start(bf16[128,256]{1,0:T(8,128)(2,1)S(1)} %collective-permute-done.10.refs_6_), channel_id=1, source_target_pairs={{0,16},{4,20},{8,24},{12,28},{16,0},{20,4},{24,8},{28,12},{1,17},{... | collective-permute-start | bytes 196616 | tf_op jit(solution)/shard_map/ppermute | solution.py:177
  38.9 7.2 %copy-start.7 = (bf16[128,256]{1,0:T(8,128)(2,1)}, bf16[128,256]{1,0:T(8,128)(2,1)S(1)}, u32[]{:S(2)}) copy-start(bf16[128,256]{1,0:T(8,128)(2,1)S(1)} %collective-permute-done.11.refs_7_) | copy-start | bytes 196612
  38.9 5.6 %collective-permute-start.15 = (bf16[128,256]{1,0:T(8,128)(2,1)S(1)}, bf16[128,256]{1,0:T(8,128)(2,1)S(1)}, u32[]{:S(2)}, u32[]{:S(2)}) collective-permute-start(bf16[128,256]{1,0:T(8,128)(2,1)S(1)} %collective-permute-done.10.refs_6_), channel_id=1, source_target_pairs={{0,20},{4,24},{8,28},{12,0},{16,4},{20,8},{24,12},{28,16},{1,21},{... | collective-permute-start | bytes 196616 | tf_op jit(solution)/shard_map/ppermute | solution.py:177
  39.9 6.2 %copy-start.8 = (bf16[128,256]{1,0:T(8,128)(2,1)}, bf16[128,256]{1,0:T(8,128)(2,1)S(1)}, u32[]{:S(2)}) copy-start(bf16[128,256]{1,0:T(8,128)(2,1)S(1)} %collective-permute-done.12.refs_8_) | copy-start | bytes 196612
  39.9 4.8 %collective-permute-start.16 = (bf16[128,256]{1,0:T(8,128)(2,1)S(1)}, bf16[128,256]{1,0:T(8,128)(2,1)S(1)}, u32[]{:S(2)}, u32[]{:S(2)}) collective-permute-start(bf16[128,256]{1,0:T(8,128)(2,1)S(1)} %collective-permute-done.10.refs_6_), channel_id=1, source_target_pairs={{0,24},{4,28},{8,0},{12,4},{16,8},{20,12},{24,16},{28,20},{1,25},{... | collective-permute-start | bytes 196616 | tf_op jit(solution)/shard_map/ppermute | solution.py:177
  41.7 4.3 %copy-start.9 = (bf16[128,256]{1,0:T(8,128)(2,1)}, bf16[128,256]{1,0:T(8,128)(2,1)S(1)}, u32[]{:S(2)}) copy-start(bf16[128,256]{1,0:T(8,128)(2,1)S(1)} %collective-permute-done.13.refs_9_) | copy-start | bytes 196612
  41.7 4.3 %collective-permute-start.17 = (bf16[128,256]{1,0:T(8,128)(2,1)S(1)}, bf16[128,256]{1,0:T(8,128)(2,1)S(1)}, u32[]{:S(2)}, u32[]{:S(2)}) collective-permute-start(bf16[128,256]{1,0:T(8,128)(2,1)S(1)} %collective-permute-done.10.refs_6_), channel_id=1, source_target_pairs={{0,28},{4,0},{8,4},{12,8},{16,12},{20,16},{24,20},{28,24},{1,29},{... | collective-permute-start | bytes 196616 | tf_op jit(solution)/shard_map/ppermute | solution.py:177
  44.4 21.3 %collective-permute-start.2 = (bf16[128,256]{1,0:T(8,128)(2,1)}, bf16[128,256]{1,0:T(8,128)(2,1)S(1)}, u32[]{:S(2)}, u32[]{:S(2)}) collective-permute-start(bf16[128,256]{1,0:T(8,128)(2,1)} %get-tuple-element.18.refs_6_), channel_id=1, source_target_pairs={{0,4},{4,8},{8,12},{12,16},{16,20},{20,24},{24,28},{28,0},{1,5},{5... | collective-permute-start | bytes 196616 | tf_op jit(solution)/shard_map/ppermute | solution.py:177
  46.6 5.8 %copy-start.1 = (bf16[128,256]{1,0:T(8,128)(2,1)S(1)}, bf16[128,256]{1,0:T(8,128)(2,1)}, u32[]{:S(2)}) copy-start(bf16[128,256]{1,0:T(8,128)(2,1)} %get-tuple-element.18.refs_6_) | copy-start | bytes 196612
  50.9 44.5 %collective-permute-start.24 = (s16[768,256]{1,0:T(8,128)(2,1)}, s16[768,256]{1,0:T(8,128)(2,1)S(1)}, u32[]{:S(2)}, u32[]{:S(2)}) collective-permute-start(s16[768,256]{1,0:T(8,128)(2,1)} %get-tuple-element.27), channel_id=1, source_target_pairs={{0,2},{1,3},{2,0},{3,1},{4,6},{5,7},{6,4},{7,5},{8,10},{9,11},{10,... | collective-permute-start | bytes 1179656 | tf_op jit(solution)/shard_map/ppermute | solution.py:221
  52.4 14.7 %collective-permute-start.3 = (bf16[128,256]{1,0:T(8,128)(2,1)S(1)}, bf16[128,256]{1,0:T(8,128)(2,1)S(1)}, u32[]{:S(2)}, u32[]{:S(2)}) collective-permute-start(bf16[128,256]{1,0:T(8,128)(2,1)S(1)} %copy-done.1), channel_id=1, source_target_pairs={{0,8},{4,12},{8,16},{12,20},{16,24},{20,28},{24,0},{28,4},{1,9},{5... | collective-permute-start | bytes 196616 | tf_op jit(solution)/shard_map/ppermute | solution.py:177
  54.1 18.8 %collective-permute-start.4 = (bf16[128,256]{1,0:T(8,128)(2,1)S(1)}, bf16[128,256]{1,0:T(8,128)(2,1)S(1)}, u32[]{:S(2)}, u32[]{:S(2)}) collective-permute-start(bf16[128,256]{1,0:T(8,128)(2,1)S(1)} %copy-done.1), channel_id=1, source_target_pairs={{0,12},{4,16},{8,20},{12,24},{16,28},{20,0},{24,4},{28,8},{1,13},{... | collective-permute-start | bytes 196616 | tf_op jit(solution)/shard_map/ppermute | solution.py:177
  60.9 41.1 %collective-permute-start.22 = (s16[768,256]{1,0:T(8,128)(2,1)}, s16[768,256]{1,0:T(8,128)(2,1)S(1)}, u32[]{:S(2)}, u32[]{:S(2)}) collective-permute-start(s16[768,256]{1,0:T(8,128)(2,1)} %get-tuple-element.25), channel_id=1, source_target_pairs={{0,2},{1,3},{2,0},{3,1},{4,6},{5,7},{6,4},{7,5},{8,10},{9,11},{10,... | collective-permute-start | bytes 1179656 | tf_op jit(solution)/shard_map/ppermute | solution.py:221
  65.7 7.1 %copy-start.2 = (bf16[128,256]{1,0:T(8,128)(2,1)}, bf16[128,256]{1,0:T(8,128)(2,1)S(1)}, u32[]{:S(2)}) copy-start(bf16[128,256]{1,0:T(8,128)(2,1)S(1)} %collective-permute-done.2.refs_7_) | copy-start | bytes 196612
  65.7 7.8 %collective-permute-start.5 = (bf16[128,256]{1,0:T(8,128)(2,1)S(1)}, bf16[128,256]{1,0:T(8,128)(2,1)S(1)}, u32[]{:S(2)}, u32[]{:S(2)}) collective-permute-start(bf16[128,256]{1,0:T(8,128)(2,1)S(1)} %copy-done.1), channel_id=1, source_target_pairs={{0,16},{4,20},{8,24},{12,28},{16,0},{20,4},{24,8},{28,12},{1,17},{... | collective-permute-start | bytes 196616 | tf_op jit(solution)/shard_map/ppermute | solution.py:177
  67.1 5.8 %copy-start.3 = (bf16[128,256]{1,0:T(8,128)(2,1)}, bf16[128,256]{1,0:T(8,128)(2,1)S(1)}, u32[]{:S(2)}) copy-start(bf16[128,256]{1,0:T(8,128)(2,1)S(1)} %collective-permute-done.3.refs_8_) | copy-start | bytes 196612
  67.1 23.1 %copy-start.32 = (f32[8,256]{1,0:T(8,128)S(1)}, f32[8,256]{1,0:T(8,128)}, u32[]{:S(2)}) copy-start(f32[8,256]{1,0:T(8,128)} %get-tuple-element.28) | copy-start | bytes 24580
  67.1 26.8 %copy-start.31 = (f32[8,256]{1,0:T(8,128)S(1)}, f32[8,256]{1,0:T(8,128)}, u32[]{:S(2)}) copy-start(f32[8,256]{1,0:T(8,128)} %get-tuple-element.26) | copy-start | bytes 24580
  67.1 28.3 %copy-start.29 = (f32[8,256]{1,0:T(8,128)S(1)}, f32[8,256]{1,0:T(8,128)}, u32[]{:S(2)}) copy-start(f32[8,256]{1,0:T(8,128)} %get-tuple-element.24) | copy-start | bytes 24580
  67.1 40.0 %collective-permute-start.20 = (s16[768,256]{1,0:T(8,128)(2,1)}, s16[768,256]{1,0:T(8,128)(2,1)S(1)}, u32[]{:S(2)}, u32[]{:S(2)}) collective-permute-start(s16[768,256]{1,0:T(8,128)(2,1)} %get-tuple-element.23), channel_id=1, source_target_pairs={{0,2},{1,3},{2,0},{3,1},{4,6},{5,7},{6,4},{7,5},{8,10},{9,11},{10,... | collective-permute-start | bytes 1179656 | tf_op jit(solution)/shard_map/ppermute | solution.py:221
  72.9 23.1 %copy-start.4 = (bf16[128,256]{1,0:T(8,128)(2,1)}, bf16[128,256]{1,0:T(8,128)(2,1)S(1)}, u32[]{:S(2)}) copy-start(bf16[128,256]{1,0:T(8,128)(2,1)S(1)} %collective-permute-done.4.refs_9_) | copy-start | bytes 196612
  72.9 39.9 %collective-permute-start.18 = (s16[768,256]{1,0:T(8,128)(2,1)}, s16[768,256]{1,0:T(8,128)(2,1)S(1)}, u32[]{:S(2)}, u32[]{:S(2)}) collective-permute-start(s16[768,256]{1,0:T(8,128)(2,1)} %get-tuple-element.21), channel_id=1, source_target_pairs={{0,2},{1,3},{2,0},{3,1},{4,6},{5,7},{6,4},{7,5},{8,10},{9,11},{10,... | collective-permute-start | bytes 1179656 | tf_op jit(solution)/shard_map/ppermute | solution.py:221
  73.5 22.5 %copy-start.6 = (bf16[128,256]{1,0:T(8,128)(2,1)}, bf16[128,256]{1,0:T(8,128)(2,1)S(1)}, u32[]{:S(2)}) copy-start(bf16[128,256]{1,0:T(8,128)(2,1)S(1)} %collective-permute-done.5.refs_10_) | copy-start | bytes 196612
  73.5 5.2 %collective-permute-start.6 = (bf16[128,256]{1,0:T(8,128)(2,1)S(1)}, bf16[128,256]{1,0:T(8,128)(2,1)S(1)}, u32[]{:S(2)}, u32[]{:S(2)}) collective-permute-start(bf16[128,256]{1,0:T(8,128)(2,1)S(1)} %copy-done.1), channel_id=1, source_target_pairs={{0,20},{4,24},{8,28},{12,0},{16,4},{20,8},{24,12},{28,16},{1,21},{... | collective-permute-start | bytes 196616 | tf_op jit(solution)/shard_map/ppermute | solution.py:177
  78.7 17.3 %copy-start.11 = (bf16[128,256]{1,0:T(8,128)(2,1)}, bf16[128,256]{1,0:T(8,128)(2,1)S(1)}, u32[]{:S(2)}) copy-start(bf16[128,256]{1,0:T(8,128)(2,1)S(1)} %collective-permute-done.6.refs_11_) | copy-start | bytes 196612
  78.7 6.5 %collective-permute-start.7 = (bf16[128,256]{1,0:T(8,128)(2,1)S(1)}, bf16[128,256]{1,0:T(8,128)(2,1)S(1)}, u32[]{:S(2)}, u32[]{:S(2)}) collective-permute-start(bf16[128,256]{1,0:T(8,128)(2,1)S(1)} %copy-done.1), channel_id=1, source_target_pairs={{0,24},{4,28},{8,0},{12,4},{16,8},{20,12},{24,16},{28,20},{1,25},{... | collective-permute-start | bytes 196616 | tf_op jit(solution)/shard_map/ppermute | solution.py:177
  85.1 10.8 %copy-start.13 = (bf16[128,256]{1,0:T(8,128)(2,1)}, bf16[128,256]{1,0:T(8,128)(2,1)S(1)}, u32[]{:S(2)}) copy-start(bf16[128,256]{1,0:T(8,128)(2,1)S(1)} %collective-permute-done.7.refs_12_) | copy-start | bytes 196612
  85.1 5.1 %collective-permute-start.8 = (bf16[128,256]{1,0:T(8,128)(2,1)S(1)}, bf16[128,256]{1,0:T(8,128)(2,1)S(1)}, u32[]{:S(2)}, u32[]{:S(2)}) collective-permute-start(bf16[128,256]{1,0:T(8,128)(2,1)S(1)} %copy-done.1), channel_id=1, source_target_pairs={{0,28},{4,0},{8,4},{12,8},{16,12},{20,16},{24,20},{28,24},{1,29},{... | collective-permute-start | bytes 196616 | tf_op jit(solution)/shard_map/ppermute | solution.py:177
  90.2 5.8 %copy-start.15 = (bf16[128,256]{1,0:T(8,128)(2,1)}, bf16[128,256]{1,0:T(8,128)(2,1)S(1)}, u32[]{:S(2)}) copy-start(bf16[128,256]{1,0:T(8,128)(2,1)S(1)} %collective-permute-done.8.refs_13_) | copy-start | bytes 196612
  90.2 3.7 %collective-permute-start.25 = (f32[8,256]{1,0:T(8,128)S(1)}, f32[8,256]{1,0:T(8,128)S(1)}, u32[]{:S(2)}, u32[]{:S(2)}) collective-permute-start(f32[8,256]{1,0:T(8,128)S(1)} %copy-done.32), channel_id=1, source_target_pairs={{0,2},{1,3},{2,0},{3,1},{4,6},{5,7},{6,4},{7,5},{8,10},{9,11},{10,... | collective-permute-start | bytes 24584 | tf_op jit(solution)/shard_map/ppermute | solution.py:221
  93.9 2.1 %copy-start.24 = (f32[8,256]{1,0:T(8,128)}, f32[8,256]{1,0:T(8,128)S(1)}, u32[]{:S(2)}) copy-start(f32[8,256]{1,0:T(8,128)S(1)} %collective-permute-done.25.refs_15_) | copy-start | bytes 24580
  93.9 6.6 %collective-permute-start.23 = (f32[8,256]{1,0:T(8,128)S(1)}, f32[8,256]{1,0:T(8,128)S(1)}, u32[]{:S(2)}, u32[]{:S(2)}) collective-permute-start(f32[8,256]{1,0:T(8,128)S(1)} %copy-done.31), channel_id=1, source_target_pairs={{0,2},{1,3},{2,0},{3,1},{4,6},{5,7},{6,4},{7,5},{8,10},{9,11},{10,... | collective-permute-start | bytes 24584 | tf_op jit(solution)/shard_map/ppermute | solution.py:221
  95.4 11.7 %collective-permute-start.21 = (f32[8,256]{1,0:T(8,128)S(1)}, f32[8,256]{1,0:T(8,128)S(1)}, u32[]{:S(2)}, u32[]{:S(2)}) collective-permute-start(f32[8,256]{1,0:T(8,128)S(1)} %copy-done.29), channel_id=1, source_target_pairs={{0,2},{1,3},{2,0},{3,1},{4,6},{5,7},{6,4},{7,5},{8,10},{9,11},{10,... | collective-permute-start | bytes 24584 | tf_op jit(solution)/shard_map/ppermute | solution.py:221
  96.1 4.4 %copy-start.30 = (f32[8,256]{1,0:T(8,128)S(1)}, f32[8,256]{1,0:T(8,128)}, u32[]{:S(2)}) copy-start(f32[8,256]{1,0:T(8,128)} %get-tuple-element.22) | copy-start | bytes 24580
  100.5 12.2 %collective-permute-start.19 = (f32[8,256]{1,0:T(8,128)S(1)}, f32[8,256]{1,0:T(8,128)S(1)}, u32[]{:S(2)}, u32[]{:S(2)}) collective-permute-start(f32[8,256]{1,0:T(8,128)S(1)} %copy-done.30), channel_id=1, source_target_pairs={{0,2},{1,3},{2,0},{3,1},{4,6},{5,7},{6,4},{7,5},{8,10},{9,11},{10,... | collective-permute-start | bytes 24584 | tf_op jit(solution)/shard_map/ppermute | solution.py:221
  (12 other events, 11.7 us)

commit v3 on v2

v3 whole, which is shorter than its diff:
```python
from functools import partial

import jax
import jax.numpy as jnp
from jax import lax
from jax.experimental import pallas as pl
from jax.experimental.pallas import tpu as pltpu
from jax.sharding import PartitionSpec as P

STEPS = 4
CORES = 2
CUTS = (0.0, 0.25, 0.58, 0.92, 1.0)
CODE_TOP = 32767.0
FRACTION = 8192.0
META_ROWS = 16
PARAMS = pltpu.CompilerParams(vmem_limit_bytes=16 * 1024 * 1024)
SMEM = pl.BlockSpec(memory_space=pltpu.SMEM)
VMEM = pl.BlockSpec(memory_space=pltpu.VMEM)


def pair_offsets(col_count):
    pairs = col_count // CORES
    offsets = set()
    for core in range(CORES):
        for step in range(STEPS):
            offsets.add(-((core - step) // CORES) % pairs)
    return sorted(offsets)


def row_chunks(block_count):
    marks = sorted({round(block_count * cut) for cut in CUTS})
    return [(first, last - first) for first, last in zip(marks, marks[1:])]


def pack_kernel(list_ref, count_ref, panel_ref, pieces_ref):
    peers, height, _ = pieces_ref.shape
    slots, tile_width = panel_ref.shape[2:4]
    share = height - META_ROWS
    lane = lax.broadcasted_iota(jnp.int32, (META_ROWS, pieces_ref.shape[2]), 1)
    info = jnp.where(lane == slots, count_ref[0, 0], 0)
    for slot in range(slots):
        info = jnp.where(lane == slot, list_ref[0, 0, slot], info)
    info = info.astype(jnp.float32).astype(pieces_ref.dtype)
    for peer in range(peers):
        slot, start = divmod(peer * share, tile_width)
        pieces_ref[peer, pl.ds(0, share), :] = panel_ref[0, 0, slot, pl.ds(start, share), :]
        pieces_ref[peer, pl.ds(share, META_ROWS), :] = info


def mask_kernel(chunks, tile_width, mask_ref, rows_ref, *out_refs):
    block = pl.program_id(0)
    for (first, span), out_ref in zip(chunks, out_refs):

        @pl.when((block >= first) & (block < first + span))
        def _():
            for tile in range(rows_ref.shape[1] // tile_width):
                live = mask_ref[block, tile].astype(jnp.float32).astype(rows_ref.dtype)
                columns = pl.ds(tile * tile_width, tile_width)
                out_ref[:, columns] = rows_ref[:, columns] * live


def choose_kernel(col_peers, offsets, owner_ref, place_ref, pieces_ref, *out_refs):
    share = pieces_ref.shape[1] - META_ROWS
    core = lax.rem(place_ref[0], CORES)
    sign = 1 - 2 * core
    line = lax.broadcasted_iota(jnp.int32, (META_ROWS, pieces_ref.shape[2]), 0)
    for offset, out_ref in zip(offsets, out_refs):
        infos = []
        for group, shift in enumerate((0, sign)):
            step = lax.rem(CORES * offset - shift + col_peers, col_peers)
            holder = owner_ref[jnp.minimum(step, STEPS - 1), 0]
            out_ref[pl.ds(group * share, share), :] = pieces_ref[holder, pl.ds(0, share), :]
            info = pieces_ref[holder, pl.ds(share, META_ROWS), :].astype(jnp.float32)
            infos.append(jnp.where(step < STEPS, info, 0.0))
        out_ref[pl.ds(CORES * share, META_ROWS), :] = jnp.where(line == 0, infos[0], infos[1]).astype(out_ref.dtype)


def fill_kernel(slots, place_ref, *refs):
    piece_refs, dense_ref = refs[:-1], refs[-1]
    peers = len(piece_refs)
    share = (piece_refs[0].shape[0] - META_ROWS) // CORES
    width, tile_width = dense_ref.shape[0] // CORES, dense_ref.shape[1]
    table = piece_refs[0][pl.ds(CORES * share, META_ROWS), :].astype(jnp.float32)
    line = lax.broadcasted_iota(jnp.int32, table.shape, 0)
    lane = lax.broadcasted_iota(jnp.int32, table.shape, 1)

    def entry(group, place):
        return jnp.max(jnp.where((line == group) & (lane == place), table, 0.0)).astype(jnp.int32)

    dense_ref[...] = jnp.zeros_like(dense_ref)
    for group in range(CORES):
        count = entry(group, slots)
        starts = [group * width + entry(group, slot) * tile_width for slot in range(slots)]
        for shift, piece_ref in enumerate(piece_refs):
            first = lax.rem(place_ref[0] - shift + peers, peers) * share
            slot = first // tile_width
            start = starts[0]
            for other in range(1, slots):
                start = jnp.where(slot == other, starts[other], start)

            @pl.when(slot < count)
            def _():
                place = pl.multiple_of(start + lax.rem(first, tile_width), META_ROWS)
                dense_ref[pl.ds(place, share), :] = piece_ref[pl.ds(group * share, share), :]


def block_product(own_ref, other_ref, dense_ref):
    width = own_ref.shape[1]
    return jnp.dot(own_ref[...], dense_ref[pl.ds(0, width), :], preferred_element_type=jnp.float32) + jnp.dot(
        other_ref[...], dense_ref[pl.ds(width, width), :], preferred_element_type=jnp.float32
    )


def send_kernel(own_ref, other_ref, dense_ref, code_ref, scale_ref):
    step, span = pl.program_id(0), pl.num_programs(0)
    height = own_ref.shape[0]
    total = block_product(own_ref, other_ref, dense_ref)
    top = jnp.max(jnp.abs(total), axis=0, keepdims=True)
    unit = jnp.where(top > 0, top, 1.0) * (1.0 / CODE_TOP)
    power = jnp.floor(jnp.log2(unit))
    fraction = jnp.ceil(unit * jnp.exp2(-power) * FRACTION)
    unit = fraction * jnp.exp2(power) * (1.0 / FRACTION)
    code = jnp.clip(jnp.round(total * (1.0 / unit)), -CODE_TOP, CODE_TOP)
    code_ref[pl.ds(pl.multiple_of(step * height, height), height), :] = code.astype(jnp.int32).astype(jnp.int16)
    scale_ref[pl.ds(2 * step, 1), :] = power
    scale_ref[pl.ds(2 * step + 1, 1), :] = fraction

    @pl.when(step == span - 1)
    def _():
        rows = scale_ref.shape[0]
        line = lax.broadcasted_iota(jnp.int32, scale_ref.shape, 0)
        kept = jnp.where(line < 2 * span, scale_ref[...], 0.0)
        code_ref[pl.ds(code_ref.shape[0] - rows, rows), :] = kept.astype(jnp.int32).astype(jnp.int16)


def join_kernel(own_ref, other_ref, dense_ref, *refs):
    code_refs, out_ref, scale_ref = refs[:-2], refs[-2], refs[-1]
    step = pl.program_id(0)
    height = own_ref.shape[0]
    rows = scale_ref.shape[0] // max(len(code_refs), 1)

    @pl.when(step == 0)
    def _():
        for number, code_ref in enumerate(code_refs):
            scales = code_ref[pl.ds(code_ref.shape[0] - rows, rows), :].astype(jnp.int32).astype(jnp.float32)
            scale_ref[pl.ds(number * rows, rows), :] = scales

    total = block_product(own_ref, other_ref, dense_ref)
    for number, code_ref in enumerate(code_refs):
        power = scale_ref[pl.ds(number * rows + 2 * step, 1), :]
        fraction = scale_ref[pl.ds(number * rows + 2 * step + 1, 1), :]
        code = code_ref[pl.ds(pl.multiple_of(step * height, height), height), :].astype(jnp.int32).astype(jnp.float32)
        total = total + code * (fraction * jnp.exp2(power) * (1.0 / FRACTION))
    out_ref[...] = total.astype(out_ref.dtype)


def after(value, *earlier):
    return lax.optimization_barrier((value, *earlier))[0]


def shards(amplitudes, pair_mask, integrals, tile_list, tile_count, owner):
    row_count, full_width = amplitudes.shape
    slots, tile_width = integrals.shape[2], integrals.shape[-1]
    block_count = pair_mask.shape[0]
    block_rows = row_count // block_count
    row_peers, col_peers = lax.axis_size("row"), lax.axis_size("col")
    share = slots * tile_width // row_peers
    offsets = pair_offsets(col_peers)
    row_place = lax.axis_index("row").reshape(1)
    col_place = lax.axis_index("col").reshape(1)
    chunks = row_chunks(block_count)

    pieces = pl.pallas_call(
        pack_kernel,
        in_specs=[SMEM, SMEM, VMEM],
        out_specs=VMEM,
        out_shape=jax.ShapeDtypeStruct((row_peers, share + META_ROWS, tile_width), integrals.dtype),
        compiler_params=PARAMS,
        name="pack",
    )(tile_list, tile_count, integrals)
    pieces = lax.all_to_all(pieces, "row", 0, 0)

    masked = pl.pallas_call(
        partial(mask_kernel, chunks, tile_width),
        grid=(block_count,),
        in_specs=[SMEM, pl.BlockSpec((block_rows, full_width), lambda i: (i, 0))],
        out_specs=[
            pl.BlockSpec(
                (block_rows, full_width), lambda i, first=first, span=span: (jnp.clip(i - first, 0, span - 1), 0)
            )
            for first, span in chunks
        ],
        out_shape=[
            jax.ShapeDtypeStruct((span * block_rows, full_width), amplitudes.dtype) for _, span in chunks
        ],
        compiler_params=PARAMS,
        cost_estimate=pl.CostEstimate(
            flops=row_count * full_width, bytes_accessed=4 * row_count * full_width, transcendentals=0
        ),
        name="screen",
    )(pair_mask, amplitudes)
    pieces = after(pieces, *masked)

    chosen = pl.pallas_call(
        partial(choose_kernel, col_peers, offsets),
        in_specs=[SMEM, SMEM, VMEM],
        out_specs=[VMEM] * len(offsets),
        out_shape=[jax.ShapeDtypeStruct((CORES * share + META_ROWS, tile_width), integrals.dtype)] * len(offsets),
        compiler_params=PARAMS,
        name="choose",
    )(owner, col_place, pieces)

    def spread(data):
        held = [data]
        for shift in range(1, row_peers):
            held.append(lax.ppermute(data, "row", [(r, (r + shift) % row_peers) for r in range(row_peers)]))
        return held

    def fill(held):
        return pl.pallas_call(
            partial(fill_kernel, slots),
            in_specs=[SMEM] + [VMEM] * row_peers,
            out_specs=VMEM,
            out_shape=jax.ShapeDtypeStruct((CORES * full_width, tile_width), integrals.dtype),
            compiler_params=PARAMS,
            name="fill",
        )(row_place, *held)

    swap = [(c, c ^ 1) for c in range(col_peers)]
    others = [lax.ppermute(after(masked[0], pieces), "col", swap)]
    plans = {}
    for offset, data in zip(offsets, chosen):
        if offset:
            data = lax.ppermute(data, "col", [(c, (c - CORES * offset) % col_peers) for c in range(col_peers)])
            held = spread(data)
            plans[offset] = fill([after(held[0], others[0])] + held[1:])

    rows = pl.BlockSpec((block_rows, full_width), lambda i: (i, 0))
    weights = pl.BlockSpec((CORES * full_width, tile_width), lambda i: (0, 0))

    def cost(span):
        return pl.CostEstimate(
            flops=2 * span * block_rows * CORES * full_width * tile_width,
            bytes_accessed=span * block_rows * (CORES * full_width + tile_width) * 2,
            transcendentals=0,
        )

    def code_shape(span):
        return (span * block_rows + -(-2 * span // META_ROWS) * META_ROWS, tile_width)

    arrived, sent = [], []
    for number, ((first, span), own) in enumerate(zip(chunks, masked)):
        if number + 1 < len(chunks):
            earlier = [others[number]] + sent[-1:]
            others.append(lax.ppermute(after(masked[number + 1], *earlier), "col", swap))
        received = []
        for offset in offsets:
            if offset == 0:
                continue
            height = code_shape(span)[0] - span * block_rows
            code = pl.pallas_call(
                send_kernel,
                grid=(span,),
                in_specs=[rows, rows, weights],
                out_specs=pl.BlockSpec(code_shape(span), lambda i: (0, 0)),
                out_shape=jax.ShapeDtypeStruct(code_shape(span), jnp.int16),
                scratch_shapes=[pltpu.VMEM((height, tile_width), jnp.float32)],
                compiler_params=PARAMS,
                cost_estimate=cost(span),
                name="send_part",
            )(own, others[number], plans[offset])
            up = [(c, (c + CORES * offset) % col_peers) for c in range(col_peers)]
            received.append(lax.ppermute(code, "col", up))
            sent.append(code)
        arrived.append(received)
    plans[0] = fill(spread(after(chosen[offsets.index(0)], *sent)))

    out = None
    for (first, span), own, other, received in zip(chunks, masked, others, arrived):
        operands = [own, other, plans[0], *received]
        specs = [rows, rows, weights] + [pl.BlockSpec(code_shape(span), lambda i: (0, 0))] * len(received)
        body = join_kernel
        aliases = {}
        if out is not None:
            body = partial(skip_operand, len(operands), body)
            aliases = {len(operands): 0}
            operands.append(out)
            specs.append(pl.BlockSpec(memory_space=pl.ANY))
        height = code_shape(span)[0] - span * block_rows
        out = pl.pallas_call(
            body,
            grid=(span,),
            in_specs=specs,
            out_specs=pl.BlockSpec((block_rows, tile_width), lambda i, first=first: (first + i, 0)),
            out_shape=jax.ShapeDtypeStruct((row_count, tile_width), jnp.bfloat16),
            scratch_shapes=[pltpu.VMEM((height * max(len(received), 1), tile_width), jnp.float32)],
            input_output_aliases=aliases,
            compiler_params=PARAMS,
            cost_estimate=cost(span),
            name="join_part",
        )(*operands)
    return out


def skip_operand(position, body, *refs):
    body(*refs[:position], *refs[position + 1 :])


def solution(mesh):
    return jax.shard_map(
        shards,
        mesh=mesh,
        in_specs=(
            P("row", "col"),
            P("row", "col"),
            P("row", "col", None, None, None),
            P("row", "col", None),
            P("row", "col"),
            P(None, "col"),
        ),
        out_specs=P("row", "col"),
        check_vma=False,
    )
```

time: 119 us -> 104 us (0.87)
  Pallas kernels: 37.5 us -> 22.6 us
  starting transfers between devices: 44.4 us -> 35.6 us
  local copies, waits for them, and re-layouts: 6.31 us -> 13.2 us
  waiting for transfers between devices: 29.3 us -> 30.8 us
    ppermute x26 -> x23, starting transfers between devices: 37.6 us -> 28.3 us  [the longest x14 21.9 us: spread(): lax.ppermute(data, 'row', [(r, (r + shift) % row_peers) for r in range(ro...]
    pallas_call x4, Pallas kernels: 17.2 us -> 9.66 us  [shards(): pl.pallas_call(body, grid=(span,), in_specs=specs, out_specs=pl.BlockSpec...]
    unnamed x68 -> x36, local copies, waits for them, and re-layouts: 6.31 us -> 13.2 us
    ppermute x26 -> x23, waiting for transfers between devices: 19.7 us -> 26.1 us  [the longest x14 19.9 us: spread(): lax.ppermute(data, 'row', [(r, (r + shift) % row_peers) for r in range(ro...]
    pallas_call x4 -> x7, Pallas kernels: 16.9 us -> 10.7 us  [the longest x4 6.95 us: shards(): pl.pallas_call(send_kernel, grid=(span,), in_specs=[rows, rows, weights],...]
    all_to_all x1, waiting for transfers between devices: 9.63 us -> 4.63 us  [shards(): pieces = lax.all_to_all(pieces, 'row', 0, 0)]
  transfers between devices with their start and end apart: 27 -> 24, of which waited for: 11 -> 12; matrix products, arithmetic and copies ran while one was open for 1% -> 1% of each run, Pallas kernels for 28% -> 20%
where the time goes in v3:
time: 104 us; the launch traced here: 103 us
  starting transfers between devices  35.6 us (34%)
  waiting for transfers between devices  30.8 us (30%)
  Pallas kernels  22.6 us (22%)
  local copies, waits for them, and re-layouts  13.2 us (13%)
    ppermute x14, starting transfers between devices, spread(): lax.ppermute(data, 'row', [(r, (r + shift) % row_peers) for r in range(ro...  21.9 us
    ppermute x14, waiting for transfers between devices, spread(): lax.ppermute(data, 'row', [(r, (r + shift) % row_peers) for r in range(ro...  19.9 us
    unnamed x36, local copies, waits for them, and re-layouts  13.2 us
    pallas_call x4, Pallas kernels, shards(): pl.pallas_call(body, grid=(span,), in_specs=specs, out_specs=pl.BlockSpec...  9.66 us
    all_to_all x1, starting transfers between devices, shards(): pieces = lax.all_to_all(pieces, 'row', 0, 0)  7.28 us
    pallas_call x4, Pallas kernels, shards(): pl.pallas_call(send_kernel, grid=(span,), in_specs=[rows, rows, weights],...  6.95 us
    all_to_all x1, waiting for transfers between devices, shards(): pieces = lax.all_to_all(pieces, 'row', 0, 0)  4.63 us
    ppermute x4, starting transfers between devices, shards(): received.append(lax.ppermute(code, 'col', up))  4.12 us
  transfers between devices with their start and end apart: 24, of which 12 were waited for; matrix products, arithmetic and copies ran while one was open for 1% of the time, Pallas kernels for 20%

profile of v3, /device:TPU:0, one launch (start us, length us, event | category | flops | bytes accessed | tf_op | source)
XLA Modules:
  0.0 103.1 jit_solution(12010148017093622915)
XLA Ops:
  0.7 0.9 copy-done.6
  1.6 0.7 copy-done.15
  2.3 1.3 %pack.1 = bf16[8,80,256]{2,1,0:T(8,128)(2,1)} custom-call(s32[1,1,2]{2,1,0:T(1,128)S(1)} %copy-done.15, s32[1,1]{1,0:T(1,128)S(6)} %copy.15.count_ref, bf16[1,1,2,256,256]{4,3,2,1,0:T(8,128)(2,1)S(1)} %copy-done.6), custom_call_target="tpu_custom_call" | custom-call | tf_op jit(solution)/shard_map/pack/pallas_call | solution.py:173
  3.6 7.3 %all-to-all-start = ((bf16[8,80,256]{2,1,0:T(8,128)(2,1)}), bf16[8,80,256]{2,1,0:T(8,128)(2,1)}, u32[]{:S(2)}, u32[]{:S(2)}) async-start(bf16[8,80,256]{2,1,0:T(8,128)(2,1)} %pack.1), calls=%async_computation | async-start | bytes 655360 | tf_op jit(solution)/shard_map/all_to_all | solution.py:181
  10.8 0.8 copy.10.mask_ref
  11.6 2.3 %copy-done.5 = bf16[3072,768]{1,0:T(8,128)(2,1)S(1)} copy-done((bf16[3072,768]{1,0:T(8,128)(2,1)S(1)}, bf16[3072,768]{1,0:T(8,128)(2,1)}, u32[]{:S(2)}) %copy-start.5) | copy-done | bytes 4718616
  13.9 1.7 %screen.1 = (bf16[768,768]{1,0:T(8,128)(2,1)S(1)}, bf16[1024,768]{1,0:T(8,128)(2,1)S(1)}, bf16[1024,768]{1,0:T(8,128)(2,1)S(1)}, bf16[256,768]{1,0:T(8,128)(2,1)S(1)}) custom-call(s32[12,3]{1,0:T(8,128)S(1)} %copy.10.mask_ref, bf16[3072,768]{1,0:T(8,128)(2,1)S(1)} %copy-done.5), custom_call_target="tpu_custom_call" | custom-call | flops 2359296 | bytes 9437184 | tf_op jit(solution)/shard_map/screen/pallas_call | solution.py:183
  15.6 1.0 copy-done
  16.6 4.6 %all-to-all-done.pieces_ref = bf16[8,80,256]{2,1,0:T(8,128)(2,1)} async-done(((bf16[8,80,256]{2,1,0:T(8,128)(2,1)}), bf16[8,80,256]{2,1,0:T(8,128)(2,1)}, u32[]{:S(2)}, u32[]{:S(2)}) %all-to-all-start) | async-done | bytes 327712 | tf_op jit(solution)/shard_map/all_to_all | solution.py:181
  21.3 3.1 %collective-permute-done.other_ref = bf16[768,768]{1,0:T(8,128)(2,1)S(1)} collective-permute-done((bf16[768,768]{1,0:T(8,128)(2,1)}, bf16[768,768]{1,0:T(8,128)(2,1)S(1)}, u32[]{:S(2)}, u32[]{:S(2)}) %collective-permute-start) | collective-permute-done | bytes 1179680 | tf_op jit(solution)/shard_map/ppermute | solution.py:230
  24.3 1.0 copy-done.2
  25.6 1.0 choose.1
  26.6 0.6 copy-done.7
  27.2 1.5 %collective-permute-start.2 = (bf16[144,256]{1,0:T(8,128)(2,1)S(1)}, bf16[144,256]{1,0:T(8,128)(2,1)}, u32[]{:S(2)}, u32[]{:S(2)}) collective-permute-start(bf16[144,256]{1,0:T(8,128)(2,1)S(1)} %get-tuple-element.25), channel_id=1, source_target_pairs={{0,2},{1,3},{2,0},{3,1},{4,6},{5,7},{6,4},{7,5},{8,10},{9,11},{10,... | collective-permute-start | bytes 221192 | tf_op jit(solution)/shard_map/ppermute | solution.py:234
  28.7 3.1 %collective-permute-done.2.refs_0_ = bf16[144,256]{1,0:T(8,128)(2,1)} collective-permute-done((bf16[144,256]{1,0:T(8,128)(2,1)S(1)}, bf16[144,256]{1,0:T(8,128)(2,1)}, u32[]{:S(2)}, u32[]{:S(2)}) %collective-permute-start.2) | collective-permute-done | bytes 73760 | tf_op jit(solution)/shard_map/ppermute | solution.py:234
  31.9 2.3 %collective-permute-start.9 = (bf16[144,256]{1,0:T(8,128)(2,1)}, bf16[144,256]{1,0:T(8,128)(2,1)S(1)}, u32[]{:S(2)}, u32[]{:S(2)}) collective-permute-start(bf16[144,256]{1,0:T(8,128)(2,1)} %collective-permute-done.2.refs_0_), channel_id=1, source_target_pairs={{0,28},{4,0},{8,4},{12,8},{16,12},{20,16},{24,20},{28,24},{1,29},{... | collective-permute-start | bytes 221192 | tf_op jit(solution)/shard_map/ppermute | solution.py:216
  34.2 1.6 %collective-permute-start.7 = (bf16[144,256]{1,0:T(8,128)(2,1)}, bf16[144,256]{1,0:T(8,128)(2,1)S(1)}, u32[]{:S(2)}, u32[]{:S(2)}) collective-permute-start(bf16[144,256]{1,0:T(8,128)(2,1)} %collective-permute-done.2.refs_0_), channel_id=1, source_target_pairs={{0,20},{4,24},{8,28},{12,0},{16,4},{20,8},{24,12},{28,16},{1,21},{... | collective-permute-start | bytes 221192 | tf_op jit(solution)/shard_map/ppermute | solution.py:216
  35.8 1.6 %collective-permute-start.6 = (bf16[144,256]{1,0:T(8,128)(2,1)}, bf16[144,256]{1,0:T(8,128)(2,1)}, u32[]{:S(2)}, u32[]{:S(2)}) collective-permute-start(bf16[144,256]{1,0:T(8,128)(2,1)} %collective-permute-done.2.refs_0_), channel_id=1, source_target_pairs={{0,16},{4,20},{8,24},{12,28},{16,0},{20,4},{24,8},{28,12},{1,17},{... | collective-permute-start | bytes 221192 | tf_op jit(solution)/shard_map/ppermute | solution.py:216
  37.4 0.6 copy-done.9
  38.0 1.7 %collective-permute-start.5 = (bf16[144,256]{1,0:T(8,128)(2,1)}, bf16[144,256]{1,0:T(8,128)(2,1)}, u32[]{:S(2)}, u32[]{:S(2)}) collective-permute-start(bf16[144,256]{1,0:T(8,128)(2,1)} %collective-permute-done.2.refs_0_), channel_id=1, source_target_pairs={{0,12},{4,16},{8,20},{12,24},{16,28},{20,0},{24,4},{28,8},{1,13},{... | collective-permute-start | bytes 221192 | tf_op jit(solution)/shard_map/ppermute | solution.py:216
  39.8 0.6 copy-done.11
  40.4 4.9 %collective-permute-start.4 = (bf16[144,256]{1,0:T(8,128)(2,1)}, bf16[144,256]{1,0:T(8,128)(2,1)}, u32[]{:S(2)}, u32[]{:S(2)}) collective-permute-start(bf16[144,256]{1,0:T(8,128)(2,1)} %collective-permute-done.2.refs_0_), channel_id=1, source_target_pairs={{0,8},{4,12},{8,16},{12,20},{16,24},{20,28},{24,0},{28,4},{1,9},{5... | collective-permute-start | bytes 221192 | tf_op jit(solution)/shard_map/ppermute | solution.py:216
  45.3 0.6 copy-done.13
  45.9 1.4 %collective-permute-start.3 = (bf16[144,256]{1,0:T(8,128)(2,1)}, bf16[144,256]{1,0:T(8,128)(2,1)}, u32[]{:S(2)}, u32[]{:S(2)}) collective-permute-start(bf16[144,256]{1,0:T(8,128)(2,1)} %collective-permute-done.2.refs_0_), channel_id=1, source_target_pairs={{0,4},{4,8},{8,12},{12,16},{16,20},{20,24},{24,28},{28,0},{1,5},{5... | collective-permute-start | bytes 221192 | tf_op jit(solution)/shard_map/ppermute | solution.py:216
  47.9 5.3 %collective-permute-done.3.refs_1_ = bf16[144,256]{1,0:T(8,128)(2,1)} collective-permute-done((bf16[144,256]{1,0:T(8,128)(2,1)}, bf16[144,256]{1,0:T(8,128)(2,1)}, u32[]{:S(2)}, u32[]{:S(2)}) %collective-permute-start.3) | collective-permute-done | bytes 73760 | tf_op jit(solution)/shard_map/ppermute | solution.py:216
  53.2 0.9 copy-done.10
  54.1 0.9 copy-done.12
  55.0 0.9 copy-done.14
  55.9 1.5 %fill.2.dense_ref = bf16[1536,256]{1,0:T(8,128)(2,1)S(1)} custom-call(s32[1]{0:T(128)} %bitcast.place_ref, bf16[144,256]{1,0:T(8,128)(2,1)} %collective-permute-done.2.refs_0_, bf16[144,256]{1,0:T(8,128)(2,1)} %collective-permute-done.3.refs_1_, bf16[144,256]{1,0:T(8,128)(2,1)} %collective-permute-done.4.refs_2_, ...), custom_call_target="tpu_custom_call" | custom-call | tf_op jit(solution)/shard_map/fill/pallas_call | solution.py:220
  57.5 1.3 %copy-done.3 = bf16[768,768]{1,0:T(8,128)(2,1)S(1)} copy-done((bf16[768,768]{1,0:T(8,128)(2,1)S(1)}, bf16[768,768]{1,0:T(8,128)(2,1)}, u32[]{:S(2)}) %copy-start.3) | copy-done | bytes 1179672
  58.7 1.3 %send_part.4 = s16[784,256]{1,0:T(8,128)(2,1)S(1)} custom-call(bf16[768,768]{1,0:T(8,128)(2,1)S(1)} %copy-done.1, bf16[768,768]{1,0:T(8,128)(2,1)S(1)} %copy-done.3, bf16[1536,256]{1,0:T(8,128)(2,1)S(1)} %fill.2.dense_ref), custom_call_target="tpu_custom_call" | custom-call | flops 603979776 | bytes 2752512 | tf_op jit(solution)/shard_map/send_part/pallas_call | solution.py:261
  60.2 3.4 %send_part.5 = s16[1040,256]{1,0:T(8,128)(2,1)S(1)} custom-call(bf16[1024,768]{1,0:T(8,128)(2,1)S(1)} %get-tuple-element.24.own_ref.refs_0_, bf16[1024,768]{1,0:T(8,128)(2,1)} %collective-permute-done.1.other_ref.refs_1_, bf16[1536,256]{1,0:T(8,128)(2,1)S(1)} %fill.2.dense_ref), custom_call_target="tpu_custom_call" | custom-call | flops 805306368 | bytes 3670016 | tf_op jit(solution)/shard_map/send_part/pallas_call | solution.py:261
  63.6 0.6 collective-permute-start.11
  64.1 1.5 %collective-permute-start.22 = (s16[784,256]{1,0:T(8,128)(2,1)S(1)}, s16[784,256]{1,0:T(8,128)(2,1)S(1)}, u32[]{:S(2)}, u32[]{:S(2)}) collective-permute-start(s16[784,256]{1,0:T(8,128)(2,1)S(1)} %send_part.4), channel_id=1, source_target_pairs={{0,2},{1,3},{2,0},{3,1},{4,6},{5,7},{6,4},{7,5},{8,10},{9,11},{10,... | collective-permute-start | bytes 1204232 | tf_op jit(solution)/shard_map/ppermute | solution.py:273
  66.2 1.8 %send_part.6 = s16[1040,256]{1,0:T(8,128)(2,1)S(1)} custom-call(bf16[1024,768]{1,0:T(8,128)(2,1)S(1)} %get-tuple-element.27.own_ref.refs_0_, bf16[1024,768]{1,0:T(8,128)(2,1)S(1)} %collective-permute-done.10.other_ref.refs_1_, bf16[1536,256]{1,0:T(8,128)(2,1)S(1)} %fill.2.dense_ref), custom_call_target="tpu_custom_call" | custom-call | flops 805306368 | bytes 3670016 | tf_op jit(solution)/shard_map/send_part/pallas_call | solution.py:261
  68.0 1.6 %collective-permute-start.20 = (s16[1040,256]{1,0:T(8,128)(2,1)S(1)}, s16[1040,256]{1,0:T(8,128)(2,1)S(1)}, u32[]{:S(2)}, u32[]{:S(2)}) collective-permute-start(s16[1040,256]{1,0:T(8,128)(2,1)S(1)} %send_part.6), channel_id=1, source_target_pairs={{0,2},{1,3},{2,0},{3,1},{4,6},{5,7},{6,4},{7,5},{8,10},{9,11},{10,... | collective-permute-start | bytes 1597448 | tf_op jit(solution)/shard_map/ppermute | solution.py:273
  70.1 4.3 %collective-permute-done.18.refs_7_ = bf16[144,256]{1,0:T(8,128)(2,1)S(1)} collective-permute-done((bf16[144,256]{1,0:T(8,128)(2,1)S(1)}, bf16[144,256]{1,0:T(8,128)(2,1)S(1)}, u32[]{:S(2)}, u32[]{:S(2)}) %collective-permute-start.18) | collective-permute-done | bytes 73760 | tf_op jit(solution)/shard_map/ppermute | solution.py:216
  74.5 2.4 %collective-permute-start.15 = (bf16[144,256]{1,0:T(8,128)(2,1)S(1)}, bf16[144,256]{1,0:T(8,128)(2,1)S(1)}, u32[]{:S(2)}, u32[]{:S(2)}) collective-permute-start(bf16[144,256]{1,0:T(8,128)(2,1)S(1)} %copy-done.8), channel_id=1, source_target_pairs={{0,16},{4,20},{8,24},{12,28},{16,0},{20,4},{24,8},{28,12},{1,17},{... | collective-permute-start | bytes 221192 | tf_op jit(solution)/shard_map/ppermute | solution.py:216
  76.9 2.8 %collective-permute-done.16.refs_5_ = bf16[144,256]{1,0:T(8,128)(2,1)S(1)} collective-permute-done((bf16[144,256]{1,0:T(8,128)(2,1)S(1)}, bf16[144,256]{1,0:T(8,128)(2,1)S(1)}, u32[]{:S(2)}, u32[]{:S(2)}) %collective-permute-start.16) | collective-permute-done | bytes 73760 | tf_op jit(solution)/shard_map/ppermute | solution.py:216
  79.8 1.1 %collective-permute-done.15.refs_4_ = bf16[144,256]{1,0:T(8,128)(2,1)S(1)} collective-permute-done((bf16[144,256]{1,0:T(8,128)(2,1)S(1)}, bf16[144,256]{1,0:T(8,128)(2,1)S(1)}, u32[]{:S(2)}, u32[]{:S(2)}) %collective-permute-start.15) | collective-permute-done | bytes 73760 | tf_op jit(solution)/shard_map/ppermute | solution.py:216
  80.8 2.9 %collective-permute-start.13 = (bf16[144,256]{1,0:T(8,128)(2,1)S(1)}, bf16[144,256]{1,0:T(8,128)(2,1)S(1)}, u32[]{:S(2)}, u32[]{:S(2)}) collective-permute-start(bf16[144,256]{1,0:T(8,128)(2,1)S(1)} %copy-done.8), channel_id=1, source_target_pairs={{0,8},{4,12},{8,16},{12,20},{16,24},{20,28},{24,0},{28,4},{1,9},{5... | collective-permute-start | bytes 221192 | tf_op jit(solution)/shard_map/ppermute | solution.py:216
  83.7 2.1 %collective-permute-done.14.refs_3_ = bf16[144,256]{1,0:T(8,128)(2,1)S(1)} collective-permute-done((bf16[144,256]{1,0:T(8,128)(2,1)S(1)}, bf16[144,256]{1,0:T(8,128)(2,1)S(1)}, u32[]{:S(2)}, u32[]{:S(2)}) %collective-permute-start.14) | collective-permute-done | bytes 73760 | tf_op jit(solution)/shard_map/ppermute | solution.py:216
  85.8 2.9 %collective-permute-start.12 = (bf16[144,256]{1,0:T(8,128)(2,1)S(1)}, bf16[144,256]{1,0:T(8,128)(2,1)S(1)}, u32[]{:S(2)}, u32[]{:S(2)}) collective-permute-start(bf16[144,256]{1,0:T(8,128)(2,1)S(1)} %copy-done.8), channel_id=1, source_target_pairs={{0,4},{4,8},{8,12},{12,16},{16,20},{20,24},{24,28},{28,0},{1,5},{5... | collective-permute-start | bytes 221192 | tf_op jit(solution)/shard_map/ppermute | solution.py:216
  89.2 3.6 %collective-permute-done.12.refs_1_ = bf16[144,256]{1,0:T(8,128)(2,1)S(1)} collective-permute-done((bf16[144,256]{1,0:T(8,128)(2,1)S(1)}, bf16[144,256]{1,0:T(8,128)(2,1)S(1)}, u32[]{:S(2)}, u32[]{:S(2)}) %collective-permute-start.12) | collective-permute-done | bytes 73760 | tf_op jit(solution)/shard_map/ppermute | solution.py:216
  93.4 2.1 %join_part.4.refs_4_ = bf16[3072,256]{1,0:T(8,128)(2,1)} custom-call(bf16[768,768]{1,0:T(8,128)(2,1)S(1)} %copy-done.1, bf16[768,768]{1,0:T(8,128)(2,1)S(1)} %copy-done.4, bf16[1536,256]{1,0:T(8,128)(2,1)S(1)} %fill.3.dense_ref.refs_2_, s16[784,256]{1,0:T(8,128)(2,1)S(1)} %collective-permute-done.22.refs_0_), custom_call_target="tpu_custom_call" | custom-call | flops 603979776 | bytes 2752512 | tf_op jit(solution)/shard_map/join_part/pallas_call | solution.py:290
  95.5 4.1 %join_part.5.refs_4_ = bf16[3072,256]{1,0:T(8,128)(2,1)} custom-call(bf16[1024,768]{1,0:T(8,128)(2,1)S(1)} %get-tuple-element.24.own_ref.refs_0_, bf16[1024,768]{1,0:T(8,128)(2,1)} %collective-permute-done.1.other_ref.refs_1_, bf16[1536,256]{1,0:T(8,128)(2,1)S(1)} %fill.3.dense_ref.refs_2_, ...), custom_call_target="tpu_custom_call", output_to_operand_aliasing={{}: (4, {})} | custom-call | flops 805306368 | bytes 3670016 | tf_op jit(solution)/shard_map/join_part/pallas_call | solution.py:290
  99.6 2.4 %join_part.6.refs_4_ = bf16[3072,256]{1,0:T(8,128)(2,1)} custom-call(bf16[1024,768]{1,0:T(8,128)(2,1)S(1)} %get-tuple-element.27.own_ref.refs_0_, bf16[1024,768]{1,0:T(8,128)(2,1)S(1)} %collective-permute-done.10.other_ref.refs_1_, bf16[1536,256]{1,0:T(8,128)(2,1)S(1)} %fill.3.dense_ref.refs_2_, ...), custom_call_target="tpu_custom_call", output_to_operand_aliasing={{}: (4, {})} | custom-call | flops 805306368 | bytes 3670016 | tf_op jit(solution)/shard_map/join_part/pallas_call | solution.py:290
  102.0 1.0 %join_part.7 = bf16[3072,256]{1,0:T(8,128)(2,1)} custom-call(bf16[256,768]{1,0:T(8,128)(2,1)S(1)} %get-tuple-element.28.own_ref.refs_0_, bf16[256,768]{1,0:T(8,128)(2,1)S(1)} %collective-permute-done.11.other_ref.refs_1_, bf16[1536,256]{1,0:T(8,128)(2,1)S(1)} %fill.3.dense_ref.refs_2_, ...), custom_call_target="tpu_custom_call", output_to_operand_aliasing={{}: (4, {})} | custom-call | flops 201326592 | bytes 917504 | tf_op jit(solution)/shard_map/join_part/pallas_call | solution.py:290
  (49 shorter events, 3.4 us)
Async XLA Ops:
  0.7 1.0 copy-start.6
  1.6 0.7 copy-start.15
  3.6 17.7 %all-to-all-start = ((bf16[8,80,256]{2,1,0:T(8,128)(2,1)}), bf16[8,80,256]{2,1,0:T(8,128)(2,1)}, u32[]{:S(2)}, u32[]{:S(2)}) async-start(bf16[8,80,256]{2,1,0:T(8,128)(2,1)} %pack.1), calls=%async_computation | async-start | bytes 655360 | tf_op jit(solution)/shard_map/all_to_all | solution.py:181
  11.6 2.3 %copy-start.5 = (bf16[3072,768]{1,0:T(8,128)(2,1)S(1)}, bf16[3072,768]{1,0:T(8,128)(2,1)}, u32[]{:S(2)}) copy-start(bf16[3072,768]{1,0:T(8,128)(2,1)} %rows_ref.1) | copy-start | bytes 14155780
  13.9 11.5 %copy-start.16 = (s32[4,1]{0,1:T(1,128)S(1)}, s32[4,1]{0,1:T(1,128)}, u32[]{:S(2)}) copy-start(s32[4,1]{0,1:T(1,128)} %param.11) | copy-start | bytes 52
  15.6 1.0 copy-start
  21.3 3.1 %collective-permute-start = (bf16[768,768]{1,0:T(8,128)(2,1)}, bf16[768,768]{1,0:T(8,128)(2,1)S(1)}, u32[]{:S(2)}, u32[]{:S(2)}) collective-permute-start(bf16[768,768]{1,0:T(8,128)(2,1)} %copy-done), channel_id=1, source_target_pairs={{0,1},{1,0},{2,3},{3,2},{4,5},{5,4},{6,7},{7,6},{8,9},{9,8},{10,11... | collective-permute-start | bytes 3538952 | tf_op jit(solution)/shard_map/ppermute | solution.py:230
  24.3 1.0 copy-start.2
  25.3 34.8 %collective-permute-start.1 = (bf16[1024,768]{1,0:T(8,128)(2,1)S(1)}, bf16[1024,768]{1,0:T(8,128)(2,1)}, u32[]{:S(2)}, u32[]{:S(2)}) collective-permute-start(bf16[1024,768]{1,0:T(8,128)(2,1)S(1)} %get-tuple-element.24.own_ref.refs_0_), channel_id=1, source_target_pairs={{0,1},{1,0},{2,3},{3,2},{4,5},{5,4},{6,7},{7,6},{8,9},{9,8},{10,11... | collective-permute-start | bytes 4718600 | tf_op jit(solution)/shard_map/ppermute | solution.py:255
  26.6 0.6 copy-start.7
  27.2 4.7 %collective-permute-start.2 = (bf16[144,256]{1,0:T(8,128)(2,1)S(1)}, bf16[144,256]{1,0:T(8,128)(2,1)}, u32[]{:S(2)}, u32[]{:S(2)}) collective-permute-start(bf16[144,256]{1,0:T(8,128)(2,1)S(1)} %get-tuple-element.25), channel_id=1, source_target_pairs={{0,2},{1,3},{2,0},{3,1},{4,6},{5,7},{6,4},{7,5},{8,10},{9,11},{10,... | collective-permute-start | bytes 221192 | tf_op jit(solution)/shard_map/ppermute | solution.py:234
  31.9 5.5 %collective-permute-start.9 = (bf16[144,256]{1,0:T(8,128)(2,1)}, bf16[144,256]{1,0:T(8,128)(2,1)S(1)}, u32[]{:S(2)}, u32[]{:S(2)}) collective-permute-start(bf16[144,256]{1,0:T(8,128)(2,1)} %collective-permute-done.2.refs_0_), channel_id=1, source_target_pairs={{0,28},{4,0},{8,4},{12,8},{16,12},{20,16},{24,20},{28,24},{1,29},{... | collective-permute-start | bytes 221192 | tf_op jit(solution)/shard_map/ppermute | solution.py:216
  34.2 5.6 %collective-permute-start.8 = (bf16[144,256]{1,0:T(8,128)(2,1)}, bf16[144,256]{1,0:T(8,128)(2,1)S(1)}, u32[]{:S(2)}, u32[]{:S(2)}) collective-permute-start(bf16[144,256]{1,0:T(8,128)(2,1)} %collective-permute-done.2.refs_0_), channel_id=1, source_target_pairs={{0,24},{4,28},{8,0},{12,4},{16,8},{20,12},{24,16},{28,20},{1,25},{... | collective-permute-start | bytes 221192 | tf_op jit(solution)/shard_map/ppermute | solution.py:216
  34.2 11.1 %collective-permute-start.7 = (bf16[144,256]{1,0:T(8,128)(2,1)}, bf16[144,256]{1,0:T(8,128)(2,1)S(1)}, u32[]{:S(2)}, u32[]{:S(2)}) collective-permute-start(bf16[144,256]{1,0:T(8,128)(2,1)} %collective-permute-done.2.refs_0_), channel_id=1, source_target_pairs={{0,20},{4,24},{8,28},{12,0},{16,4},{20,8},{24,12},{28,16},{1,21},{... | collective-permute-start | bytes 221192 | tf_op jit(solution)/shard_map/ppermute | solution.py:216
  35.8 11.8 %collective-permute-start.6 = (bf16[144,256]{1,0:T(8,128)(2,1)}, bf16[144,256]{1,0:T(8,128)(2,1)}, u32[]{:S(2)}, u32[]{:S(2)}) collective-permute-start(bf16[144,256]{1,0:T(8,128)(2,1)} %collective-permute-done.2.refs_0_), channel_id=1, source_target_pairs={{0,16},{4,20},{8,24},{12,28},{16,0},{20,4},{24,8},{28,12},{1,17},{... | collective-permute-start | bytes 221192 | tf_op jit(solution)/shard_map/ppermute | solution.py:216
  37.4 0.6 copy-start.9
  38.0 9.9 %collective-permute-start.5 = (bf16[144,256]{1,0:T(8,128)(2,1)}, bf16[144,256]{1,0:T(8,128)(2,1)}, u32[]{:S(2)}, u32[]{:S(2)}) collective-permute-start(bf16[144,256]{1,0:T(8,128)(2,1)} %collective-permute-done.2.refs_0_), channel_id=1, source_target_pairs={{0,12},{4,16},{8,20},{12,24},{16,28},{20,0},{24,4},{28,8},{1,13},{... | collective-permute-start | bytes 221192 | tf_op jit(solution)/shard_map/ppermute | solution.py:216
  39.8 0.6 copy-start.11
  40.4 7.5 %collective-permute-start.4 = (bf16[144,256]{1,0:T(8,128)(2,1)}, bf16[144,256]{1,0:T(8,128)(2,1)}, u32[]{:S(2)}, u32[]{:S(2)}) collective-permute-start(bf16[144,256]{1,0:T(8,128)(2,1)} %collective-permute-done.2.refs_0_), channel_id=1, source_target_pairs={{0,8},{4,12},{8,16},{12,20},{16,24},{20,28},{24,0},{28,4},{1,9},{5... | collective-permute-start | bytes 221192 | tf_op jit(solution)/shard_map/ppermute | solution.py:216
  45.3 0.6 copy-start.13
  45.9 7.4 %collective-permute-start.3 = (bf16[144,256]{1,0:T(8,128)(2,1)}, bf16[144,256]{1,0:T(8,128)(2,1)}, u32[]{:S(2)}, u32[]{:S(2)}) collective-permute-start(bf16[144,256]{1,0:T(8,128)(2,1)} %collective-permute-done.2.refs_0_), channel_id=1, source_target_pairs={{0,4},{4,8},{8,12},{12,16},{16,20},{20,24},{24,28},{28,0},{1,5},{5... | collective-permute-start | bytes 221192 | tf_op jit(solution)/shard_map/ppermute | solution.py:216
  47.2 10.2 %copy-start.1 = (bf16[768,768]{1,0:T(8,128)(2,1)S(1)}, bf16[768,768]{1,0:T(8,128)(2,1)}, u32[]{:S(2)}) copy-start(bf16[768,768]{1,0:T(8,128)(2,1)} %copy-done) | copy-start | bytes 3538948
  53.2 0.9 copy-start.10
  54.1 0.9 copy-start.12
  55.0 0.9 copy-start.14
  57.5 1.3 %copy-start.3 = (bf16[768,768]{1,0:T(8,128)(2,1)S(1)}, bf16[768,768]{1,0:T(8,128)(2,1)}, u32[]{:S(2)}) copy-start(bf16[768,768]{1,0:T(8,128)(2,1)} %copy-done.2) | copy-start | bytes 3538948
  60.1 3.5 %collective-permute-start.10 = (bf16[1024,768]{1,0:T(8,128)(2,1)S(1)}, bf16[1024,768]{1,0:T(8,128)(2,1)S(1)}, u32[]{:S(2)}, u32[]{:S(2)}) collective-permute-start(bf16[1024,768]{1,0:T(8,128)(2,1)S(1)} %get-tuple-element.27.own_ref.refs_0_), channel_id=1, source_target_pairs={{0,1},{1,0},{2,3},{3,2},{4,5},{5,4},{6,7},{7,6},{8,9},{9,8},{10,11... | collective-permute-start | bytes 4718600 | tf_op jit(solution)/shard_map/ppermute | solution.py:255
  63.6 6.0 %collective-permute-start.11 = (bf16[256,768]{1,0:T(8,128)(2,1)S(1)}, bf16[256,768]{1,0:T(8,128)(2,1)S(1)}, u32[]{:S(2)}, u32[]{:S(2)}) collective-permute-start(bf16[256,768]{1,0:T(8,128)(2,1)S(1)} %get-tuple-element.28.own_ref.refs_0_), channel_id=1, source_target_pairs={{0,1},{1,0},{2,3},{3,2},{4,5},{5,4},{6,7},{7,6},{8,9},{9,8},{10,11... | collective-permute-start | bytes 1179656 | tf_op jit(solution)/shard_map/ppermute | solution.py:255
  64.1 29.3 %collective-permute-start.22 = (s16[784,256]{1,0:T(8,128)(2,1)S(1)}, s16[784,256]{1,0:T(8,128)(2,1)S(1)}, u32[]{:S(2)}, u32[]{:S(2)}) collective-permute-start(s16[784,256]{1,0:T(8,128)(2,1)S(1)} %send_part.4), channel_id=1, source_target_pairs={{0,2},{1,3},{2,0},{3,1},{4,6},{5,7},{6,4},{7,5},{8,10},{9,11},{10,... | collective-permute-start | bytes 1204232 | tf_op jit(solution)/shard_map/ppermute | solution.py:273
  65.6 29.9 %collective-permute-start.21 = (s16[1040,256]{1,0:T(8,128)(2,1)S(1)}, s16[1040,256]{1,0:T(8,128)(2,1)S(1)}, u32[]{:S(2)}, u32[]{:S(2)}) collective-permute-start(s16[1040,256]{1,0:T(8,128)(2,1)S(1)} %send_part.5), channel_id=1, source_target_pairs={{0,2},{1,3},{2,0},{3,1},{4,6},{5,7},{6,4},{7,5},{8,10},{9,11},{10,... | collective-permute-start | bytes 1597448 | tf_op jit(solution)/shard_map/ppermute | solution.py:273
  67.9 2.0 %copy-start.8 = (bf16[144,256]{1,0:T(8,128)(2,1)S(1)}, bf16[144,256]{1,0:T(8,128)(2,1)}, u32[]{:S(2)}) copy-start(bf16[144,256]{1,0:T(8,128)(2,1)} %copy-done.7) | copy-start | bytes 221188
  68.0 25.4 %copy-start.4 = (bf16[768,768]{1,0:T(8,128)(2,1)S(1)}, bf16[768,768]{1,0:T(8,128)(2,1)}, u32[]{:S(2)}) copy-start(bf16[768,768]{1,0:T(8,128)(2,1)} %copy-done.2) | copy-start | bytes 3538948
  68.0 31.6 %collective-permute-start.20 = (s16[1040,256]{1,0:T(8,128)(2,1)S(1)}, s16[1040,256]{1,0:T(8,128)(2,1)S(1)}, u32[]{:S(2)}, u32[]{:S(2)}) collective-permute-start(s16[1040,256]{1,0:T(8,128)(2,1)S(1)} %send_part.6), channel_id=1, source_target_pairs={{0,2},{1,3},{2,0},{3,1},{4,6},{5,7},{6,4},{7,5},{8,10},{9,11},{10,... | collective-permute-start | bytes 1597448 | tf_op jit(solution)/shard_map/ppermute | solution.py:273
  70.0 4.4 %collective-permute-start.18 = (bf16[144,256]{1,0:T(8,128)(2,1)S(1)}, bf16[144,256]{1,0:T(8,128)(2,1)S(1)}, u32[]{:S(2)}, u32[]{:S(2)}) collective-permute-start(bf16[144,256]{1,0:T(8,128)(2,1)S(1)} %copy-done.8), channel_id=1, source_target_pairs={{0,28},{4,0},{8,4},{12,8},{16,12},{20,16},{24,20},{28,24},{1,29},{... | collective-permute-start | bytes 221192 | tf_op jit(solution)/shard_map/ppermute | solution.py:216
  70.1 4.4 %collective-permute-start.17 = (bf16[144,256]{1,0:T(8,128)(2,1)S(1)}, bf16[144,256]{1,0:T(8,128)(2,1)S(1)}, u32[]{:S(2)}, u32[]{:S(2)}) collective-permute-start(bf16[144,256]{1,0:T(8,128)(2,1)S(1)} %copy-done.8), channel_id=1, source_target_pairs={{0,24},{4,28},{8,0},{12,4},{16,8},{20,12},{24,16},{28,20},{1,25},{... | collective-permute-start | bytes 221192 | tf_op jit(solution)/shard_map/ppermute | solution.py:216
  74.4 5.3 %collective-permute-start.16 = (bf16[144,256]{1,0:T(8,128)(2,1)S(1)}, bf16[144,256]{1,0:T(8,128)(2,1)S(1)}, u32[]{:S(2)}, u32[]{:S(2)}) collective-permute-start(bf16[144,256]{1,0:T(8,128)(2,1)S(1)} %copy-done.8), channel_id=1, source_target_pairs={{0,20},{4,24},{8,28},{12,0},{16,4},{20,8},{24,12},{28,16},{1,21},{... | collective-permute-start | bytes 221192 | tf_op jit(solution)/shard_map/ppermute | solution.py:216
  74.5 6.4 %collective-permute-start.15 = (bf16[144,256]{1,0:T(8,128)(2,1)S(1)}, bf16[144,256]{1,0:T(8,128)(2,1)S(1)}, u32[]{:S(2)}, u32[]{:S(2)}) collective-permute-start(bf16[144,256]{1,0:T(8,128)(2,1)S(1)} %copy-done.8), channel_id=1, source_target_pairs={{0,16},{4,20},{8,24},{12,28},{16,0},{20,4},{24,8},{28,12},{1,17},{... | collective-permute-start | bytes 221192 | tf_op jit(solution)/shard_map/ppermute | solution.py:216
  79.7 6.2 %collective-permute-start.14 = (bf16[144,256]{1,0:T(8,128)(2,1)S(1)}, bf16[144,256]{1,0:T(8,128)(2,1)S(1)}, u32[]{:S(2)}, u32[]{:S(2)}) collective-permute-start(bf16[144,256]{1,0:T(8,128)(2,1)S(1)} %copy-done.8), channel_id=1, source_target_pairs={{0,12},{4,16},{8,20},{12,24},{16,28},{20,0},{24,4},{28,8},{1,13},{... | collective-permute-start | bytes 221192 | tf_op jit(solution)/shard_map/ppermute | solution.py:216
  80.8 7.8 %collective-permute-start.13 = (bf16[144,256]{1,0:T(8,128)(2,1)S(1)}, bf16[144,256]{1,0:T(8,128)(2,1)S(1)}, u32[]{:S(2)}, u32[]{:S(2)}) collective-permute-start(bf16[144,256]{1,0:T(8,128)(2,1)S(1)} %copy-done.8), channel_id=1, source_target_pairs={{0,8},{4,12},{8,16},{12,20},{16,24},{20,28},{24,0},{28,4},{1,9},{5... | collective-permute-start | bytes 221192 | tf_op jit(solution)/shard_map/ppermute | solution.py:216
  85.8 7.0 %collective-permute-start.12 = (bf16[144,256]{1,0:T(8,128)(2,1)S(1)}, bf16[144,256]{1,0:T(8,128)(2,1)S(1)}, u32[]{:S(2)}, u32[]{:S(2)}) collective-permute-start(bf16[144,256]{1,0:T(8,128)(2,1)S(1)} %copy-done.8), channel_id=1, source_target_pairs={{0,4},{4,8},{8,12},{12,16},{16,20},{20,24},{24,28},{28,0},{1,5},{5... | collective-permute-start | bytes 221192 | tf_op jit(solution)/shard_map/ppermute | solution.py:216
  88.7 13.4 %collective-permute-start.19 = (s16[272,256]{1,0:T(8,128)(2,1)S(1)}, s16[272,256]{1,0:T(8,128)(2,1)S(1)}, u32[]{:S(2)}, u32[]{:S(2)}) collective-permute-start(s16[272,256]{1,0:T(8,128)(2,1)S(1)} %send_part.7), channel_id=1, source_target_pairs={{0,2},{1,3},{2,0},{3,1},{4,6},{5,7},{6,4},{7,5},{8,10},{9,11},{10,... | collective-permute-start | bytes 417800 | tf_op jit(solution)/shard_map/ppermute | solution.py:273

commit v4 on v0

v4 whole, which is shorter than its diff:
```python
from functools import partial

import jax
import jax.numpy as jnp
from jax import lax
from jax.experimental import pallas as pl
from jax.experimental.pallas import tpu as pltpu
from jax.sharding import PartitionSpec as P

STEPS = 4
CORES = 2
HALVES = 2
CUTS = (0.0, 0.08, 0.42, 0.75, 0.92, 1.0)
CODE_TOP = 32767.0
FRACTION = 8192.0
META_ROWS = 16
PARAMS = pltpu.CompilerParams(vmem_limit_bytes=16 * 1024 * 1024)
SMEM = pl.BlockSpec(memory_space=pltpu.SMEM)
VMEM = pl.BlockSpec(memory_space=pltpu.VMEM)
HBM = pl.BlockSpec(memory_space=pltpu.HBM)


def pair_offsets(col_count):
    pairs = col_count // CORES
    offsets = set()
    for core in range(CORES):
        for step in range(STEPS):
            offsets.add(-((core - step) // CORES) % pairs)
    return sorted(offsets)


def row_chunks(block_count):
    marks = sorted({round(block_count * cut) for cut in CUTS})
    return [(first, last - first) for first, last in zip(marks, marks[1:])]


def pack_kernel(list_ref, count_ref, panel_ref, *piece_refs):
    peers = len(piece_refs)
    slots, tile_width = panel_ref.shape[2:4]
    share = slots * tile_width // peers
    place = lax.axis_index("row") // HALVES
    lane = lax.broadcasted_iota(jnp.int32, (META_ROWS, tile_width), 1)
    info = jnp.where(lane == slots, count_ref[0, 0], 0)
    for slot in range(slots):
        info = jnp.where(lane == slot, list_ref[0, 0, slot], info)
    info = info.astype(jnp.float32).astype(panel_ref.dtype)
    for shift, piece_ref in enumerate(piece_refs):
        first = lax.rem(place + shift, peers) * share
        start = pl.multiple_of(lax.rem(first, tile_width), META_ROWS)
        piece_ref[pl.ds(0, share), :] = panel_ref[0, 0, first // tile_width, pl.ds(start, share), :]
        piece_ref[pl.ds(share, META_ROWS), :] = info


def choose_kernel(col_peers, offsets, owner_ref, *refs):
    out_refs = refs[len(refs) - len(offsets) :]
    piece_refs = refs[: len(refs) - len(offsets)]
    peers = len(piece_refs)
    share = piece_refs[0].shape[0] - META_ROWS
    row = lax.axis_index("row")
    core = lax.rem(lax.axis_index("col"), CORES)
    sign = 1 - 2 * core
    line = lax.broadcasted_iota(jnp.int32, (META_ROWS, piece_refs[0].shape[1]), 0)
    for offset, out_ref in zip(offsets, out_refs):
        out_ref[...] = jnp.zeros_like(out_ref)
        for group, shift in enumerate((0, sign)):
            step = lax.rem(CORES * offset - shift + col_peers, col_peers)
            holder = owner_ref[0, jnp.minimum(step, STEPS - 1)]
            here = (step < STEPS) & (lax.rem(holder, HALVES) == lax.rem(row, HALVES))
            back = lax.rem(row // HALVES - holder // HALVES + peers, peers)
            for number, piece_ref in enumerate(piece_refs):

                @pl.when(here & (back == number))
                def _():
                    out_ref[pl.ds(group * share, share), :] = piece_ref[pl.ds(0, share), :]
                    rows = pl.ds(CORES * share, META_ROWS)
                    out_ref[rows, :] = jnp.where(line == group, piece_ref[pl.ds(share, META_ROWS), :], out_ref[rows, :])


def fill_kernel(slots, *refs):
    piece_refs, dense_ref = refs[:-1], refs[-1]
    peers = len(piece_refs)
    share = (piece_refs[0].shape[0] - META_ROWS) // CORES
    width, tile_width = dense_ref.shape[0] // CORES, dense_ref.shape[1]
    place = lax.axis_index("row") // HALVES
    table = piece_refs[0][pl.ds(CORES * share, META_ROWS), :].astype(jnp.float32)
    line = lax.broadcasted_iota(jnp.int32, table.shape, 0)
    lane = lax.broadcasted_iota(jnp.int32, table.shape, 1)

    def entry(group, spot):
        return jnp.max(jnp.where((line == group) & (lane == spot), table, 0.0)).astype(jnp.int32)

    dense_ref[...] = jnp.zeros_like(dense_ref)
    for group in range(CORES):
        count = entry(group, slots)
        starts = [group * width + entry(group, slot) * tile_width for slot in range(slots)]
        for shift, piece_ref in enumerate(piece_refs):
            first = lax.rem(place - shift + peers, peers) * share
            slot = first // tile_width
            start = starts[0]
            for other in range(1, slots):
                start = jnp.where(slot == other, starts[other], start)

            @pl.when(slot < count)
            def _():
                spot = pl.multiple_of(start + lax.rem(first, tile_width), META_ROWS)
                dense_ref[pl.ds(spot, share), :] = piece_ref[pl.ds(group * share, share), :]


def screened(mask_ref, block, rows_ref):
    tiles = mask_ref.shape[0]
    tile_width = rows_ref.shape[1] // tiles
    parts = []
    for tile in range(tiles):
        live = mask_ref[tile, block].astype(jnp.float32).astype(rows_ref.dtype)
        parts.append(rows_ref[:, pl.ds(tile * tile_width, tile_width)] * live)
    return jnp.concatenate(parts, axis=1)


def block_product(mask_refs, block, row_refs, dense_ref):
    width = row_refs[0].shape[1]
    return sum(
        jnp.dot(
            screened(mask_ref, block, rows_ref),
            dense_ref[pl.ds(group * width, width), :],
            preferred_element_type=jnp.float32,
        )
        for group, (mask_ref, rows_ref) in enumerate(zip(mask_refs, row_refs))
    )


def send_kernel(first, span, height, mask_ref, other_mask_ref, own_ref, other_ref, dense_ref, code_ref, scale_ref):
    scale_ref[...] = jnp.zeros_like(scale_ref)

    def body(own_block, other_block):
        step = pl.program_id(0)
        total = block_product((mask_ref, other_mask_ref), first + step, (own_block, other_block), dense_ref)
        top = jnp.max(jnp.abs(total), axis=0, keepdims=True)
        unit = jnp.where(top > 0, top, 1.0) * (1.0 / CODE_TOP)
        power = jnp.floor(jnp.log2(unit))
        fraction = jnp.ceil(unit * jnp.exp2(-power) * FRACTION)
        unit = fraction * jnp.exp2(power) * (1.0 / FRACTION)
        code = jnp.clip(jnp.round(total * (1.0 / unit)), -CODE_TOP, CODE_TOP)
        code_ref[pl.ds(pl.multiple_of(step * height, height), height), :] = code.astype(jnp.int32).astype(jnp.int16)
        scale_ref[pl.ds(2 * step, 1), :] = power
        scale_ref[pl.ds(2 * step + 1, 1), :] = fraction

    block = pl.BlockSpec((height, own_ref.shape[1]), lambda i: (first + i, 0))
    pltpu.emit_pipeline(body, grid=(span,), in_specs=[block, block])(own_ref, other_ref)
    rows = scale_ref.shape[0]
    code_ref[pl.ds(code_ref.shape[0] - rows, rows), :] = scale_ref[...].astype(jnp.int32).astype(jnp.int16)


def join_kernel(first, span, height, arrivals, mask_ref, other_mask_ref, own_ref, other_ref, dense_ref, *refs):
    code_refs, out_ref, scale_ref = refs[:arrivals], refs[-2], refs[-1]
    rows = scale_ref.shape[0] // max(arrivals, 1)
    for number, code_ref in enumerate(code_refs):
        scales = code_ref[pl.ds(code_ref.shape[0] - rows, rows), :].astype(jnp.int32).astype(jnp.float32)
        scale_ref[pl.ds(number * rows, rows), :] = scales

    def body(own_block, other_block, out_block):
        step = pl.program_id(0)
        total = block_product((mask_ref, other_mask_ref), first + step, (own_block, other_block), dense_ref)
        for number, code_ref in enumerate(code_refs):
            power = scale_ref[pl.ds(number * rows + 2 * step, 1), :]
            fraction = scale_ref[pl.ds(number * rows + 2 * step + 1, 1), :]
            code = code_ref[pl.ds(pl.multiple_of(step * height, height), height), :]
            unit = fraction * jnp.exp2(power) * (1.0 / FRACTION)
            total = total + code.astype(jnp.int32).astype(jnp.float32) * unit
        out_block[...] = total.astype(out_block.dtype)

    block = pl.BlockSpec((height, own_ref.shape[1]), lambda i: (first + i, 0))
    out_block = pl.BlockSpec((height, out_ref.shape[1]), lambda i: (first + i, 0))
    pltpu.emit_pipeline(
        body, grid=(span,), in_specs=[block, block], out_specs=[out_block]
    )(own_ref, other_ref, out_ref)


def after(value, *earlier):
    return lax.optimization_barrier((value, *earlier))[0]


def shards(amplitudes, pair_mask, integrals, tile_list, tile_count, owner):
    row_count, full_width = amplitudes.shape
    slots, tile_width = integrals.shape[2], integrals.shape[-1]
    block_count = pair_mask.shape[0]
    block_rows = row_count // block_count
    row_peers, col_peers = lax.axis_size("row"), lax.axis_size("col")
    peers = row_peers // HALVES
    share = slots * tile_width // peers
    offsets = pair_offsets(col_peers)
    chunks = row_chunks(block_count)

    def along(value, shift):
        return lax.ppermute(value, "row", [(r, (r + HALVES * shift) % row_peers) for r in range(row_peers)])

    def across(value, flip, down):
        pairs = []
        for r in range(row_peers):
            for c in range(col_peers):
                pairs.append((r * col_peers + c, (r ^ flip) * col_peers + (c - CORES * down) % col_peers))
        return lax.ppermute(value, ("row", "col"), pairs)

    swap = [(c, c ^ 1) for c in range(col_peers)]
    other = lax.ppermute(amplitudes, "col", swap)
    coupled = pair_mask.T
    other_coupled = lax.ppermute(coupled, "col", swap)

    pieces = pl.pallas_call(
        pack_kernel,
        in_specs=[SMEM, SMEM, VMEM],
        out_specs=[VMEM] * peers,
        out_shape=[jax.ShapeDtypeStruct((share + META_ROWS, tile_width), integrals.dtype)] * peers,
        compiler_params=PARAMS,
        name="pack",
    )(tile_list, tile_count, integrals)
    pieces = [piece if shift == 0 else along(piece, shift) for shift, piece in enumerate(pieces)]

    chosen = pl.pallas_call(
        partial(choose_kernel, col_peers, offsets),
        in_specs=[SMEM] + [VMEM] * peers,
        out_specs=[VMEM] * len(offsets),
        out_shape=[jax.ShapeDtypeStruct((CORES * share + META_ROWS, tile_width), integrals.dtype)] * len(offsets),
        compiler_params=PARAMS,
        name="choose",
    )(owner.T, *pieces)

    def weights_of(data):
        held = [data] + [along(data, shift) for shift in range(1, peers)]
        return pl.pallas_call(
            partial(fill_kernel, slots),
            in_specs=[VMEM] * peers,
            out_specs=VMEM,
            out_shape=jax.ShapeDtypeStruct((CORES * full_width, tile_width), integrals.dtype),
            compiler_params=PARAMS,
            name="fill",
        )(*held)

    plans = {}
    for offset, data in zip(offsets, chosen):
        if offset:
            plans[offset] = weights_of(across(data, 0, offset) + across(data, 1, offset))

    def cost(span):
        return pl.CostEstimate(
            flops=2 * span * block_rows * CORES * full_width * tile_width,
            bytes_accessed=span * block_rows * (CORES * full_width + tile_width) * 2,
            transcendentals=0,
        )

    arrived, sent = [], []
    for first, span in chunks:
        height = -(-2 * span // META_ROWS) * META_ROWS
        received = []
        earlier = sent[-1:] + [part for parts in arrived[:-1] for part in parts]
        for offset in offsets:
            if offset == 0:
                continue
            code = pl.pallas_call(
                partial(send_kernel, first, span, block_rows),
                in_specs=[SMEM, SMEM, HBM, HBM, VMEM],
                out_specs=VMEM,
                out_shape=jax.ShapeDtypeStruct((span * block_rows + height, tile_width), jnp.int16),
                scratch_shapes=[pltpu.VMEM((height, tile_width), jnp.float32)],
                compiler_params=PARAMS,
                cost_estimate=cost(span),
                name="send_part",
            )(coupled, other_coupled, amplitudes, other, after(plans[offset], *earlier))
            received.append(across(code, 0, -offset))
            sent.append(code)
        arrived.append(received)

    own = after(chosen[offsets.index(0)], *arrived[0])
    plans[0] = weights_of(own + across(own, 1, 0))

    out = None
    for (first, span), received in zip(chunks, arrived):
        height = -(-2 * span // META_ROWS) * META_ROWS
        operands = [coupled, other_coupled, amplitudes, other, plans[0], *received]
        specs = [SMEM, SMEM, HBM, HBM, VMEM] + [VMEM] * len(received)
        aliases = {}
        if out is not None:
            aliases = {len(operands): 0}
            operands.append(out)
            specs.append(HBM)
        out = pl.pallas_call(
            partial(join_kernel, first, span, block_rows, len(received)),
            in_specs=specs,
            out_specs=HBM,
            out_shape=jax.ShapeDtypeStruct((row_count, tile_width), jnp.bfloat16),
            scratch_shapes=[pltpu.VMEM((height * max(len(received), 1), tile_width), jnp.float32)],
            input_output_aliases=aliases,
            compiler_params=PARAMS,
            cost_estimate=cost(span),
            name="join_part",
        )(*operands)
    return out


def solution(mesh):
    return jax.shard_map(
        shards,
        mesh=mesh,
        in_specs=(
            P("row", "col"),
            P("row", "col"),
            P("row", "col", None, None, None),
            P("row", "col", None),
            P("row", "col"),
            P(None, "col"),
        ),
        out_specs=P("row", "col"),
        check_vma=False,
    )
```

time: 206 us -> 88.5 us (0.43)
  waiting for transfers between devices: 123 us -> 35.7 us
  Pallas kernels: 0 us -> 24.8 us
  starting transfers between devices: 0.46 us -> 22.2 us
  between operations: 16.6 us -> 0.83 us
  matrix products: 15.7 us -> 0 us
  local copies, waits for them, and re-layouts: 18.9 us -> 4.6 us
  blocking collectives: 13 us -> 0 us
  loops' own time: 10.6 us -> 0 us
  other arithmetic: 8.71 us -> 0.07 us
    ppermute x3 -> x19, waiting for transfers between devices: 105 us -> 35.7 us  [the longest x9 20.3 us: along(): lax.ppermute(value, 'row', [(r, (r + HALVES * shift) % row_peers) for r i...]
    pallas_call x0 -> x14, Pallas kernels: none -> 24.8 us  [the longest x5 12.8 us: shards(): pl.pallas_call(partial(join_kernel, first, span, block_rows, len(received...]
    ppermute x3 -> x19, starting transfers between devices: 0.46 us -> 22.2 us  [the longest x9 12.8 us: along(): lax.ppermute(value, 'row', [(r, (r + HALVES * shift) % row_peers) for r i...]
    psum x1 -> x0, waiting for transfers between devices: 18.1 us -> none  [broadcast(): return lax.psum(kept, axis)]
    dot_general x6 -> x0, matrix products: 15.7 us -> none  [slot_product(): return jnp.dot(tile_block, weights, preferred_element_type=jnp.float32)]
    psum x1 -> x0, blocking collectives: 13 us -> none  [broadcast(): return lax.psum(kept, axis)]
    another operation x4 -> x0, loops' own time: 10.6 us -> none  [shards(): lax.fori_loop(0, live_count, partial(live_update, current, panel_tiles, s...]
    unnamed x14, local copies, waits for them, and re-layouts: 14.1 us -> 4.6 us
  transfers between devices with their start and end apart: 4 -> 19, of which waited for: 4 -> 11; matrix products, arithmetic and copies ran while one was open for 7% -> 0% of each run, Pallas kernels for 0% -> 25%
where the time goes in v4:
time: 88.5 us; the launch traced here: 88.3 us
  waiting for transfers between devices  35.7 us (40%)
  Pallas kernels  24.8 us (28%)
  starting transfers between devices  22.2 us (25%)
  local copies, waits for them, and re-layouts  4.6 us (5%)
    ppermute x9, waiting for transfers between devices, along(): lax.ppermute(value, 'row', [(r, (r + HALVES * shift) % row_peers) for r i...  20.3 us
    ppermute x8, waiting for transfers between devices, across(): return lax.ppermute(value, ('row', 'col'), pairs)  15.5 us
    ppermute x9, starting transfers between devices, along(): lax.ppermute(value, 'row', [(r, (r + HALVES * shift) % row_peers) for r i...  12.8 us
    pallas_call x5, Pallas kernels, shards(): pl.pallas_call(partial(join_kernel, first, span, block_rows, len(received...  12.8 us
    pallas_call x5, Pallas kernels, shards(): pl.pallas_call(partial(send_kernel, first, span, block_rows), in_specs=[S...  10 us
    ppermute x8, starting transfers between devices, across(): return lax.ppermute(value, ('row', 'col'), pairs)  8.95 us
    unnamed x14, local copies, waits for them, and re-layouts  4.6 us
  transfers between devices with their start and end apart: 19, of which 11 were waited for; matrix products, arithmetic and copies ran while one was open for 0% of the time, Pallas kernels for 25%

profile of v4, /device:TPU:0, one launch (start us, length us, event | category | flops | bytes accessed | tf_op | source)
XLA Modules:
  0.0 88.3 jit_solution(8264239063849777080)
XLA Ops:
  0.0 0.5 collective-permute-start.1
  1.1 0.9 %copy-done.1 = bf16[1,1,2,256,256]{4,3,2,1,0:T(8,128)(2,1)S(1)} copy-done((bf16[1,1,2,256,256]{4,3,2,1,0:T(8,128)(2,1)S(1)}, bf16[1,1,2,256,256]{4,3,2,1,0:T(8,128)(2,1)}, u32[]{:S(2)}) %copy-start.1) | copy-done | bytes 262168
  2.1 0.7 copy-done.3
  2.7 0.6 pack.1
  3.3 2.6 %collective-permute-start.2 = (bf16[144,256]{1,0:T(8,128)(2,1)S(1)}, bf16[144,256]{1,0:T(8,128)(2,1)S(1)}, u32[]{:S(2)}, u32[]{:S(2)}) collective-permute-start(bf16[144,256]{1,0:T(8,128)(2,1)S(1)} %get-tuple-element.17), channel_id=1, source_target_pairs={{0,8},{4,12},{8,16},{12,20},{16,24},{20,28},{24,0},{28,4},{1,9},{5... | collective-permute-start | bytes 221192 | tf_op jit(solution)/shard_map/ppermute | solution.py:194
  5.9 2.6 %collective-permute-start.3 = (bf16[144,256]{1,0:T(8,128)(2,1)S(1)}, bf16[144,256]{1,0:T(8,128)(2,1)S(1)}, u32[]{:S(2)}, u32[]{:S(2)}) collective-permute-start(bf16[144,256]{1,0:T(8,128)(2,1)S(1)} %get-tuple-element.18), channel_id=1, source_target_pairs={{0,16},{4,20},{8,24},{12,28},{16,0},{20,4},{24,8},{28,12},{1,17},{... | collective-permute-start | bytes 221192 | tf_op jit(solution)/shard_map/ppermute | solution.py:194
  8.5 1.3 %collective-permute-start.4 = (bf16[144,256]{1,0:T(8,128)(2,1)S(1)}, bf16[144,256]{1,0:T(8,128)(2,1)S(1)}, u32[]{:S(2)}, u32[]{:S(2)}) collective-permute-start(bf16[144,256]{1,0:T(8,128)(2,1)S(1)} %get-tuple-element.19), channel_id=1, source_target_pairs={{0,24},{4,28},{8,0},{12,4},{16,8},{20,12},{24,16},{28,20},{1,25},{... | collective-permute-start | bytes 221192 | tf_op jit(solution)/shard_map/ppermute | solution.py:194
  9.9 1.3 %collective-permute-done.2.refs_1_ = bf16[144,256]{1,0:T(8,128)(2,1)S(1)} collective-permute-done((bf16[144,256]{1,0:T(8,128)(2,1)S(1)}, bf16[144,256]{1,0:T(8,128)(2,1)S(1)}, u32[]{:S(2)}, u32[]{:S(2)}) %collective-permute-start.2) | collective-permute-done | bytes 73760 | tf_op jit(solution)/shard_map/ppermute | solution.py:194
  11.2 3.0 %collective-permute-done.3.refs_2_ = bf16[144,256]{1,0:T(8,128)(2,1)S(1)} collective-permute-done((bf16[144,256]{1,0:T(8,128)(2,1)S(1)}, bf16[144,256]{1,0:T(8,128)(2,1)S(1)}, u32[]{:S(2)}, u32[]{:S(2)}) %collective-permute-start.3) | collective-permute-done | bytes 73760 | tf_op jit(solution)/shard_map/ppermute | solution.py:194
  14.2 0.2 collective-permute-done.4.refs_3_
  14.4 0.7 copy-done.4
  15.0 0.7 choose.1
  15.7 2.5 %collective-permute-start.6 = (bf16[272,256]{1,0:T(8,128)(2,1)S(1)}, bf16[272,256]{1,0:T(8,128)(2,1)S(1)}, u32[]{:S(2)}, u32[]{:S(2)}) collective-permute-start(bf16[272,256]{1,0:T(8,128)(2,1)S(1)} %get-tuple-element.21), channel_id=1, source_target_pairs={{0,6},{1,7},{2,4},{3,5},{4,2},{5,3},{6,0},{7,1},{8,14},{9,15},{10,... | collective-permute-start | bytes 417800 | tf_op jit(solution)/shard_map/ppermute | solution.py:201
  18.2 0.5 collective-permute-start.5
  18.8 4.5 %collective-permute-done.6 = bf16[272,256]{1,0:T(8,128)(2,1)S(1)} collective-permute-done((bf16[272,256]{1,0:T(8,128)(2,1)S(1)}, bf16[272,256]{1,0:T(8,128)(2,1)S(1)}, u32[]{:S(2)}, u32[]{:S(2)}) %collective-permute-start.6) | collective-permute-done | bytes 139296 | tf_op jit(solution)/shard_map/ppermute | solution.py:201
  23.3 1.8 %collective-permute-done.5 = bf16[272,256]{1,0:T(8,128)(2,1)S(1)} collective-permute-done((bf16[272,256]{1,0:T(8,128)(2,1)S(1)}, bf16[272,256]{1,0:T(8,128)(2,1)S(1)}, u32[]{:S(2)}, u32[]{:S(2)}) %collective-permute-start.5) | collective-permute-done | bytes 139296 | tf_op jit(solution)/shard_map/ppermute | solution.py:201
  25.1 2.9 %collective-permute-start.9 = (bf16[272,256]{1,0:T(8,128)(2,1)S(1)}, bf16[272,256]{1,0:T(8,128)(2,1)S(1)}, u32[]{:S(2)}, u32[]{:S(2)}) collective-permute-start(bf16[272,256]{1,0:T(8,128)(2,1)S(1)} %add.6.refs_0_), channel_id=1, source_target_pairs={{0,24},{4,28},{8,0},{12,4},{16,8},{20,12},{24,16},{28,20},{1,25},{... | collective-permute-start | bytes 417800 | tf_op jit(solution)/shard_map/ppermute | solution.py:194
  28.0 0.8 collective-permute-start.8
  28.8 3.4 %collective-permute-done.9.refs_3_ = bf16[272,256]{1,0:T(8,128)(2,1)S(1)} collective-permute-done((bf16[272,256]{1,0:T(8,128)(2,1)S(1)}, bf16[272,256]{1,0:T(8,128)(2,1)S(1)}, u32[]{:S(2)}, u32[]{:S(2)}) %collective-permute-start.9) | collective-permute-done | bytes 139296 | tf_op jit(solution)/shard_map/ppermute | solution.py:194
  32.2 8.3 %collective-permute-done.8.refs_2_ = bf16[272,256]{1,0:T(8,128)(2,1)S(1)} collective-permute-done((bf16[272,256]{1,0:T(8,128)(2,1)S(1)}, bf16[272,256]{1,0:T(8,128)(2,1)S(1)}, u32[]{:S(2)}, u32[]{:S(2)}) %collective-permute-start.8) | collective-permute-done | bytes 139296 | tf_op jit(solution)/shard_map/ppermute | solution.py:194
  40.5 0.3 fill.2.dense_ref
  40.9 0.0 copy-start
  40.9 2.3 %copy-done = bf16[3072,768]{1,0:T(8,128)(2,1)S(1)} copy-done((bf16[3072,768]{1,0:T(8,128)(2,1)S(1)}, bf16[3072,768]{1,0:T(8,128)(2,1)}, u32[]{:S(2)}) %copy-start) | copy-done | bytes 4718616
  43.2 1.2 %send_part.5 = s16[272,256]{1,0:T(8,128)(2,1)S(1)} custom-call(s32[3,12]{1,0:T(4,128)S(1)} %bitcast.5, s32[3,12]{1,0:T(4,128)S(1)} %collective-permute-done.other_mask_ref, bf16[3072,768]{1,0:T(8,128)(2,1)S(1)} %copy-done, bf16[3072,768]{1,0:T(8,128)(2,1)S(1)} %collective-permute-done.1.other_ref, bf16[1536,256]{1,0:T(8,128)(2,1)S(1)} %fill.2.dense_ref), custom_call_target="tpu_custom_call" | custom-call | flops 201326592 | bytes 917504 | tf_op jit(solution)/shard_map/send_part/pallas_call | solution.py:258
  44.4 1.6 %collective-permute-start.10 = (s16[272,256]{1,0:T(8,128)(2,1)S(1)}, s16[272,256]{1,0:T(8,128)(2,1)S(1)}, u32[]{:S(2)}, u32[]{:S(2)}) collective-permute-start(s16[272,256]{1,0:T(8,128)(2,1)S(1)} %send_part.5), channel_id=1, source_target_pairs={{0,2},{1,3},{2,0},{3,1},{4,6},{5,7},{6,4},{7,5},{8,10},{9,11},{10,... | collective-permute-start | bytes 417800 | tf_op jit(solution)/shard_map/ppermute | solution.py:201
  46.0 2.9 %send_part.6 = s16[1040,256]{1,0:T(8,128)(2,1)S(1)} custom-call(s32[3,12]{1,0:T(4,128)S(1)} %bitcast.6, s32[3,12]{1,0:T(4,128)S(1)} %collective-permute-done.other_mask_ref, bf16[3072,768]{1,0:T(8,128)(2,1)S(1)} %copy-done, bf16[3072,768]{1,0:T(8,128)(2,1)S(1)} %collective-permute-done.1.other_ref, bf16[1536,256]{1,0:T(8,128)(2,1)S(1)} %fill.2.dense_ref), custom_call_target="tpu_custom_call" | custom-call | flops 805306368 | bytes 3670016 | tf_op jit(solution)/shard_map/send_part/pallas_call | solution.py:258
  48.9 0.6 collective-permute-start.15
  49.5 0.0 collective-permute-done.10.refs_0_
  49.5 2.9 %send_part.7 = s16[1040,256]{1,0:T(8,128)(2,1)S(1)} custom-call(s32[3,12]{1,0:T(4,128)S(1)} %bitcast.7, s32[3,12]{1,0:T(4,128)S(1)} %collective-permute-done.other_mask_ref, bf16[3072,768]{1,0:T(8,128)(2,1)S(1)} %copy-done, bf16[3072,768]{1,0:T(8,128)(2,1)S(1)} %collective-permute-done.1.other_ref, bf16[1536,256]{1,0:T(8,128)(2,1)S(1)} %fill.2.dense_ref), custom_call_target="tpu_custom_call" | custom-call | flops 805306368 | bytes 3670016 | tf_op jit(solution)/shard_map/send_part/pallas_call | solution.py:258
  52.5 2.1 %collective-permute-start.16 = (s16[1040,256]{1,0:T(8,128)(2,1)S(1)}, s16[1040,256]{1,0:T(8,128)(2,1)S(1)}, u32[]{:S(2)}, u32[]{:S(2)}) collective-permute-start(s16[1040,256]{1,0:T(8,128)(2,1)S(1)} %send_part.7), channel_id=1, source_target_pairs={{0,2},{1,3},{2,0},{3,1},{4,6},{5,7},{6,4},{7,5},{8,10},{9,11},{10,... | collective-permute-start | bytes 1597448 | tf_op jit(solution)/shard_map/ppermute | solution.py:201
  54.5 0.5 collective-permute-start.11
  55.0 4.6 %collective-permute-done.11 = bf16[272,256]{1,0:T(8,128)(2,1)S(1)} collective-permute-done((bf16[272,256]{1,0:T(8,128)(2,1)S(1)}, bf16[272,256]{1,0:T(8,128)(2,1)S(1)}, u32[]{:S(2)}, u32[]{:S(2)}) %collective-permute-start.11) | collective-permute-done | bytes 139296 | tf_op jit(solution)/shard_map/ppermute | solution.py:201
  59.6 0.0 slice-start.1
  59.7 0.9 %collective-permute-start.14 = (bf16[272,256]{1,0:T(8,128)(2,1)S(1)}, bf16[272,256]{1,0:T(8,128)(2,1)S(1)}, u32[]{:S(2)}, u32[]{:S(2)}) collective-permute-start(bf16[272,256]{1,0:T(8,128)(2,1)S(1)} %add.7.refs_0_), channel_id=1, source_target_pairs={{0,24},{4,28},{8,0},{12,4},{16,8},{20,12},{24,16},{28,20},{1,25},{... | collective-permute-start | bytes 417800 | tf_op jit(solution)/shard_map/ppermute | solution.py:194
  60.6 1.7 %collective-permute-start.12 = (bf16[272,256]{1,0:T(8,128)(2,1)S(1)}, bf16[272,256]{1,0:T(8,128)(2,1)S(1)}, u32[]{:S(2)}, u32[]{:S(2)}) collective-permute-start(bf16[272,256]{1,0:T(8,128)(2,1)S(1)} %add.7.refs_0_), channel_id=1, source_target_pairs={{0,8},{4,12},{8,16},{12,20},{16,24},{20,28},{24,0},{28,4},{1,9},{5... | collective-permute-start | bytes 417800 | tf_op jit(solution)/shard_map/ppermute | solution.py:194
  62.3 1.8 %collective-permute-done.15.refs_0_ = s16[1040,256]{1,0:T(8,128)(2,1)S(1)} collective-permute-done((s16[1040,256]{1,0:T(8,128)(2,1)S(1)}, s16[1040,256]{1,0:T(8,128)(2,1)S(1)}, u32[]{:S(2)}, u32[]{:S(2)}) %collective-permute-start.15) | collective-permute-done | bytes 532512 | tf_op jit(solution)/shard_map/ppermute | solution.py:201
  64.0 1.8 %send_part.8 = s16[528,256]{1,0:T(8,128)(2,1)S(1)} custom-call(s32[3,12]{1,0:T(4,128)S(1)} %bitcast.8, s32[3,12]{1,0:T(4,128)S(1)} %collective-permute-done.other_mask_ref, bf16[3072,768]{1,0:T(8,128)(2,1)S(1)} %copy-done, bf16[3072,768]{1,0:T(8,128)(2,1)S(1)} %collective-permute-done.1.other_ref, bf16[1536,256]{1,0:T(8,128)(2,1)S(1)} %fill.2.dense_ref), custom_call_target="tpu_custom_call" | custom-call | flops 402653184 | bytes 1835008 | tf_op jit(solution)/shard_map/send_part/pallas_call | solution.py:258
  65.8 0.6 collective-permute-start.18
  66.4 4.1 %collective-permute-done.13.refs_2_ = bf16[272,256]{1,0:T(8,128)(2,1)S(1)} collective-permute-done((bf16[272,256]{1,0:T(8,128)(2,1)S(1)}, bf16[272,256]{1,0:T(8,128)(2,1)S(1)}, u32[]{:S(2)}, u32[]{:S(2)}) %collective-permute-start.13) | collective-permute-done | bytes 139296 | tf_op jit(solution)/shard_map/ppermute | solution.py:194
  70.5 0.3 fill.3.dense_ref
  70.9 1.8 %join_part.5.refs_1_ = bf16[3072,256]{1,0:T(8,128)(2,1)} custom-call(s32[3,12]{1,0:T(4,128)S(1)} %bitcast.9, s32[3,12]{1,0:T(4,128)S(1)} %collective-permute-done.other_mask_ref, bf16[3072,768]{1,0:T(8,128)(2,1)S(1)} %bitcast.3, bf16[3072,768]{1,0:T(8,128)(2,1)S(1)} %collective-permute-done.1.other_ref, bf16[1536,256]{1,0:T(8,128)(2,1)S(1)} %fill.3.dense_ref, ...), custom_call_target="tpu_custom_call" | custom-call | flops 201326592 | bytes 917504 | tf_op jit(solution)/shard_map/join_part/pallas_call | solution.py:285
  72.6 2.8 %collective-permute-done.16.refs_0_ = s16[1040,256]{1,0:T(8,128)(2,1)S(1)} collective-permute-done((s16[1040,256]{1,0:T(8,128)(2,1)S(1)}, s16[1040,256]{1,0:T(8,128)(2,1)S(1)}, u32[]{:S(2)}, u32[]{:S(2)}) %collective-permute-start.16) | collective-permute-done | bytes 532512 | tf_op jit(solution)/shard_map/ppermute | solution.py:201
  75.4 1.2 %send_part.9 = s16[272,256]{1,0:T(8,128)(2,1)S(1)} custom-call(s32[3,12]{1,0:T(4,128)S(1)} %bitcast.10, s32[3,12]{1,0:T(4,128)S(1)} %collective-permute-done.other_mask_ref, bf16[3072,768]{1,0:T(8,128)(2,1)S(1)} %bitcast.3, bf16[3072,768]{1,0:T(8,128)(2,1)S(1)} %collective-permute-done.1.other_ref, bf16[1536,256]{1,0:T(8,128)(2,1)S(1)} %fill.2.dense_ref), custom_call_target="tpu_custom_call" | custom-call | flops 201326592 | bytes 917504 | tf_op jit(solution)/shard_map/send_part/pallas_call | solution.py:258
  76.6 0.6 collective-permute-start.17
  77.2 3.5 %join_part.6.refs_1_ = bf16[3072,256]{1,0:T(8,128)(2,1)} custom-call(s32[3,12]{1,0:T(4,128)S(1)} %bitcast.11, s32[3,12]{1,0:T(4,128)S(1)} %collective-permute-done.other_mask_ref, bf16[3072,768]{1,0:T(8,128)(2,1)S(1)} %bitcast.3, bf16[3072,768]{1,0:T(8,128)(2,1)S(1)} %collective-permute-done.1.other_ref, ...), custom_call_target="tpu_custom_call", output_to_operand_aliasing={{}: (6, {})} | custom-call | flops 805306368 | bytes 3670016 | tf_op jit(solution)/shard_map/join_part/pallas_call | solution.py:285
  80.7 3.5 %join_part.7.refs_1_ = bf16[3072,256]{1,0:T(8,128)(2,1)} custom-call(s32[3,12]{1,0:T(4,128)S(1)} %bitcast.12, s32[3,12]{1,0:T(4,128)S(1)} %collective-permute-done.other_mask_ref, bf16[3072,768]{1,0:T(8,128)(2,1)S(1)} %bitcast.3, bf16[3072,768]{1,0:T(8,128)(2,1)S(1)} %collective-permute-done.1.other_ref, ...), custom_call_target="tpu_custom_call", output_to_operand_aliasing={{}: (6, {})} | custom-call | flops 805306368 | bytes 3670016 | tf_op jit(solution)/shard_map/join_part/pallas_call | solution.py:285
  84.2 2.3 %join_part.8.refs_1_ = bf16[3072,256]{1,0:T(8,128)(2,1)} custom-call(s32[3,12]{1,0:T(4,128)S(1)} %bitcast.13, s32[3,12]{1,0:T(4,128)S(1)} %collective-permute-done.other_mask_ref, bf16[3072,768]{1,0:T(8,128)(2,1)S(1)} %bitcast.3, bf16[3072,768]{1,0:T(8,128)(2,1)S(1)} %collective-permute-done.1.other_ref, ...), custom_call_target="tpu_custom_call", output_to_operand_aliasing={{}: (6, {})} | custom-call | flops 402653184 | bytes 1835008 | tf_op jit(solution)/shard_map/join_part/pallas_call | solution.py:285
  86.5 1.8 %join_part.9 = bf16[3072,256]{1,0:T(8,128)(2,1)} custom-call(s32[3,12]{1,0:T(4,128)S(1)} %bitcast.14, s32[3,12]{1,0:T(4,128)S(1)} %collective-permute-done.other_mask_ref, bf16[3072,768]{1,0:T(8,128)(2,1)S(1)} %bitcast.3, bf16[3072,768]{1,0:T(8,128)(2,1)S(1)} %collective-permute-done.1.other_ref, ...), custom_call_target="tpu_custom_call", output_to_operand_aliasing={{}: (6, {})} | custom-call | flops 201326592 | bytes 917504 | tf_op jit(solution)/shard_map/join_part/pallas_call | solution.py:285
  (21 shorter events, 0.1 us)
Async XLA Ops:
  0.0 40.9 %collective-permute-start.1 = (bf16[3072,768]{1,0:T(8,128)(2,1)}, bf16[3072,768]{1,0:T(8,128)(2,1)S(1)}, u32[]{:S(2)}, u32[]{:S(2)}) collective-permute-start(bf16[3072,768]{1,0:T(8,128)(2,1)} %own_ref.19), channel_id=1, source_target_pairs={{0,1},{1,0},{2,3},{3,2},{4,5},{5,4},{6,7},{7,6},{8,9},{9,8},{10,11... | collective-permute-start | bytes 14155784 | tf_op jit(solution)/shard_map/ppermute | solution.py:204
  1.1 1.0 %copy-start.1 = (bf16[1,1,2,256,256]{4,3,2,1,0:T(8,128)(2,1)S(1)}, bf16[1,1,2,256,256]{4,3,2,1,0:T(8,128)(2,1)}, u32[]{:S(2)}) copy-start(bf16[1,1,2,256,256]{4,3,2,1,0:T(8,128)(2,1)} %panel_ref.1) | copy-start | bytes 786436
  2.1 0.7 copy-start.3
  2.7 38.2 %copy-start.2 = (s32[12,3]{0,1:T(4,128)S(1)}, s32[12,3]{0,1:T(4,128)}, u32[]{:S(2)}) copy-start(s32[12,3]{0,1:T(4,128)} %param.7) | copy-start | bytes 436
  3.3 7.9 %collective-permute-start.2 = (bf16[144,256]{1,0:T(8,128)(2,1)S(1)}, bf16[144,256]{1,0:T(8,128)(2,1)S(1)}, u32[]{:S(2)}, u32[]{:S(2)}) collective-permute-start(bf16[144,256]{1,0:T(8,128)(2,1)S(1)} %get-tuple-element.17), channel_id=1, source_target_pairs={{0,8},{4,12},{8,16},{12,20},{16,24},{20,28},{24,0},{28,4},{1,9},{5... | collective-permute-start | bytes 221192 | tf_op jit(solution)/shard_map/ppermute | solution.py:194
  5.9 8.2 %collective-permute-start.3 = (bf16[144,256]{1,0:T(8,128)(2,1)S(1)}, bf16[144,256]{1,0:T(8,128)(2,1)S(1)}, u32[]{:S(2)}, u32[]{:S(2)}) collective-permute-start(bf16[144,256]{1,0:T(8,128)(2,1)S(1)} %get-tuple-element.18), channel_id=1, source_target_pairs={{0,16},{4,20},{8,24},{12,28},{16,0},{20,4},{24,8},{28,12},{1,17},{... | collective-permute-start | bytes 221192 | tf_op jit(solution)/shard_map/ppermute | solution.py:194
  8.5 5.8 %collective-permute-start.4 = (bf16[144,256]{1,0:T(8,128)(2,1)S(1)}, bf16[144,256]{1,0:T(8,128)(2,1)S(1)}, u32[]{:S(2)}, u32[]{:S(2)}) collective-permute-start(bf16[144,256]{1,0:T(8,128)(2,1)S(1)} %get-tuple-element.19), channel_id=1, source_target_pairs={{0,24},{4,28},{8,0},{12,4},{16,8},{20,12},{24,16},{28,20},{1,25},{... | collective-permute-start | bytes 221192 | tf_op jit(solution)/shard_map/ppermute | solution.py:194
  14.4 0.7 copy-start.4
  15.7 7.5 %collective-permute-start.6 = (bf16[272,256]{1,0:T(8,128)(2,1)S(1)}, bf16[272,256]{1,0:T(8,128)(2,1)S(1)}, u32[]{:S(2)}, u32[]{:S(2)}) collective-permute-start(bf16[272,256]{1,0:T(8,128)(2,1)S(1)} %get-tuple-element.21), channel_id=1, source_target_pairs={{0,6},{1,7},{2,4},{3,5},{4,2},{5,3},{6,0},{7,1},{8,14},{9,15},{10,... | collective-permute-start | bytes 417800 | tf_op jit(solution)/shard_map/ppermute | solution.py:201
  18.2 6.9 %collective-permute-start.5 = (bf16[272,256]{1,0:T(8,128)(2,1)S(1)}, bf16[272,256]{1,0:T(8,128)(2,1)S(1)}, u32[]{:S(2)}, u32[]{:S(2)}) collective-permute-start(bf16[272,256]{1,0:T(8,128)(2,1)S(1)} %get-tuple-element.21), channel_id=1, source_target_pairs={{0,2},{1,3},{2,0},{3,1},{4,6},{5,7},{6,4},{7,5},{8,10},{9,11},{10,... | collective-permute-start | bytes 417800 | tf_op jit(solution)/shard_map/ppermute | solution.py:201
  25.1 7.0 %collective-permute-start.9 = (bf16[272,256]{1,0:T(8,128)(2,1)S(1)}, bf16[272,256]{1,0:T(8,128)(2,1)S(1)}, u32[]{:S(2)}, u32[]{:S(2)}) collective-permute-start(bf16[272,256]{1,0:T(8,128)(2,1)S(1)} %add.6.refs_0_), channel_id=1, source_target_pairs={{0,24},{4,28},{8,0},{12,4},{16,8},{20,12},{24,16},{28,20},{1,25},{... | collective-permute-start | bytes 417800 | tf_op jit(solution)/shard_map/ppermute | solution.py:194
  28.0 12.5 %collective-permute-start.8 = (bf16[272,256]{1,0:T(8,128)(2,1)S(1)}, bf16[272,256]{1,0:T(8,128)(2,1)S(1)}, u32[]{:S(2)}, u32[]{:S(2)}) collective-permute-start(bf16[272,256]{1,0:T(8,128)(2,1)S(1)} %add.6.refs_0_), channel_id=1, source_target_pairs={{0,16},{4,20},{8,24},{12,28},{16,0},{20,4},{24,8},{28,12},{1,17},{... | collective-permute-start | bytes 417800 | tf_op jit(solution)/shard_map/ppermute | solution.py:194
  28.8 11.7 %collective-permute-start.7 = (bf16[272,256]{1,0:T(8,128)(2,1)S(1)}, bf16[272,256]{1,0:T(8,128)(2,1)S(1)}, u32[]{:S(2)}, u32[]{:S(2)}) collective-permute-start(bf16[272,256]{1,0:T(8,128)(2,1)S(1)} %add.6.refs_0_), channel_id=1, source_target_pairs={{0,8},{4,12},{8,16},{12,20},{16,24},{20,28},{24,0},{28,4},{1,9},{5... | collective-permute-start | bytes 417800 | tf_op jit(solution)/shard_map/ppermute | solution.py:194
  28.8 12.0 %collective-permute-start = (s32[3,12]{1,0:T(4,128)}, s32[3,12]{1,0:T(4,128)S(1)}, u32[]{:S(2)}, u32[]{:S(2)}) collective-permute-start(s32[3,12]{1,0:T(4,128)} %bitcast.4), channel_id=1, source_target_pairs={{0,1},{1,0},{2,3},{3,2},{4,5},{5,4},{6,7},{7,6},{8,9},{9,8},{10,11... | collective-permute-start | bytes 440 | tf_op jit(solution)/shard_map/ppermute | solution.py:206
  40.9 2.3 %copy-start = (bf16[3072,768]{1,0:T(8,128)(2,1)S(1)}, bf16[3072,768]{1,0:T(8,128)(2,1)}, u32[]{:S(2)}) copy-start(bf16[3072,768]{1,0:T(8,128)(2,1)} %own_ref.19) | copy-start | bytes 14155780
  44.4 5.1 %collective-permute-start.10 = (s16[272,256]{1,0:T(8,128)(2,1)S(1)}, s16[272,256]{1,0:T(8,128)(2,1)S(1)}, u32[]{:S(2)}, u32[]{:S(2)}) collective-permute-start(s16[272,256]{1,0:T(8,128)(2,1)S(1)} %send_part.5), channel_id=1, source_target_pairs={{0,2},{1,3},{2,0},{3,1},{4,6},{5,7},{6,4},{7,5},{8,10},{9,11},{10,... | collective-permute-start | bytes 417800 | tf_op jit(solution)/shard_map/ppermute | solution.py:201
  48.9 15.1 %collective-permute-start.15 = (s16[1040,256]{1,0:T(8,128)(2,1)S(1)}, s16[1040,256]{1,0:T(8,128)(2,1)S(1)}, u32[]{:S(2)}, u32[]{:S(2)}) collective-permute-start(s16[1040,256]{1,0:T(8,128)(2,1)S(1)} %send_part.6), channel_id=1, source_target_pairs={{0,2},{1,3},{2,0},{3,1},{4,6},{5,7},{6,4},{7,5},{8,10},{9,11},{10,... | collective-permute-start | bytes 1597448 | tf_op jit(solution)/shard_map/ppermute | solution.py:201
  49.5 21.3 %slice-start = ((s8[4718592]{0:T(1024)(128)(4,1)}), s8[4194304]{0:T(1024)(128)(4,1)S(1)}, s32[]{:S(2)}) async-start(s8[4718592]{0:T(1024)(128)(4,1)} %bitcast.2), calls=%async_computation | async-start | bytes 8388608
  52.5 23.0 %collective-permute-start.16 = (s16[1040,256]{1,0:T(8,128)(2,1)S(1)}, s16[1040,256]{1,0:T(8,128)(2,1)S(1)}, u32[]{:S(2)}, u32[]{:S(2)}) collective-permute-start(s16[1040,256]{1,0:T(8,128)(2,1)S(1)} %send_part.7), channel_id=1, source_target_pairs={{0,2},{1,3},{2,0},{3,1},{4,6},{5,7},{6,4},{7,5},{8,10},{9,11},{10,... | collective-permute-start | bytes 1597448 | tf_op jit(solution)/shard_map/ppermute | solution.py:201
  54.5 5.1 %collective-permute-start.11 = (bf16[272,256]{1,0:T(8,128)(2,1)S(1)}, bf16[272,256]{1,0:T(8,128)(2,1)S(1)}, u32[]{:S(2)}, u32[]{:S(2)}) collective-permute-start(bf16[272,256]{1,0:T(8,128)(2,1)S(1)} %get-tuple-element.22), channel_id=1, source_target_pairs={{0,4},{1,5},{2,6},{3,7},{4,0},{5,1},{6,2},{7,3},{8,12},{9,13},{10,... | collective-permute-start | bytes 417800 | tf_op jit(solution)/shard_map/ppermute | solution.py:201
  59.6 11.2 %slice-start.1 = ((s8[4718592]{0:T(1024)(128)(4,1)}), s8[524288]{0:T(1024)(128)(4,1)S(1)}, s32[]{:S(2)}) async-start(s8[4718592]{0:T(1024)(128)(4,1)} %bitcast.2), calls=%async_computation.1 | async-start | bytes 1048576
  59.7 6.7 %collective-permute-start.14 = (bf16[272,256]{1,0:T(8,128)(2,1)S(1)}, bf16[272,256]{1,0:T(8,128)(2,1)S(1)}, u32[]{:S(2)}, u32[]{:S(2)}) collective-permute-start(bf16[272,256]{1,0:T(8,128)(2,1)S(1)} %add.7.refs_0_), channel_id=1, source_target_pairs={{0,24},{4,28},{8,0},{12,4},{16,8},{20,12},{24,16},{28,20},{1,25},{... | collective-permute-start | bytes 417800 | tf_op jit(solution)/shard_map/ppermute | solution.py:194
  60.5 9.9 %collective-permute-start.13 = (bf16[272,256]{1,0:T(8,128)(2,1)S(1)}, bf16[272,256]{1,0:T(8,128)(2,1)S(1)}, u32[]{:S(2)}, u32[]{:S(2)}) collective-permute-start(bf16[272,256]{1,0:T(8,128)(2,1)S(1)} %add.7.refs_0_), channel_id=1, source_target_pairs={{0,16},{4,20},{8,24},{12,28},{16,0},{20,4},{24,8},{28,12},{1,17},{... | collective-permute-start | bytes 417800 | tf_op jit(solution)/shard_map/ppermute | solution.py:194
  60.6 9.9 %collective-permute-start.12 = (bf16[272,256]{1,0:T(8,128)(2,1)S(1)}, bf16[272,256]{1,0:T(8,128)(2,1)S(1)}, u32[]{:S(2)}, u32[]{:S(2)}) collective-permute-start(bf16[272,256]{1,0:T(8,128)(2,1)S(1)} %add.7.refs_0_), channel_id=1, source_target_pairs={{0,8},{4,12},{8,16},{12,20},{16,24},{20,28},{24,0},{28,4},{1,9},{5... | collective-permute-start | bytes 417800 | tf_op jit(solution)/shard_map/ppermute | solution.py:194
  65.8 18.4 %collective-permute-start.18 = (s16[528,256]{1,0:T(8,128)(2,1)S(1)}, s16[528,256]{1,0:T(8,128)(2,1)S(1)}, u32[]{:S(2)}, u32[]{:S(2)}) collective-permute-start(s16[528,256]{1,0:T(8,128)(2,1)S(1)} %send_part.8), channel_id=1, source_target_pairs={{0,2},{1,3},{2,0},{3,1},{4,6},{5,7},{6,4},{7,5},{8,10},{9,11},{10,... | collective-permute-start | bytes 811016 | tf_op jit(solution)/shard_map/ppermute | solution.py:201
  76.6 9.9 %collective-permute-start.17 = (s16[272,256]{1,0:T(8,128)(2,1)S(1)}, s16[272,256]{1,0:T(8,128)(2,1)S(1)}, u32[]{:S(2)}, u32[]{:S(2)}) collective-permute-start(s16[272,256]{1,0:T(8,128)(2,1)S(1)} %send_part.9), channel_id=1, source_target_pairs={{0,2},{1,3},{2,0},{3,1},{4,6},{5,7},{6,4},{7,5},{8,10},{9,11},{10,... | collective-permute-start | bytes 417800 | tf_op jit(solution)/shard_map/ppermute | solution.py:201

commit v5 on v4

v5 whole, which is shorter than its diff:
```python
from functools import partial

import jax
import jax.numpy as jnp
from jax import lax
from jax.experimental import pallas as pl
from jax.experimental.pallas import tpu as pltpu
from jax.sharding import PartitionSpec as P

STEPS = 4
CORES = 2
HALVES = 2
CUTS = (0.0, 0.08, 0.33, 0.67, 0.92, 1.0)
CODE_TOP = 32767.0
FRACTION = 8192.0
META_ROWS = 16
PARAMS = pltpu.CompilerParams(vmem_limit_bytes=16 * 1024 * 1024)
SMEM = pl.BlockSpec(memory_space=pltpu.SMEM)
VMEM = pl.BlockSpec(memory_space=pltpu.VMEM)


def pair_offsets(col_count):
    pairs = col_count // CORES
    offsets = set()
    for core in range(CORES):
        for step in range(STEPS):
            offsets.add(-((core - step) // CORES) % pairs)
    return sorted(offsets)


def row_chunks(block_count):
    marks = sorted({round(block_count * cut) for cut in CUTS})
    return [(first, last - first) for first, last in zip(marks, marks[1:])]


def pack_kernel(table_ref, panel_ref, *piece_refs):
    peers = len(piece_refs)
    slots, tile_width = panel_ref.shape[2:4]
    share = slots * tile_width // peers
    place = lax.axis_index("row") // HALVES
    lane = lax.broadcasted_iota(jnp.int32, (META_ROWS, tile_width), 1)
    info = jnp.zeros((META_ROWS, tile_width), jnp.int32)
    for spot in range(slots + 1):
        info = jnp.where(lane == spot, table_ref[spot], info)
    info = info.astype(jnp.float32).astype(panel_ref.dtype)
    for shift, piece_ref in enumerate(piece_refs):
        first = lax.rem(place + shift, peers) * share
        start = pl.multiple_of(lax.rem(first, tile_width), META_ROWS)
        piece_ref[pl.ds(0, share), :] = panel_ref[0, 0, first // tile_width, pl.ds(start, share), :]
        piece_ref[pl.ds(share, META_ROWS), :] = info


def choose_kernel(col_peers, offsets, slots, table_ref, *refs):
    out_refs = refs[len(refs) - len(offsets) :]
    piece_refs = refs[: len(refs) - len(offsets)]
    peers = len(piece_refs)
    share = piece_refs[0].shape[0] - META_ROWS
    row = lax.axis_index("row")
    core = lax.rem(lax.axis_index("col"), CORES)
    sign = 1 - 2 * core
    line = lax.broadcasted_iota(jnp.int32, (META_ROWS, piece_refs[0].shape[1]), 0)
    for offset, out_ref in zip(offsets, out_refs):
        out_ref[...] = jnp.zeros_like(out_ref)
        for group, shift in enumerate((0, sign)):
            step = lax.rem(CORES * offset - shift + col_peers, col_peers)
            holder = table_ref[slots + 1 + jnp.minimum(step, STEPS - 1)]
            here = (step < STEPS) & (lax.rem(holder, HALVES) == lax.rem(row, HALVES))
            back = lax.rem(row // HALVES - holder // HALVES + peers, peers)
            for number, piece_ref in enumerate(piece_refs):

                @pl.when(here & (back == number))
                def _():
                    out_ref[pl.ds(group * share, share), :] = piece_ref[pl.ds(0, share), :]
                    rows = pl.ds(CORES * share, META_ROWS)
                    out_ref[rows, :] = jnp.where(line == group, piece_ref[pl.ds(share, META_ROWS), :], out_ref[rows, :])


def fill_kernel(slots, *refs):
    piece_refs, dense_ref = refs[:-1], refs[-1]
    peers = len(piece_refs)
    share = (piece_refs[0].shape[0] - META_ROWS) // CORES
    width, tile_width = dense_ref.shape[0] // CORES, dense_ref.shape[1]
    place = lax.axis_index("row") // HALVES
    table = piece_refs[0][pl.ds(CORES * share, META_ROWS), :].astype(jnp.float32)
    line = lax.broadcasted_iota(jnp.int32, table.shape, 0)
    lane = lax.broadcasted_iota(jnp.int32, table.shape, 1)

    def entry(group, spot):
        return jnp.max(jnp.where((line == group) & (lane == spot), table, 0.0)).astype(jnp.int32)

    dense_ref[...] = jnp.zeros_like(dense_ref)
    for group in range(CORES):
        count = entry(group, slots)
        starts = [group * width + entry(group, slot) * tile_width for slot in range(slots)]
        for shift, piece_ref in enumerate(piece_refs):
            first = lax.rem(place - shift + peers, peers) * share
            slot = first // tile_width
            start = starts[0]
            for other in range(1, slots):
                start = jnp.where(slot == other, starts[other], start)

            @pl.when(slot < count)
            def _():
                spot = pl.multiple_of(start + lax.rem(first, tile_width), META_ROWS)
                dense_ref[pl.ds(spot, share), :] = piece_ref[pl.ds(group * share, share), :]


def block_product(first, mask_ref, own_ref, other_ref, dense_ref):
    block = first + pl.program_id(0)
    width, tile_width = own_ref.shape[1], dense_ref.shape[1]
    total = None
    for group, rows_ref in enumerate((own_ref, other_ref)):
        parts = []
        for tile in range(width // tile_width):
            live = mask_ref[group * width // tile_width + tile, block].astype(jnp.float32).astype(rows_ref.dtype)
            parts.append(rows_ref[:, pl.ds(tile * tile_width, tile_width)] * live)
        weights = dense_ref[pl.ds(group * width, width), :]
        term = jnp.dot(jnp.concatenate(parts, axis=1), weights, preferred_element_type=jnp.float32)
        total = term if total is None else total + term
    return total


def send_kernel(first, mask_ref, own_ref, other_ref, dense_ref, code_ref, scale_ref):
    step, span = pl.program_id(0), pl.num_programs(0)
    height = own_ref.shape[0]
    total = block_product(first, mask_ref, own_ref, other_ref, dense_ref)
    top = jnp.max(jnp.abs(total), axis=0, keepdims=True)
    unit = jnp.where(top > 0, top, 1.0) * (1.0 / CODE_TOP)
    power = jnp.floor(jnp.log2(unit))
    fraction = jnp.ceil(unit * jnp.exp2(-power) * FRACTION)
    unit = fraction * jnp.exp2(power) * (1.0 / FRACTION)
    code = jnp.clip(jnp.round(total * (1.0 / unit)), -CODE_TOP, CODE_TOP)
    code_ref[pl.ds(pl.multiple_of(step * height, height), height), :] = code.astype(jnp.int32).astype(jnp.int16)
    scale_ref[pl.ds(2 * step, 1), :] = power
    scale_ref[pl.ds(2 * step + 1, 1), :] = fraction

    @pl.when(step == span - 1)
    def _():
        rows = scale_ref.shape[0]
        line = lax.broadcasted_iota(jnp.int32, scale_ref.shape, 0)
        kept = jnp.where(line < 2 * span, scale_ref[...], 0.0)
        code_ref[pl.ds(code_ref.shape[0] - rows, rows), :] = kept.astype(jnp.int32).astype(jnp.int16)


def join_kernel(first, mask_ref, own_ref, other_ref, dense_ref, *refs):
    code_refs, out_ref, scale_ref = refs[:-2], refs[-2], refs[-1]
    step = pl.program_id(0)
    height = own_ref.shape[0]
    rows = scale_ref.shape[0] // max(len(code_refs), 1)

    @pl.when(step == 0)
    def _():
        for number, code_ref in enumerate(code_refs):
            scales = code_ref[pl.ds(code_ref.shape[0] - rows, rows), :].astype(jnp.int32).astype(jnp.float32)
            scale_ref[pl.ds(number * rows, rows), :] = scales

    total = block_product(first, mask_ref, own_ref, other_ref, dense_ref)
    for number, code_ref in enumerate(code_refs):
        power = scale_ref[pl.ds(number * rows + 2 * step, 1), :]
        fraction = scale_ref[pl.ds(number * rows + 2 * step + 1, 1), :]
        code = code_ref[pl.ds(pl.multiple_of(step * height, height), height), :].astype(jnp.int32).astype(jnp.float32)
        total = total + code * (fraction * jnp.exp2(power) * (1.0 / FRACTION))
    out_ref[...] = total.astype(out_ref.dtype)


def after(value, *earlier):
    return lax.optimization_barrier((value, *earlier))[0]


def shards(amplitudes, pair_mask, integrals, tile_list, tile_count, owner):
    row_count, full_width = amplitudes.shape
    slots, tile_width = integrals.shape[2], integrals.shape[-1]
    block_count = pair_mask.shape[0]
    block_rows = row_count // block_count
    row_peers, col_peers = lax.axis_size("row"), lax.axis_size("col")
    peers = row_peers // HALVES
    share = slots * tile_width // peers
    offsets = pair_offsets(col_peers)
    chunks = row_chunks(block_count)

    def along(value, shift):
        return lax.ppermute(value, "row", [(r, (r + HALVES * shift) % row_peers) for r in range(row_peers)])

    def across(value, flip, down):
        pairs = []
        for r in range(row_peers):
            for c in range(col_peers):
                pairs.append((r * col_peers + c, (r ^ flip) * col_peers + (c - CORES * down) % col_peers))
        return lax.ppermute(value, ("row", "col"), pairs)

    swap = [(c, c ^ 1) for c in range(col_peers)]
    other = lax.ppermute(amplitudes, "col", swap)
    other_mask = lax.ppermute(pair_mask.T, "col", swap)
    masks = jnp.concatenate([pair_mask.T, other_mask])
    stored = pltpu.with_memory_space_constraint(amplitudes, pltpu.HBM)
    panels = pltpu.with_memory_space_constraint(integrals, pltpu.HBM)

    table = jnp.concatenate([tile_list[0, 0], tile_count[0], owner[:, 0]])

    pieces = pl.pallas_call(
        pack_kernel,
        in_specs=[SMEM, VMEM],
        out_specs=[VMEM] * peers,
        out_shape=[jax.ShapeDtypeStruct((share + META_ROWS, tile_width), integrals.dtype)] * peers,
        compiler_params=PARAMS,
        name="pack",
    )(table, panels)
    pieces = [piece if shift == 0 else along(piece, shift) for shift, piece in enumerate(pieces)]

    chosen = pl.pallas_call(
        partial(choose_kernel, col_peers, offsets, slots),
        in_specs=[SMEM] + [VMEM] * peers,
        out_specs=[VMEM] * len(offsets),
        out_shape=[jax.ShapeDtypeStruct((CORES * share + META_ROWS, tile_width), integrals.dtype)] * len(offsets),
        compiler_params=PARAMS,
        name="choose",
    )(after(table, masks), *pieces)

    def weights_of(data):
        held = [data] + [along(data, shift) for shift in range(1, peers)]
        return pl.pallas_call(
            partial(fill_kernel, slots),
            in_specs=[VMEM] * peers,
            out_specs=VMEM,
            out_shape=jax.ShapeDtypeStruct((CORES * full_width, tile_width), integrals.dtype),
            compiler_params=PARAMS,
            name="fill",
        )(*held)

    plans = {}
    for offset, data in zip(offsets, chosen):
        if offset:
            plans[offset] = weights_of(across(data, 0, offset) + across(data, 1, offset))

    def cost(span):
        return pl.CostEstimate(
            flops=2 * span * block_rows * CORES * full_width * tile_width,
            bytes_accessed=span * block_rows * (CORES * full_width + tile_width) * 2,
            transcendentals=0,
        )

    def chunk_specs(first, span):
        part = pl.BlockSpec((block_rows, full_width), lambda i: (first + i, 0))
        return [SMEM, part, part, pl.BlockSpec((CORES * full_width, tile_width), lambda i: (0, 0))]

    def code_shape(span):
        return (span * block_rows + -(-2 * span // META_ROWS) * META_ROWS, tile_width)

    arrived, sent = [], []
    for first, span in chunks:
        shape = code_shape(span)
        received = []
        earlier = sent[-1:] + [part for parts in arrived[:-1] for part in parts]
        for offset in offsets:
            if offset == 0:
                continue
            code = pl.pallas_call(
                partial(send_kernel, first),
                grid=(span,),
                in_specs=chunk_specs(first, span),
                out_specs=pl.BlockSpec(shape, lambda i: (0, 0)),
                out_shape=jax.ShapeDtypeStruct(shape, jnp.int16),
                scratch_shapes=[pltpu.VMEM((shape[0] - span * block_rows, tile_width), jnp.float32)],
                compiler_params=PARAMS,
                cost_estimate=cost(span),
                name="send_part",
            )(masks, stored, other, after(plans[offset], *earlier))
            received.append(across(code, 0, -offset))
            sent.append(code)
        arrived.append(received)

    own = after(chosen[offsets.index(0)], *arrived[0])
    plans[0] = weights_of(own + across(own, 1, 0))

    out = None
    for (first, span), received in zip(chunks, arrived):
        shape = code_shape(span)
        operands = [masks, stored, other, plans[0], *received]
        specs = chunk_specs(first, span) + [pl.BlockSpec(shape, lambda i: (0, 0))] * len(received)
        body, aliases = partial(join_kernel, first), {}
        if out is not None:
            body = partial(skip_operand, len(operands), body)
            aliases = {len(operands): 0}
            operands.append(out)
            specs.append(pl.BlockSpec(memory_space=pl.ANY))
        out = pl.pallas_call(
            body,
            grid=(span,),
            in_specs=specs,
            out_specs=pl.BlockSpec((block_rows, tile_width), lambda i, first=first: (first + i, 0)),
            out_shape=jax.ShapeDtypeStruct((row_count, tile_width), jnp.bfloat16),
            scratch_shapes=[
                pltpu.VMEM(((shape[0] - span * block_rows) * max(len(received), 1), tile_width), jnp.float32)
            ],
            input_output_aliases=aliases,
            compiler_params=PARAMS,
            cost_estimate=cost(span),
            name="join_part",
        )(*operands)
    return out


def skip_operand(position, body, *refs):
    body(*refs[:position], *refs[position + 1 :])


def solution(mesh):
    return jax.shard_map(
        shards,
        mesh=mesh,
        in_specs=(
            P("row", "col"),
            P("row", "col"),
            P("row", "col", None, None, None),
            P("row", "col", None),
            P("row", "col"),
            P(None, "col"),
        ),
        out_specs=P("row", "col"),
        check_vma=False,
    )
```

time: 88.5 us -> 90 us (1.017)
  Pallas kernels: 24.8 us -> 29.9 us
  local copies, waits for them, and re-layouts: 4.6 us -> 0 us
  waiting for transfers between devices: 35.7 us -> 33.8 us
  other arithmetic: 0.07 us -> 1.51 us
  starting transfers between devices: 22.2 us -> 23.3 us
    pallas_call x12, Pallas kernels: 24.1 us -> 29.2 us  [the longest x5 15.3 us: shards(): pl.pallas_call(body, grid=(span,), in_specs=specs, out_specs=pl.BlockSpec...]
    unnamed x14 -> x0, local copies, waits for them, and re-layouts: 4.6 us -> none
    ppermute x8, waiting for transfers between devices: 15.5 us -> 12 us  [across(): return lax.ppermute(value, ('row', 'col'), pairs)]
    ppermute x9, waiting for transfers between devices: 20.3 us -> 21.8 us  [along(): lax.ppermute(value, 'row', [(r, (r + HALVES * shift) % row_peers) for r i...]
    concatenate x0 -> x2, other arithmetic: none -> 1.44 us  [the longest x1 0.75 us: shards(): table = jnp.concatenate([tile_list[0, 0], tile_count[0], owner[:, 0]])]
  transfers between devices with their start and end apart: 19 -> 19, of which waited for: 11 -> 10; matrix products, arithmetic and copies ran while one was open for 0% -> 2% of each run, Pallas kernels for 25% -> 30%
where the time goes in v5:
time: 90 us; the launch traced here: 89.3 us
  waiting for transfers between devices  33.8 us (38%)
  Pallas kernels  29.9 us (33%)
  starting transfers between devices  23.3 us (26%)
  other arithmetic  1.51 us (2%)
    ppermute x9, waiting for transfers between devices, along(): lax.ppermute(value, 'row', [(r, (r + HALVES * shift) % row_peers) for r i...  21.8 us
    pallas_call x5, Pallas kernels, shards(): pl.pallas_call(body, grid=(span,), in_specs=specs, out_specs=pl.BlockSpec...  15.3 us
    ppermute x9, starting transfers between devices, along(): lax.ppermute(value, 'row', [(r, (r + HALVES * shift) % row_peers) for r i...  13.5 us
    pallas_call x5, Pallas kernels, shards(): pl.pallas_call(partial(send_kernel, first), grid=(span,), in_specs=chunk_...  12.2 us
    ppermute x8, waiting for transfers between devices, across(): return lax.ppermute(value, ('row', 'col'), pairs)  12 us
    ppermute x8, starting transfers between devices, across(): return lax.ppermute(value, ('row', 'col'), pairs)  9.3 us
  transfers between devices with their start and end apart: 19, of which 10 were waited for; matrix products, arithmetic and copies ran while one was open for 2% of the time, Pallas kernels for 30%

profile of v5, /device:TPU:0, one launch (start us, length us, event | category | flops | bytes accessed | tf_op | source)
XLA Modules:
  0.0 89.3 jit_solution(3907079116634620369)
XLA Ops:
  0.0 0.5 collective-permute-start.1
  0.5 0.1 collective-permute-start
  1.2 0.7 pad_add_fusion.1.table_ref
  1.9 1.0 %pack.1 = (bf16[144,256]{1,0:T(8,128)(2,1)S(1)}, bf16[144,256]{1,0:T(8,128)(2,1)S(1)}, bf16[144,256]{1,0:T(8,128)(2,1)S(1)}, bf16[144,256]{1,0:T(8,128)(2,1)S(1)}) custom-call(s32[7]{0:T(128)S(1)} %pad_add_fusion.1.table_ref, bf16[1,1,2,256,256]{4,3,2,1,0:T(8,128)(2,1)} %panel_ref.1), custom_call_target="tpu_custom_call" | custom-call | tf_op jit(solution)/shard_map/pack/pallas_call | solution.py:200
  2.9 3.1 %collective-permute-start.2 = (bf16[144,256]{1,0:T(8,128)(2,1)S(1)}, bf16[144,256]{1,0:T(8,128)(2,1)S(1)}, u32[]{:S(2)}, u32[]{:S(2)}) collective-permute-start(bf16[144,256]{1,0:T(8,128)(2,1)S(1)} %get-tuple-element.19), channel_id=1, source_target_pairs={{0,8},{4,12},{8,16},{12,20},{16,24},{20,28},{24,0},{28,4},{1,9},{5... | collective-permute-start | bytes 221192 | tf_op jit(solution)/shard_map/ppermute | solution.py:182
  6.0 2.6 %collective-permute-start.3 = (bf16[144,256]{1,0:T(8,128)(2,1)S(1)}, bf16[144,256]{1,0:T(8,128)(2,1)S(1)}, u32[]{:S(2)}, u32[]{:S(2)}) collective-permute-start(bf16[144,256]{1,0:T(8,128)(2,1)S(1)} %get-tuple-element.20), channel_id=1, source_target_pairs={{0,16},{4,20},{8,24},{12,28},{16,0},{20,4},{24,8},{28,12},{1,17},{... | collective-permute-start | bytes 221192 | tf_op jit(solution)/shard_map/ppermute | solution.py:182
  8.6 1.3 %collective-permute-start.4 = (bf16[144,256]{1,0:T(8,128)(2,1)S(1)}, bf16[144,256]{1,0:T(8,128)(2,1)S(1)}, u32[]{:S(2)}, u32[]{:S(2)}) collective-permute-start(bf16[144,256]{1,0:T(8,128)(2,1)S(1)} %get-tuple-element.21), channel_id=1, source_target_pairs={{0,24},{4,28},{8,0},{12,4},{16,8},{20,12},{24,16},{28,20},{1,25},{... | collective-permute-start | bytes 221192 | tf_op jit(solution)/shard_map/ppermute | solution.py:182
  9.9 0.0 collective-permute-done
  10.0 0.7 pad_add_fusion.mask_ref.refs_0_
  10.6 0.2 collective-permute-done.2.refs_1_
  10.9 2.9 %collective-permute-done.3.refs_2_ = bf16[144,256]{1,0:T(8,128)(2,1)S(1)} collective-permute-done((bf16[144,256]{1,0:T(8,128)(2,1)S(1)}, bf16[144,256]{1,0:T(8,128)(2,1)S(1)}, u32[]{:S(2)}, u32[]{:S(2)}) %collective-permute-start.3) | collective-permute-done | bytes 73760 | tf_op jit(solution)/shard_map/ppermute | solution.py:182
  13.7 0.2 collective-permute-done.4.refs_3_
  14.0 0.7 choose.1
  14.7 2.5 %collective-permute-start.6 = (bf16[272,256]{1,0:T(8,128)(2,1)S(1)}, bf16[272,256]{1,0:T(8,128)(2,1)S(1)}, u32[]{:S(2)}, u32[]{:S(2)}) collective-permute-start(bf16[272,256]{1,0:T(8,128)(2,1)S(1)} %get-tuple-element.23), channel_id=1, source_target_pairs={{0,6},{1,7},{2,4},{3,5},{4,2},{5,3},{6,0},{7,1},{8,14},{9,15},{10,... | collective-permute-start | bytes 417800 | tf_op jit(solution)/shard_map/ppermute | solution.py:189
  17.2 0.5 collective-permute-start.5
  17.7 4.5 %collective-permute-done.6 = bf16[272,256]{1,0:T(8,128)(2,1)S(1)} collective-permute-done((bf16[272,256]{1,0:T(8,128)(2,1)S(1)}, bf16[272,256]{1,0:T(8,128)(2,1)S(1)}, u32[]{:S(2)}, u32[]{:S(2)}) %collective-permute-start.6) | collective-permute-done | bytes 139296 | tf_op jit(solution)/shard_map/ppermute | solution.py:189
  22.2 1.7 %collective-permute-done.5 = bf16[272,256]{1,0:T(8,128)(2,1)S(1)} collective-permute-done((bf16[272,256]{1,0:T(8,128)(2,1)S(1)}, bf16[272,256]{1,0:T(8,128)(2,1)S(1)}, u32[]{:S(2)}, u32[]{:S(2)}) %collective-permute-start.5) | collective-permute-done | bytes 139296 | tf_op jit(solution)/shard_map/ppermute | solution.py:189
  24.0 2.9 %collective-permute-start.9 = (bf16[272,256]{1,0:T(8,128)(2,1)S(1)}, bf16[272,256]{1,0:T(8,128)(2,1)S(1)}, u32[]{:S(2)}, u32[]{:S(2)}) collective-permute-start(bf16[272,256]{1,0:T(8,128)(2,1)S(1)} %add.6.refs_0_), channel_id=1, source_target_pairs={{0,24},{4,28},{8,0},{12,4},{16,8},{20,12},{24,16},{28,20},{1,25},{... | collective-permute-start | bytes 417800 | tf_op jit(solution)/shard_map/ppermute | solution.py:182
  26.9 0.8 collective-permute-start.8
  27.6 3.4 %collective-permute-done.9.refs_3_ = bf16[272,256]{1,0:T(8,128)(2,1)S(1)} collective-permute-done((bf16[272,256]{1,0:T(8,128)(2,1)S(1)}, bf16[272,256]{1,0:T(8,128)(2,1)S(1)}, u32[]{:S(2)}, u32[]{:S(2)}) %collective-permute-start.9) | collective-permute-done | bytes 139296 | tf_op jit(solution)/shard_map/ppermute | solution.py:182
  31.0 8.3 %collective-permute-done.8.refs_2_ = bf16[272,256]{1,0:T(8,128)(2,1)S(1)} collective-permute-done((bf16[272,256]{1,0:T(8,128)(2,1)S(1)}, bf16[272,256]{1,0:T(8,128)(2,1)S(1)}, u32[]{:S(2)}, u32[]{:S(2)}) %collective-permute-start.8) | collective-permute-done | bytes 139296 | tf_op jit(solution)/shard_map/ppermute | solution.py:182
  39.3 0.3 fill.2.dense_ref
  39.6 1.5 %send_part.5 = s16[272,256]{1,0:T(8,128)(2,1)S(1)} custom-call(s32[6,12]{1,0:T(8,128)S(1)} %pad_add_fusion.mask_ref.refs_0_, bf16[3072,768]{1,0:T(8,128)(2,1)} %refs_1_.7, bf16[3072,768]{1,0:T(8,128)(2,1)S(1)} %collective-permute-done.1.other_ref.refs_2_, bf16[1536,256]{1,0:T(8,128)(2,1)S(1)} %fill.2.dense_ref), custom_call_target="tpu_custom_call" | custom-call | flops 201326592 | bytes 917504 | tf_op jit(solution)/shard_map/send_part/pallas_call | solution.py:257
  41.1 1.6 %collective-permute-start.10 = (s16[272,256]{1,0:T(8,128)(2,1)S(1)}, s16[272,256]{1,0:T(8,128)(2,1)S(1)}, u32[]{:S(2)}, u32[]{:S(2)}) collective-permute-start(s16[272,256]{1,0:T(8,128)(2,1)S(1)} %send_part.5), channel_id=1, source_target_pairs={{0,2},{1,3},{2,0},{3,1},{4,6},{5,7},{6,4},{7,5},{8,10},{9,11},{10,... | collective-permute-start | bytes 417800 | tf_op jit(solution)/shard_map/ppermute | solution.py:189
  42.7 2.9 %send_part.6 = s16[784,256]{1,0:T(8,128)(2,1)S(1)} custom-call(s32[6,12]{1,0:T(8,128)S(1)} %pad_add_fusion.mask_ref.refs_0_, bf16[3072,768]{1,0:T(8,128)(2,1)} %refs_1_.7, bf16[3072,768]{1,0:T(8,128)(2,1)S(1)} %collective-permute-done.1.other_ref.refs_2_, bf16[1536,256]{1,0:T(8,128)(2,1)S(1)} %fill.2.dense_ref), custom_call_target="tpu_custom_call" | custom-call | flops 603979776 | bytes 2752512 | tf_op jit(solution)/shard_map/send_part/pallas_call | solution.py:257
  45.6 0.6 collective-permute-start.15
  46.2 0.0 collective-permute-done.10.refs_0_
  46.2 3.4 %send_part.7 = s16[1040,256]{1,0:T(8,128)(2,1)S(1)} custom-call(s32[6,12]{1,0:T(8,128)S(1)} %pad_add_fusion.mask_ref.refs_0_, bf16[3072,768]{1,0:T(8,128)(2,1)} %refs_1_.7, bf16[3072,768]{1,0:T(8,128)(2,1)S(1)} %collective-permute-done.1.other_ref.refs_2_, bf16[1536,256]{1,0:T(8,128)(2,1)S(1)} %fill.2.dense_ref), custom_call_target="tpu_custom_call" | custom-call | flops 805306368 | bytes 3670016 | tf_op jit(solution)/shard_map/send_part/pallas_call | solution.py:257
  49.7 2.1 %collective-permute-start.16 = (s16[1040,256]{1,0:T(8,128)(2,1)S(1)}, s16[1040,256]{1,0:T(8,128)(2,1)S(1)}, u32[]{:S(2)}, u32[]{:S(2)}) collective-permute-start(s16[1040,256]{1,0:T(8,128)(2,1)S(1)} %send_part.7), channel_id=1, source_target_pairs={{0,2},{1,3},{2,0},{3,1},{4,6},{5,7},{6,4},{7,5},{8,10},{9,11},{10,... | collective-permute-start | bytes 1597448 | tf_op jit(solution)/shard_map/ppermute | solution.py:189
  51.8 0.4 collective-permute-start.11
  52.2 5.7 %collective-permute-done.15.refs_4_ = s16[784,256]{1,0:T(8,128)(2,1)S(1)} collective-permute-done((s16[784,256]{1,0:T(8,128)(2,1)S(1)}, s16[784,256]{1,0:T(8,128)(2,1)S(1)}, u32[]{:S(2)}, u32[]{:S(2)}) %collective-permute-start.15) | collective-permute-done | bytes 401440 | tf_op jit(solution)/shard_map/ppermute | solution.py:189
  57.9 2.9 %send_part.8 = s16[784,256]{1,0:T(8,128)(2,1)S(1)} custom-call(s32[6,12]{1,0:T(8,128)S(1)} %pad_add_fusion.mask_ref.refs_0_, bf16[3072,768]{1,0:T(8,128)(2,1)} %refs_1_.7, bf16[3072,768]{1,0:T(8,128)(2,1)S(1)} %collective-permute-done.1.other_ref.refs_2_, bf16[1536,256]{1,0:T(8,128)(2,1)S(1)} %fill.2.dense_ref), custom_call_target="tpu_custom_call" | custom-call | flops 603979776 | bytes 2752512 | tf_op jit(solution)/shard_map/send_part/pallas_call | solution.py:257
  60.9 0.6 collective-permute-start.18
  61.5 0.1 collective-permute-start.14
  61.6 0.8 collective-permute-start.13
  62.4 1.9 %collective-permute-start.12 = (bf16[272,256]{1,0:T(8,128)(2,1)S(1)}, bf16[272,256]{1,0:T(8,128)(2,1)S(1)}, u32[]{:S(2)}, u32[]{:S(2)}) collective-permute-start(bf16[272,256]{1,0:T(8,128)(2,1)S(1)} %add.7.refs_0_), channel_id=1, source_target_pairs={{0,8},{4,12},{8,16},{12,20},{16,24},{20,28},{24,0},{28,4},{1,9},{5... | collective-permute-start | bytes 417800 | tf_op jit(solution)/shard_map/ppermute | solution.py:182
  64.3 2.5 %collective-permute-done.14.refs_3_ = bf16[272,256]{1,0:T(8,128)(2,1)S(1)} collective-permute-done((bf16[272,256]{1,0:T(8,128)(2,1)S(1)}, bf16[272,256]{1,0:T(8,128)(2,1)S(1)}, u32[]{:S(2)}, u32[]{:S(2)}) %collective-permute-start.14) | collective-permute-done | bytes 139296 | tf_op jit(solution)/shard_map/ppermute | solution.py:182
  66.8 4.4 %collective-permute-done.13.refs_2_ = bf16[272,256]{1,0:T(8,128)(2,1)S(1)} collective-permute-done((bf16[272,256]{1,0:T(8,128)(2,1)S(1)}, bf16[272,256]{1,0:T(8,128)(2,1)S(1)}, u32[]{:S(2)}, u32[]{:S(2)}) %collective-permute-start.13) | collective-permute-done | bytes 139296 | tf_op jit(solution)/shard_map/ppermute | solution.py:182
  71.2 0.0 collective-permute-done.12.refs_1_
  71.2 0.3 fill.3.dense_ref.refs_3_
  71.6 2.0 %join_part.5.refs_5_ = bf16[3072,256]{1,0:T(8,128)(2,1)} custom-call(s32[6,12]{1,0:T(8,128)S(1)} %pad_add_fusion.mask_ref.refs_0_, bf16[3072,768]{1,0:T(8,128)(2,1)} %refs_1_.7, bf16[3072,768]{1,0:T(8,128)(2,1)S(1)} %collective-permute-done.1.other_ref.refs_2_, bf16[1536,256]{1,0:T(8,128)(2,1)S(1)} %fill.3.dense_ref.refs_3_, ...), custom_call_target="tpu_custom_call" | custom-call | flops 201326592 | bytes 917504 | tf_op jit(solution)/shard_map/join_part/pallas_call | solution.py:286
  73.6 0.0 collective-permute-done.16.refs_4_
  73.6 1.5 %send_part.9 = s16[272,256]{1,0:T(8,128)(2,1)S(1)} custom-call(s32[6,12]{1,0:T(8,128)S(1)} %pad_add_fusion.mask_ref.refs_0_, bf16[3072,768]{1,0:T(8,128)(2,1)} %refs_1_.7, bf16[3072,768]{1,0:T(8,128)(2,1)S(1)} %collective-permute-done.1.other_ref.refs_2_, bf16[1536,256]{1,0:T(8,128)(2,1)S(1)} %fill.2.dense_ref), custom_call_target="tpu_custom_call" | custom-call | flops 201326592 | bytes 917504 | tf_op jit(solution)/shard_map/send_part/pallas_call | solution.py:257
  75.1 1.0 %collective-permute-start.17 = (s16[272,256]{1,0:T(8,128)(2,1)S(1)}, s16[272,256]{1,0:T(8,128)(2,1)S(1)}, u32[]{:S(2)}, u32[]{:S(2)}) collective-permute-start(s16[272,256]{1,0:T(8,128)(2,1)S(1)} %send_part.9), channel_id=1, source_target_pairs={{0,2},{1,3},{2,0},{3,1},{4,6},{5,7},{6,4},{7,5},{8,10},{9,11},{10,... | collective-permute-start | bytes 417800 | tf_op jit(solution)/shard_map/ppermute | solution.py:189
  76.1 3.5 %join_part.6.refs_5_ = bf16[3072,256]{1,0:T(8,128)(2,1)} custom-call(s32[6,12]{1,0:T(8,128)S(1)} %pad_add_fusion.mask_ref.refs_0_, bf16[3072,768]{1,0:T(8,128)(2,1)} %refs_1_.7, bf16[3072,768]{1,0:T(8,128)(2,1)S(1)} %collective-permute-done.1.other_ref.refs_2_, bf16[1536,256]{1,0:T(8,128)(2,1)S(1)} %fill.3.dense_ref.refs_3_, ...), custom_call_target="tpu_custom_call", output_to_operand_aliasing={{}: (5, {})} | custom-call | flops 603979776 | bytes 2752512 | tf_op jit(solution)/shard_map/join_part/pallas_call | solution.py:286
  79.6 4.1 %join_part.7.refs_5_ = bf16[3072,256]{1,0:T(8,128)(2,1)} custom-call(s32[6,12]{1,0:T(8,128)S(1)} %pad_add_fusion.mask_ref.refs_0_, bf16[3072,768]{1,0:T(8,128)(2,1)} %refs_1_.7, bf16[3072,768]{1,0:T(8,128)(2,1)S(1)} %collective-permute-done.1.other_ref.refs_2_, bf16[1536,256]{1,0:T(8,128)(2,1)S(1)} %fill.3.dense_ref.refs_3_, ...), custom_call_target="tpu_custom_call", output_to_operand_aliasing={{}: (5, {})} | custom-call | flops 805306368 | bytes 3670016 | tf_op jit(solution)/shard_map/join_part/pallas_call | solution.py:286
  83.7 3.5 %join_part.8.refs_5_ = bf16[3072,256]{1,0:T(8,128)(2,1)} custom-call(s32[6,12]{1,0:T(8,128)S(1)} %pad_add_fusion.mask_ref.refs_0_, bf16[3072,768]{1,0:T(8,128)(2,1)} %refs_1_.7, bf16[3072,768]{1,0:T(8,128)(2,1)S(1)} %collective-permute-done.1.other_ref.refs_2_, bf16[1536,256]{1,0:T(8,128)(2,1)S(1)} %fill.3.dense_ref.refs_3_, ...), custom_call_target="tpu_custom_call", output_to_operand_aliasing={{}: (5, {})} | custom-call | flops 603979776 | bytes 2752512 | tf_op jit(solution)/shard_map/join_part/pallas_call | solution.py:286
  87.3 2.0 %join_part.9 = bf16[3072,256]{1,0:T(8,128)(2,1)} custom-call(s32[6,12]{1,0:T(8,128)S(1)} %pad_add_fusion.mask_ref.refs_0_, bf16[3072,768]{1,0:T(8,128)(2,1)} %refs_1_.7, bf16[3072,768]{1,0:T(8,128)(2,1)S(1)} %collective-permute-done.1.other_ref.refs_2_, bf16[1536,256]{1,0:T(8,128)(2,1)S(1)} %fill.3.dense_ref.refs_3_, ...), custom_call_target="tpu_custom_call", output_to_operand_aliasing={{}: (5, {})} | custom-call | flops 201326592 | bytes 917504 | tf_op jit(solution)/shard_map/join_part/pallas_call | solution.py:286
  (8 shorter events, 0.1 us)
Async XLA Ops:
  0.0 39.6 %collective-permute-start.1 = (bf16[3072,768]{1,0:T(8,128)(2,1)}, bf16[3072,768]{1,0:T(8,128)(2,1)S(1)}, u32[]{:S(2)}, u32[]{:S(2)}) collective-permute-start(bf16[3072,768]{1,0:T(8,128)(2,1)} %refs_1_.7), channel_id=1, source_target_pairs={{0,1},{1,0},{2,3},{3,2},{4,5},{5,4},{6,7},{7,6},{8,9},{9,8},{10,11... | collective-permute-start | bytes 14155784 | tf_op jit(solution)/shard_map/ppermute | solution.py:192
  0.5 9.5 %collective-permute-start = (s32[3,12]{1,0:T(4,128)}, s32[3,12]{1,0:T(4,128)S(1)}, u32[]{:S(2)}, u32[]{:S(2)}) collective-permute-start(s32[3,12]{1,0:T(4,128)} %bitcast.5), channel_id=1, source_target_pairs={{0,1},{1,0},{2,3},{3,2},{4,5},{5,4},{6,7},{7,6},{8,9},{9,8},{10,11... | collective-permute-start | bytes 440 | tf_op jit(solution)/shard_map/ppermute | solution.py:193
  2.9 7.9 %collective-permute-start.2 = (bf16[144,256]{1,0:T(8,128)(2,1)S(1)}, bf16[144,256]{1,0:T(8,128)(2,1)S(1)}, u32[]{:S(2)}, u32[]{:S(2)}) collective-permute-start(bf16[144,256]{1,0:T(8,128)(2,1)S(1)} %get-tuple-element.19), channel_id=1, source_target_pairs={{0,8},{4,12},{8,16},{12,20},{16,24},{20,28},{24,0},{28,4},{1,9},{5... | collective-permute-start | bytes 221192 | tf_op jit(solution)/shard_map/ppermute | solution.py:182
  6.0 7.7 %collective-permute-start.3 = (bf16[144,256]{1,0:T(8,128)(2,1)S(1)}, bf16[144,256]{1,0:T(8,128)(2,1)S(1)}, u32[]{:S(2)}, u32[]{:S(2)}) collective-permute-start(bf16[144,256]{1,0:T(8,128)(2,1)S(1)} %get-tuple-element.20), channel_id=1, source_target_pairs={{0,16},{4,20},{8,24},{12,28},{16,0},{20,4},{24,8},{28,12},{1,17},{... | collective-permute-start | bytes 221192 | tf_op jit(solution)/shard_map/ppermute | solution.py:182
  8.6 5.4 %collective-permute-start.4 = (bf16[144,256]{1,0:T(8,128)(2,1)S(1)}, bf16[144,256]{1,0:T(8,128)(2,1)S(1)}, u32[]{:S(2)}, u32[]{:S(2)}) collective-permute-start(bf16[144,256]{1,0:T(8,128)(2,1)S(1)} %get-tuple-element.21), channel_id=1, source_target_pairs={{0,24},{4,28},{8,0},{12,4},{16,8},{20,12},{24,16},{28,20},{1,25},{... | collective-permute-start | bytes 221192 | tf_op jit(solution)/shard_map/ppermute | solution.py:182
  14.7 7.5 %collective-permute-start.6 = (bf16[272,256]{1,0:T(8,128)(2,1)S(1)}, bf16[272,256]{1,0:T(8,128)(2,1)S(1)}, u32[]{:S(2)}, u32[]{:S(2)}) collective-permute-start(bf16[272,256]{1,0:T(8,128)(2,1)S(1)} %get-tuple-element.23), channel_id=1, source_target_pairs={{0,6},{1,7},{2,4},{3,5},{4,2},{5,3},{6,0},{7,1},{8,14},{9,15},{10,... | collective-permute-start | bytes 417800 | tf_op jit(solution)/shard_map/ppermute | solution.py:189
  17.2 6.8 %collective-permute-start.5 = (bf16[272,256]{1,0:T(8,128)(2,1)S(1)}, bf16[272,256]{1,0:T(8,128)(2,1)S(1)}, u32[]{:S(2)}, u32[]{:S(2)}) collective-permute-start(bf16[272,256]{1,0:T(8,128)(2,1)S(1)} %get-tuple-element.23), channel_id=1, source_target_pairs={{0,2},{1,3},{2,0},{3,1},{4,6},{5,7},{6,4},{7,5},{8,10},{9,11},{10,... | collective-permute-start | bytes 417800 | tf_op jit(solution)/shard_map/ppermute | solution.py:189
  24.0 7.0 %collective-permute-start.9 = (bf16[272,256]{1,0:T(8,128)(2,1)S(1)}, bf16[272,256]{1,0:T(8,128)(2,1)S(1)}, u32[]{:S(2)}, u32[]{:S(2)}) collective-permute-start(bf16[272,256]{1,0:T(8,128)(2,1)S(1)} %add.6.refs_0_), channel_id=1, source_target_pairs={{0,24},{4,28},{8,0},{12,4},{16,8},{20,12},{24,16},{28,20},{1,25},{... | collective-permute-start | bytes 417800 | tf_op jit(solution)/shard_map/ppermute | solution.py:182
  26.9 12.4 %collective-permute-start.8 = (bf16[272,256]{1,0:T(8,128)(2,1)S(1)}, bf16[272,256]{1,0:T(8,128)(2,1)S(1)}, u32[]{:S(2)}, u32[]{:S(2)}) collective-permute-start(bf16[272,256]{1,0:T(8,128)(2,1)S(1)} %add.6.refs_0_), channel_id=1, source_target_pairs={{0,16},{4,20},{8,24},{12,28},{16,0},{20,4},{24,8},{28,12},{1,17},{... | collective-permute-start | bytes 417800 | tf_op jit(solution)/shard_map/ppermute | solution.py:182
  27.6 11.7 %collective-permute-start.7 = (bf16[272,256]{1,0:T(8,128)(2,1)S(1)}, bf16[272,256]{1,0:T(8,128)(2,1)S(1)}, u32[]{:S(2)}, u32[]{:S(2)}) collective-permute-start(bf16[272,256]{1,0:T(8,128)(2,1)S(1)} %add.6.refs_0_), channel_id=1, source_target_pairs={{0,8},{4,12},{8,16},{12,20},{16,24},{20,28},{24,0},{28,4},{1,9},{5... | collective-permute-start | bytes 417800 | tf_op jit(solution)/shard_map/ppermute | solution.py:182
  41.1 5.1 %collective-permute-start.10 = (s16[272,256]{1,0:T(8,128)(2,1)S(1)}, s16[272,256]{1,0:T(8,128)(2,1)S(1)}, u32[]{:S(2)}, u32[]{:S(2)}) collective-permute-start(s16[272,256]{1,0:T(8,128)(2,1)S(1)} %send_part.5), channel_id=1, source_target_pairs={{0,2},{1,3},{2,0},{3,1},{4,6},{5,7},{6,4},{7,5},{8,10},{9,11},{10,... | collective-permute-start | bytes 417800 | tf_op jit(solution)/shard_map/ppermute | solution.py:189
  45.6 12.3 %collective-permute-start.15 = (s16[784,256]{1,0:T(8,128)(2,1)S(1)}, s16[784,256]{1,0:T(8,128)(2,1)S(1)}, u32[]{:S(2)}, u32[]{:S(2)}) collective-permute-start(s16[784,256]{1,0:T(8,128)(2,1)S(1)} %send_part.6), channel_id=1, source_target_pairs={{0,2},{1,3},{2,0},{3,1},{4,6},{5,7},{6,4},{7,5},{8,10},{9,11},{10,... | collective-permute-start | bytes 1204232 | tf_op jit(solution)/shard_map/ppermute | solution.py:189
  49.7 23.9 %collective-permute-start.16 = (s16[1040,256]{1,0:T(8,128)(2,1)S(1)}, s16[1040,256]{1,0:T(8,128)(2,1)S(1)}, u32[]{:S(2)}, u32[]{:S(2)}) collective-permute-start(s16[1040,256]{1,0:T(8,128)(2,1)S(1)} %send_part.7), channel_id=1, source_target_pairs={{0,2},{1,3},{2,0},{3,1},{4,6},{5,7},{6,4},{7,5},{8,10},{9,11},{10,... | collective-permute-start | bytes 1597448 | tf_op jit(solution)/shard_map/ppermute | solution.py:189
  51.8 9.7 %collective-permute-start.11 = (bf16[272,256]{1,0:T(8,128)(2,1)S(1)}, bf16[272,256]{1,0:T(8,128)(2,1)S(1)}, u32[]{:S(2)}, u32[]{:S(2)}) collective-permute-start(bf16[272,256]{1,0:T(8,128)(2,1)S(1)} %get-tuple-element.24), channel_id=1, source_target_pairs={{0,4},{1,5},{2,6},{3,7},{4,0},{5,1},{6,2},{7,3},{8,12},{9,13},{10,... | collective-permute-start | bytes 417800 | tf_op jit(solution)/shard_map/ppermute | solution.py:189
  60.9 22.9 %collective-permute-start.18 = (s16[784,256]{1,0:T(8,128)(2,1)S(1)}, s16[784,256]{1,0:T(8,128)(2,1)S(1)}, u32[]{:S(2)}, u32[]{:S(2)}) collective-permute-start(s16[784,256]{1,0:T(8,128)(2,1)S(1)} %send_part.8), channel_id=1, source_target_pairs={{0,2},{1,3},{2,0},{3,1},{4,6},{5,7},{6,4},{7,5},{8,10},{9,11},{10,... | collective-permute-start | bytes 1204232 | tf_op jit(solution)/shard_map/ppermute | solution.py:189
  61.5 5.3 %collective-permute-start.14 = (bf16[272,256]{1,0:T(8,128)(2,1)S(1)}, bf16[272,256]{1,0:T(8,128)(2,1)S(1)}, u32[]{:S(2)}, u32[]{:S(2)}) collective-permute-start(bf16[272,256]{1,0:T(8,128)(2,1)S(1)} %add.7.refs_0_), channel_id=1, source_target_pairs={{0,24},{4,28},{8,0},{12,4},{16,8},{20,12},{24,16},{28,20},{1,25},{... | collective-permute-start | bytes 417800 | tf_op jit(solution)/shard_map/ppermute | solution.py:182
  61.6 9.7 %collective-permute-start.13 = (bf16[272,256]{1,0:T(8,128)(2,1)S(1)}, bf16[272,256]{1,0:T(8,128)(2,1)S(1)}, u32[]{:S(2)}, u32[]{:S(2)}) collective-permute-start(bf16[272,256]{1,0:T(8,128)(2,1)S(1)} %add.7.refs_0_), channel_id=1, source_target_pairs={{0,16},{4,20},{8,24},{12,28},{16,0},{20,4},{24,8},{28,12},{1,17},{... | collective-permute-start | bytes 417800 | tf_op jit(solution)/shard_map/ppermute | solution.py:182
  62.4 8.8 %collective-permute-start.12 = (bf16[272,256]{1,0:T(8,128)(2,1)S(1)}, bf16[272,256]{1,0:T(8,128)(2,1)S(1)}, u32[]{:S(2)}, u32[]{:S(2)}) collective-permute-start(bf16[272,256]{1,0:T(8,128)(2,1)S(1)} %add.7.refs_0_), channel_id=1, source_target_pairs={{0,8},{4,12},{8,16},{12,20},{16,24},{20,28},{24,0},{28,4},{1,9},{5... | collective-permute-start | bytes 417800 | tf_op jit(solution)/shard_map/ppermute | solution.py:182
  75.1 12.2 %collective-permute-start.17 = (s16[272,256]{1,0:T(8,128)(2,1)S(1)}, s16[272,256]{1,0:T(8,128)(2,1)S(1)}, u32[]{:S(2)}, u32[]{:S(2)}) collective-permute-start(s16[272,256]{1,0:T(8,128)(2,1)S(1)} %send_part.9), channel_id=1, source_target_pairs={{0,2},{1,3},{2,0},{3,1},{4,6},{5,7},{6,4},{7,5},{8,10},{9,11},{10,... | collective-permute-start | bytes 417800 | tf_op jit(solution)/shard_map/ppermute | solution.py:189

commit v6 on v5

v6 whole, which is shorter than its diff:
```python
from functools import partial

import jax
import jax.numpy as jnp
from jax import lax
from jax.experimental import pallas as pl
from jax.experimental.pallas import tpu as pltpu
from jax.sharding import PartitionSpec as P

STEPS = 4
CORES = 2
HALVES = 2
CUTS = (0.0, 0.167, 0.583, 0.917, 1.0)
CODE_TOP = 32767.0
FRACTION = 8192.0
META_ROWS = 16
PARAMS = pltpu.CompilerParams(vmem_limit_bytes=16 * 1024 * 1024)
SMEM = pl.BlockSpec(memory_space=pltpu.SMEM)
VMEM = pl.BlockSpec(memory_space=pltpu.VMEM)


def pair_offsets(col_count):
    pairs = col_count // CORES
    offsets = set()
    for core in range(CORES):
        for step in range(STEPS):
            offsets.add(-((core - step) // CORES) % pairs)
    return sorted(offsets)


def row_chunks(block_count):
    marks = sorted({round(block_count * cut) for cut in CUTS})
    return [(first, last - first) for first, last in zip(marks, marks[1:])]


def pack_kernel(table_ref, panel_ref, *piece_refs):
    peers = len(piece_refs)
    slots, tile_width = panel_ref.shape[2:4]
    share = slots * tile_width // peers
    place = lax.axis_index("row") // HALVES
    lane = lax.broadcasted_iota(jnp.int32, (META_ROWS, tile_width), 1)
    lane = lax.rem(lane, tile_width // HALVES)
    info = jnp.zeros((META_ROWS, tile_width), jnp.int32)
    for spot in range(slots + 1):
        info = jnp.where(lane == spot, table_ref[spot], info)
    info = info.astype(jnp.float32).astype(panel_ref.dtype)
    for shift, piece_ref in enumerate(piece_refs):
        first = lax.rem(place + shift, peers) * share
        start = pl.multiple_of(lax.rem(first, tile_width), META_ROWS)
        piece_ref[pl.ds(0, share), :] = panel_ref[0, 0, first // tile_width, pl.ds(start, share), :]
        piece_ref[pl.ds(share, META_ROWS), :] = info


def choose_kernel(col_peers, offsets, slots, peers, table_ref, *refs):
    piece_refs, out_refs = refs[:peers], list(refs[peers:])
    share, tile_width = piece_refs[0].shape[0] - META_ROWS, piece_refs[0].shape[1]
    half_width = tile_width // HALVES
    row = lax.axis_index("row")
    half = lax.rem(row, HALVES)
    core = lax.rem(lax.axis_index("col"), CORES)
    sign = 1 - 2 * core
    for offset in offsets:
        if offset:
            spots = [pl.multiple_of(part * half_width, half_width) for part in (half, 1 - half)]
            targets = [(out_refs.pop(0), pl.ds(spot, half_width)) for spot in spots]
        else:
            targets = [(out_refs.pop(0), pl.ds(0, tile_width))]
        for out_ref, _ in targets:
            out_ref[...] = jnp.zeros_like(out_ref)
        for group, shift in enumerate((0, sign)):
            step = lax.rem(CORES * offset - shift + col_peers, col_peers)
            holder = table_ref[slots + 1 + jnp.minimum(step, STEPS - 1)]
            here = (step < STEPS) & (lax.rem(holder, HALVES) == half)
            back = lax.rem(row // HALVES - holder // HALVES + peers, peers)
            for number, piece_ref in enumerate(piece_refs):

                @pl.when(here & (back == number))
                def _():
                    for out_ref, columns in targets:
                        line = lax.broadcasted_iota(jnp.int32, (META_ROWS, out_ref.shape[1]), 0)
                        out_ref[pl.ds(group * share, share), :] = piece_ref[pl.ds(0, share), columns]
                        rows = pl.ds(CORES * share, META_ROWS)
                        info = piece_ref[pl.ds(share, META_ROWS), columns]
                        out_ref[rows, :] = jnp.where(line == group, info, out_ref[rows, :])


def fill_kernel(slots, tile_width, *refs):
    piece_refs, dense_ref = refs[:-1], refs[-1]
    peers = len(piece_refs)
    share = (piece_refs[0].shape[0] - META_ROWS) // CORES
    width = dense_ref.shape[0] // CORES
    place = lax.axis_index("row") // HALVES
    table = piece_refs[0][pl.ds(CORES * share, META_ROWS), :].astype(jnp.float32)
    line = lax.broadcasted_iota(jnp.int32, table.shape, 0)
    lane = lax.broadcasted_iota(jnp.int32, table.shape, 1)

    def entry(group, spot):
        return jnp.max(jnp.where((line == group) & (lane == spot), table, 0.0)).astype(jnp.int32)

    dense_ref[...] = jnp.zeros_like(dense_ref)
    for group in range(CORES):
        count = entry(group, slots)
        starts = [group * width + entry(group, slot) * tile_width for slot in range(slots)]
        for shift, piece_ref in enumerate(piece_refs):
            first = lax.rem(place - shift + peers, peers) * share
            slot = first // tile_width
            start = starts[0]
            for other in range(1, slots):
                start = jnp.where(slot == other, starts[other], start)

            @pl.when(slot < count)
            def _():
                spot = pl.multiple_of(start + lax.rem(first, tile_width), META_ROWS)
                dense_ref[pl.ds(spot, share), :] = piece_ref[pl.ds(group * share, share), :]


def screen_kernel(tile_width, mask_ref, own_ref, other_ref, out_ref):
    block = pl.program_id(0)
    tiles = own_ref.shape[1] // tile_width
    for group, rows_ref in enumerate((own_ref, other_ref)):
        for tile in range(tiles):
            live = mask_ref[group * tiles + tile, block].astype(jnp.float32).astype(rows_ref.dtype)
            columns = pl.ds((group * tiles + tile) * tile_width, tile_width)
            out_ref[:, columns] = rows_ref[:, pl.ds(tile * tile_width, tile_width)] * live


def send_kernel(rows_ref, dense_ref, code_ref, scale_ref):
    step, span = pl.program_id(0), pl.num_programs(0)
    height = rows_ref.shape[0]
    total = jnp.dot(rows_ref[...], dense_ref[...], preferred_element_type=jnp.float32)
    top = jnp.max(jnp.abs(total), axis=0, keepdims=True)
    unit = jnp.where(top > 0, top, 1.0) * (1.0 / CODE_TOP)
    power = jnp.floor(jnp.log2(unit))
    fraction = jnp.ceil(unit * jnp.exp2(-power) * FRACTION)
    unit = fraction * jnp.exp2(power) * (1.0 / FRACTION)
    code = jnp.clip(jnp.round(total * (1.0 / unit)), -CODE_TOP, CODE_TOP)
    code_ref[pl.ds(pl.multiple_of(step * height, height), height), :] = code.astype(jnp.int32).astype(jnp.int16)
    scale_ref[pl.ds(2 * step, 1), :] = power
    scale_ref[pl.ds(2 * step + 1, 1), :] = fraction

    @pl.when(step == span - 1)
    def _():
        rows = scale_ref.shape[0]
        line = lax.broadcasted_iota(jnp.int32, scale_ref.shape, 0)
        kept = jnp.where(line < 2 * span, scale_ref[...], 0.0)
        code_ref[pl.ds(code_ref.shape[0] - rows, rows), :] = kept.astype(jnp.int32).astype(jnp.int16)


def join_kernel(skips, rows_ref, dense_ref, *refs):
    code_refs, out_ref, scale_ref = refs[:-2], refs[-2], refs[-1]
    step = pl.program_id(0)
    height = rows_ref.shape[0]
    tails = [code_ref.shape[0] % height for code_ref in code_refs]
    starts = [sum(tails[:number]) for number in range(len(tails))]
    first_half = lax.rem(lax.axis_index("row"), HALVES) == 0

    @pl.when(step == 0)
    def _():
        for code_ref, start, lines in zip(code_refs, starts, tails):
            scales = code_ref[pl.ds(code_ref.shape[0] - lines, lines), :].astype(jnp.int32).astype(jnp.float32)
            scale_ref[pl.ds(start, lines), :] = scales

    def decoded(number):
        block = skips[number] + step
        power = scale_ref[pl.ds(starts[number] + 2 * block, 1), :]
        fraction = scale_ref[pl.ds(starts[number] + 2 * block + 1, 1), :]
        code = code_refs[number][pl.ds(pl.multiple_of(block * height, height), height), :]
        return code.astype(jnp.int32).astype(jnp.float32) * (fraction * jnp.exp2(power) * (1.0 / FRACTION))

    total = jnp.dot(rows_ref[...], dense_ref[...], preferred_element_type=jnp.float32)
    for number in range(0, len(code_refs), HALVES):
        near, far = decoded(number), decoded(number + 1)
        left = jnp.where(first_half, near, far)
        right = jnp.where(first_half, far, near)
        total = total + jnp.concatenate([left, right], axis=1)
    out_ref[...] = total.astype(out_ref.dtype)


def after(value, *earlier):
    return lax.optimization_barrier((value, *earlier))[0]


def shards(amplitudes, pair_mask, integrals, tile_list, tile_count, owner):
    row_count, full_width = amplitudes.shape
    slots, tile_width = integrals.shape[2], integrals.shape[-1]
    half_width = tile_width // HALVES
    block_count = pair_mask.shape[0]
    block_rows = row_count // block_count
    row_peers, col_peers = lax.axis_size("row"), lax.axis_size("col")
    peers = row_peers // HALVES
    share = slots * tile_width // peers
    offsets = pair_offsets(col_peers)
    remote = [offset for offset in offsets if offset]
    chunks = row_chunks(block_count)

    def along(value, shift):
        return lax.ppermute(value, "row", [(r, (r + HALVES * shift) % row_peers) for r in range(row_peers)])

    def across(value, flip, down):
        pairs = []
        for r in range(row_peers):
            for c in range(col_peers):
                pairs.append((r * col_peers + c, (r ^ flip) * col_peers + (c - CORES * down) % col_peers))
        return lax.ppermute(value, ("row", "col"), pairs)

    swap = [(c, c ^ 1) for c in range(col_peers)]
    other = lax.ppermute(amplitudes, "col", swap)
    other_mask = lax.ppermute(pair_mask.T, "col", swap)
    masks = jnp.concatenate([pair_mask.T, other_mask])
    stored = pltpu.with_memory_space_constraint(amplitudes, pltpu.HBM)
    panels = pltpu.with_memory_space_constraint(integrals, pltpu.HBM)
    table = jnp.concatenate([tile_list[0, 0], tile_count[0], owner[:, 0]])

    pieces = pl.pallas_call(
        pack_kernel,
        in_specs=[SMEM, VMEM],
        out_specs=[VMEM] * peers,
        out_shape=[jax.ShapeDtypeStruct((share + META_ROWS, tile_width), integrals.dtype)] * peers,
        compiler_params=PARAMS,
        name="pack",
    )(table, panels)
    pieces = [piece if shift == 0 else along(piece, shift) for shift, piece in enumerate(pieces)]

    height = CORES * share + META_ROWS
    widths = []
    for offset in offsets:
        widths += [half_width] * HALVES if offset else [tile_width]
    chosen = list(
        pl.pallas_call(
            partial(choose_kernel, col_peers, offsets, slots, peers),
            in_specs=[SMEM] + [VMEM] * peers,
            out_specs=[VMEM] * len(widths),
            out_shape=[jax.ShapeDtypeStruct((height, width), integrals.dtype) for width in widths],
            compiler_params=PARAMS,
            name="choose",
        )(after(table, masks), *pieces)
    )

    def fill(held):
        return pl.pallas_call(
            partial(fill_kernel, slots, tile_width),
            in_specs=[VMEM] * peers,
            out_specs=VMEM,
            out_shape=jax.ShapeDtypeStruct((CORES * full_width, held[0].shape[1]), integrals.dtype),
            compiler_params=PARAMS,
            name="fill",
        )(*held)

    row_block = pl.BlockSpec((block_rows, full_width), lambda i: (i, 0))
    wide_block = pl.BlockSpec((block_rows, CORES * full_width), lambda i: (i, 0))
    def screen(latest):
        return pl.pallas_call(
            partial(screen_kernel, tile_width),
            grid=(block_count,),
            in_specs=[SMEM, row_block, row_block],
            out_specs=wide_block,
            out_shape=jax.ShapeDtypeStruct((row_count, CORES * full_width), amplitudes.dtype),
            compiler_params=PARAMS,
            cost_estimate=pl.CostEstimate(
                flops=CORES * row_count * full_width,
                bytes_accessed=4 * CORES * row_count * full_width,
                transcendentals=0,
            ),
            name="screen",
        )(after(masks, latest), stored, other)

    own = chosen.pop(0)
    own = own + across(own, 1, 0)
    near_weights, far_weights, screened = {}, {}, None
    for offset in remote:
        near, far = chosen.pop(0), chosen.pop(0)
        data = across(near, 0, offset) + across(far, 1, offset)
        held = [data] + [along(data, shift) for shift in range(1, peers)]
        if screened is None:
            screened = screen(held[-1])
        near_weights[offset] = fill([after(held[0], screened)] + held[1:])
        far_weights[offset] = across(near_weights[offset], 1, 0)

    def cost(span, width):
        return pl.CostEstimate(
            flops=2 * span * block_rows * CORES * full_width * width,
            bytes_accessed=span * block_rows * (CORES * full_width + width) * 2,
            transcendentals=0,
        )

    def code_shape(span):
        return (span * block_rows + -(-2 * span // META_ROWS) * META_ROWS, half_width)

    def scratch_rows(span):
        return code_shape(span)[0] - span * block_rows

    near_chunks = chunks[:-2] + [(chunks[-2][0], chunks[-2][1] + chunks[-1][1])] if len(chunks) > 1 else chunks
    rounds = [(half, first, span) for half, parts in enumerate((near_chunks, chunks)) for first, span in parts]
    arrived, sent = {}, []
    order = []
    for number, (half, first, span) in enumerate(rounds):
        earlier = sent[-1:] + [part for key in order[:-1] for part in arrived[key]]
        if number == 0:
            earlier.append(own)
        if number == len(near_chunks) - 1:
            earlier += list(far_weights.values())
        if number == len(rounds) - 2:
            earlier.append(own_weights)
        arrived[half, first] = []
        order.append((half, first))
        for offset in remote:
            weights = (near_weights, far_weights)[half][offset]
            code = pl.pallas_call(
                send_kernel,
                grid=(span,),
                in_specs=[
                    pl.BlockSpec((block_rows, CORES * full_width), lambda i, first=first: (first + i, 0)),
                    pl.BlockSpec((CORES * full_width, half_width), lambda i: (0, 0)),
                ],
                out_specs=pl.BlockSpec(code_shape(span), lambda i: (0, 0)),
                out_shape=jax.ShapeDtypeStruct(code_shape(span), jnp.int16),
                scratch_shapes=[pltpu.VMEM((scratch_rows(span), half_width), jnp.float32)],
                compiler_params=PARAMS,
                cost_estimate=cost(span, half_width),
                name="send_part",
            )(screened, after(weights, *earlier))
            arrived[half, first].append(across(code, 0, -offset))
            sent.append(code)
        if number == 0:
            own = after(own, *arrived[half, first])
            own_weights = fill([own] + [along(own, shift) for shift in range(1, peers)])

    out = None
    for first, span in chunks:
        near_first = max(start for start, _ in near_chunks if start <= first)
        received = [part for pair in zip(arrived[0, near_first], arrived[1, first]) for part in pair]
        skips = [first - near_first, 0] * len(remote)
        operands = [screened, own_weights, *received]
        specs = [
            pl.BlockSpec((block_rows, CORES * full_width), lambda i, first=first: (first + i, 0)),
            pl.BlockSpec((CORES * full_width, tile_width), lambda i: (0, 0)),
        ] + [pl.BlockSpec(part.shape, lambda i: (0, 0)) for part in received]
        body, aliases = partial(join_kernel, skips), {}
        if out is not None:
            body = partial(skip_operand, len(operands), body)
            aliases = {len(operands): 0}
            operands.append(out)
            specs.append(pl.BlockSpec(memory_space=pl.ANY))
        out = pl.pallas_call(
            body,
            grid=(span,),
            in_specs=specs,
            out_specs=pl.BlockSpec((block_rows, tile_width), lambda i, first=first: (first + i, 0)),
            out_shape=jax.ShapeDtypeStruct((row_count, tile_width), jnp.bfloat16),
            scratch_shapes=[
                pltpu.VMEM((sum(part.shape[0] % block_rows for part in received), half_width), jnp.float32)
            ],
            input_output_aliases=aliases,
            compiler_params=PARAMS,
            cost_estimate=cost(span, tile_width),
            name="join_part",
        )(*operands)
    return out


def skip_operand(position, body, *refs):
    body(*refs[:position], *refs[position + 1 :])


def solution(mesh):
    return jax.shard_map(
        shards,
        mesh=mesh,
        in_specs=(
            P("row", "col"),
            P("row", "col"),
            P("row", "col", None, None, None),
            P("row", "col", None),
            P("row", "col"),
            P(None, "col"),
        ),
        out_specs=P("row", "col"),
        check_vma=False,
    )
```

time: 90 us -> 86.2 us (0.958)
  waiting for transfers between devices: 33.8 us -> 27.7 us
  starting transfers between devices: 23.3 us -> 28.8 us
  Pallas kernels: 29.9 us -> 27.2 us
    ppermute x9, waiting for transfers between devices: 21.8 us -> 4.63 us  [along(): lax.ppermute(value, 'row', [(r, (r + HALVES * shift) % row_peers) for r i...]
    ppermute x8 -> x11, waiting for transfers between devices: 12 us -> 23.1 us  [across(): return lax.ppermute(value, ('row', 'col'), pairs)]
    pallas_call x5 -> x4, Pallas kernels: 15.3 us -> 8 us  [shards(): pl.pallas_call(body, grid=(span,), in_specs=specs, out_specs=pl.BlockSpec...]
    pallas_call x8 -> x11, Pallas kernels: 13.6 us -> 18.1 us  [the longest x7 10 us: shards(): pl.pallas_call(send_kernel, grid=(span,), in_specs=[pl.BlockSpec((block_r...]
    ppermute x8 -> x11, starting transfers between devices: 9.3 us -> 13.1 us  [across(): return lax.ppermute(value, ('row', 'col'), pairs)]
    ppermute x9, starting transfers between devices: 13.5 us -> 15.1 us  [along(): lax.ppermute(value, 'row', [(r, (r + HALVES * shift) % row_peers) for r i...]
  transfers between devices with their start and end apart: 19 -> 22, of which waited for: 10 -> 10; matrix products, arithmetic and copies ran while one was open for 2% -> 2% of each run, Pallas kernels for 30% -> 30%
where the time goes in v6:
time: 86.2 us; the launch traced here: 85.9 us
  starting transfers between devices  28.8 us (33%)
  waiting for transfers between devices  27.7 us (32%)
  Pallas kernels  27.2 us (32%)
  other arithmetic  1.5 us (2%)
    ppermute x11, waiting for transfers between devices, across(): return lax.ppermute(value, ('row', 'col'), pairs)  23.1 us
    ppermute x9, starting transfers between devices, along(): lax.ppermute(value, 'row', [(r, (r + HALVES * shift) % row_peers) for r i...  15.1 us
    ppermute x11, starting transfers between devices, across(): return lax.ppermute(value, ('row', 'col'), pairs)  13.1 us
    pallas_call x7, Pallas kernels, shards(): pl.pallas_call(send_kernel, grid=(span,), in_specs=[pl.BlockSpec((block_r...  10 us
    pallas_call x4, Pallas kernels, shards(): pl.pallas_call(body, grid=(span,), in_specs=specs, out_specs=pl.BlockSpec...  8 us
    pallas_call x1, Pallas kernels, screen(): pl.pallas_call(partial(screen_kernel, tile_width), grid=(block_count,), i...  6.73 us
    ppermute x9, waiting for transfers between devices, along(): lax.ppermute(value, 'row', [(r, (r + HALVES * shift) % row_peers) for r i...  4.63 us
  transfers between devices with their start and end apart: 22, of which 10 were waited for; matrix products, arithmetic and copies ran while one was open for 2% of the time, Pallas kernels for 30%

profile of v6, /device:TPU:0, one launch (start us, length us, event | category | flops | bytes accessed | tf_op | source)
XLA Modules:
  0.0 85.9 jit_solution(8345184616610864726)
XLA Ops:
  0.0 0.5 collective-permute-start.7
  1.2 0.7 pad_add_fusion.1.table_ref
  1.9 1.0 %pack.1 = (bf16[144,256]{1,0:T(8,128)(2,1)S(1)}, bf16[144,256]{1,0:T(8,128)(2,1)S(1)}, bf16[144,256]{1,0:T(8,128)(2,1)S(1)}, bf16[144,256]{1,0:T(8,128)(2,1)S(1)}) custom-call(s32[7]{0:T(128)S(1)} %pad_add_fusion.1.table_ref, bf16[1,1,2,256,256]{4,3,2,1,0:T(8,128)(2,1)} %panel_ref.1), custom_call_target="tpu_custom_call" | custom-call | tf_op jit(solution)/shard_map/pack/pallas_call | solution.py:214
  2.9 3.1 %collective-permute-start.1 = (bf16[144,256]{1,0:T(8,128)(2,1)S(1)}, bf16[144,256]{1,0:T(8,128)(2,1)S(1)}, u32[]{:S(2)}, u32[]{:S(2)}) collective-permute-start(bf16[144,256]{1,0:T(8,128)(2,1)S(1)} %get-tuple-element.25), channel_id=1, source_target_pairs={{0,8},{4,12},{8,16},{12,20},{16,24},{20,28},{24,0},{28,4},{1,9},{5... | collective-permute-start | bytes 221192 | tf_op jit(solution)/shard_map/ppermute | solution.py:197
  6.0 2.6 %collective-permute-start.2 = (bf16[144,256]{1,0:T(8,128)(2,1)S(1)}, bf16[144,256]{1,0:T(8,128)(2,1)S(1)}, u32[]{:S(2)}, u32[]{:S(2)}) collective-permute-start(bf16[144,256]{1,0:T(8,128)(2,1)S(1)} %get-tuple-element.26), channel_id=1, source_target_pairs={{0,16},{4,20},{8,24},{12,28},{16,0},{20,4},{24,8},{28,12},{1,17},{... | collective-permute-start | bytes 221192 | tf_op jit(solution)/shard_map/ppermute | solution.py:197
  8.6 1.3 %collective-permute-start.3 = (bf16[144,256]{1,0:T(8,128)(2,1)S(1)}, bf16[144,256]{1,0:T(8,128)(2,1)S(1)}, u32[]{:S(2)}, u32[]{:S(2)}) collective-permute-start(bf16[144,256]{1,0:T(8,128)(2,1)S(1)} %get-tuple-element.27), channel_id=1, source_target_pairs={{0,24},{4,28},{8,0},{12,4},{16,8},{20,12},{24,16},{28,20},{1,25},{... | collective-permute-start | bytes 221192 | tf_op jit(solution)/shard_map/ppermute | solution.py:197
  10.0 0.7 pad_add_fusion.mask_ref
  10.6 0.2 collective-permute-done.1.refs_1_
  10.9 2.9 %collective-permute-done.2.refs_2_ = bf16[144,256]{1,0:T(8,128)(2,1)S(1)} collective-permute-done((bf16[144,256]{1,0:T(8,128)(2,1)S(1)}, bf16[144,256]{1,0:T(8,128)(2,1)S(1)}, u32[]{:S(2)}, u32[]{:S(2)}) %collective-permute-start.2) | collective-permute-done | bytes 73760 | tf_op jit(solution)/shard_map/ppermute | solution.py:197
  13.7 0.2 collective-permute-done.3.refs_3_
  14.0 0.7 choose.1
  14.7 1.5 %collective-permute-start.4 = (bf16[272,128]{1,0:T(8,128)(2,1)S(1)}, bf16[272,128]{1,0:T(8,128)(2,1)S(1)}, u32[]{:S(2)}, u32[]{:S(2)}) collective-permute-start(bf16[272,128]{1,0:T(8,128)(2,1)S(1)} %get-tuple-element.28), channel_id=1, source_target_pairs={{0,2},{1,3},{2,0},{3,1},{4,6},{5,7},{6,4},{7,5},{8,10},{9,11},{10,... | collective-permute-start | bytes 208904 | tf_op jit(solution)/shard_map/ppermute | solution.py:204
  16.2 1.5 %collective-permute-start.5 = (bf16[272,128]{1,0:T(8,128)(2,1)S(1)}, bf16[272,128]{1,0:T(8,128)(2,1)S(1)}, u32[]{:S(2)}, u32[]{:S(2)}) collective-permute-start(bf16[272,128]{1,0:T(8,128)(2,1)S(1)} %get-tuple-element.29), channel_id=1, source_target_pairs={{0,6},{1,7},{2,4},{3,5},{4,2},{5,3},{6,0},{7,1},{8,14},{9,15},{10,... | collective-permute-start | bytes 208904 | tf_op jit(solution)/shard_map/ppermute | solution.py:204
  17.7 1.3 %collective-permute-done.4 = bf16[272,128]{1,0:T(8,128)(2,1)S(1)} collective-permute-done((bf16[272,128]{1,0:T(8,128)(2,1)S(1)}, bf16[272,128]{1,0:T(8,128)(2,1)S(1)}, u32[]{:S(2)}, u32[]{:S(2)}) %collective-permute-start.4) | collective-permute-done | bytes 69664 | tf_op jit(solution)/shard_map/ppermute | solution.py:204
  19.1 2.4 %collective-permute-done.5 = bf16[272,128]{1,0:T(8,128)(2,1)S(1)} collective-permute-done((bf16[272,128]{1,0:T(8,128)(2,1)S(1)}, bf16[272,128]{1,0:T(8,128)(2,1)S(1)}, u32[]{:S(2)}, u32[]{:S(2)}) %collective-permute-start.5) | collective-permute-done | bytes 69664 | tf_op jit(solution)/shard_map/ppermute | solution.py:204
  21.5 3.1 %collective-permute-start.6 = (bf16[272,128]{1,0:T(8,128)(2,1)S(1)}, bf16[272,128]{1,0:T(8,128)(2,1)S(1)}, u32[]{:S(2)}, u32[]{:S(2)}) collective-permute-start(bf16[272,128]{1,0:T(8,128)(2,1)S(1)} %add.6.refs_0_), channel_id=1, source_target_pairs={{0,24},{4,28},{8,0},{12,4},{16,8},{20,12},{24,16},{28,20},{1,25},{... | collective-permute-start | bytes 208904 | tf_op jit(solution)/shard_map/ppermute | solution.py:197
  24.6 0.3 collective-permute-start.10
  24.9 0.4 collective-permute-start.9
  25.2 1.3 %collective-permute-done.6.refs_3_ = bf16[272,128]{1,0:T(8,128)(2,1)S(1)} collective-permute-done((bf16[272,128]{1,0:T(8,128)(2,1)S(1)}, bf16[272,128]{1,0:T(8,128)(2,1)S(1)}, u32[]{:S(2)}, u32[]{:S(2)}) %collective-permute-start.6) | collective-permute-done | bytes 69664 | tf_op jit(solution)/shard_map/ppermute | solution.py:197
  26.5 6.7 %screen.1.rows_ref.refs_0_ = bf16[3072,1536]{1,0:T(8,128)(2,1)S(1)} custom-call(s32[6,12]{1,0:T(8,128)S(1)} %pad_add_fusion.mask_ref, bf16[3072,768]{1,0:T(8,128)(2,1)} %own_ref.1, bf16[3072,768]{1,0:T(8,128)(2,1)S(1)} %collective-permute-done.7.other_ref), custom_call_target="tpu_custom_call" | custom-call | flops 4718592 | bytes 18874368 | tf_op jit(solution)/shard_map/screen/pallas_call | solution.py:252
  33.3 0.3 fill.2.dense_ref
  33.6 1.6 %collective-permute-start.15 = (bf16[1536,128]{1,0:T(8,128)(2,1)S(1)}, bf16[1536,128]{1,0:T(8,128)(2,1)S(1)}, u32[]{:S(2)}, u32[]{:S(2)}) collective-permute-start(bf16[1536,128]{1,0:T(8,128)(2,1)S(1)} %fill.2.dense_ref), channel_id=1, source_target_pairs={{0,4},{1,5},{2,6},{3,7},{4,0},{5,1},{6,2},{7,3},{8,12},{9,13},{10,... | collective-permute-start | bytes 1179656 | tf_op jit(solution)/shard_map/ppermute | solution.py:204
  35.2 0.5 collective-permute-start.8
  35.7 9.6 %collective-permute-done.8 = bf16[272,256]{1,0:T(8,128)(2,1)S(1)} collective-permute-done((bf16[272,256]{1,0:T(8,128)(2,1)S(1)}, bf16[272,256]{1,0:T(8,128)(2,1)S(1)}, u32[]{:S(2)}, u32[]{:S(2)}) %collective-permute-start.8) | collective-permute-done | bytes 139296 | tf_op jit(solution)/shard_map/ppermute | solution.py:204
  45.4 0.9 send_part.7
  46.3 0.8 collective-permute-start.11
  47.1 2.1 %send_part.8 = s16[1296,128]{1,0:T(8,128)(2,1)S(1)} custom-call(bf16[3072,1536]{1,0:T(8,128)(2,1)S(1)} %screen.1.rows_ref.refs_0_, bf16[1536,128]{1,0:T(8,128)(2,1)S(1)} %fill.2.dense_ref), custom_call_target="tpu_custom_call" | custom-call | flops 503316480 | bytes 4259840 | tf_op jit(solution)/shard_map/send_part/pallas_call | solution.py:308
  49.2 1.4 %collective-permute-start.17 = (s16[1296,128]{1,0:T(8,128)(2,1)S(1)}, s16[1296,128]{1,0:T(8,128)(2,1)S(1)}, u32[]{:S(2)}, u32[]{:S(2)}) collective-permute-start(s16[1296,128]{1,0:T(8,128)(2,1)S(1)} %send_part.8), channel_id=1, source_target_pairs={{0,2},{1,3},{2,0},{3,1},{4,6},{5,7},{6,4},{7,5},{8,10},{9,11},{10,... | collective-permute-start | bytes 995336 | tf_op jit(solution)/shard_map/ppermute | solution.py:204
  50.5 2.3 %collective-permute-done.11.refs_0_ = s16[528,128]{1,0:T(8,128)(2,1)S(1)} collective-permute-done((s16[528,128]{1,0:T(8,128)(2,1)S(1)}, s16[528,128]{1,0:T(8,128)(2,1)S(1)}, u32[]{:S(2)}, u32[]{:S(2)}) %collective-permute-start.11) | collective-permute-done | bytes 135200 | tf_op jit(solution)/shard_map/ppermute | solution.py:204
  52.9 2.1 %send_part.9 = s16[1296,128]{1,0:T(8,128)(2,1)S(1)} custom-call(bf16[3072,1536]{1,0:T(8,128)(2,1)S(1)} %screen.1.rows_ref.refs_0_, bf16[1536,128]{1,0:T(8,128)(2,1)S(1)} %fill.2.dense_ref), custom_call_target="tpu_custom_call" | custom-call | flops 503316480 | bytes 4259840 | tf_op jit(solution)/shard_map/send_part/pallas_call | solution.py:308
  54.9 0.7 collective-permute-start.16
  55.7 3.8 %collective-permute-start.14 = (bf16[272,256]{1,0:T(8,128)(2,1)S(1)}, bf16[272,256]{1,0:T(8,128)(2,1)S(1)}, u32[]{:S(2)}, u32[]{:S(2)}) collective-permute-start(bf16[272,256]{1,0:T(8,128)(2,1)S(1)} %add.7.refs_0_), channel_id=1, source_target_pairs={{0,24},{4,28},{8,0},{12,4},{16,8},{20,12},{24,16},{28,20},{1,25},{... | collective-permute-start | bytes 417800 | tf_op jit(solution)/shard_map/ppermute | solution.py:197
  59.5 0.6 collective-permute-start.12
  60.1 0.8 send_part.10
  60.9 1.5 %collective-permute-start.18 = (s16[528,128]{1,0:T(8,128)(2,1)S(1)}, s16[528,128]{1,0:T(8,128)(2,1)S(1)}, u32[]{:S(2)}, u32[]{:S(2)}) collective-permute-start(s16[528,128]{1,0:T(8,128)(2,1)S(1)} %send_part.10), channel_id=1, source_target_pairs={{0,2},{1,3},{2,0},{3,1},{4,6},{5,7},{6,4},{7,5},{8,10},{9,11},{10,... | collective-permute-start | bytes 405512 | tf_op jit(solution)/shard_map/ppermute | solution.py:204
  62.4 2.9 %collective-permute-done.16.refs_2_ = s16[1296,128]{1,0:T(8,128)(2,1)S(1)} collective-permute-done((s16[1296,128]{1,0:T(8,128)(2,1)S(1)}, s16[1296,128]{1,0:T(8,128)(2,1)S(1)}, u32[]{:S(2)}, u32[]{:S(2)}) %collective-permute-start.16) | collective-permute-done | bytes 331808 | tf_op jit(solution)/shard_map/ppermute | solution.py:204
  65.3 2.1 %send_part.11 = s16[1296,128]{1,0:T(8,128)(2,1)S(1)} custom-call(bf16[3072,1536]{1,0:T(8,128)(2,1)S(1)} %screen.1.rows_ref.refs_0_, bf16[1536,128]{1,0:T(8,128)(2,1)S(1)} %collective-permute-done.15.dense_ref), custom_call_target="tpu_custom_call" | custom-call | flops 503316480 | bytes 4259840 | tf_op jit(solution)/shard_map/send_part/pallas_call | solution.py:308
  67.4 1.4 %collective-permute-start.19 = (s16[1296,128]{1,0:T(8,128)(2,1)S(1)}, s16[1296,128]{1,0:T(8,128)(2,1)S(1)}, u32[]{:S(2)}, u32[]{:S(2)}) collective-permute-start(s16[1296,128]{1,0:T(8,128)(2,1)S(1)} %send_part.11), channel_id=1, source_target_pairs={{0,2},{1,3},{2,0},{3,1},{4,6},{5,7},{6,4},{7,5},{8,10},{9,11},{10,... | collective-permute-start | bytes 995336 | tf_op jit(solution)/shard_map/ppermute | solution.py:204
  68.9 0.3 fill.3.dense_ref.refs_1_
  69.2 1.7 %send_part.12 = s16[1040,128]{1,0:T(8,128)(2,1)S(1)} custom-call(bf16[3072,1536]{1,0:T(8,128)(2,1)S(1)} %screen.1.rows_ref.refs_0_, bf16[1536,128]{1,0:T(8,128)(2,1)S(1)} %collective-permute-done.15.dense_ref), custom_call_target="tpu_custom_call" | custom-call | flops 402653184 | bytes 3407872 | tf_op jit(solution)/shard_map/send_part/pallas_call | solution.py:308
  70.9 0.7 collective-permute-start.21
  71.6 1.4 %join_part.4.refs_4_ = bf16[3072,256]{1,0:T(8,128)(2,1)} custom-call(bf16[3072,1536]{1,0:T(8,128)(2,1)S(1)} %screen.1.rows_ref.refs_0_, bf16[1536,256]{1,0:T(8,128)(2,1)S(1)} %fill.3.dense_ref.refs_1_, s16[528,128]{1,0:T(8,128)(2,1)S(1)} %collective-permute-done.11.refs_0_, s16[528,128]{1,0:T(8,128)(2,1)S(1)} %collective-permute-done.18.refs_1_), custom_call_target="tpu_custom_call" | custom-call | flops 402653184 | bytes 1835008 | tf_op jit(solution)/shard_map/join_part/pallas_call | solution.py:344
  73.1 4.4 %collective-permute-done.19.refs_3_ = s16[1296,128]{1,0:T(8,128)(2,1)S(1)} collective-permute-done((s16[1296,128]{1,0:T(8,128)(2,1)S(1)}, s16[1296,128]{1,0:T(8,128)(2,1)S(1)}, u32[]{:S(2)}, u32[]{:S(2)}) %collective-permute-start.19) | collective-permute-done | bytes 331808 | tf_op jit(solution)/shard_map/ppermute | solution.py:204
  77.5 0.4 send_part.13
  77.9 1.4 %collective-permute-start.20 = (s16[272,128]{1,0:T(8,128)(2,1)S(1)}, s16[272,128]{1,0:T(8,128)(2,1)S(1)}, u32[]{:S(2)}, u32[]{:S(2)}) collective-permute-start(s16[272,128]{1,0:T(8,128)(2,1)S(1)} %send_part.13), channel_id=1, source_target_pairs={{0,2},{1,3},{2,0},{3,1},{4,6},{5,7},{6,4},{7,5},{8,10},{9,11},{10,... | collective-permute-start | bytes 208904 | tf_op jit(solution)/shard_map/ppermute | solution.py:204
  79.3 3.1 %join_part.5.refs_4_ = bf16[3072,256]{1,0:T(8,128)(2,1)} custom-call(bf16[3072,1536]{1,0:T(8,128)(2,1)S(1)} %screen.1.rows_ref.refs_0_, bf16[1536,256]{1,0:T(8,128)(2,1)S(1)} %fill.3.dense_ref.refs_1_, s16[1296,128]{1,0:T(8,128)(2,1)S(1)} %collective-permute-done.17.refs_2_, ...), custom_call_target="tpu_custom_call", output_to_operand_aliasing={{}: (4, {})} | custom-call | flops 1006632960 | bytes 4587520 | tf_op jit(solution)/shard_map/join_part/pallas_call | solution.py:344
  82.4 2.5 %join_part.6.refs_4_ = bf16[3072,256]{1,0:T(8,128)(2,1)} custom-call(bf16[3072,1536]{1,0:T(8,128)(2,1)S(1)} %screen.1.rows_ref.refs_0_, bf16[1536,256]{1,0:T(8,128)(2,1)S(1)} %fill.3.dense_ref.refs_1_, s16[1296,128]{1,0:T(8,128)(2,1)S(1)} %collective-permute-done.16.refs_2_, ...), custom_call_target="tpu_custom_call", output_to_operand_aliasing={{}: (4, {})} | custom-call | flops 805306368 | bytes 3670016 | tf_op jit(solution)/shard_map/join_part/pallas_call | solution.py:344
  84.9 1.0 %join_part.7 = bf16[3072,256]{1,0:T(8,128)(2,1)} custom-call(bf16[3072,1536]{1,0:T(8,128)(2,1)S(1)} %screen.1.rows_ref.refs_0_, bf16[1536,256]{1,0:T(8,128)(2,1)S(1)} %fill.3.dense_ref.refs_1_, s16[1296,128]{1,0:T(8,128)(2,1)S(1)} %collective-permute-done.16.refs_2_, ...), custom_call_target="tpu_custom_call", output_to_operand_aliasing={{}: (4, {})} | custom-call | flops 201326592 | bytes 917504 | tf_op jit(solution)/shard_map/join_part/pallas_call | solution.py:344
  (16 shorter events, 0.2 us)
Async XLA Ops:
  0.0 26.5 %collective-permute-start.7 = (bf16[3072,768]{1,0:T(8,128)(2,1)}, bf16[3072,768]{1,0:T(8,128)(2,1)S(1)}, u32[]{:S(2)}, u32[]{:S(2)}) collective-permute-start(bf16[3072,768]{1,0:T(8,128)(2,1)} %own_ref.1), channel_id=1, source_target_pairs={{0,1},{1,0},{2,3},{3,2},{4,5},{5,4},{6,7},{7,6},{8,9},{9,8},{10,11... | collective-permute-start | bytes 14155784 | tf_op jit(solution)/shard_map/ppermute | solution.py:207
  0.5 9.5 %collective-permute-start = (s32[3,12]{1,0:T(4,128)}, s32[3,12]{1,0:T(4,128)S(1)}, u32[]{:S(2)}, u32[]{:S(2)}) collective-permute-start(s32[3,12]{1,0:T(4,128)} %bitcast.5), channel_id=1, source_target_pairs={{0,1},{1,0},{2,3},{3,2},{4,5},{5,4},{6,7},{7,6},{8,9},{9,8},{10,11... | collective-permute-start | bytes 440 | tf_op jit(solution)/shard_map/ppermute | solution.py:208
  2.9 7.9 %collective-permute-start.1 = (bf16[144,256]{1,0:T(8,128)(2,1)S(1)}, bf16[144,256]{1,0:T(8,128)(2,1)S(1)}, u32[]{:S(2)}, u32[]{:S(2)}) collective-permute-start(bf16[144,256]{1,0:T(8,128)(2,1)S(1)} %get-tuple-element.25), channel_id=1, source_target_pairs={{0,8},{4,12},{8,16},{12,20},{16,24},{20,28},{24,0},{28,4},{1,9},{5... | collective-permute-start | bytes 221192 | tf_op jit(solution)/shard_map/ppermute | solution.py:197
  6.0 7.7 %collective-permute-start.2 = (bf16[144,256]{1,0:T(8,128)(2,1)S(1)}, bf16[144,256]{1,0:T(8,128)(2,1)S(1)}, u32[]{:S(2)}, u32[]{:S(2)}) collective-permute-start(bf16[144,256]{1,0:T(8,128)(2,1)S(1)} %get-tuple-element.26), channel_id=1, source_target_pairs={{0,16},{4,20},{8,24},{12,28},{16,0},{20,4},{24,8},{28,12},{1,17},{... | collective-permute-start | bytes 221192 | tf_op jit(solution)/shard_map/ppermute | solution.py:197
  8.6 5.4 %collective-permute-start.3 = (bf16[144,256]{1,0:T(8,128)(2,1)S(1)}, bf16[144,256]{1,0:T(8,128)(2,1)S(1)}, u32[]{:S(2)}, u32[]{:S(2)}) collective-permute-start(bf16[144,256]{1,0:T(8,128)(2,1)S(1)} %get-tuple-element.27), channel_id=1, source_target_pairs={{0,24},{4,28},{8,0},{12,4},{16,8},{20,12},{24,16},{28,20},{1,25},{... | collective-permute-start | bytes 221192 | tf_op jit(solution)/shard_map/ppermute | solution.py:197
  14.7 4.4 %collective-permute-start.4 = (bf16[272,128]{1,0:T(8,128)(2,1)S(1)}, bf16[272,128]{1,0:T(8,128)(2,1)S(1)}, u32[]{:S(2)}, u32[]{:S(2)}) collective-permute-start(bf16[272,128]{1,0:T(8,128)(2,1)S(1)} %get-tuple-element.28), channel_id=1, source_target_pairs={{0,2},{1,3},{2,0},{3,1},{4,6},{5,7},{6,4},{7,5},{8,10},{9,11},{10,... | collective-permute-start | bytes 208904 | tf_op jit(solution)/shard_map/ppermute | solution.py:204
  16.2 5.2 %collective-permute-start.5 = (bf16[272,128]{1,0:T(8,128)(2,1)S(1)}, bf16[272,128]{1,0:T(8,128)(2,1)S(1)}, u32[]{:S(2)}, u32[]{:S(2)}) collective-permute-start(bf16[272,128]{1,0:T(8,128)(2,1)S(1)} %get-tuple-element.29), channel_id=1, source_target_pairs={{0,6},{1,7},{2,4},{3,5},{4,2},{5,3},{6,0},{7,1},{8,14},{9,15},{10,... | collective-permute-start | bytes 208904 | tf_op jit(solution)/shard_map/ppermute | solution.py:204
  21.5 5.1 %collective-permute-start.6 = (bf16[272,128]{1,0:T(8,128)(2,1)S(1)}, bf16[272,128]{1,0:T(8,128)(2,1)S(1)}, u32[]{:S(2)}, u32[]{:S(2)}) collective-permute-start(bf16[272,128]{1,0:T(8,128)(2,1)S(1)} %add.6.refs_0_), channel_id=1, source_target_pairs={{0,24},{4,28},{8,0},{12,4},{16,8},{20,12},{24,16},{28,20},{1,25},{... | collective-permute-start | bytes 208904 | tf_op jit(solution)/shard_map/ppermute | solution.py:197
  24.6 8.7 %collective-permute-start.10 = (bf16[272,128]{1,0:T(8,128)(2,1)S(1)}, bf16[272,128]{1,0:T(8,128)(2,1)S(1)}, u32[]{:S(2)}, u32[]{:S(2)}) collective-permute-start(bf16[272,128]{1,0:T(8,128)(2,1)S(1)} %add.6.refs_0_), channel_id=1, source_target_pairs={{0,16},{4,20},{8,24},{12,28},{16,0},{20,4},{24,8},{28,12},{1,17},{... | collective-permute-start | bytes 208904 | tf_op jit(solution)/shard_map/ppermute | solution.py:197
  24.9 8.4 %collective-permute-start.9 = (bf16[272,128]{1,0:T(8,128)(2,1)S(1)}, bf16[272,128]{1,0:T(8,128)(2,1)S(1)}, u32[]{:S(2)}, u32[]{:S(2)}) collective-permute-start(bf16[272,128]{1,0:T(8,128)(2,1)S(1)} %add.6.refs_0_), channel_id=1, source_target_pairs={{0,8},{4,12},{8,16},{12,20},{16,24},{20,28},{24,0},{28,4},{1,9},{5... | collective-permute-start | bytes 208904 | tf_op jit(solution)/shard_map/ppermute | solution.py:197
  33.6 19.2 %collective-permute-start.15 = (bf16[1536,128]{1,0:T(8,128)(2,1)S(1)}, bf16[1536,128]{1,0:T(8,128)(2,1)S(1)}, u32[]{:S(2)}, u32[]{:S(2)}) collective-permute-start(bf16[1536,128]{1,0:T(8,128)(2,1)S(1)} %fill.2.dense_ref), channel_id=1, source_target_pairs={{0,4},{1,5},{2,6},{3,7},{4,0},{5,1},{6,2},{7,3},{8,12},{9,13},{10,... | collective-permute-start | bytes 1179656 | tf_op jit(solution)/shard_map/ppermute | solution.py:204
  35.2 10.1 %collective-permute-start.8 = (bf16[272,256]{1,0:T(8,128)(2,1)S(1)}, bf16[272,256]{1,0:T(8,128)(2,1)S(1)}, u32[]{:S(2)}, u32[]{:S(2)}) collective-permute-start(bf16[272,256]{1,0:T(8,128)(2,1)S(1)} %get-tuple-element.31), channel_id=1, source_target_pairs={{0,4},{1,5},{2,6},{3,7},{4,0},{5,1},{6,2},{7,3},{8,12},{9,13},{10,... | collective-permute-start | bytes 417800 | tf_op jit(solution)/shard_map/ppermute | solution.py:204
  46.3 6.6 %collective-permute-start.11 = (s16[528,128]{1,0:T(8,128)(2,1)S(1)}, s16[528,128]{1,0:T(8,128)(2,1)S(1)}, u32[]{:S(2)}, u32[]{:S(2)}) collective-permute-start(s16[528,128]{1,0:T(8,128)(2,1)S(1)} %send_part.7), channel_id=1, source_target_pairs={{0,2},{1,3},{2,0},{3,1},{4,6},{5,7},{6,4},{7,5},{8,10},{9,11},{10,... | collective-permute-start | bytes 405512 | tf_op jit(solution)/shard_map/ppermute | solution.py:204
  49.2 10.9 %collective-permute-start.17 = (s16[1296,128]{1,0:T(8,128)(2,1)S(1)}, s16[1296,128]{1,0:T(8,128)(2,1)S(1)}, u32[]{:S(2)}, u32[]{:S(2)}) collective-permute-start(s16[1296,128]{1,0:T(8,128)(2,1)S(1)} %send_part.8), channel_id=1, source_target_pairs={{0,2},{1,3},{2,0},{3,1},{4,6},{5,7},{6,4},{7,5},{8,10},{9,11},{10,... | collective-permute-start | bytes 995336 | tf_op jit(solution)/shard_map/ppermute | solution.py:204
  54.9 10.4 %collective-permute-start.16 = (s16[1296,128]{1,0:T(8,128)(2,1)S(1)}, s16[1296,128]{1,0:T(8,128)(2,1)S(1)}, u32[]{:S(2)}, u32[]{:S(2)}) collective-permute-start(s16[1296,128]{1,0:T(8,128)(2,1)S(1)} %send_part.9), channel_id=1, source_target_pairs={{0,2},{1,3},{2,0},{3,1},{4,6},{5,7},{6,4},{7,5},{8,10},{9,11},{10,... | collective-permute-start | bytes 995336 | tf_op jit(solution)/shard_map/ppermute | solution.py:204
  55.7 13.2 %collective-permute-start.14 = (bf16[272,256]{1,0:T(8,128)(2,1)S(1)}, bf16[272,256]{1,0:T(8,128)(2,1)S(1)}, u32[]{:S(2)}, u32[]{:S(2)}) collective-permute-start(bf16[272,256]{1,0:T(8,128)(2,1)S(1)} %add.7.refs_0_), channel_id=1, source_target_pairs={{0,24},{4,28},{8,0},{12,4},{16,8},{20,12},{24,16},{28,20},{1,25},{... | collective-permute-start | bytes 417800 | tf_op jit(solution)/shard_map/ppermute | solution.py:197
  59.5 9.4 %collective-permute-start.13 = (bf16[272,256]{1,0:T(8,128)(2,1)S(1)}, bf16[272,256]{1,0:T(8,128)(2,1)S(1)}, u32[]{:S(2)}, u32[]{:S(2)}) collective-permute-start(bf16[272,256]{1,0:T(8,128)(2,1)S(1)} %add.7.refs_0_), channel_id=1, source_target_pairs={{0,16},{4,20},{8,24},{12,28},{16,0},{20,4},{24,8},{28,12},{1,17},{... | collective-permute-start | bytes 417800 | tf_op jit(solution)/shard_map/ppermute | solution.py:197
  59.5 9.4 %collective-permute-start.12 = (bf16[272,256]{1,0:T(8,128)(2,1)S(1)}, bf16[272,256]{1,0:T(8,128)(2,1)S(1)}, u32[]{:S(2)}, u32[]{:S(2)}) collective-permute-start(bf16[272,256]{1,0:T(8,128)(2,1)S(1)} %add.7.refs_0_), channel_id=1, source_target_pairs={{0,8},{4,12},{8,16},{12,20},{16,24},{20,28},{24,0},{28,4},{1,9},{5... | collective-permute-start | bytes 417800 | tf_op jit(solution)/shard_map/ppermute | solution.py:197
  60.9 8.3 %collective-permute-start.18 = (s16[528,128]{1,0:T(8,128)(2,1)S(1)}, s16[528,128]{1,0:T(8,128)(2,1)S(1)}, u32[]{:S(2)}, u32[]{:S(2)}) collective-permute-start(s16[528,128]{1,0:T(8,128)(2,1)S(1)} %send_part.10), channel_id=1, source_target_pairs={{0,2},{1,3},{2,0},{3,1},{4,6},{5,7},{6,4},{7,5},{8,10},{9,11},{10,... | collective-permute-start | bytes 405512 | tf_op jit(solution)/shard_map/ppermute | solution.py:204
  67.4 10.1 %collective-permute-start.19 = (s16[1296,128]{1,0:T(8,128)(2,1)S(1)}, s16[1296,128]{1,0:T(8,128)(2,1)S(1)}, u32[]{:S(2)}, u32[]{:S(2)}) collective-permute-start(s16[1296,128]{1,0:T(8,128)(2,1)S(1)} %send_part.11), channel_id=1, source_target_pairs={{0,2},{1,3},{2,0},{3,1},{4,6},{5,7},{6,4},{7,5},{8,10},{9,11},{10,... | collective-permute-start | bytes 995336 | tf_op jit(solution)/shard_map/ppermute | solution.py:204
  70.9 11.5 %collective-permute-start.21 = (s16[1040,128]{1,0:T(8,128)(2,1)S(1)}, s16[1040,128]{1,0:T(8,128)(2,1)S(1)}, u32[]{:S(2)}, u32[]{:S(2)}) collective-permute-start(s16[1040,128]{1,0:T(8,128)(2,1)S(1)} %send_part.12), channel_id=1, source_target_pairs={{0,2},{1,3},{2,0},{3,1},{4,6},{5,7},{6,4},{7,5},{8,10},{9,11},{10,... | collective-permute-start | bytes 798728 | tf_op jit(solution)/shard_map/ppermute | solution.py:204
  77.9 7.0 %collective-permute-start.20 = (s16[272,128]{1,0:T(8,128)(2,1)S(1)}, s16[272,128]{1,0:T(8,128)(2,1)S(1)}, u32[]{:S(2)}, u32[]{:S(2)}) collective-permute-start(s16[272,128]{1,0:T(8,128)(2,1)S(1)} %send_part.13), channel_id=1, source_target_pairs={{0,2},{1,3},{2,0},{3,1},{4,6},{5,7},{6,4},{7,5},{8,10},{9,11},{10,... | collective-permute-start | bytes 208904 | tf_op jit(solution)/shard_map/ppermute | solution.py:204

commit v7 on v6

--- a/solution.py
+++ b/solution.py
@@ -10,10 +10,12 @@
 STEPS = 4
 CORES = 2
 HALVES = 2
-CUTS = (0.0, 0.167, 0.583, 0.917, 1.0)
+NEAR_CUTS = (0.0, 0.167, 0.583, 1.0)
+FAR_CUTS = (0.0, 0.167, 0.583, 0.917, 1.0)
 CODE_TOP = 32767.0
 FRACTION = 8192.0
 META_ROWS = 16
+SCREEN_BLOCKS = 3
 PARAMS = pltpu.CompilerParams(vmem_limit_bytes=16 * 1024 * 1024)
 SMEM = pl.BlockSpec(memory_space=pltpu.SMEM)
 VMEM = pl.BlockSpec(memory_space=pltpu.VMEM)
@@ -28,8 +30,8 @@
     return sorted(offsets)
 
 
-def row_chunks(block_count):
-    marks = sorted({round(block_count * cut) for cut in CUTS})
+def row_chunks(block_count, cuts):
+    marks = sorted({round(block_count * cut) for cut in cuts})
     return [(first, last - first) for first, last in zip(marks, marks[1:])]
 
 
@@ -114,14 +116,16 @@
                 dense_ref[pl.ds(spot, share), :] = piece_ref[pl.ds(group * share, share), :]
 
 
-def screen_kernel(tile_width, mask_ref, own_ref, other_ref, out_ref):
-    block = pl.program_id(0)
-    tiles = own_ref.shape[1] // tile_width
-    for group, rows_ref in enumerate((own_ref, other_ref)):
-        for tile in range(tiles):
-            live = mask_ref[group * tiles + tile, block].astype(jnp.float32).astype(rows_ref.dtype)
-            columns = pl.ds((group * tiles + tile) * tile_width, tile_width)
-            out_ref[:, columns] = rows_ref[:, pl.ds(tile * tile_width, tile_width)] * live
+def screen_kernel(tile_width, block_rows, mask_ref, own_ref, other_ref, out_ref):
+    blocks, tiles = own_ref.shape[0] // block_rows, own_ref.shape[1] // tile_width
+    for number in range(blocks):
+        block = pl.program_id(0) * blocks + number
+        lines = pl.ds(number * block_rows, block_rows)
+        for group, rows_ref in enumerate((own_ref, other_ref)):
+            for tile in range(tiles):
+                live = mask_ref[group * tiles + tile, block].astype(jnp.float32).astype(rows_ref.dtype)
+                columns = pl.ds((group * tiles + tile) * tile_width, tile_width)
+                out_ref[lines, columns] = rows_ref[lines, pl.ds(tile * tile_width, tile_width)] * live
 
 
 def send_kernel(rows_ref, dense_ref, code_ref, scale_ref):
@@ -191,7 +195,8 @@
     share = slots * tile_width // peers
     offsets = pair_offsets(col_peers)
     remote = [offset for offset in offsets if offset]
-    chunks = row_chunks(block_count)
+    near_chunks, far_chunks = row_chunks(block_count, NEAR_CUTS), row_chunks(block_count, FAR_CUTS)
+    chunks = row_chunks(block_count, NEAR_CUTS + FAR_CUTS)
 
     def along(value, shift):
         return lax.ppermute(value, "row", [(r, (r + HALVES * shift) % row_peers) for r in range(row_peers)])
@@ -246,12 +251,13 @@
             name="fill",
         )(*held)
 
-    row_block = pl.BlockSpec((block_rows, full_width), lambda i: (i, 0))
-    wide_block = pl.BlockSpec((block_rows, CORES * full_width), lambda i: (i, 0))
-    def screen(latest):
+    together = SCREEN_BLOCKS if block_count % SCREEN_BLOCKS == 0 else 1
+    row_block = pl.BlockSpec((together * block_rows, full_width), lambda i: (i, 0))
+    wide_block = pl.BlockSpec((together * block_rows, CORES * full_width), lambda i: (i, 0))
+    def screen(*earlier):
         return pl.pallas_call(
-            partial(screen_kernel, tile_width),
-            grid=(block_count,),
+            partial(screen_kernel, tile_width, block_rows),
+            grid=(block_count // together,),
             in_specs=[SMEM, row_block, row_block],
             out_specs=wide_block,
             out_shape=jax.ShapeDtypeStruct((row_count, CORES * full_width), amplitudes.dtype),
@@ -262,7 +268,7 @@
                 transcendentals=0,
             ),
             name="screen",
-        )(after(masks, latest), stored, other)
+        )(after(masks, *earlier), stored, other)
 
     own = chosen.pop(0)
     own = own + across(own, 1, 0)
@@ -272,7 +278,7 @@
         data = across(near, 0, offset) + across(far, 1, offset)
         held = [data] + [along(data, shift) for shift in range(1, peers)]
         if screened is None:
-            screened = screen(held[-1])
+            screened = screen(held[-1], own)
         near_weights[offset] = fill([after(held[0], screened)] + held[1:])
         far_weights[offset] = across(near_weights[offset], 1, 0)
 
@@ -289,14 +295,12 @@
     def scratch_rows(span):
         return code_shape(span)[0] - span * block_rows
 
-    near_chunks = chunks[:-2] + [(chunks[-2][0], chunks[-2][1] + chunks[-1][1])] if len(chunks) > 1 else chunks
-    rounds = [(half, first, span) for half, parts in enumerate((near_chunks, chunks)) for first, span in parts]
+    rounds = [(half, first, span) for half, parts in enumerate((near_chunks, far_chunks)) for first, span in parts]
     arrived, sent = {}, []
     order = []
     for number, (half, first, span) in enumerate(rounds):
-        earlier = sent[-1:] + [part for key in order[:-1] for part in arrived[key]]
-        if number == 0:
-            earlier.append(own)
+        ahead = 1
+        earlier = sent[-1:] + [part for key in order[:-ahead] for part in arrived[key]]
         if number == len(near_chunks) - 1:
             earlier += list(far_weights.values())
         if number == len(rounds) - 2:
@@ -328,8 +332,9 @@
     out = None
     for first, span in chunks:
         near_first = max(start for start, _ in near_chunks if start <= first)
-        received = [part for pair in zip(arrived[0, near_first], arrived[1, first]) for part in pair]
-        skips = [first - near_first, 0] * len(remote)
+        far_first = max(start for start, _ in far_chunks if start <= first)
+        received = [part for pair in zip(arrived[0, near_first], arrived[1, far_first]) for part in pair]
+        skips = [first - near_first, first - far_first] * len(remote)
         operands = [screened, own_weights, *received]
         specs = [
             pl.BlockSpec((block_rows, CORES * full_width), lambda i, first=first: (first + i, 0)),

time: 86.2 us -> 74.1 us (0.86)
  waiting for transfers between devices: 27.7 us -> 20.2 us
  Pallas kernels: 27.2 us -> 23.8 us
  starting transfers between devices: 28.8 us -> 27.6 us
    ppermute x11, waiting for transfers between devices: 23.1 us -> 14.6 us  [across(): return lax.ppermute(value, ('row', 'col'), pairs)]
    pallas_call x1, Pallas kernels: 6.73 us -> 3.35 us  [screen(): pl.pallas_call(partial(screen_kernel, tile_width, block_rows), grid=(bloc...]
    ppermute x9, waiting for transfers between devices: 4.63 us -> 5.65 us  [along(): lax.ppermute(value, 'row', [(r, (r + HALVES * shift) % row_peers) for r i...]
  transfers between devices with their start and end apart: 22 -> 22, of which waited for: 10 -> 13; matrix products, arithmetic and copies ran while one was open for 2% -> 2% of each run, Pallas kernels for 30% -> 30%
where the time goes in v7:
time: 74.1 us; the launch traced here: 73.9 us
  starting transfers between devices  27.6 us (37%)
  Pallas kernels  23.8 us (32%)
  waiting for transfers between devices  20.2 us (27%)
  other arithmetic  1.5 us (2%)
  between operations  0.79 us (1%)
    ppermute x11, waiting for transfers between devices, across(): return lax.ppermute(value, ('row', 'col'), pairs)  14.6 us
    ppermute x9, starting transfers between devices, along(): lax.ppermute(value, 'row', [(r, (r + HALVES * shift) % row_peers) for r i...  14.3 us
    ppermute x11, starting transfers between devices, across(): return lax.ppermute(value, ('row', 'col'), pairs)  12.8 us
    pallas_call x7, Pallas kernels, shards(): pl.pallas_call(send_kernel, grid=(span,), in_specs=[pl.BlockSpec((block_r...  10 us
    pallas_call x4, Pallas kernels, shards(): pl.pallas_call(body, grid=(span,), in_specs=specs, out_specs=pl.BlockSpec...  8 us
    ppermute x9, waiting for transfers between devices, along(): lax.ppermute(value, 'row', [(r, (r + HALVES * shift) % row_peers) for r i...  5.65 us
    pallas_call x1, Pallas kernels, screen(): pl.pallas_call(partial(screen_kernel, tile_width, block_rows), grid=(bloc...  3.35 us
  transfers between devices with their start and end apart: 22, of which 13 were waited for; matrix products, arithmetic and copies ran while one was open for 2% of the time, Pallas kernels for 30%

profile of v7, /device:TPU:0, one launch (start us, length us, event | category | flops | bytes accessed | tf_op | source)
XLA Modules:
  0.0 73.9 jit_solution(5376397288912989602)
XLA Ops:
  0.0 0.5 collective-permute-start.8
  1.2 0.7 %pad_add_fusion.1.table_ref = s32[7]{0:T(128)S(1)} fusion(s32[4]{0:T(128)} %bitcast.7, s32[1]{0:T(128)} %bitcast.4, s32[2]{0:T(128)} %bitcast.8), kind=kLoop, calls=%fused_computation.1 | loop fusion | flops 14 | bytes 56 | tf_op jit(solution)/shard_map/concatenate | solution.py:217
  1.9 1.0 %pack.1 = (bf16[144,256]{1,0:T(8,128)(2,1)S(1)}, bf16[144,256]{1,0:T(8,128)(2,1)S(1)}, bf16[144,256]{1,0:T(8,128)(2,1)S(1)}, bf16[144,256]{1,0:T(8,128)(2,1)S(1)}) custom-call(s32[7]{0:T(128)S(1)} %pad_add_fusion.1.table_ref, bf16[1,1,2,256,256]{4,3,2,1,0:T(8,128)(2,1)} %panel_ref.1), custom_call_target="tpu_custom_call" | custom-call | tf_op jit(solution)/shard_map/pack/pallas_call | solution.py:219
  2.9 3.1 %collective-permute-start.1 = (bf16[144,256]{1,0:T(8,128)(2,1)S(1)}, bf16[144,256]{1,0:T(8,128)(2,1)S(1)}, u32[]{:S(2)}, u32[]{:S(2)}) collective-permute-start(bf16[144,256]{1,0:T(8,128)(2,1)S(1)} %get-tuple-element.24), channel_id=1, source_target_pairs={{0,8},{4,12},{8,16},{12,20},{16,24},{20,28},{24,0},{28,4},{1,9},{5... | collective-permute-start | bytes 221192 | tf_op jit(solution)/shard_map/ppermute | solution.py:202
  6.0 2.6 %collective-permute-start.2 = (bf16[144,256]{1,0:T(8,128)(2,1)S(1)}, bf16[144,256]{1,0:T(8,128)(2,1)S(1)}, u32[]{:S(2)}, u32[]{:S(2)}) collective-permute-start(bf16[144,256]{1,0:T(8,128)(2,1)S(1)} %get-tuple-element.25), channel_id=1, source_target_pairs={{0,16},{4,20},{8,24},{12,28},{16,0},{20,4},{24,8},{28,12},{1,17},{... | collective-permute-start | bytes 221192 | tf_op jit(solution)/shard_map/ppermute | solution.py:202
  8.6 1.3 %collective-permute-start.3 = (bf16[144,256]{1,0:T(8,128)(2,1)S(1)}, bf16[144,256]{1,0:T(8,128)(2,1)S(1)}, u32[]{:S(2)}, u32[]{:S(2)}) collective-permute-start(bf16[144,256]{1,0:T(8,128)(2,1)S(1)} %get-tuple-element.26), channel_id=1, source_target_pairs={{0,24},{4,28},{8,0},{12,4},{16,8},{20,12},{24,16},{28,20},{1,25},{... | collective-permute-start | bytes 221192 | tf_op jit(solution)/shard_map/ppermute | solution.py:202
  10.0 0.7 pad_add_fusion.mask_ref
  10.9 2.9 %collective-permute-done.2.refs_2_ = bf16[144,256]{1,0:T(8,128)(2,1)S(1)} collective-permute-done((bf16[144,256]{1,0:T(8,128)(2,1)S(1)}, bf16[144,256]{1,0:T(8,128)(2,1)S(1)}, u32[]{:S(2)}, u32[]{:S(2)}) %collective-permute-start.2) | collective-permute-done | bytes 73760 | tf_op jit(solution)/shard_map/ppermute | solution.py:202
  14.0 0.7 choose.1
  14.7 1.6 %collective-permute-start.4 = (bf16[272,128]{1,0:T(8,128)(2,1)S(1)}, bf16[272,128]{1,0:T(8,128)(2,1)S(1)}, u32[]{:S(2)}, u32[]{:S(2)}) collective-permute-start(bf16[272,128]{1,0:T(8,128)(2,1)S(1)} %get-tuple-element.27), channel_id=1, source_target_pairs={{0,2},{1,3},{2,0},{3,1},{4,6},{5,7},{6,4},{7,5},{8,10},{9,11},{10,... | collective-permute-start | bytes 208904 | tf_op jit(solution)/shard_map/ppermute | solution.py:209
  16.2 1.5 %collective-permute-start.5 = (bf16[272,128]{1,0:T(8,128)(2,1)S(1)}, bf16[272,128]{1,0:T(8,128)(2,1)S(1)}, u32[]{:S(2)}, u32[]{:S(2)}) collective-permute-start(bf16[272,128]{1,0:T(8,128)(2,1)S(1)} %get-tuple-element.28), channel_id=1, source_target_pairs={{0,6},{1,7},{2,4},{3,5},{4,2},{5,3},{6,0},{7,1},{8,14},{9,15},{10,... | collective-permute-start | bytes 208904 | tf_op jit(solution)/shard_map/ppermute | solution.py:209
  17.7 0.5 collective-permute-start.7
  18.2 0.8 %collective-permute-done.4 = bf16[272,128]{1,0:T(8,128)(2,1)S(1)} collective-permute-done((bf16[272,128]{1,0:T(8,128)(2,1)S(1)}, bf16[272,128]{1,0:T(8,128)(2,1)S(1)}, u32[]{:S(2)}, u32[]{:S(2)}) %collective-permute-start.4) | collective-permute-done | bytes 69664 | tf_op jit(solution)/shard_map/ppermute | solution.py:209
  19.1 2.5 %collective-permute-done.5 = bf16[272,128]{1,0:T(8,128)(2,1)S(1)} collective-permute-done((bf16[272,128]{1,0:T(8,128)(2,1)S(1)}, bf16[272,128]{1,0:T(8,128)(2,1)S(1)}, u32[]{:S(2)}, u32[]{:S(2)}) %collective-permute-start.5) | collective-permute-done | bytes 69664 | tf_op jit(solution)/shard_map/ppermute | solution.py:209
  21.6 3.1 %collective-permute-start.6 = (bf16[272,128]{1,0:T(8,128)(2,1)S(1)}, bf16[272,128]{1,0:T(8,128)(2,1)S(1)}, u32[]{:S(2)}, u32[]{:S(2)}) collective-permute-start(bf16[272,128]{1,0:T(8,128)(2,1)S(1)} %add.6.refs_0_), channel_id=1, source_target_pairs={{0,24},{4,28},{8,0},{12,4},{16,8},{20,12},{24,16},{28,20},{1,25},{... | collective-permute-start | bytes 208904 | tf_op jit(solution)/shard_map/ppermute | solution.py:202
  25.0 0.4 collective-permute-start.9
  25.4 1.3 %collective-permute-done.6.refs_3_ = bf16[272,128]{1,0:T(8,128)(2,1)S(1)} collective-permute-done((bf16[272,128]{1,0:T(8,128)(2,1)S(1)}, bf16[272,128]{1,0:T(8,128)(2,1)S(1)}, u32[]{:S(2)}, u32[]{:S(2)}) %collective-permute-start.6) | collective-permute-done | bytes 69664 | tf_op jit(solution)/shard_map/ppermute | solution.py:202
  26.6 3.4 %screen.1.rows_ref.refs_0_ = bf16[3072,1536]{1,0:T(8,128)(2,1)S(1)} custom-call(s32[6,12]{1,0:T(8,128)S(1)} %pad_add_fusion.mask_ref, bf16[3072,768]{1,0:T(8,128)(2,1)} %own_ref.1, bf16[3072,768]{1,0:T(8,128)(2,1)S(1)} %collective-permute-done.8.other_ref), custom_call_target="tpu_custom_call" | custom-call | flops 4718592 | bytes 18874368 | tf_op jit(solution)/shard_map/screen/pallas_call | solution.py:258
  30.0 0.3 collective-permute-done.10.refs_2_
  30.3 0.8 %collective-permute-done.9.refs_1_ = bf16[272,128]{1,0:T(8,128)(2,1)S(1)} collective-permute-done((bf16[272,128]{1,0:T(8,128)(2,1)S(1)}, bf16[272,128]{1,0:T(8,128)(2,1)S(1)}, u32[]{:S(2)}, u32[]{:S(2)}) %collective-permute-start.9) | collective-permute-done | bytes 69664 | tf_op jit(solution)/shard_map/ppermute | solution.py:202
  31.1 0.3 fill.2.dense_ref
  31.4 1.5 %collective-permute-start.15 = (bf16[1536,128]{1,0:T(8,128)(2,1)S(1)}, bf16[1536,128]{1,0:T(8,128)(2,1)S(1)}, u32[]{:S(2)}, u32[]{:S(2)}) collective-permute-start(bf16[1536,128]{1,0:T(8,128)(2,1)S(1)} %fill.2.dense_ref), channel_id=1, source_target_pairs={{0,4},{1,5},{2,6},{3,7},{4,0},{5,1},{6,2},{7,3},{8,12},{9,13},{10,... | collective-permute-start | bytes 1179656 | tf_op jit(solution)/shard_map/ppermute | solution.py:209
  32.9 0.8 %send_part.7 = s16[528,128]{1,0:T(8,128)(2,1)S(1)} custom-call(bf16[3072,1536]{1,0:T(8,128)(2,1)S(1)} %screen.1.rows_ref.refs_0_, bf16[1536,128]{1,0:T(8,128)(2,1)S(1)} %fill.2.dense_ref), custom_call_target="tpu_custom_call" | custom-call | flops 201326592 | bytes 1703936 | tf_op jit(solution)/shard_map/send_part/pallas_call | solution.py:312
  33.7 0.6 collective-permute-start.11
  34.4 2.1 %send_part.8 = s16[1296,128]{1,0:T(8,128)(2,1)S(1)} custom-call(bf16[3072,1536]{1,0:T(8,128)(2,1)S(1)} %screen.1.rows_ref.refs_0_, bf16[1536,128]{1,0:T(8,128)(2,1)S(1)} %fill.2.dense_ref), custom_call_target="tpu_custom_call" | custom-call | flops 503316480 | bytes 4259840 | tf_op jit(solution)/shard_map/send_part/pallas_call | solution.py:312
  36.5 1.5 %collective-permute-start.17 = (s16[1296,128]{1,0:T(8,128)(2,1)S(1)}, s16[1296,128]{1,0:T(8,128)(2,1)S(1)}, u32[]{:S(2)}, u32[]{:S(2)}) collective-permute-start(s16[1296,128]{1,0:T(8,128)(2,1)S(1)} %send_part.8), channel_id=1, source_target_pairs={{0,2},{1,3},{2,0},{3,1},{4,6},{5,7},{6,4},{7,5},{8,10},{9,11},{10,... | collective-permute-start | bytes 995336 | tf_op jit(solution)/shard_map/ppermute | solution.py:209
  38.0 2.3 %collective-permute-done.11.refs_0_ = s16[528,128]{1,0:T(8,128)(2,1)S(1)} collective-permute-done((s16[528,128]{1,0:T(8,128)(2,1)S(1)}, s16[528,128]{1,0:T(8,128)(2,1)S(1)}, u32[]{:S(2)}, u32[]{:S(2)}) %collective-permute-start.11) | collective-permute-done | bytes 135200 | tf_op jit(solution)/shard_map/ppermute | solution.py:209
  40.2 0.4 collective-permute-done.15.dense_ref
  40.6 2.1 %send_part.9 = s16[1296,128]{1,0:T(8,128)(2,1)S(1)} custom-call(bf16[3072,1536]{1,0:T(8,128)(2,1)S(1)} %screen.1.rows_ref.refs_0_, bf16[1536,128]{1,0:T(8,128)(2,1)S(1)} %fill.2.dense_ref), custom_call_target="tpu_custom_call" | custom-call | flops 503316480 | bytes 4259840 | tf_op jit(solution)/shard_map/send_part/pallas_call | solution.py:312
  42.7 1.0 %collective-permute-start.16 = (s16[1296,128]{1,0:T(8,128)(2,1)S(1)}, s16[1296,128]{1,0:T(8,128)(2,1)S(1)}, u32[]{:S(2)}, u32[]{:S(2)}) collective-permute-start(s16[1296,128]{1,0:T(8,128)(2,1)S(1)} %send_part.9), channel_id=1, source_target_pairs={{0,2},{1,3},{2,0},{3,1},{4,6},{5,7},{6,4},{7,5},{8,10},{9,11},{10,... | collective-permute-start | bytes 995336 | tf_op jit(solution)/shard_map/ppermute | solution.py:209
  43.7 2.6 %collective-permute-start.14 = (bf16[272,256]{1,0:T(8,128)(2,1)S(1)}, bf16[272,256]{1,0:T(8,128)(2,1)S(1)}, u32[]{:S(2)}, u32[]{:S(2)}) collective-permute-start(bf16[272,256]{1,0:T(8,128)(2,1)S(1)} %add.7.refs_0_), channel_id=1, source_target_pairs={{0,24},{4,28},{8,0},{12,4},{16,8},{20,12},{24,16},{28,20},{1,25},{... | collective-permute-start | bytes 417800 | tf_op jit(solution)/shard_map/ppermute | solution.py:202
  46.3 0.4 collective-permute-start.13
  46.7 0.5 collective-permute-start.12
  47.3 0.8 %send_part.10 = s16[528,128]{1,0:T(8,128)(2,1)S(1)} custom-call(bf16[3072,1536]{1,0:T(8,128)(2,1)S(1)} %screen.1.rows_ref.refs_0_, bf16[1536,128]{1,0:T(8,128)(2,1)S(1)} %collective-permute-done.15.dense_ref), custom_call_target="tpu_custom_call" | custom-call | flops 201326592 | bytes 1703936 | tf_op jit(solution)/shard_map/send_part/pallas_call | solution.py:312
  48.2 1.4 %collective-permute-start.18 = (s16[528,128]{1,0:T(8,128)(2,1)S(1)}, s16[528,128]{1,0:T(8,128)(2,1)S(1)}, u32[]{:S(2)}, u32[]{:S(2)}) collective-permute-start(s16[528,128]{1,0:T(8,128)(2,1)S(1)} %send_part.10), channel_id=1, source_target_pairs={{0,2},{1,3},{2,0},{3,1},{4,6},{5,7},{6,4},{7,5},{8,10},{9,11},{10,... | collective-permute-start | bytes 405512 | tf_op jit(solution)/shard_map/ppermute | solution.py:209
  49.6 4.0 %collective-permute-done.16.refs_2_ = s16[1296,128]{1,0:T(8,128)(2,1)S(1)} collective-permute-done((s16[1296,128]{1,0:T(8,128)(2,1)S(1)}, s16[1296,128]{1,0:T(8,128)(2,1)S(1)}, u32[]{:S(2)}, u32[]{:S(2)}) %collective-permute-start.16) | collective-permute-done | bytes 331808 | tf_op jit(solution)/shard_map/ppermute | solution.py:209
  53.6 2.1 %send_part.11 = s16[1296,128]{1,0:T(8,128)(2,1)S(1)} custom-call(bf16[3072,1536]{1,0:T(8,128)(2,1)S(1)} %screen.1.rows_ref.refs_0_, bf16[1536,128]{1,0:T(8,128)(2,1)S(1)} %collective-permute-done.15.dense_ref), custom_call_target="tpu_custom_call" | custom-call | flops 503316480 | bytes 4259840 | tf_op jit(solution)/shard_map/send_part/pallas_call | solution.py:312
  55.7 1.1 %collective-permute-start.19 = (s16[1296,128]{1,0:T(8,128)(2,1)S(1)}, s16[1296,128]{1,0:T(8,128)(2,1)S(1)}, u32[]{:S(2)}, u32[]{:S(2)}) collective-permute-start(s16[1296,128]{1,0:T(8,128)(2,1)S(1)} %send_part.11), channel_id=1, source_target_pairs={{0,2},{1,3},{2,0},{3,1},{4,6},{5,7},{6,4},{7,5},{8,10},{9,11},{10,... | collective-permute-start | bytes 995336 | tf_op jit(solution)/shard_map/ppermute | solution.py:209
  56.8 0.3 fill.3.dense_ref.refs_1_
  57.2 1.7 %send_part.12 = s16[1040,128]{1,0:T(8,128)(2,1)S(1)} custom-call(bf16[3072,1536]{1,0:T(8,128)(2,1)S(1)} %screen.1.rows_ref.refs_0_, bf16[1536,128]{1,0:T(8,128)(2,1)S(1)} %collective-permute-done.15.dense_ref), custom_call_target="tpu_custom_call" | custom-call | flops 402653184 | bytes 3407872 | tf_op jit(solution)/shard_map/send_part/pallas_call | solution.py:312
  58.9 1.1 %collective-permute-start.21 = (s16[1040,128]{1,0:T(8,128)(2,1)S(1)}, s16[1040,128]{1,0:T(8,128)(2,1)S(1)}, u32[]{:S(2)}, u32[]{:S(2)}) collective-permute-start(s16[1040,128]{1,0:T(8,128)(2,1)S(1)} %send_part.12), channel_id=1, source_target_pairs={{0,2},{1,3},{2,0},{3,1},{4,6},{5,7},{6,4},{7,5},{8,10},{9,11},{10,... | collective-permute-start | bytes 798728 | tf_op jit(solution)/shard_map/ppermute | solution.py:209
  59.9 1.4 %join_part.4.refs_4_ = bf16[3072,256]{1,0:T(8,128)(2,1)} custom-call(bf16[3072,1536]{1,0:T(8,128)(2,1)S(1)} %screen.1.rows_ref.refs_0_, bf16[1536,256]{1,0:T(8,128)(2,1)S(1)} %fill.3.dense_ref.refs_1_, s16[528,128]{1,0:T(8,128)(2,1)S(1)} %collective-permute-done.11.refs_0_, s16[528,128]{1,0:T(8,128)(2,1)S(1)} %collective-permute-done.18.refs_1_), custom_call_target="tpu_custom_call" | custom-call | flops 402653184 | bytes 1835008 | tf_op jit(solution)/shard_map/join_part/pallas_call | solution.py:349
  61.4 4.4 %collective-permute-done.19.refs_3_ = s16[1296,128]{1,0:T(8,128)(2,1)S(1)} collective-permute-done((s16[1296,128]{1,0:T(8,128)(2,1)S(1)}, s16[1296,128]{1,0:T(8,128)(2,1)S(1)}, u32[]{:S(2)}, u32[]{:S(2)}) %collective-permute-start.19) | collective-permute-done | bytes 331808 | tf_op jit(solution)/shard_map/ppermute | solution.py:209
  65.8 0.4 send_part.13
  66.2 1.1 %collective-permute-start.20 = (s16[272,128]{1,0:T(8,128)(2,1)S(1)}, s16[272,128]{1,0:T(8,128)(2,1)S(1)}, u32[]{:S(2)}, u32[]{:S(2)}) collective-permute-start(s16[272,128]{1,0:T(8,128)(2,1)S(1)} %send_part.13), channel_id=1, source_target_pairs={{0,2},{1,3},{2,0},{3,1},{4,6},{5,7},{6,4},{7,5},{8,10},{9,11},{10,... | collective-permute-start | bytes 208904 | tf_op jit(solution)/shard_map/ppermute | solution.py:209
  67.3 3.1 %join_part.5.refs_4_ = bf16[3072,256]{1,0:T(8,128)(2,1)} custom-call(bf16[3072,1536]{1,0:T(8,128)(2,1)S(1)} %screen.1.rows_ref.refs_0_, bf16[1536,256]{1,0:T(8,128)(2,1)S(1)} %fill.3.dense_ref.refs_1_, s16[1296,128]{1,0:T(8,128)(2,1)S(1)} %collective-permute-done.17.refs_2_, ...), custom_call_target="tpu_custom_call", output_to_operand_aliasing={{}: (4, {})} | custom-call | flops 1006632960 | bytes 4587520 | tf_op jit(solution)/shard_map/join_part/pallas_call | solution.py:349
  70.4 2.5 %join_part.6.refs_4_ = bf16[3072,256]{1,0:T(8,128)(2,1)} custom-call(bf16[3072,1536]{1,0:T(8,128)(2,1)S(1)} %screen.1.rows_ref.refs_0_, bf16[1536,256]{1,0:T(8,128)(2,1)S(1)} %fill.3.dense_ref.refs_1_, s16[1296,128]{1,0:T(8,128)(2,1)S(1)} %collective-permute-done.16.refs_2_, ...), custom_call_target="tpu_custom_call", output_to_operand_aliasing={{}: (4, {})} | custom-call | flops 805306368 | bytes 3670016 | tf_op jit(solution)/shard_map/join_part/pallas_call | solution.py:349
  72.9 1.0 %join_part.7 = bf16[3072,256]{1,0:T(8,128)(2,1)} custom-call(bf16[3072,1536]{1,0:T(8,128)(2,1)S(1)} %screen.1.rows_ref.refs_0_, bf16[1536,256]{1,0:T(8,128)(2,1)S(1)} %fill.3.dense_ref.refs_1_, s16[1296,128]{1,0:T(8,128)(2,1)S(1)} %collective-permute-done.16.refs_2_, ...), custom_call_target="tpu_custom_call", output_to_operand_aliasing={{}: (4, {})} | custom-call | flops 201326592 | bytes 917504 | tf_op jit(solution)/shard_map/join_part/pallas_call | solution.py:349
  (16 shorter events, 1.0 us)
Async XLA Ops:
  0.0 26.6 %collective-permute-start.8 = (bf16[3072,768]{1,0:T(8,128)(2,1)}, bf16[3072,768]{1,0:T(8,128)(2,1)S(1)}, u32[]{:S(2)}, u32[]{:S(2)}) collective-permute-start(bf16[3072,768]{1,0:T(8,128)(2,1)} %own_ref.1), channel_id=1, source_target_pairs={{0,1},{1,0},{2,3},{3,2},{4,5},{5,4},{6,7},{7,6},{8,9},{9,8},{10,11... | collective-permute-start | bytes 14155784 | tf_op jit(solution)/shard_map/ppermute | solution.py:212
  0.5 9.5 %collective-permute-start = (s32[3,12]{1,0:T(4,128)}, s32[3,12]{1,0:T(4,128)S(1)}, u32[]{:S(2)}, u32[]{:S(2)}) collective-permute-start(s32[3,12]{1,0:T(4,128)} %bitcast.5), channel_id=1, source_target_pairs={{0,1},{1,0},{2,3},{3,2},{4,5},{5,4},{6,7},{7,6},{8,9},{9,8},{10,11... | collective-permute-start | bytes 440 | tf_op jit(solution)/shard_map/ppermute | solution.py:213
  2.9 7.9 %collective-permute-start.1 = (bf16[144,256]{1,0:T(8,128)(2,1)S(1)}, bf16[144,256]{1,0:T(8,128)(2,1)S(1)}, u32[]{:S(2)}, u32[]{:S(2)}) collective-permute-start(bf16[144,256]{1,0:T(8,128)(2,1)S(1)} %get-tuple-element.24), channel_id=1, source_target_pairs={{0,8},{4,12},{8,16},{12,20},{16,24},{20,28},{24,0},{28,4},{1,9},{5... | collective-permute-start | bytes 221192 | tf_op jit(solution)/shard_map/ppermute | solution.py:202
  6.0 7.7 %collective-permute-start.2 = (bf16[144,256]{1,0:T(8,128)(2,1)S(1)}, bf16[144,256]{1,0:T(8,128)(2,1)S(1)}, u32[]{:S(2)}, u32[]{:S(2)}) collective-permute-start(bf16[144,256]{1,0:T(8,128)(2,1)S(1)} %get-tuple-element.25), channel_id=1, source_target_pairs={{0,16},{4,20},{8,24},{12,28},{16,0},{20,4},{24,8},{28,12},{1,17},{... | collective-permute-start | bytes 221192 | tf_op jit(solution)/shard_map/ppermute | solution.py:202
  8.6 5.4 %collective-permute-start.3 = (bf16[144,256]{1,0:T(8,128)(2,1)S(1)}, bf16[144,256]{1,0:T(8,128)(2,1)S(1)}, u32[]{:S(2)}, u32[]{:S(2)}) collective-permute-start(bf16[144,256]{1,0:T(8,128)(2,1)S(1)} %get-tuple-element.26), channel_id=1, source_target_pairs={{0,24},{4,28},{8,0},{12,4},{16,8},{20,12},{24,16},{28,20},{1,25},{... | collective-permute-start | bytes 221192 | tf_op jit(solution)/shard_map/ppermute | solution.py:202
  14.7 4.4 %collective-permute-start.4 = (bf16[272,128]{1,0:T(8,128)(2,1)S(1)}, bf16[272,128]{1,0:T(8,128)(2,1)S(1)}, u32[]{:S(2)}, u32[]{:S(2)}) collective-permute-start(bf16[272,128]{1,0:T(8,128)(2,1)S(1)} %get-tuple-element.27), channel_id=1, source_target_pairs={{0,2},{1,3},{2,0},{3,1},{4,6},{5,7},{6,4},{7,5},{8,10},{9,11},{10,... | collective-permute-start | bytes 208904 | tf_op jit(solution)/shard_map/ppermute | solution.py:209
  16.2 5.3 %collective-permute-start.5 = (bf16[272,128]{1,0:T(8,128)(2,1)S(1)}, bf16[272,128]{1,0:T(8,128)(2,1)S(1)}, u32[]{:S(2)}, u32[]{:S(2)}) collective-permute-start(bf16[272,128]{1,0:T(8,128)(2,1)S(1)} %get-tuple-element.28), channel_id=1, source_target_pairs={{0,6},{1,7},{2,4},{3,5},{4,2},{5,3},{6,0},{7,1},{8,14},{9,15},{10,... | collective-permute-start | bytes 208904 | tf_op jit(solution)/shard_map/ppermute | solution.py:209
  17.7 7.6 %collective-permute-start.7 = (bf16[272,256]{1,0:T(8,128)(2,1)S(1)}, bf16[272,256]{1,0:T(8,128)(2,1)S(1)}, u32[]{:S(2)}, u32[]{:S(2)}) collective-permute-start(bf16[272,256]{1,0:T(8,128)(2,1)S(1)} %get-tuple-element.29), channel_id=1, source_target_pairs={{0,4},{1,5},{2,6},{3,7},{4,0},{5,1},{6,2},{7,3},{8,12},{9,13},{10,... | collective-permute-start | bytes 417800 | tf_op jit(solution)/shard_map/ppermute | solution.py:209
  21.6 5.1 %collective-permute-start.6 = (bf16[272,128]{1,0:T(8,128)(2,1)S(1)}, bf16[272,128]{1,0:T(8,128)(2,1)S(1)}, u32[]{:S(2)}, u32[]{:S(2)}) collective-permute-start(bf16[272,128]{1,0:T(8,128)(2,1)S(1)} %add.6.refs_0_), channel_id=1, source_target_pairs={{0,24},{4,28},{8,0},{12,4},{16,8},{20,12},{24,16},{28,20},{1,25},{... | collective-permute-start | bytes 208904 | tf_op jit(solution)/shard_map/ppermute | solution.py:202
  24.7 5.6 %collective-permute-start.10 = (bf16[272,128]{1,0:T(8,128)(2,1)S(1)}, bf16[272,128]{1,0:T(8,128)(2,1)S(1)}, u32[]{:S(2)}, u32[]{:S(2)}) collective-permute-start(bf16[272,128]{1,0:T(8,128)(2,1)S(1)} %add.6.refs_0_), channel_id=1, source_target_pairs={{0,16},{4,20},{8,24},{12,28},{16,0},{20,4},{24,8},{28,12},{1,17},{... | collective-permute-start | bytes 208904 | tf_op jit(solution)/shard_map/ppermute | solution.py:202
  25.0 6.1 %collective-permute-start.9 = (bf16[272,128]{1,0:T(8,128)(2,1)S(1)}, bf16[272,128]{1,0:T(8,128)(2,1)S(1)}, u32[]{:S(2)}, u32[]{:S(2)}) collective-permute-start(bf16[272,128]{1,0:T(8,128)(2,1)S(1)} %add.6.refs_0_), channel_id=1, source_target_pairs={{0,8},{4,12},{8,16},{12,20},{16,24},{20,28},{24,0},{28,4},{1,9},{5... | collective-permute-start | bytes 208904 | tf_op jit(solution)/shard_map/ppermute | solution.py:202
  31.4 9.2 %collective-permute-start.15 = (bf16[1536,128]{1,0:T(8,128)(2,1)S(1)}, bf16[1536,128]{1,0:T(8,128)(2,1)S(1)}, u32[]{:S(2)}, u32[]{:S(2)}) collective-permute-start(bf16[1536,128]{1,0:T(8,128)(2,1)S(1)} %fill.2.dense_ref), channel_id=1, source_target_pairs={{0,4},{1,5},{2,6},{3,7},{4,0},{5,1},{6,2},{7,3},{8,12},{9,13},{10,... | collective-permute-start | bytes 1179656 | tf_op jit(solution)/shard_map/ppermute | solution.py:209
  33.7 6.5 %collective-permute-start.11 = (s16[528,128]{1,0:T(8,128)(2,1)S(1)}, s16[528,128]{1,0:T(8,128)(2,1)S(1)}, u32[]{:S(2)}, u32[]{:S(2)}) collective-permute-start(s16[528,128]{1,0:T(8,128)(2,1)S(1)} %send_part.7), channel_id=1, source_target_pairs={{0,2},{1,3},{2,0},{3,1},{4,6},{5,7},{6,4},{7,5},{8,10},{9,11},{10,... | collective-permute-start | bytes 405512 | tf_op jit(solution)/shard_map/ppermute | solution.py:209
  36.5 10.9 %collective-permute-start.17 = (s16[1296,128]{1,0:T(8,128)(2,1)S(1)}, s16[1296,128]{1,0:T(8,128)(2,1)S(1)}, u32[]{:S(2)}, u32[]{:S(2)}) collective-permute-start(s16[1296,128]{1,0:T(8,128)(2,1)S(1)} %send_part.8), channel_id=1, source_target_pairs={{0,2},{1,3},{2,0},{3,1},{4,6},{5,7},{6,4},{7,5},{8,10},{9,11},{10,... | collective-permute-start | bytes 995336 | tf_op jit(solution)/shard_map/ppermute | solution.py:209
  42.7 10.9 %collective-permute-start.16 = (s16[1296,128]{1,0:T(8,128)(2,1)S(1)}, s16[1296,128]{1,0:T(8,128)(2,1)S(1)}, u32[]{:S(2)}, u32[]{:S(2)}) collective-permute-start(s16[1296,128]{1,0:T(8,128)(2,1)S(1)} %send_part.9), channel_id=1, source_target_pairs={{0,2},{1,3},{2,0},{3,1},{4,6},{5,7},{6,4},{7,5},{8,10},{9,11},{10,... | collective-permute-start | bytes 995336 | tf_op jit(solution)/shard_map/ppermute | solution.py:209
  43.7 13.1 %collective-permute-start.14 = (bf16[272,256]{1,0:T(8,128)(2,1)S(1)}, bf16[272,256]{1,0:T(8,128)(2,1)S(1)}, u32[]{:S(2)}, u32[]{:S(2)}) collective-permute-start(bf16[272,256]{1,0:T(8,128)(2,1)S(1)} %add.7.refs_0_), channel_id=1, source_target_pairs={{0,24},{4,28},{8,0},{12,4},{16,8},{20,12},{24,16},{28,20},{1,25},{... | collective-permute-start | bytes 417800 | tf_op jit(solution)/shard_map/ppermute | solution.py:202
  46.3 10.5 %collective-permute-start.13 = (bf16[272,256]{1,0:T(8,128)(2,1)S(1)}, bf16[272,256]{1,0:T(8,128)(2,1)S(1)}, u32[]{:S(2)}, u32[]{:S(2)}) collective-permute-start(bf16[272,256]{1,0:T(8,128)(2,1)S(1)} %add.7.refs_0_), channel_id=1, source_target_pairs={{0,16},{4,20},{8,24},{12,28},{16,0},{20,4},{24,8},{28,12},{1,17},{... | collective-permute-start | bytes 417800 | tf_op jit(solution)/shard_map/ppermute | solution.py:202
  46.7 10.2 %collective-permute-start.12 = (bf16[272,256]{1,0:T(8,128)(2,1)S(1)}, bf16[272,256]{1,0:T(8,128)(2,1)S(1)}, u32[]{:S(2)}, u32[]{:S(2)}) collective-permute-start(bf16[272,256]{1,0:T(8,128)(2,1)S(1)} %add.7.refs_0_), channel_id=1, source_target_pairs={{0,8},{4,12},{8,16},{12,20},{16,24},{20,28},{24,0},{28,4},{1,9},{5... | collective-permute-start | bytes 417800 | tf_op jit(solution)/shard_map/ppermute | solution.py:202
  48.2 9.0 %collective-permute-start.18 = (s16[528,128]{1,0:T(8,128)(2,1)S(1)}, s16[528,128]{1,0:T(8,128)(2,1)S(1)}, u32[]{:S(2)}, u32[]{:S(2)}) collective-permute-start(s16[528,128]{1,0:T(8,128)(2,1)S(1)} %send_part.10), channel_id=1, source_target_pairs={{0,2},{1,3},{2,0},{3,1},{4,6},{5,7},{6,4},{7,5},{8,10},{9,11},{10,... | collective-permute-start | bytes 405512 | tf_op jit(solution)/shard_map/ppermute | solution.py:209
  55.7 10.1 %collective-permute-start.19 = (s16[1296,128]{1,0:T(8,128)(2,1)S(1)}, s16[1296,128]{1,0:T(8,128)(2,1)S(1)}, u32[]{:S(2)}, u32[]{:S(2)}) collective-permute-start(s16[1296,128]{1,0:T(8,128)(2,1)S(1)} %send_part.11), channel_id=1, source_target_pairs={{0,2},{1,3},{2,0},{3,1},{4,6},{5,7},{6,4},{7,5},{8,10},{9,11},{10,... | collective-permute-start | bytes 995336 | tf_op jit(solution)/shard_map/ppermute | solution.py:209
  58.9 11.5 %collective-permute-start.21 = (s16[1040,128]{1,0:T(8,128)(2,1)S(1)}, s16[1040,128]{1,0:T(8,128)(2,1)S(1)}, u32[]{:S(2)}, u32[]{:S(2)}) collective-permute-start(s16[1040,128]{1,0:T(8,128)(2,1)S(1)} %send_part.12), channel_id=1, source_target_pairs={{0,2},{1,3},{2,0},{3,1},{4,6},{5,7},{6,4},{7,5},{8,10},{9,11},{10,... | collective-permute-start | bytes 798728 | tf_op jit(solution)/shard_map/ppermute | solution.py:209
  66.2 6.6 %collective-permute-start.20 = (s16[272,128]{1,0:T(8,128)(2,1)S(1)}, s16[272,128]{1,0:T(8,128)(2,1)S(1)}, u32[]{:S(2)}, u32[]{:S(2)}) collective-permute-start(s16[272,128]{1,0:T(8,128)(2,1)S(1)} %send_part.13), channel_id=1, source_target_pairs={{0,2},{1,3},{2,0},{3,1},{4,6},{5,7},{6,4},{7,5},{8,10},{9,11},{10,... | collective-permute-start | bytes 208904 | tf_op jit(solution)/shard_map/ppermute | solution.py:209

commit v8 on v7

--- a/solution.py
+++ b/solution.py
@@ -19,6 +19,7 @@
 PARAMS = pltpu.CompilerParams(vmem_limit_bytes=16 * 1024 * 1024)
 SMEM = pl.BlockSpec(memory_space=pltpu.SMEM)
 VMEM = pl.BlockSpec(memory_space=pltpu.VMEM)
+HBM = pl.BlockSpec(memory_space=pltpu.HBM)
 
 
 def pair_offsets(col_count):
@@ -117,67 +118,85 @@
 
 
 def screen_kernel(tile_width, block_rows, mask_ref, own_ref, other_ref, out_ref):
-    blocks, tiles = own_ref.shape[0] // block_rows, own_ref.shape[1] // tile_width
-    for number in range(blocks):
-        block = pl.program_id(0) * blocks + number
-        lines = pl.ds(number * block_rows, block_rows)
-        for group, rows_ref in enumerate((own_ref, other_ref)):
-            for tile in range(tiles):
-                live = mask_ref[group * tiles + tile, block].astype(jnp.float32).astype(rows_ref.dtype)
-                columns = pl.ds((group * tiles + tile) * tile_width, tile_width)
-                out_ref[lines, columns] = rows_ref[lines, pl.ds(tile * tile_width, tile_width)] * live
-
-
-def send_kernel(rows_ref, dense_ref, code_ref, scale_ref):
-    step, span = pl.program_id(0), pl.num_programs(0)
-    height = rows_ref.shape[0]
-    total = jnp.dot(rows_ref[...], dense_ref[...], preferred_element_type=jnp.float32)
-    top = jnp.max(jnp.abs(total), axis=0, keepdims=True)
-    unit = jnp.where(top > 0, top, 1.0) * (1.0 / CODE_TOP)
-    power = jnp.floor(jnp.log2(unit))
-    fraction = jnp.ceil(unit * jnp.exp2(-power) * FRACTION)
-    unit = fraction * jnp.exp2(power) * (1.0 / FRACTION)
-    code = jnp.clip(jnp.round(total * (1.0 / unit)), -CODE_TOP, CODE_TOP)
-    code_ref[pl.ds(pl.multiple_of(step * height, height), height), :] = code.astype(jnp.int32).astype(jnp.int16)
-    scale_ref[pl.ds(2 * step, 1), :] = power
-    scale_ref[pl.ds(2 * step + 1, 1), :] = fraction
-
-    @pl.when(step == span - 1)
-    def _():
-        rows = scale_ref.shape[0]
-        line = lax.broadcasted_iota(jnp.int32, scale_ref.shape, 0)
-        kept = jnp.where(line < 2 * span, scale_ref[...], 0.0)
-        code_ref[pl.ds(code_ref.shape[0] - rows, rows), :] = kept.astype(jnp.int32).astype(jnp.int16)
-
-
-def join_kernel(skips, rows_ref, dense_ref, *refs):
-    code_refs, out_ref, scale_ref = refs[:-2], refs[-2], refs[-1]
-    step = pl.program_id(0)
-    height = rows_ref.shape[0]
+    full_width = own_ref.shape[1]
+    tiles = full_width // tile_width
+    block_count = own_ref.shape[0] // block_rows
+    together = SCREEN_BLOCKS if block_count % SCREEN_BLOCKS == 0 else 1
+
+    def body(own_block):
+        for number in range(together):
+            block = pl.program_id(0) * together + number
+            lines = pl.ds(pl.multiple_of(block * block_rows, block_rows), block_rows)
+            for tile in range(CORES * tiles):
+                live = mask_ref[tile, block].astype(jnp.float32).astype(own_block.dtype)
+                if tile < tiles:
+                    part = own_block[pl.ds(number * block_rows, block_rows), pl.ds(tile * tile_width, tile_width)]
+                else:
+                    part = other_ref[lines, pl.ds((tile - tiles) * tile_width, tile_width)]
+                out_ref[lines, pl.ds(tile * tile_width, tile_width)] = part * live
+
+    pltpu.emit_pipeline(
+        body,
+        grid=(block_count // together,),
+        in_specs=[pl.BlockSpec((together * block_rows, full_width), lambda i: (i, 0))],
+    )(own_ref)
+
+
+def send_kernel(first, span, height, rows_ref, dense_ref, code_ref, scale_ref):
+    scale_ref[...] = jnp.zeros_like(scale_ref)
+
+    @pl.loop(0, span)
+    def _(step):
+        lines = pl.ds(pl.multiple_of((first + step) * height, height), height)
+        total = jnp.dot(rows_ref[lines, :], dense_ref[...], preferred_element_type=jnp.float32)
+        top = jnp.max(jnp.abs(total), axis=0, keepdims=True)
+        unit = jnp.where(top > 0, top, 1.0) * (1.0 / CODE_TOP)
+        power = jnp.floor(jnp.log2(unit))
+        fraction = jnp.ceil(unit * jnp.exp2(-power) * FRACTION)
+        unit = fraction * jnp.exp2(power) * (1.0 / FRACTION)
+        code = jnp.clip(jnp.round(total * (1.0 / unit)), -CODE_TOP, CODE_TOP)
+        code_ref[pl.ds(pl.multiple_of(step * height, height), height), :] = code.astype(jnp.int32).astype(jnp.int16)
+        scale_ref[pl.ds(2 * step, 1), :] = power
+        scale_ref[pl.ds(2 * step + 1, 1), :] = fraction
+
+    tail = scale_ref.shape[0]
+    code_ref[pl.ds(code_ref.shape[0] - tail, tail), :] = scale_ref[...].astype(jnp.int32).astype(jnp.int16)
+
+
+def join_kernel(first, span, height, skips, rows_ref, dense_ref, *refs):
+    code_refs, (out_ref, scale_ref, done_ref, sems) = refs[: len(skips)], refs[-4:]
     tails = [code_ref.shape[0] % height for code_ref in code_refs]
     starts = [sum(tails[:number]) for number in range(len(tails))]
     first_half = lax.rem(lax.axis_index("row"), HALVES) == 0
-
-    @pl.when(step == 0)
-    def _():
-        for code_ref, start, lines in zip(code_refs, starts, tails):
-            scales = code_ref[pl.ds(code_ref.shape[0] - lines, lines), :].astype(jnp.int32).astype(jnp.float32)
-            scale_ref[pl.ds(start, lines), :] = scales
-
-    def decoded(number):
-        block = skips[number] + step
-        power = scale_ref[pl.ds(starts[number] + 2 * block, 1), :]
-        fraction = scale_ref[pl.ds(starts[number] + 2 * block + 1, 1), :]
-        code = code_refs[number][pl.ds(pl.multiple_of(block * height, height), height), :]
-        return code.astype(jnp.int32).astype(jnp.float32) * (fraction * jnp.exp2(power) * (1.0 / FRACTION))
-
-    total = jnp.dot(rows_ref[...], dense_ref[...], preferred_element_type=jnp.float32)
-    for number in range(0, len(code_refs), HALVES):
-        near, far = decoded(number), decoded(number + 1)
-        left = jnp.where(first_half, near, far)
-        right = jnp.where(first_half, far, near)
-        total = total + jnp.concatenate([left, right], axis=1)
-    out_ref[...] = total.astype(out_ref.dtype)
+    for code_ref, start, tail in zip(code_refs, starts, tails):
+        scales = code_ref[pl.ds(code_ref.shape[0] - tail, tail), :].astype(jnp.int32).astype(jnp.float32)
+        scale_ref[pl.ds(start, tail), :] = scales
+
+    def copy(step):
+        lines = pl.ds(pl.multiple_of((first + step) * height, height), height)
+        return pltpu.make_async_copy(done_ref.at[step], out_ref.at[lines, :], sems.at[step])
+
+    @pl.loop(0, span)
+    def _(step):
+        def decoded(number):
+            block = skips[number] + step
+            power = scale_ref[pl.ds(starts[number] + 2 * block, 1), :]
+            fraction = scale_ref[pl.ds(starts[number] + 2 * block + 1, 1), :]
+            code = code_refs[number][pl.ds(pl.multiple_of(block * height, height), height), :]
+            return code.astype(jnp.int32).astype(jnp.float32) * (fraction * jnp.exp2(power) * (1.0 / FRACTION))
+
+        lines = pl.ds(pl.multiple_of((first + step) * height, height), height)
+        total = jnp.dot(rows_ref[lines, :], dense_ref[...], preferred_element_type=jnp.float32)
+        for number in range(0, len(code_refs), HALVES):
+            near, far = decoded(number), decoded(number + 1)
+            left = jnp.where(first_half, near, far)
+            right = jnp.where(first_half, far, near)
+            total = total + jnp.concatenate([left, right], axis=1)
+        done_ref[step] = total.astype(done_ref.dtype)
+        copy(step).start()
+
+    for step in range(span):
+        copy(step).wait()
 
 
 def after(value, *earlier):
@@ -251,15 +270,11 @@
             name="fill",
         )(*held)
 
-    together = SCREEN_BLOCKS if block_count % SCREEN_BLOCKS == 0 else 1
-    row_block = pl.BlockSpec((together * block_rows, full_width), lambda i: (i, 0))
-    wide_block = pl.BlockSpec((together * block_rows, CORES * full_width), lambda i: (i, 0))
     def screen(*earlier):
         return pl.pallas_call(
             partial(screen_kernel, tile_width, block_rows),
-            grid=(block_count // together,),
-            in_specs=[SMEM, row_block, row_block],
-            out_specs=wide_block,
+            in_specs=[SMEM, HBM, VMEM],
+            out_specs=VMEM,
             out_shape=jax.ShapeDtypeStruct((row_count, CORES * full_width), amplitudes.dtype),
             compiler_params=PARAMS,
             cost_estimate=pl.CostEstimate(
@@ -310,13 +325,9 @@
         for offset in remote:
             weights = (near_weights, far_weights)[half][offset]
             code = pl.pallas_call(
-                send_kernel,
-                grid=(span,),
-                in_specs=[
-                    pl.BlockSpec((block_rows, CORES * full_width), lambda i, first=first: (first + i, 0)),
-                    pl.BlockSpec((CORES * full_width, half_width), lambda i: (0, 0)),
-                ],
-                out_specs=pl.BlockSpec(code_shape(span), lambda i: (0, 0)),
+                partial(send_kernel, first, span, block_rows),
+                in_specs=[VMEM, VMEM],
+                out_specs=VMEM,
                 out_shape=jax.ShapeDtypeStruct(code_shape(span), jnp.int16),
                 scratch_shapes=[pltpu.VMEM((scratch_rows(span), half_width), jnp.float32)],
                 compiler_params=PARAMS,
@@ -336,24 +347,21 @@
         received = [part for pair in zip(arrived[0, near_first], arrived[1, far_first]) for part in pair]
         skips = [first - near_first, first - far_first] * len(remote)
         operands = [screened, own_weights, *received]
-        specs = [
-            pl.BlockSpec((block_rows, CORES * full_width), lambda i, first=first: (first + i, 0)),
-            pl.BlockSpec((CORES * full_width, tile_width), lambda i: (0, 0)),
-        ] + [pl.BlockSpec(part.shape, lambda i: (0, 0)) for part in received]
-        body, aliases = partial(join_kernel, skips), {}
+        specs = [VMEM] * len(operands)
+        aliases = {}
         if out is not None:
-            body = partial(skip_operand, len(operands), body)
             aliases = {len(operands): 0}
             operands.append(out)
-            specs.append(pl.BlockSpec(memory_space=pl.ANY))
+            specs.append(HBM)
         out = pl.pallas_call(
-            body,
-            grid=(span,),
+            partial(join_kernel, first, span, block_rows, skips),
             in_specs=specs,
-            out_specs=pl.BlockSpec((block_rows, tile_width), lambda i, first=first: (first + i, 0)),
+            out_specs=HBM,
             out_shape=jax.ShapeDtypeStruct((row_count, tile_width), jnp.bfloat16),
             scratch_shapes=[
-                pltpu.VMEM((sum(part.shape[0] % block_rows for part in received), half_width), jnp.float32)
+                pltpu.VMEM((sum(part.shape[0] % block_rows for part in received), half_width), jnp.float32),
+                pltpu.VMEM((span, block_rows, tile_width), jnp.bfloat16),
+                pltpu.SemaphoreType.DMA((span,)),
             ],
             input_output_aliases=aliases,
             compiler_params=PARAMS,
@@ -361,10 +369,6 @@
             name="join_part",
         )(*operands)
     return out
-
-
-def skip_operand(position, body, *refs):
-    body(*refs[:position], *refs[position + 1 :])
 
 
 def solution(mesh):

time: 74.1 us -> 73.4 us (level)
  waiting for transfers between devices: 20.2 us -> 19.2 us
  transfers between devices with their start and end apart: 22 -> 22, of which waited for: 13 -> 11; matrix products, arithmetic and copies ran while one was open for 2% -> 2% of each run, Pallas kernels for 30% -> 30%
where the time goes in v8:
time: 73.4 us; the launch traced here: 73.1 us
  starting transfers between devices  28.1 us (38%)
  Pallas kernels  23.5 us (32%)
  waiting for transfers between devices  19.2 us (26%)
  other arithmetic  1.5 us (2%)
  between operations  0.83 us (1%)
    ppermute x9, starting transfers between devices, along(): lax.ppermute(value, 'row', [(r, (r + HALVES * shift) % row_peers) for r i...  14.6 us
    ppermute x11, waiting for transfers between devices, across(): return lax.ppermute(value, ('row', 'col'), pairs)  14.2 us
    ppermute x11, starting transfers between devices, across(): return lax.ppermute(value, ('row', 'col'), pairs)  12.9 us
    pallas_call x7, Pallas kernels, shards(): pl.pallas_call(partial(send_kernel, first, span, block_rows), in_specs=[V...  9.87 us
    pallas_call x4, Pallas kernels, shards(): pl.pallas_call(partial(join_kernel, first, span, block_rows, skips), in_s...  7.23 us
    ppermute x9, waiting for transfers between devices, along(): lax.ppermute(value, 'row', [(r, (r + HALVES * shift) % row_peers) for r i...  4.98 us
    pallas_call x1, Pallas kernels, screen(): pl.pallas_call(partial(screen_kernel, tile_width, block_rows), in_specs=[...  4.03 us
  transfers between devices with their start and end apart: 22, of which 11 were waited for; matrix products, arithmetic and copies ran while one was open for 2% of the time, Pallas kernels for 30%

profile of v8, /device:TPU:0, one launch (start us, length us, event | category | flops | bytes accessed | tf_op | source)
XLA Modules:
  0.0 73.1 jit_solution(24437287195210715)
XLA Ops:
  0.0 0.5 collective-permute-start.8
  1.2 0.7 %pad_add_fusion.1.table_ref = s32[7]{0:T(128)S(1)} fusion(s32[4]{0:T(128)} %bitcast.7, s32[1]{0:T(128)} %bitcast.4, s32[2]{0:T(128)} %bitcast.8), kind=kLoop, calls=%fused_computation.1 | loop fusion | flops 14 | bytes 56 | tf_op jit(solution)/shard_map/concatenate | solution.py:236
  1.9 1.0 %pack.1 = (bf16[144,256]{1,0:T(8,128)(2,1)S(1)}, bf16[144,256]{1,0:T(8,128)(2,1)S(1)}, bf16[144,256]{1,0:T(8,128)(2,1)S(1)}, bf16[144,256]{1,0:T(8,128)(2,1)S(1)}) custom-call(s32[7]{0:T(128)S(1)} %pad_add_fusion.1.table_ref, bf16[1,1,2,256,256]{4,3,2,1,0:T(8,128)(2,1)} %panel_ref.1), custom_call_target="tpu_custom_call" | custom-call | tf_op jit(solution)/shard_map/pack/pallas_call | solution.py:238
  2.9 3.1 %collective-permute-start.1 = (bf16[144,256]{1,0:T(8,128)(2,1)S(1)}, bf16[144,256]{1,0:T(8,128)(2,1)S(1)}, u32[]{:S(2)}, u32[]{:S(2)}) collective-permute-start(bf16[144,256]{1,0:T(8,128)(2,1)S(1)} %get-tuple-element.24), channel_id=1, source_target_pairs={{0,8},{4,12},{8,16},{12,20},{16,24},{20,28},{24,0},{28,4},{1,9},{5... | collective-permute-start | bytes 221192 | tf_op jit(solution)/shard_map/ppermute | solution.py:221
  6.0 2.6 %collective-permute-start.2 = (bf16[144,256]{1,0:T(8,128)(2,1)S(1)}, bf16[144,256]{1,0:T(8,128)(2,1)S(1)}, u32[]{:S(2)}, u32[]{:S(2)}) collective-permute-start(bf16[144,256]{1,0:T(8,128)(2,1)S(1)} %get-tuple-element.25), channel_id=1, source_target_pairs={{0,16},{4,20},{8,24},{12,28},{16,0},{20,4},{24,8},{28,12},{1,17},{... | collective-permute-start | bytes 221192 | tf_op jit(solution)/shard_map/ppermute | solution.py:221
  8.6 1.3 %collective-permute-start.3 = (bf16[144,256]{1,0:T(8,128)(2,1)S(1)}, bf16[144,256]{1,0:T(8,128)(2,1)S(1)}, u32[]{:S(2)}, u32[]{:S(2)}) collective-permute-start(bf16[144,256]{1,0:T(8,128)(2,1)S(1)} %get-tuple-element.26), channel_id=1, source_target_pairs={{0,24},{4,28},{8,0},{12,4},{16,8},{20,12},{24,16},{28,20},{1,25},{... | collective-permute-start | bytes 221192 | tf_op jit(solution)/shard_map/ppermute | solution.py:221
  10.0 0.7 pad_add_fusion.mask_ref
  10.9 2.9 %collective-permute-done.2.refs_2_ = bf16[144,256]{1,0:T(8,128)(2,1)S(1)} collective-permute-done((bf16[144,256]{1,0:T(8,128)(2,1)S(1)}, bf16[144,256]{1,0:T(8,128)(2,1)S(1)}, u32[]{:S(2)}, u32[]{:S(2)}) %collective-permute-start.2) | collective-permute-done | bytes 73760 | tf_op jit(solution)/shard_map/ppermute | solution.py:221
  14.0 0.7 choose.1
  14.7 1.6 %collective-permute-start.4 = (bf16[272,128]{1,0:T(8,128)(2,1)S(1)}, bf16[272,128]{1,0:T(8,128)(2,1)S(1)}, u32[]{:S(2)}, u32[]{:S(2)}) collective-permute-start(bf16[272,128]{1,0:T(8,128)(2,1)S(1)} %get-tuple-element.27), channel_id=1, source_target_pairs={{0,2},{1,3},{2,0},{3,1},{4,6},{5,7},{6,4},{7,5},{8,10},{9,11},{10,... | collective-permute-start | bytes 208904 | tf_op jit(solution)/shard_map/ppermute | solution.py:228
  16.2 1.5 %collective-permute-start.5 = (bf16[272,128]{1,0:T(8,128)(2,1)S(1)}, bf16[272,128]{1,0:T(8,128)(2,1)S(1)}, u32[]{:S(2)}, u32[]{:S(2)}) collective-permute-start(bf16[272,128]{1,0:T(8,128)(2,1)S(1)} %get-tuple-element.28), channel_id=1, source_target_pairs={{0,6},{1,7},{2,4},{3,5},{4,2},{5,3},{6,0},{7,1},{8,14},{9,15},{10,... | collective-permute-start | bytes 208904 | tf_op jit(solution)/shard_map/ppermute | solution.py:228
  17.7 0.5 collective-permute-start.7
  18.2 0.8 %collective-permute-done.4 = bf16[272,128]{1,0:T(8,128)(2,1)S(1)} collective-permute-done((bf16[272,128]{1,0:T(8,128)(2,1)S(1)}, bf16[272,128]{1,0:T(8,128)(2,1)S(1)}, u32[]{:S(2)}, u32[]{:S(2)}) %collective-permute-start.4) | collective-permute-done | bytes 69664 | tf_op jit(solution)/shard_map/ppermute | solution.py:228
  19.1 2.5 %collective-permute-done.5 = bf16[272,128]{1,0:T(8,128)(2,1)S(1)} collective-permute-done((bf16[272,128]{1,0:T(8,128)(2,1)S(1)}, bf16[272,128]{1,0:T(8,128)(2,1)S(1)}, u32[]{:S(2)}, u32[]{:S(2)}) %collective-permute-start.5) | collective-permute-done | bytes 69664 | tf_op jit(solution)/shard_map/ppermute | solution.py:228
  21.6 3.1 %collective-permute-start.6 = (bf16[272,128]{1,0:T(8,128)(2,1)S(1)}, bf16[272,128]{1,0:T(8,128)(2,1)S(1)}, u32[]{:S(2)}, u32[]{:S(2)}) collective-permute-start(bf16[272,128]{1,0:T(8,128)(2,1)S(1)} %add.6.refs_0_), channel_id=1, source_target_pairs={{0,24},{4,28},{8,0},{12,4},{16,8},{20,12},{24,16},{28,20},{1,25},{... | collective-permute-start | bytes 208904 | tf_op jit(solution)/shard_map/ppermute | solution.py:221
  24.7 0.3 collective-permute-start.10
  25.0 0.4 collective-permute-start.9
  25.4 1.3 %collective-permute-done.6.refs_3_ = bf16[272,128]{1,0:T(8,128)(2,1)S(1)} collective-permute-done((bf16[272,128]{1,0:T(8,128)(2,1)S(1)}, bf16[272,128]{1,0:T(8,128)(2,1)S(1)}, u32[]{:S(2)}, u32[]{:S(2)}) %collective-permute-start.6) | collective-permute-done | bytes 69664 | tf_op jit(solution)/shard_map/ppermute | solution.py:221
  26.6 4.0 %screen.1.rows_ref = bf16[3072,1536]{1,0:T(8,128)(2,1)S(1)} custom-call(s32[6,12]{1,0:T(8,128)S(1)} %pad_add_fusion.mask_ref, bf16[3072,768]{1,0:T(8,128)(2,1)} %own_ref.1, bf16[3072,768]{1,0:T(8,128)(2,1)S(1)} %collective-permute-done.8.other_ref), custom_call_target="tpu_custom_call" | custom-call | flops 4718592 | bytes 18874368 | tf_op jit(solution)/shard_map/screen/pallas_call | solution.py:274
  30.7 0.4 collective-permute-done.9.refs_1_
  31.1 0.3 fill.2.dense_ref
  31.4 1.5 %collective-permute-start.15 = (bf16[1536,128]{1,0:T(8,128)(2,1)S(1)}, bf16[1536,128]{1,0:T(8,128)(2,1)S(1)}, u32[]{:S(2)}, u32[]{:S(2)}) collective-permute-start(bf16[1536,128]{1,0:T(8,128)(2,1)S(1)} %fill.2.dense_ref), channel_id=1, source_target_pairs={{0,4},{1,5},{2,6},{3,7},{4,0},{5,1},{6,2},{7,3},{8,12},{9,13},{10,... | collective-permute-start | bytes 1179656 | tf_op jit(solution)/shard_map/ppermute | solution.py:228
  32.9 0.8 %send_part.7 = s16[528,128]{1,0:T(8,128)(2,1)S(1)} custom-call(bf16[3072,1536]{1,0:T(8,128)(2,1)S(1)} %screen.1.rows_ref, bf16[1536,128]{1,0:T(8,128)(2,1)S(1)} %fill.2.dense_ref), custom_call_target="tpu_custom_call" | custom-call | flops 201326592 | bytes 1703936 | tf_op jit(solution)/shard_map/send_part/pallas_call | solution.py:327
  33.7 0.6 collective-permute-start.11
  34.4 2.1 %send_part.8 = s16[1296,128]{1,0:T(8,128)(2,1)S(1)} custom-call(bf16[3072,1536]{1,0:T(8,128)(2,1)S(1)} %screen.1.rows_ref, bf16[1536,128]{1,0:T(8,128)(2,1)S(1)} %fill.2.dense_ref), custom_call_target="tpu_custom_call" | custom-call | flops 503316480 | bytes 4259840 | tf_op jit(solution)/shard_map/send_part/pallas_call | solution.py:327
  36.4 1.5 %collective-permute-start.17 = (s16[1296,128]{1,0:T(8,128)(2,1)S(1)}, s16[1296,128]{1,0:T(8,128)(2,1)S(1)}, u32[]{:S(2)}, u32[]{:S(2)}) collective-permute-start(s16[1296,128]{1,0:T(8,128)(2,1)S(1)} %send_part.8), channel_id=1, source_target_pairs={{0,2},{1,3},{2,0},{3,1},{4,6},{5,7},{6,4},{7,5},{8,10},{9,11},{10,... | collective-permute-start | bytes 995336 | tf_op jit(solution)/shard_map/ppermute | solution.py:228
  37.9 2.3 %collective-permute-done.11.refs_0_ = s16[528,128]{1,0:T(8,128)(2,1)S(1)} collective-permute-done((s16[528,128]{1,0:T(8,128)(2,1)S(1)}, s16[528,128]{1,0:T(8,128)(2,1)S(1)}, u32[]{:S(2)}, u32[]{:S(2)}) %collective-permute-start.11) | collective-permute-done | bytes 135200 | tf_op jit(solution)/shard_map/ppermute | solution.py:228
  40.2 0.4 collective-permute-done.15.dense_ref
  40.7 2.1 %send_part.9 = s16[1296,128]{1,0:T(8,128)(2,1)S(1)} custom-call(bf16[3072,1536]{1,0:T(8,128)(2,1)S(1)} %screen.1.rows_ref, bf16[1536,128]{1,0:T(8,128)(2,1)S(1)} %fill.2.dense_ref), custom_call_target="tpu_custom_call" | custom-call | flops 503316480 | bytes 4259840 | tf_op jit(solution)/shard_map/send_part/pallas_call | solution.py:327
  42.7 0.9 %collective-permute-start.16 = (s16[1296,128]{1,0:T(8,128)(2,1)S(1)}, s16[1296,128]{1,0:T(8,128)(2,1)S(1)}, u32[]{:S(2)}, u32[]{:S(2)}) collective-permute-start(s16[1296,128]{1,0:T(8,128)(2,1)S(1)} %send_part.9), channel_id=1, source_target_pairs={{0,2},{1,3},{2,0},{3,1},{4,6},{5,7},{6,4},{7,5},{8,10},{9,11},{10,... | collective-permute-start | bytes 995336 | tf_op jit(solution)/shard_map/ppermute | solution.py:228
  43.7 3.3 %collective-permute-start.14 = (bf16[272,256]{1,0:T(8,128)(2,1)S(1)}, bf16[272,256]{1,0:T(8,128)(2,1)S(1)}, u32[]{:S(2)}, u32[]{:S(2)}) collective-permute-start(bf16[272,256]{1,0:T(8,128)(2,1)S(1)} %add.7.refs_0_), channel_id=1, source_target_pairs={{0,24},{4,28},{8,0},{12,4},{16,8},{20,12},{24,16},{28,20},{1,25},{... | collective-permute-start | bytes 417800 | tf_op jit(solution)/shard_map/ppermute | solution.py:221
  46.9 0.3 collective-permute-start.13
  47.2 0.3 collective-permute-start.12
  47.5 0.8 %send_part.10 = s16[528,128]{1,0:T(8,128)(2,1)S(1)} custom-call(bf16[3072,1536]{1,0:T(8,128)(2,1)S(1)} %screen.1.rows_ref, bf16[1536,128]{1,0:T(8,128)(2,1)S(1)} %collective-permute-done.15.dense_ref), custom_call_target="tpu_custom_call" | custom-call | flops 201326592 | bytes 1703936 | tf_op jit(solution)/shard_map/send_part/pallas_call | solution.py:327
  48.3 1.6 %collective-permute-start.18 = (s16[528,128]{1,0:T(8,128)(2,1)S(1)}, s16[528,128]{1,0:T(8,128)(2,1)S(1)}, u32[]{:S(2)}, u32[]{:S(2)}) collective-permute-start(s16[528,128]{1,0:T(8,128)(2,1)S(1)} %send_part.10), channel_id=1, source_target_pairs={{0,2},{1,3},{2,0},{3,1},{4,6},{5,7},{6,4},{7,5},{8,10},{9,11},{10,... | collective-permute-start | bytes 405512 | tf_op jit(solution)/shard_map/ppermute | solution.py:228
  49.9 3.7 %collective-permute-done.16.refs_0_ = s16[1296,128]{1,0:T(8,128)(2,1)S(1)} collective-permute-done((s16[1296,128]{1,0:T(8,128)(2,1)S(1)}, s16[1296,128]{1,0:T(8,128)(2,1)S(1)}, u32[]{:S(2)}, u32[]{:S(2)}) %collective-permute-start.16) | collective-permute-done | bytes 331808 | tf_op jit(solution)/shard_map/ppermute | solution.py:228
  53.6 2.1 %send_part.11 = s16[1296,128]{1,0:T(8,128)(2,1)S(1)} custom-call(bf16[3072,1536]{1,0:T(8,128)(2,1)S(1)} %screen.1.rows_ref, bf16[1536,128]{1,0:T(8,128)(2,1)S(1)} %collective-permute-done.15.dense_ref), custom_call_target="tpu_custom_call" | custom-call | flops 503316480 | bytes 4259840 | tf_op jit(solution)/shard_map/send_part/pallas_call | solution.py:327
  55.7 1.1 %collective-permute-start.19 = (s16[1296,128]{1,0:T(8,128)(2,1)S(1)}, s16[1296,128]{1,0:T(8,128)(2,1)S(1)}, u32[]{:S(2)}, u32[]{:S(2)}) collective-permute-start(s16[1296,128]{1,0:T(8,128)(2,1)S(1)} %send_part.11), channel_id=1, source_target_pairs={{0,2},{1,3},{2,0},{3,1},{4,6},{5,7},{6,4},{7,5},{8,10},{9,11},{10,... | collective-permute-start | bytes 995336 | tf_op jit(solution)/shard_map/ppermute | solution.py:228
  56.8 0.3 fill.3.dense_ref
  57.1 1.6 %send_part.12 = s16[1040,128]{1,0:T(8,128)(2,1)S(1)} custom-call(bf16[3072,1536]{1,0:T(8,128)(2,1)S(1)} %screen.1.rows_ref, bf16[1536,128]{1,0:T(8,128)(2,1)S(1)} %collective-permute-done.15.dense_ref), custom_call_target="tpu_custom_call" | custom-call | flops 402653184 | bytes 3407872 | tf_op jit(solution)/shard_map/send_part/pallas_call | solution.py:327
  58.8 1.1 %collective-permute-start.21 = (s16[1040,128]{1,0:T(8,128)(2,1)S(1)}, s16[1040,128]{1,0:T(8,128)(2,1)S(1)}, u32[]{:S(2)}, u32[]{:S(2)}) collective-permute-start(s16[1040,128]{1,0:T(8,128)(2,1)S(1)} %send_part.12), channel_id=1, source_target_pairs={{0,2},{1,3},{2,0},{3,1},{4,6},{5,7},{6,4},{7,5},{8,10},{9,11},{10,... | collective-permute-start | bytes 798728 | tf_op jit(solution)/shard_map/ppermute | solution.py:228
  59.8 1.4 %join_part.4.refs_2_ = bf16[3072,256]{1,0:T(8,128)(2,1)} custom-call(bf16[3072,1536]{1,0:T(8,128)(2,1)S(1)} %screen.1.rows_ref, bf16[1536,256]{1,0:T(8,128)(2,1)S(1)} %fill.3.dense_ref, s16[528,128]{1,0:T(8,128)(2,1)S(1)} %collective-permute-done.11.refs_0_, s16[528,128]{1,0:T(8,128)(2,1)S(1)} %collective-permute-done.18.refs_1_), custom_call_target="tpu_custom_call" | custom-call | flops 402653184 | bytes 1835008 | tf_op jit(solution)/shard_map/join_part/pallas_call | solution.py:356
  61.3 4.5 %collective-permute-done.19.refs_1_ = s16[1296,128]{1,0:T(8,128)(2,1)S(1)} collective-permute-done((s16[1296,128]{1,0:T(8,128)(2,1)S(1)}, s16[1296,128]{1,0:T(8,128)(2,1)S(1)}, u32[]{:S(2)}, u32[]{:S(2)}) %collective-permute-start.19) | collective-permute-done | bytes 331808 | tf_op jit(solution)/shard_map/ppermute | solution.py:228
  65.8 0.4 send_part.13
  66.2 1.1 %collective-permute-start.20 = (s16[272,128]{1,0:T(8,128)(2,1)S(1)}, s16[272,128]{1,0:T(8,128)(2,1)S(1)}, u32[]{:S(2)}, u32[]{:S(2)}) collective-permute-start(s16[272,128]{1,0:T(8,128)(2,1)S(1)} %send_part.13), channel_id=1, source_target_pairs={{0,2},{1,3},{2,0},{3,1},{4,6},{5,7},{6,4},{7,5},{8,10},{9,11},{10,... | collective-permute-start | bytes 208904 | tf_op jit(solution)/shard_map/ppermute | solution.py:228
  67.3 2.6 %join_part.5.refs_2_ = bf16[3072,256]{1,0:T(8,128)(2,1)} custom-call(bf16[3072,1536]{1,0:T(8,128)(2,1)S(1)} %screen.1.rows_ref, bf16[1536,256]{1,0:T(8,128)(2,1)S(1)} %fill.3.dense_ref, s16[1296,128]{1,0:T(8,128)(2,1)S(1)} %collective-permute-done.17.refs_0_, s16[1296,128]{1,0:T(8,128)(2,1)S(1)} %collective-permute-done.19.refs_1_, ...), custom_call_target="tpu_custom_call", output_to_operand_aliasing={{}: (4, {})} | custom-call | flops 1006632960 | bytes 4587520 | tf_op jit(solution)/shard_map/join_part/pallas_call | solution.py:356
  69.8 2.2 %join_part.6.refs_2_ = bf16[3072,256]{1,0:T(8,128)(2,1)} custom-call(bf16[3072,1536]{1,0:T(8,128)(2,1)S(1)} %screen.1.rows_ref, bf16[1536,256]{1,0:T(8,128)(2,1)S(1)} %fill.3.dense_ref, s16[1296,128]{1,0:T(8,128)(2,1)S(1)} %collective-permute-done.16.refs_0_, s16[1040,128]{1,0:T(8,128)(2,1)S(1)} %collective-permute-done.21.refs_1_, ...), custom_call_target="tpu_custom_call", output_to_operand_aliasing={{}: (4, {})} | custom-call | flops 805306368 | bytes 3670016 | tf_op jit(solution)/shard_map/join_part/pallas_call | solution.py:356
  72.1 1.0 %join_part.7 = bf16[3072,256]{1,0:T(8,128)(2,1)} custom-call(bf16[3072,1536]{1,0:T(8,128)(2,1)S(1)} %screen.1.rows_ref, bf16[1536,256]{1,0:T(8,128)(2,1)S(1)} %fill.3.dense_ref, s16[1296,128]{1,0:T(8,128)(2,1)S(1)} %collective-permute-done.16.refs_0_, s16[272,128]{1,0:T(8,128)(2,1)S(1)} %collective-permute-done.20.refs_1_, ...), custom_call_target="tpu_custom_call", output_to_operand_aliasing={{}: (4, {})} | custom-call | flops 201326592 | bytes 917504 | tf_op jit(solution)/shard_map/join_part/pallas_call | solution.py:356
  (16 shorter events, 0.6 us)
Async XLA Ops:
  0.0 26.6 %collective-permute-start.8 = (bf16[3072,768]{1,0:T(8,128)(2,1)}, bf16[3072,768]{1,0:T(8,128)(2,1)S(1)}, u32[]{:S(2)}, u32[]{:S(2)}) collective-permute-start(bf16[3072,768]{1,0:T(8,128)(2,1)} %own_ref.1), channel_id=1, source_target_pairs={{0,1},{1,0},{2,3},{3,2},{4,5},{5,4},{6,7},{7,6},{8,9},{9,8},{10,11... | collective-permute-start | bytes 14155784 | tf_op jit(solution)/shard_map/ppermute | solution.py:231
  0.5 9.5 %collective-permute-start = (s32[3,12]{1,0:T(4,128)}, s32[3,12]{1,0:T(4,128)S(1)}, u32[]{:S(2)}, u32[]{:S(2)}) collective-permute-start(s32[3,12]{1,0:T(4,128)} %bitcast.5), channel_id=1, source_target_pairs={{0,1},{1,0},{2,3},{3,2},{4,5},{5,4},{6,7},{7,6},{8,9},{9,8},{10,11... | collective-permute-start | bytes 440 | tf_op jit(solution)/shard_map/ppermute | solution.py:232
  2.9 7.9 %collective-permute-start.1 = (bf16[144,256]{1,0:T(8,128)(2,1)S(1)}, bf16[144,256]{1,0:T(8,128)(2,1)S(1)}, u32[]{:S(2)}, u32[]{:S(2)}) collective-permute-start(bf16[144,256]{1,0:T(8,128)(2,1)S(1)} %get-tuple-element.24), channel_id=1, source_target_pairs={{0,8},{4,12},{8,16},{12,20},{16,24},{20,28},{24,0},{28,4},{1,9},{5... | collective-permute-start | bytes 221192 | tf_op jit(solution)/shard_map/ppermute | solution.py:221
  6.0 7.7 %collective-permute-start.2 = (bf16[144,256]{1,0:T(8,128)(2,1)S(1)}, bf16[144,256]{1,0:T(8,128)(2,1)S(1)}, u32[]{:S(2)}, u32[]{:S(2)}) collective-permute-start(bf16[144,256]{1,0:T(8,128)(2,1)S(1)} %get-tuple-element.25), channel_id=1, source_target_pairs={{0,16},{4,20},{8,24},{12,28},{16,0},{20,4},{24,8},{28,12},{1,17},{... | collective-permute-start | bytes 221192 | tf_op jit(solution)/shard_map/ppermute | solution.py:221
  8.6 5.4 %collective-permute-start.3 = (bf16[144,256]{1,0:T(8,128)(2,1)S(1)}, bf16[144,256]{1,0:T(8,128)(2,1)S(1)}, u32[]{:S(2)}, u32[]{:S(2)}) collective-permute-start(bf16[144,256]{1,0:T(8,128)(2,1)S(1)} %get-tuple-element.26), channel_id=1, source_target_pairs={{0,24},{4,28},{8,0},{12,4},{16,8},{20,12},{24,16},{28,20},{1,25},{... | collective-permute-start | bytes 221192 | tf_op jit(solution)/shard_map/ppermute | solution.py:221
  14.7 4.4 %collective-permute-start.4 = (bf16[272,128]{1,0:T(8,128)(2,1)S(1)}, bf16[272,128]{1,0:T(8,128)(2,1)S(1)}, u32[]{:S(2)}, u32[]{:S(2)}) collective-permute-start(bf16[272,128]{1,0:T(8,128)(2,1)S(1)} %get-tuple-element.27), channel_id=1, source_target_pairs={{0,2},{1,3},{2,0},{3,1},{4,6},{5,7},{6,4},{7,5},{8,10},{9,11},{10,... | collective-permute-start | bytes 208904 | tf_op jit(solution)/shard_map/ppermute | solution.py:228
  16.2 5.3 %collective-permute-start.5 = (bf16[272,128]{1,0:T(8,128)(2,1)S(1)}, bf16[272,128]{1,0:T(8,128)(2,1)S(1)}, u32[]{:S(2)}, u32[]{:S(2)}) collective-permute-start(bf16[272,128]{1,0:T(8,128)(2,1)S(1)} %get-tuple-element.28), channel_id=1, source_target_pairs={{0,6},{1,7},{2,4},{3,5},{4,2},{5,3},{6,0},{7,1},{8,14},{9,15},{10,... | collective-permute-start | bytes 208904 | tf_op jit(solution)/shard_map/ppermute | solution.py:228
  17.7 7.6 %collective-permute-start.7 = (bf16[272,256]{1,0:T(8,128)(2,1)S(1)}, bf16[272,256]{1,0:T(8,128)(2,1)S(1)}, u32[]{:S(2)}, u32[]{:S(2)}) collective-permute-start(bf16[272,256]{1,0:T(8,128)(2,1)S(1)} %get-tuple-element.29), channel_id=1, source_target_pairs={{0,4},{1,5},{2,6},{3,7},{4,0},{5,1},{6,2},{7,3},{8,12},{9,13},{10,... | collective-permute-start | bytes 417800 | tf_op jit(solution)/shard_map/ppermute | solution.py:228
  21.6 5.1 %collective-permute-start.6 = (bf16[272,128]{1,0:T(8,128)(2,1)S(1)}, bf16[272,128]{1,0:T(8,128)(2,1)S(1)}, u32[]{:S(2)}, u32[]{:S(2)}) collective-permute-start(bf16[272,128]{1,0:T(8,128)(2,1)S(1)} %add.6.refs_0_), channel_id=1, source_target_pairs={{0,24},{4,28},{8,0},{12,4},{16,8},{20,12},{24,16},{28,20},{1,25},{... | collective-permute-start | bytes 208904 | tf_op jit(solution)/shard_map/ppermute | solution.py:221
  24.7 6.0 %collective-permute-start.10 = (bf16[272,128]{1,0:T(8,128)(2,1)S(1)}, bf16[272,128]{1,0:T(8,128)(2,1)S(1)}, u32[]{:S(2)}, u32[]{:S(2)}) collective-permute-start(bf16[272,128]{1,0:T(8,128)(2,1)S(1)} %add.6.refs_0_), channel_id=1, source_target_pairs={{0,16},{4,20},{8,24},{12,28},{16,0},{20,4},{24,8},{28,12},{1,17},{... | collective-permute-start | bytes 208904 | tf_op jit(solution)/shard_map/ppermute | solution.py:221
  25.0 6.1 %collective-permute-start.9 = (bf16[272,128]{1,0:T(8,128)(2,1)S(1)}, bf16[272,128]{1,0:T(8,128)(2,1)S(1)}, u32[]{:S(2)}, u32[]{:S(2)}) collective-permute-start(bf16[272,128]{1,0:T(8,128)(2,1)S(1)} %add.6.refs_0_), channel_id=1, source_target_pairs={{0,8},{4,12},{8,16},{12,20},{16,24},{20,28},{24,0},{28,4},{1,9},{5... | collective-permute-start | bytes 208904 | tf_op jit(solution)/shard_map/ppermute | solution.py:221
  31.4 9.2 %collective-permute-start.15 = (bf16[1536,128]{1,0:T(8,128)(2,1)S(1)}, bf16[1536,128]{1,0:T(8,128)(2,1)S(1)}, u32[]{:S(2)}, u32[]{:S(2)}) collective-permute-start(bf16[1536,128]{1,0:T(8,128)(2,1)S(1)} %fill.2.dense_ref), channel_id=1, source_target_pairs={{0,4},{1,5},{2,6},{3,7},{4,0},{5,1},{6,2},{7,3},{8,12},{9,13},{10,... | collective-permute-start | bytes 1179656 | tf_op jit(solution)/shard_map/ppermute | solution.py:228
  33.7 6.5 %collective-permute-start.11 = (s16[528,128]{1,0:T(8,128)(2,1)S(1)}, s16[528,128]{1,0:T(8,128)(2,1)S(1)}, u32[]{:S(2)}, u32[]{:S(2)}) collective-permute-start(s16[528,128]{1,0:T(8,128)(2,1)S(1)} %send_part.7), channel_id=1, source_target_pairs={{0,2},{1,3},{2,0},{3,1},{4,6},{5,7},{6,4},{7,5},{8,10},{9,11},{10,... | collective-permute-start | bytes 405512 | tf_op jit(solution)/shard_map/ppermute | solution.py:228
  36.4 11.1 %collective-permute-start.17 = (s16[1296,128]{1,0:T(8,128)(2,1)S(1)}, s16[1296,128]{1,0:T(8,128)(2,1)S(1)}, u32[]{:S(2)}, u32[]{:S(2)}) collective-permute-start(s16[1296,128]{1,0:T(8,128)(2,1)S(1)} %send_part.8), channel_id=1, source_target_pairs={{0,2},{1,3},{2,0},{3,1},{4,6},{5,7},{6,4},{7,5},{8,10},{9,11},{10,... | collective-permute-start | bytes 995336 | tf_op jit(solution)/shard_map/ppermute | solution.py:228
  42.7 10.9 %collective-permute-start.16 = (s16[1296,128]{1,0:T(8,128)(2,1)S(1)}, s16[1296,128]{1,0:T(8,128)(2,1)S(1)}, u32[]{:S(2)}, u32[]{:S(2)}) collective-permute-start(s16[1296,128]{1,0:T(8,128)(2,1)S(1)} %send_part.9), channel_id=1, source_target_pairs={{0,2},{1,3},{2,0},{3,1},{4,6},{5,7},{6,4},{7,5},{8,10},{9,11},{10,... | collective-permute-start | bytes 995336 | tf_op jit(solution)/shard_map/ppermute | solution.py:228
  43.7 13.1 %collective-permute-start.14 = (bf16[272,256]{1,0:T(8,128)(2,1)S(1)}, bf16[272,256]{1,0:T(8,128)(2,1)S(1)}, u32[]{:S(2)}, u32[]{:S(2)}) collective-permute-start(bf16[272,256]{1,0:T(8,128)(2,1)S(1)} %add.7.refs_0_), channel_id=1, source_target_pairs={{0,24},{4,28},{8,0},{12,4},{16,8},{20,12},{24,16},{28,20},{1,25},{... | collective-permute-start | bytes 417800 | tf_op jit(solution)/shard_map/ppermute | solution.py:221
  46.9 9.8 %collective-permute-start.13 = (bf16[272,256]{1,0:T(8,128)(2,1)S(1)}, bf16[272,256]{1,0:T(8,128)(2,1)S(1)}, u32[]{:S(2)}, u32[]{:S(2)}) collective-permute-start(bf16[272,256]{1,0:T(8,128)(2,1)S(1)} %add.7.refs_0_), channel_id=1, source_target_pairs={{0,16},{4,20},{8,24},{12,28},{16,0},{20,4},{24,8},{28,12},{1,17},{... | collective-permute-start | bytes 417800 | tf_op jit(solution)/shard_map/ppermute | solution.py:221
  47.2 9.5 %collective-permute-start.12 = (bf16[272,256]{1,0:T(8,128)(2,1)S(1)}, bf16[272,256]{1,0:T(8,128)(2,1)S(1)}, u32[]{:S(2)}, u32[]{:S(2)}) collective-permute-start(bf16[272,256]{1,0:T(8,128)(2,1)S(1)} %add.7.refs_0_), channel_id=1, source_target_pairs={{0,8},{4,12},{8,16},{12,20},{16,24},{20,28},{24,0},{28,4},{1,9},{5... | collective-permute-start | bytes 417800 | tf_op jit(solution)/shard_map/ppermute | solution.py:221
  48.3 8.8 %collective-permute-start.18 = (s16[528,128]{1,0:T(8,128)(2,1)S(1)}, s16[528,128]{1,0:T(8,128)(2,1)S(1)}, u32[]{:S(2)}, u32[]{:S(2)}) collective-permute-start(s16[528,128]{1,0:T(8,128)(2,1)S(1)} %send_part.10), channel_id=1, source_target_pairs={{0,2},{1,3},{2,0},{3,1},{4,6},{5,7},{6,4},{7,5},{8,10},{9,11},{10,... | collective-permute-start | bytes 405512 | tf_op jit(solution)/shard_map/ppermute | solution.py:228
  55.7 10.1 %collective-permute-start.19 = (s16[1296,128]{1,0:T(8,128)(2,1)S(1)}, s16[1296,128]{1,0:T(8,128)(2,1)S(1)}, u32[]{:S(2)}, u32[]{:S(2)}) collective-permute-start(s16[1296,128]{1,0:T(8,128)(2,1)S(1)} %send_part.11), channel_id=1, source_target_pairs={{0,2},{1,3},{2,0},{3,1},{4,6},{5,7},{6,4},{7,5},{8,10},{9,11},{10,... | collective-permute-start | bytes 995336 | tf_op jit(solution)/shard_map/ppermute | solution.py:228
  58.8 11.1 %collective-permute-start.21 = (s16[1040,128]{1,0:T(8,128)(2,1)S(1)}, s16[1040,128]{1,0:T(8,128)(2,1)S(1)}, u32[]{:S(2)}, u32[]{:S(2)}) collective-permute-start(s16[1040,128]{1,0:T(8,128)(2,1)S(1)} %send_part.12), channel_id=1, source_target_pairs={{0,2},{1,3},{2,0},{3,1},{4,6},{5,7},{6,4},{7,5},{8,10},{9,11},{10,... | collective-permute-start | bytes 798728 | tf_op jit(solution)/shard_map/ppermute | solution.py:228
  66.2 5.9 %collective-permute-start.20 = (s16[272,128]{1,0:T(8,128)(2,1)S(1)}, s16[272,128]{1,0:T(8,128)(2,1)S(1)}, u32[]{:S(2)}, u32[]{:S(2)}) collective-permute-start(s16[272,128]{1,0:T(8,128)(2,1)S(1)} %send_part.13), channel_id=1, source_target_pairs={{0,2},{1,3},{2,0},{3,1},{4,6},{5,7},{6,4},{7,5},{8,10},{9,11},{10,... | collective-permute-start | bytes 208904 | tf_op jit(solution)/shard_map/ppermute | solution.py:228

commit v9 on v8

--- a/solution.py
+++ b/solution.py
@@ -36,16 +36,16 @@
     return [(first, last - first) for first, last in zip(marks, marks[1:])]
 
 
-def pack_kernel(table_ref, panel_ref, *piece_refs):
+def pack_kernel(list_ref, count_ref, panel_ref, *piece_refs):
     peers = len(piece_refs)
     slots, tile_width = panel_ref.shape[2:4]
     share = slots * tile_width // peers
     place = lax.axis_index("row") // HALVES
     lane = lax.broadcasted_iota(jnp.int32, (META_ROWS, tile_width), 1)
     lane = lax.rem(lane, tile_width // HALVES)
-    info = jnp.zeros((META_ROWS, tile_width), jnp.int32)
-    for spot in range(slots + 1):
-        info = jnp.where(lane == spot, table_ref[spot], info)
+    info = jnp.where(lane == slots, count_ref[0, 0], 0)
+    for slot in range(slots):
+        info = jnp.where(lane == slot, jnp.broadcast_to(list_ref[0, :, slot : slot + 1], lane.shape), info)
     info = info.astype(jnp.float32).astype(panel_ref.dtype)
     for shift, piece_ref in enumerate(piece_refs):
         first = lax.rem(place + shift, peers) * share
@@ -54,7 +54,7 @@
         piece_ref[pl.ds(share, META_ROWS), :] = info
 
 
-def choose_kernel(col_peers, offsets, slots, peers, table_ref, *refs):
+def choose_kernel(col_peers, offsets, peers, plan_ref, *refs):
     piece_refs, out_refs = refs[:peers], list(refs[peers:])
     share, tile_width = piece_refs[0].shape[0] - META_ROWS, piece_refs[0].shape[1]
     half_width = tile_width // HALVES
@@ -72,7 +72,7 @@
             out_ref[...] = jnp.zeros_like(out_ref)
         for group, shift in enumerate((0, sign)):
             step = lax.rem(CORES * offset - shift + col_peers, col_peers)
-            holder = table_ref[slots + 1 + jnp.minimum(step, STEPS - 1)]
+            holder = plan_ref[plan_ref.shape[0] - 1, jnp.minimum(step, STEPS - 1)]
             here = (step < STEPS) & (lax.rem(holder, HALVES) == half)
             back = lax.rem(row // HALVES - holder // HALVES + peers, peers)
             for number, piece_ref in enumerate(piece_refs):
@@ -144,21 +144,18 @@
 
 def send_kernel(first, span, height, rows_ref, dense_ref, code_ref, scale_ref):
     scale_ref[...] = jnp.zeros_like(scale_ref)
-
-    @pl.loop(0, span)
-    def _(step):
-        lines = pl.ds(pl.multiple_of((first + step) * height, height), height)
-        total = jnp.dot(rows_ref[lines, :], dense_ref[...], preferred_element_type=jnp.float32)
+    sums = jnp.dot(rows_ref[pl.ds(first * height, span * height), :], dense_ref[...], preferred_element_type=jnp.float32)
+    for step in range(span):
+        total = sums[step * height : (step + 1) * height]
         top = jnp.max(jnp.abs(total), axis=0, keepdims=True)
         unit = jnp.where(top > 0, top, 1.0) * (1.0 / CODE_TOP)
         power = jnp.floor(jnp.log2(unit))
         fraction = jnp.ceil(unit * jnp.exp2(-power) * FRACTION)
         unit = fraction * jnp.exp2(power) * (1.0 / FRACTION)
         code = jnp.clip(jnp.round(total * (1.0 / unit)), -CODE_TOP, CODE_TOP)
-        code_ref[pl.ds(pl.multiple_of(step * height, height), height), :] = code.astype(jnp.int32).astype(jnp.int16)
+        code_ref[pl.ds(step * height, height), :] = code.astype(jnp.int32).astype(jnp.int16)
         scale_ref[pl.ds(2 * step, 1), :] = power
         scale_ref[pl.ds(2 * step + 1, 1), :] = fraction
-
     tail = scale_ref.shape[0]
     code_ref[pl.ds(code_ref.shape[0] - tail, tail), :] = scale_ref[...].astype(jnp.int32).astype(jnp.int16)
 
@@ -172,31 +169,28 @@
         scales = code_ref[pl.ds(code_ref.shape[0] - tail, tail), :].astype(jnp.int32).astype(jnp.float32)
         scale_ref[pl.ds(start, tail), :] = scales
 
-    def copy(step):
-        lines = pl.ds(pl.multiple_of((first + step) * height, height), height)
-        return pltpu.make_async_copy(done_ref.at[step], out_ref.at[lines, :], sems.at[step])
-
-    @pl.loop(0, span)
-    def _(step):
-        def decoded(number):
-            block = skips[number] + step
-            power = scale_ref[pl.ds(starts[number] + 2 * block, 1), :]
-            fraction = scale_ref[pl.ds(starts[number] + 2 * block + 1, 1), :]
-            code = code_refs[number][pl.ds(pl.multiple_of(block * height, height), height), :]
-            return code.astype(jnp.int32).astype(jnp.float32) * (fraction * jnp.exp2(power) * (1.0 / FRACTION))
-
-        lines = pl.ds(pl.multiple_of((first + step) * height, height), height)
-        total = jnp.dot(rows_ref[lines, :], dense_ref[...], preferred_element_type=jnp.float32)
+    def decoded(number, step):
+        block = skips[number] + step
+        power = scale_ref[pl.ds(starts[number] + 2 * block, 1), :]
+        fraction = scale_ref[pl.ds(starts[number] + 2 * block + 1, 1), :]
+        code = code_refs[number][pl.ds(block * height, height), :]
+        return code.astype(jnp.int32).astype(jnp.float32) * (fraction * jnp.exp2(power) * (1.0 / FRACTION))
+
+    sums = jnp.dot(rows_ref[pl.ds(first * height, span * height), :], dense_ref[...], preferred_element_type=jnp.float32)
+    copies = []
+    for step in range(span):
+        total = sums[step * height : (step + 1) * height]
         for number in range(0, len(code_refs), HALVES):
-            near, far = decoded(number), decoded(number + 1)
+            near, far = decoded(number, step), decoded(number + 1, step)
             left = jnp.where(first_half, near, far)
             right = jnp.where(first_half, far, near)
             total = total + jnp.concatenate([left, right], axis=1)
         done_ref[step] = total.astype(done_ref.dtype)
-        copy(step).start()
-
-    for step in range(span):
-        copy(step).wait()
+        lines = pl.ds((first + step) * height, height)
+        copies.append(pltpu.make_async_copy(done_ref.at[step], out_ref.at[lines, :], sems.at[step]))
+        copies[-1].start()
+    for copy in copies:
+        copy.wait()
 
 
 def after(value, *earlier):
@@ -230,19 +224,20 @@
     swap = [(c, c ^ 1) for c in range(col_peers)]
     other = lax.ppermute(amplitudes, "col", swap)
     other_mask = lax.ppermute(pair_mask.T, "col", swap)
-    masks = jnp.concatenate([pair_mask.T, other_mask])
-    stored = pltpu.with_memory_space_constraint(amplitudes, pltpu.HBM)
-    panels = pltpu.with_memory_space_constraint(integrals, pltpu.HBM)
-    table = jnp.concatenate([tile_list[0, 0], tile_count[0], owner[:, 0]])
+    length = max(block_count, STEPS)
+    plan = jnp.concatenate(
+        [jnp.pad(part, ((0, 0), (0, length - part.shape[1]))) for part in (pair_mask.T, other_mask, owner.T)]
+    )
+    in_hbm = partial(pltpu.with_memory_space_constraint, memory_space=pltpu.HBM)
 
     pieces = pl.pallas_call(
         pack_kernel,
-        in_specs=[SMEM, VMEM],
+        in_specs=[VMEM, SMEM, VMEM],
         out_specs=[VMEM] * peers,
         out_shape=[jax.ShapeDtypeStruct((share + META_ROWS, tile_width), integrals.dtype)] * peers,
         compiler_params=PARAMS,
         name="pack",
-    )(table, panels)
+    )(in_hbm(tile_list), tile_count, in_hbm(integrals))
     pieces = [piece if shift == 0 else along(piece, shift) for shift, piece in enumerate(pieces)]
 
     height = CORES * share + META_ROWS
@@ -251,13 +246,13 @@
         widths += [half_width] * HALVES if offset else [tile_width]
     chosen = list(
         pl.pallas_call(
-            partial(choose_kernel, col_peers, offsets, slots, peers),
+            partial(choose_kernel, col_peers, offsets, peers),
             in_specs=[SMEM] + [VMEM] * peers,
             out_specs=[VMEM] * len(widths),
             out_shape=[jax.ShapeDtypeStruct((height, width), integrals.dtype) for width in widths],
             compiler_params=PARAMS,
             name="choose",
-        )(after(table, masks), *pieces)
+        )(plan, *pieces)
     )
 
     def fill(held):
@@ -283,7 +278,7 @@
                 transcendentals=0,
             ),
             name="screen",
-        )(after(masks, *earlier), stored, other)
+        )(after(plan, *earlier), in_hbm(amplitudes), other)
 
     own = chosen.pop(0)
     own = own + across(own, 1, 0)
@@ -314,7 +309,7 @@
     arrived, sent = {}, []
     order = []
     for number, (half, first, span) in enumerate(rounds):
-        ahead = 1
+        ahead = 2 if number in (3, 4) else 1
         earlier = sent[-1:] + [part for key in order[:-ahead] for part in arrived[key]]
         if number == len(near_chunks) - 1:
             earlier += list(far_weights.values())

time: 73.4 us -> 69.8 us (0.951)
  Pallas kernels: 23.5 us -> 18.8 us
  starting transfers between devices: 28.1 us -> 29.3 us
    ppermute x9, waiting for transfers between devices: 4.98 us -> 8.62 us  [along(): lax.ppermute(value, 'row', [(r, (r + HALVES * shift) % row_peers) for r i...]
    pallas_call x7, Pallas kernels: 9.87 us -> 6.43 us  [shards(): pl.pallas_call(partial(send_kernel, first, span, block_rows), in_specs=[V...]
    ppermute x11, waiting for transfers between devices: 14.2 us -> 11.3 us  [across(): return lax.ppermute(value, ('row', 'col'), pairs)]
    ppermute x11, starting transfers between devices: 12.9 us -> 14.3 us  [across(): return lax.ppermute(value, ('row', 'col'), pairs)]
    pallas_call x4, Pallas kernels: 7.23 us -> 5.87 us  [shards(): pl.pallas_call(partial(join_kernel, first, span, block_rows, skips), in_s...]
  transfers between devices with their start and end apart: 22 -> 22, of which waited for: 11 -> 13; matrix products, arithmetic and copies ran while one was open for 2% -> 1% of each run, Pallas kernels for 30% -> 25%
where the time goes in v9:
time: 69.8 us; the launch traced here: 69.6 us
  starting transfers between devices  29.3 us (42%)
  waiting for transfers between devices  19.9 us (29%)
  Pallas kernels  18.8 us (27%)
  between operations  0.81 us (1%)
  other arithmetic  0.77 us (1%)
    ppermute x9, starting transfers between devices, along(): lax.ppermute(value, 'row', [(r, (r + HALVES * shift) % row_peers) for r i...  14.5 us
    ppermute x11, starting transfers between devices, across(): return lax.ppermute(value, ('row', 'col'), pairs)  14.3 us
    ppermute x11, waiting for transfers between devices, across(): return lax.ppermute(value, ('row', 'col'), pairs)  11.3 us
    ppermute x9, waiting for transfers between devices, along(): lax.ppermute(value, 'row', [(r, (r + HALVES * shift) % row_peers) for r i...  8.62 us
    pallas_call x7, Pallas kernels, shards(): pl.pallas_call(partial(send_kernel, first, span, block_rows), in_specs=[V...  6.43 us
    pallas_call x4, Pallas kernels, shards(): pl.pallas_call(partial(join_kernel, first, span, block_rows, skips), in_s...  5.87 us
    pallas_call x1, Pallas kernels, screen(): pl.pallas_call(partial(screen_kernel, tile_width, block_rows), in_specs=[...  4.03 us
  transfers between devices with their start and end apart: 22, of which 13 were waited for; matrix products, arithmetic and copies ran while one was open for 1% of the time, Pallas kernels for 25%

profile of v9, /device:TPU:0, one launch (start us, length us, event | category | flops | bytes accessed | tf_op | source)
XLA Modules:
  0.0 69.6 jit_solution(2623889449510774164)
XLA Ops:
  0.0 0.5 collective-permute-start.8
  1.2 1.0 %pack.1 = (bf16[144,256]{1,0:T(8,128)(2,1)S(1)}, bf16[144,256]{1,0:T(8,128)(2,1)S(1)}, bf16[144,256]{1,0:T(8,128)(2,1)S(1)}, bf16[144,256]{1,0:T(8,128)(2,1)S(1)}) custom-call(s32[1,1,2]{2,1,0:T(1,128)} %list_ref.1, s32[1,1]{1,0:T(1,128)S(6)} %copy.13.count_ref, bf16[1,1,2,256,256]{4,3,2,1,0:T(8,128)(2,1)} %panel_ref.1), custom_call_target="tpu_custom_call" | custom-call | tf_op jit(solution)/shard_map/pack/pallas_call | solution.py:233
  2.2 3.0 %collective-permute-start.1 = (bf16[144,256]{1,0:T(8,128)(2,1)S(1)}, bf16[144,256]{1,0:T(8,128)(2,1)S(1)}, u32[]{:S(2)}, u32[]{:S(2)}) collective-permute-start(bf16[144,256]{1,0:T(8,128)(2,1)S(1)} %get-tuple-element.22), channel_id=1, source_target_pairs={{0,8},{4,12},{8,16},{12,20},{16,24},{20,28},{24,0},{28,4},{1,9},{5... | collective-permute-start | bytes 221192 | tf_op jit(solution)/shard_map/ppermute | solution.py:215
  5.2 2.6 %collective-permute-start.2 = (bf16[144,256]{1,0:T(8,128)(2,1)S(1)}, bf16[144,256]{1,0:T(8,128)(2,1)S(1)}, u32[]{:S(2)}, u32[]{:S(2)}) collective-permute-start(bf16[144,256]{1,0:T(8,128)(2,1)S(1)} %get-tuple-element.23), channel_id=1, source_target_pairs={{0,16},{4,20},{8,24},{12,28},{16,0},{20,4},{24,8},{28,12},{1,17},{... | collective-permute-start | bytes 221192 | tf_op jit(solution)/shard_map/ppermute | solution.py:215
  7.8 1.3 %collective-permute-start.3 = (bf16[144,256]{1,0:T(8,128)(2,1)S(1)}, bf16[144,256]{1,0:T(8,128)(2,1)S(1)}, u32[]{:S(2)}, u32[]{:S(2)}) collective-permute-start(bf16[144,256]{1,0:T(8,128)(2,1)S(1)} %get-tuple-element.24), channel_id=1, source_target_pairs={{0,24},{4,28},{8,0},{12,4},{16,8},{20,12},{24,16},{28,20},{1,25},{... | collective-permute-start | bytes 221192 | tf_op jit(solution)/shard_map/ppermute | solution.py:215
  9.2 0.7 %pad_add_fusion.plan_ref.mask_ref = s32[7,12]{1,0:T(8,128)S(1)} fusion(s32[1,4]{1,0:T(1,128)} %bitcast.4, s32[3,12]{1,0:T(4,128)S(1)} %collective-permute-done, s32[3,12]{1,0:T(4,128)} %bitcast.3), kind=kLoop, calls=%fused_computation | loop fusion | flops 168 | bytes 640 | tf_op jit(solution)/shard_map/concatenate | solution.py:228
  10.1 2.9 %collective-permute-done.2.refs_2_ = bf16[144,256]{1,0:T(8,128)(2,1)S(1)} collective-permute-done((bf16[144,256]{1,0:T(8,128)(2,1)S(1)}, bf16[144,256]{1,0:T(8,128)(2,1)S(1)}, u32[]{:S(2)}, u32[]{:S(2)}) %collective-permute-start.2) | collective-permute-done | bytes 73760 | tf_op jit(solution)/shard_map/ppermute | solution.py:215
  13.2 0.8 %choose.1 = (bf16[272,256]{1,0:T(8,128)(2,1)S(1)}, bf16[272,128]{1,0:T(8,128)(2,1)S(1)}, bf16[272,128]{1,0:T(8,128)(2,1)S(1)}) custom-call(s32[7,12]{1,0:T(8,128)S(1)} %pad_add_fusion.plan_ref.mask_ref, bf16[144,256]{1,0:T(8,128)(2,1)S(1)} %get-tuple-element.21.refs_0_, bf16[144,256]{1,0:T(8,128)(2,1)S(1)} %collective-permute-done.1.refs_1_, ...), custom_call_target="tpu_custom_call" | custom-call | tf_op jit(solution)/shard_map/choose/pallas_call | solution.py:248
  14.0 1.6 %collective-permute-start.4 = (bf16[272,128]{1,0:T(8,128)(2,1)S(1)}, bf16[272,128]{1,0:T(8,128)(2,1)S(1)}, u32[]{:S(2)}, u32[]{:S(2)}) collective-permute-start(bf16[272,128]{1,0:T(8,128)(2,1)S(1)} %get-tuple-element.25), channel_id=1, source_target_pairs={{0,2},{1,3},{2,0},{3,1},{4,6},{5,7},{6,4},{7,5},{8,10},{9,11},{10,... | collective-permute-start | bytes 208904 | tf_op jit(solution)/shard_map/ppermute | solution.py:222
  15.5 1.5 %collective-permute-start.5 = (bf16[272,128]{1,0:T(8,128)(2,1)S(1)}, bf16[272,128]{1,0:T(8,128)(2,1)S(1)}, u32[]{:S(2)}, u32[]{:S(2)}) collective-permute-start(bf16[272,128]{1,0:T(8,128)(2,1)S(1)} %get-tuple-element.26), channel_id=1, source_target_pairs={{0,6},{1,7},{2,4},{3,5},{4,2},{5,3},{6,0},{7,1},{8,14},{9,15},{10,... | collective-permute-start | bytes 208904 | tf_op jit(solution)/shard_map/ppermute | solution.py:222
  17.0 0.5 collective-permute-start.7
  17.5 0.8 %collective-permute-done.4 = bf16[272,128]{1,0:T(8,128)(2,1)S(1)} collective-permute-done((bf16[272,128]{1,0:T(8,128)(2,1)S(1)}, bf16[272,128]{1,0:T(8,128)(2,1)S(1)}, u32[]{:S(2)}, u32[]{:S(2)}) %collective-permute-start.4) | collective-permute-done | bytes 69664 | tf_op jit(solution)/shard_map/ppermute | solution.py:222
  18.4 2.5 %collective-permute-done.5 = bf16[272,128]{1,0:T(8,128)(2,1)S(1)} collective-permute-done((bf16[272,128]{1,0:T(8,128)(2,1)S(1)}, bf16[272,128]{1,0:T(8,128)(2,1)S(1)}, u32[]{:S(2)}, u32[]{:S(2)}) %collective-permute-start.5) | collective-permute-done | bytes 69664 | tf_op jit(solution)/shard_map/ppermute | solution.py:222
  20.9 3.1 %collective-permute-start.6 = (bf16[272,128]{1,0:T(8,128)(2,1)S(1)}, bf16[272,128]{1,0:T(8,128)(2,1)S(1)}, u32[]{:S(2)}, u32[]{:S(2)}) collective-permute-start(bf16[272,128]{1,0:T(8,128)(2,1)S(1)} %add.8.refs_0_), channel_id=1, source_target_pairs={{0,24},{4,28},{8,0},{12,4},{16,8},{20,12},{24,16},{28,20},{1,25},{... | collective-permute-start | bytes 208904 | tf_op jit(solution)/shard_map/ppermute | solution.py:215
  24.0 0.3 collective-permute-start.10
  24.3 0.4 collective-permute-start.9
  24.7 1.3 %collective-permute-done.6.refs_3_ = bf16[272,128]{1,0:T(8,128)(2,1)S(1)} collective-permute-done((bf16[272,128]{1,0:T(8,128)(2,1)S(1)}, bf16[272,128]{1,0:T(8,128)(2,1)S(1)}, u32[]{:S(2)}, u32[]{:S(2)}) %collective-permute-start.6) | collective-permute-done | bytes 69664 | tf_op jit(solution)/shard_map/ppermute | solution.py:215
  25.9 4.0 %screen.1.rows_ref = bf16[3072,1536]{1,0:T(8,128)(2,1)S(1)} custom-call(s32[7,12]{1,0:T(8,128)S(1)} %pad_add_fusion.plan_ref.mask_ref, bf16[3072,768]{1,0:T(8,128)(2,1)} %own_ref.1, bf16[3072,768]{1,0:T(8,128)(2,1)S(1)} %collective-permute-done.8.other_ref), custom_call_target="tpu_custom_call" | custom-call | flops 4718592 | bytes 18874368 | tf_op jit(solution)/shard_map/screen/pallas_call | solution.py:269
  30.0 0.4 collective-permute-done.9.refs_1_
  30.4 0.3 fill.2.dense_ref
  30.7 1.5 %collective-permute-start.15 = (bf16[1536,128]{1,0:T(8,128)(2,1)S(1)}, bf16[1536,128]{1,0:T(8,128)(2,1)S(1)}, u32[]{:S(2)}, u32[]{:S(2)}) collective-permute-start(bf16[1536,128]{1,0:T(8,128)(2,1)S(1)} %fill.2.dense_ref), channel_id=1, source_target_pairs={{0,4},{1,5},{2,6},{3,7},{4,0},{5,1},{6,2},{7,3},{8,12},{9,13},{10,... | collective-permute-start | bytes 1179656 | tf_op jit(solution)/shard_map/ppermute | solution.py:222
  32.2 0.6 send_part.7
  32.8 0.6 collective-permute-start.11
  33.5 1.2 %send_part.8 = s16[1296,128]{1,0:T(8,128)(2,1)S(1)} custom-call(bf16[3072,1536]{1,0:T(8,128)(2,1)S(1)} %screen.1.rows_ref, bf16[1536,128]{1,0:T(8,128)(2,1)S(1)} %fill.2.dense_ref), custom_call_target="tpu_custom_call" | custom-call | flops 503316480 | bytes 4259840 | tf_op jit(solution)/shard_map/send_part/pallas_call | solution.py:322
  34.7 1.5 %collective-permute-start.17 = (s16[1296,128]{1,0:T(8,128)(2,1)S(1)}, s16[1296,128]{1,0:T(8,128)(2,1)S(1)}, u32[]{:S(2)}, u32[]{:S(2)}) collective-permute-start(s16[1296,128]{1,0:T(8,128)(2,1)S(1)} %send_part.8), channel_id=1, source_target_pairs={{0,2},{1,3},{2,0},{3,1},{4,6},{5,7},{6,4},{7,5},{8,10},{9,11},{10,... | collective-permute-start | bytes 995336 | tf_op jit(solution)/shard_map/ppermute | solution.py:222
  36.2 3.2 %collective-permute-done.11.refs_0_ = s16[528,128]{1,0:T(8,128)(2,1)S(1)} collective-permute-done((s16[528,128]{1,0:T(8,128)(2,1)S(1)}, s16[528,128]{1,0:T(8,128)(2,1)S(1)}, u32[]{:S(2)}, u32[]{:S(2)}) %collective-permute-start.11) | collective-permute-done | bytes 135200 | tf_op jit(solution)/shard_map/ppermute | solution.py:222
  39.4 0.6 collective-permute-done.15.dense_ref
  40.0 1.2 %send_part.9 = s16[1296,128]{1,0:T(8,128)(2,1)S(1)} custom-call(bf16[3072,1536]{1,0:T(8,128)(2,1)S(1)} %screen.1.rows_ref, bf16[1536,128]{1,0:T(8,128)(2,1)S(1)} %fill.2.dense_ref), custom_call_target="tpu_custom_call" | custom-call | flops 503316480 | bytes 4259840 | tf_op jit(solution)/shard_map/send_part/pallas_call | solution.py:322
  41.3 0.8 %collective-permute-start.16 = (s16[1296,128]{1,0:T(8,128)(2,1)S(1)}, s16[1296,128]{1,0:T(8,128)(2,1)S(1)}, u32[]{:S(2)}, u32[]{:S(2)}) collective-permute-start(s16[1296,128]{1,0:T(8,128)(2,1)S(1)} %send_part.9), channel_id=1, source_target_pairs={{0,2},{1,3},{2,0},{3,1},{4,6},{5,7},{6,4},{7,5},{8,10},{9,11},{10,... | collective-permute-start | bytes 995336 | tf_op jit(solution)/shard_map/ppermute | solution.py:222
  42.1 3.2 %collective-permute-start.14 = (bf16[272,256]{1,0:T(8,128)(2,1)S(1)}, bf16[272,256]{1,0:T(8,128)(2,1)S(1)}, u32[]{:S(2)}, u32[]{:S(2)}) collective-permute-start(bf16[272,256]{1,0:T(8,128)(2,1)S(1)} %add.9.refs_0_), channel_id=1, source_target_pairs={{0,24},{4,28},{8,0},{12,4},{16,8},{20,12},{24,16},{28,20},{1,25},{... | collective-permute-start | bytes 417800 | tf_op jit(solution)/shard_map/ppermute | solution.py:215
  45.3 0.6 collective-permute-start.12
  45.8 0.6 send_part.10
  46.5 1.2 %collective-permute-start.18 = (s16[528,128]{1,0:T(8,128)(2,1)S(1)}, s16[528,128]{1,0:T(8,128)(2,1)S(1)}, u32[]{:S(2)}, u32[]{:S(2)}) collective-permute-start(s16[528,128]{1,0:T(8,128)(2,1)S(1)} %send_part.10), channel_id=1, source_target_pairs={{0,2},{1,3},{2,0},{3,1},{4,6},{5,7},{6,4},{7,5},{8,10},{9,11},{10,... | collective-permute-start | bytes 405512 | tf_op jit(solution)/shard_map/ppermute | solution.py:222
  47.7 1.2 %send_part.11 = s16[1296,128]{1,0:T(8,128)(2,1)S(1)} custom-call(bf16[3072,1536]{1,0:T(8,128)(2,1)S(1)} %screen.1.rows_ref, bf16[1536,128]{1,0:T(8,128)(2,1)S(1)} %collective-permute-done.15.dense_ref), custom_call_target="tpu_custom_call" | custom-call | flops 503316480 | bytes 4259840 | tf_op jit(solution)/shard_map/send_part/pallas_call | solution.py:322
  49.0 1.6 %collective-permute-start.19 = (s16[1296,128]{1,0:T(8,128)(2,1)S(1)}, s16[1296,128]{1,0:T(8,128)(2,1)S(1)}, u32[]{:S(2)}, u32[]{:S(2)}) collective-permute-start(s16[1296,128]{1,0:T(8,128)(2,1)S(1)} %send_part.11), channel_id=1, source_target_pairs={{0,2},{1,3},{2,0},{3,1},{4,6},{5,7},{6,4},{7,5},{8,10},{9,11},{10,... | collective-permute-start | bytes 995336 | tf_op jit(solution)/shard_map/ppermute | solution.py:222
  50.5 3.7 %collective-permute-done.13.refs_2_ = bf16[272,256]{1,0:T(8,128)(2,1)S(1)} collective-permute-done((bf16[272,256]{1,0:T(8,128)(2,1)S(1)}, bf16[272,256]{1,0:T(8,128)(2,1)S(1)}, u32[]{:S(2)}, u32[]{:S(2)}) %collective-permute-start.13) | collective-permute-done | bytes 139296 | tf_op jit(solution)/shard_map/ppermute | solution.py:215
  54.2 0.3 fill.3.dense_ref
  54.5 0.8 %collective-permute-done.18.refs_1_ = s16[528,128]{1,0:T(8,128)(2,1)S(1)} collective-permute-done((s16[528,128]{1,0:T(8,128)(2,1)S(1)}, s16[528,128]{1,0:T(8,128)(2,1)S(1)}, u32[]{:S(2)}, u32[]{:S(2)}) %collective-permute-start.18) | collective-permute-done | bytes 135200 | tf_op jit(solution)/shard_map/ppermute | solution.py:222
  55.4 1.0 %send_part.12 = s16[1040,128]{1,0:T(8,128)(2,1)S(1)} custom-call(bf16[3072,1536]{1,0:T(8,128)(2,1)S(1)} %screen.1.rows_ref, bf16[1536,128]{1,0:T(8,128)(2,1)S(1)} %collective-permute-done.15.dense_ref), custom_call_target="tpu_custom_call" | custom-call | flops 402653184 | bytes 3407872 | tf_op jit(solution)/shard_map/send_part/pallas_call | solution.py:322
  56.4 1.8 %collective-permute-start.21 = (s16[1040,128]{1,0:T(8,128)(2,1)S(1)}, s16[1040,128]{1,0:T(8,128)(2,1)S(1)}, u32[]{:S(2)}, u32[]{:S(2)}) collective-permute-start(s16[1040,128]{1,0:T(8,128)(2,1)S(1)} %send_part.12), channel_id=1, source_target_pairs={{0,2},{1,3},{2,0},{3,1},{4,6},{5,7},{6,4},{7,5},{8,10},{9,11},{10,... | collective-permute-start | bytes 798728 | tf_op jit(solution)/shard_map/ppermute | solution.py:222
  58.2 1.2 %join_part.4.refs_2_ = bf16[3072,256]{1,0:T(8,128)(2,1)} custom-call(bf16[3072,1536]{1,0:T(8,128)(2,1)S(1)} %screen.1.rows_ref, bf16[1536,256]{1,0:T(8,128)(2,1)S(1)} %fill.3.dense_ref, s16[528,128]{1,0:T(8,128)(2,1)S(1)} %collective-permute-done.11.refs_0_, s16[528,128]{1,0:T(8,128)(2,1)S(1)} %collective-permute-done.18.refs_1_), custom_call_target="tpu_custom_call" | custom-call | flops 402653184 | bytes 1835008 | tf_op jit(solution)/shard_map/join_part/pallas_call | solution.py:351
  59.4 3.0 %collective-permute-done.19.refs_1_ = s16[1296,128]{1,0:T(8,128)(2,1)S(1)} collective-permute-done((s16[1296,128]{1,0:T(8,128)(2,1)S(1)}, s16[1296,128]{1,0:T(8,128)(2,1)S(1)}, u32[]{:S(2)}, u32[]{:S(2)}) %collective-permute-start.19) | collective-permute-done | bytes 331808 | tf_op jit(solution)/shard_map/ppermute | solution.py:222
  62.5 0.4 send_part.13
  62.9 1.8 %collective-permute-start.20 = (s16[272,128]{1,0:T(8,128)(2,1)S(1)}, s16[272,128]{1,0:T(8,128)(2,1)S(1)}, u32[]{:S(2)}, u32[]{:S(2)}) collective-permute-start(s16[272,128]{1,0:T(8,128)(2,1)S(1)} %send_part.13), channel_id=1, source_target_pairs={{0,2},{1,3},{2,0},{3,1},{4,6},{5,7},{6,4},{7,5},{8,10},{9,11},{10,... | collective-permute-start | bytes 208904 | tf_op jit(solution)/shard_map/ppermute | solution.py:222
  64.7 1.9 %join_part.5.refs_2_ = bf16[3072,256]{1,0:T(8,128)(2,1)} custom-call(bf16[3072,1536]{1,0:T(8,128)(2,1)S(1)} %screen.1.rows_ref, bf16[1536,256]{1,0:T(8,128)(2,1)S(1)} %fill.3.dense_ref, s16[1296,128]{1,0:T(8,128)(2,1)S(1)} %collective-permute-done.17.refs_0_, s16[1296,128]{1,0:T(8,128)(2,1)S(1)} %collective-permute-done.19.refs_1_, ...), custom_call_target="tpu_custom_call", output_to_operand_aliasing={{}: (4, {})} | custom-call | flops 1006632960 | bytes 4587520 | tf_op jit(solution)/shard_map/join_part/pallas_call | solution.py:351
  66.6 0.3 collective-permute-done.21.refs_1_
  66.9 1.7 %join_part.6.refs_2_ = bf16[3072,256]{1,0:T(8,128)(2,1)} custom-call(bf16[3072,1536]{1,0:T(8,128)(2,1)S(1)} %screen.1.rows_ref, bf16[1536,256]{1,0:T(8,128)(2,1)S(1)} %fill.3.dense_ref, s16[1296,128]{1,0:T(8,128)(2,1)S(1)} %collective-permute-done.16.refs_0_, s16[1040,128]{1,0:T(8,128)(2,1)S(1)} %collective-permute-done.21.refs_1_, ...), custom_call_target="tpu_custom_call", output_to_operand_aliasing={{}: (4, {})} | custom-call | flops 805306368 | bytes 3670016 | tf_op jit(solution)/shard_map/join_part/pallas_call | solution.py:351
  68.6 1.0 %join_part.7 = bf16[3072,256]{1,0:T(8,128)(2,1)} custom-call(bf16[3072,1536]{1,0:T(8,128)(2,1)S(1)} %screen.1.rows_ref, bf16[1536,256]{1,0:T(8,128)(2,1)S(1)} %fill.3.dense_ref, s16[1296,128]{1,0:T(8,128)(2,1)S(1)} %collective-permute-done.16.refs_0_, s16[272,128]{1,0:T(8,128)(2,1)S(1)} %collective-permute-done.20.refs_1_, ...), custom_call_target="tpu_custom_call", output_to_operand_aliasing={{}: (4, {})} | custom-call | flops 201326592 | bytes 917504 | tf_op jit(solution)/shard_map/join_part/pallas_call | solution.py:351
  (15 shorter events, 0.6 us)
Async XLA Ops:
  0.0 25.9 %collective-permute-start.8 = (bf16[3072,768]{1,0:T(8,128)(2,1)}, bf16[3072,768]{1,0:T(8,128)(2,1)S(1)}, u32[]{:S(2)}, u32[]{:S(2)}) collective-permute-start(bf16[3072,768]{1,0:T(8,128)(2,1)} %own_ref.1), channel_id=1, source_target_pairs={{0,1},{1,0},{2,3},{3,2},{4,5},{5,4},{6,7},{7,6},{8,9},{9,8},{10,11... | collective-permute-start | bytes 14155784 | tf_op jit(solution)/shard_map/ppermute | solution.py:225
  0.5 8.7 %collective-permute-start = (s32[3,12]{1,0:T(4,128)}, s32[3,12]{1,0:T(4,128)S(1)}, u32[]{:S(2)}, u32[]{:S(2)}) collective-permute-start(s32[3,12]{1,0:T(4,128)} %bitcast.2), channel_id=1, source_target_pairs={{0,1},{1,0},{2,3},{3,2},{4,5},{5,4},{6,7},{7,6},{8,9},{9,8},{10,11... | collective-permute-start | bytes 440 | tf_op jit(solution)/shard_map/ppermute | solution.py:226
  2.2 7.9 %collective-permute-start.1 = (bf16[144,256]{1,0:T(8,128)(2,1)S(1)}, bf16[144,256]{1,0:T(8,128)(2,1)S(1)}, u32[]{:S(2)}, u32[]{:S(2)}) collective-permute-start(bf16[144,256]{1,0:T(8,128)(2,1)S(1)} %get-tuple-element.22), channel_id=1, source_target_pairs={{0,8},{4,12},{8,16},{12,20},{16,24},{20,28},{24,0},{28,4},{1,9},{5... | collective-permute-start | bytes 221192 | tf_op jit(solution)/shard_map/ppermute | solution.py:215
  5.2 7.7 %collective-permute-start.2 = (bf16[144,256]{1,0:T(8,128)(2,1)S(1)}, bf16[144,256]{1,0:T(8,128)(2,1)S(1)}, u32[]{:S(2)}, u32[]{:S(2)}) collective-permute-start(bf16[144,256]{1,0:T(8,128)(2,1)S(1)} %get-tuple-element.23), channel_id=1, source_target_pairs={{0,16},{4,20},{8,24},{12,28},{16,0},{20,4},{24,8},{28,12},{1,17},{... | collective-permute-start | bytes 221192 | tf_op jit(solution)/shard_map/ppermute | solution.py:215
  7.8 5.4 %collective-permute-start.3 = (bf16[144,256]{1,0:T(8,128)(2,1)S(1)}, bf16[144,256]{1,0:T(8,128)(2,1)S(1)}, u32[]{:S(2)}, u32[]{:S(2)}) collective-permute-start(bf16[144,256]{1,0:T(8,128)(2,1)S(1)} %get-tuple-element.24), channel_id=1, source_target_pairs={{0,24},{4,28},{8,0},{12,4},{16,8},{20,12},{24,16},{28,20},{1,25},{... | collective-permute-start | bytes 221192 | tf_op jit(solution)/shard_map/ppermute | solution.py:215
  14.0 4.4 %collective-permute-start.4 = (bf16[272,128]{1,0:T(8,128)(2,1)S(1)}, bf16[272,128]{1,0:T(8,128)(2,1)S(1)}, u32[]{:S(2)}, u32[]{:S(2)}) collective-permute-start(bf16[272,128]{1,0:T(8,128)(2,1)S(1)} %get-tuple-element.25), channel_id=1, source_target_pairs={{0,2},{1,3},{2,0},{3,1},{4,6},{5,7},{6,4},{7,5},{8,10},{9,11},{10,... | collective-permute-start | bytes 208904 | tf_op jit(solution)/shard_map/ppermute | solution.py:222
  15.5 5.3 %collective-permute-start.5 = (bf16[272,128]{1,0:T(8,128)(2,1)S(1)}, bf16[272,128]{1,0:T(8,128)(2,1)S(1)}, u32[]{:S(2)}, u32[]{:S(2)}) collective-permute-start(bf16[272,128]{1,0:T(8,128)(2,1)S(1)} %get-tuple-element.26), channel_id=1, source_target_pairs={{0,6},{1,7},{2,4},{3,5},{4,2},{5,3},{6,0},{7,1},{8,14},{9,15},{10,... | collective-permute-start | bytes 208904 | tf_op jit(solution)/shard_map/ppermute | solution.py:222
  17.0 7.6 %collective-permute-start.7 = (bf16[272,256]{1,0:T(8,128)(2,1)S(1)}, bf16[272,256]{1,0:T(8,128)(2,1)S(1)}, u32[]{:S(2)}, u32[]{:S(2)}) collective-permute-start(bf16[272,256]{1,0:T(8,128)(2,1)S(1)} %get-tuple-element.27), channel_id=1, source_target_pairs={{0,4},{1,5},{2,6},{3,7},{4,0},{5,1},{6,2},{7,3},{8,12},{9,13},{10,... | collective-permute-start | bytes 417800 | tf_op jit(solution)/shard_map/ppermute | solution.py:222
  20.9 5.1 %collective-permute-start.6 = (bf16[272,128]{1,0:T(8,128)(2,1)S(1)}, bf16[272,128]{1,0:T(8,128)(2,1)S(1)}, u32[]{:S(2)}, u32[]{:S(2)}) collective-permute-start(bf16[272,128]{1,0:T(8,128)(2,1)S(1)} %add.8.refs_0_), channel_id=1, source_target_pairs={{0,24},{4,28},{8,0},{12,4},{16,8},{20,12},{24,16},{28,20},{1,25},{... | collective-permute-start | bytes 208904 | tf_op jit(solution)/shard_map/ppermute | solution.py:215
  24.0 6.0 %collective-permute-start.10 = (bf16[272,128]{1,0:T(8,128)(2,1)S(1)}, bf16[272,128]{1,0:T(8,128)(2,1)S(1)}, u32[]{:S(2)}, u32[]{:S(2)}) collective-permute-start(bf16[272,128]{1,0:T(8,128)(2,1)S(1)} %add.8.refs_0_), channel_id=1, source_target_pairs={{0,16},{4,20},{8,24},{12,28},{16,0},{20,4},{24,8},{28,12},{1,17},{... | collective-permute-start | bytes 208904 | tf_op jit(solution)/shard_map/ppermute | solution.py:215
  24.3 6.1 %collective-permute-start.9 = (bf16[272,128]{1,0:T(8,128)(2,1)S(1)}, bf16[272,128]{1,0:T(8,128)(2,1)S(1)}, u32[]{:S(2)}, u32[]{:S(2)}) collective-permute-start(bf16[272,128]{1,0:T(8,128)(2,1)S(1)} %add.8.refs_0_), channel_id=1, source_target_pairs={{0,8},{4,12},{8,16},{12,20},{16,24},{20,28},{24,0},{28,4},{1,9},{5... | collective-permute-start | bytes 208904 | tf_op jit(solution)/shard_map/ppermute | solution.py:215
  30.7 9.3 %collective-permute-start.15 = (bf16[1536,128]{1,0:T(8,128)(2,1)S(1)}, bf16[1536,128]{1,0:T(8,128)(2,1)S(1)}, u32[]{:S(2)}, u32[]{:S(2)}) collective-permute-start(bf16[1536,128]{1,0:T(8,128)(2,1)S(1)} %fill.2.dense_ref), channel_id=1, source_target_pairs={{0,4},{1,5},{2,6},{3,7},{4,0},{5,1},{6,2},{7,3},{8,12},{9,13},{10,... | collective-permute-start | bytes 1179656 | tf_op jit(solution)/shard_map/ppermute | solution.py:222
  32.8 6.6 %collective-permute-start.11 = (s16[528,128]{1,0:T(8,128)(2,1)S(1)}, s16[528,128]{1,0:T(8,128)(2,1)S(1)}, u32[]{:S(2)}, u32[]{:S(2)}) collective-permute-start(s16[528,128]{1,0:T(8,128)(2,1)S(1)} %send_part.7), channel_id=1, source_target_pairs={{0,2},{1,3},{2,0},{3,1},{4,6},{5,7},{6,4},{7,5},{8,10},{9,11},{10,... | collective-permute-start | bytes 405512 | tf_op jit(solution)/shard_map/ppermute | solution.py:222
  34.7 11.8 %collective-permute-start.17 = (s16[1296,128]{1,0:T(8,128)(2,1)S(1)}, s16[1296,128]{1,0:T(8,128)(2,1)S(1)}, u32[]{:S(2)}, u32[]{:S(2)}) collective-permute-start(s16[1296,128]{1,0:T(8,128)(2,1)S(1)} %send_part.8), channel_id=1, source_target_pairs={{0,2},{1,3},{2,0},{3,1},{4,6},{5,7},{6,4},{7,5},{8,10},{9,11},{10,... | collective-permute-start | bytes 995336 | tf_op jit(solution)/shard_map/ppermute | solution.py:222
  41.3 14.1 %collective-permute-start.16 = (s16[1296,128]{1,0:T(8,128)(2,1)S(1)}, s16[1296,128]{1,0:T(8,128)(2,1)S(1)}, u32[]{:S(2)}, u32[]{:S(2)}) collective-permute-start(s16[1296,128]{1,0:T(8,128)(2,1)S(1)} %send_part.9), channel_id=1, source_target_pairs={{0,2},{1,3},{2,0},{3,1},{4,6},{5,7},{6,4},{7,5},{8,10},{9,11},{10,... | collective-permute-start | bytes 995336 | tf_op jit(solution)/shard_map/ppermute | solution.py:222
  42.1 6.8 %collective-permute-start.14 = (bf16[272,256]{1,0:T(8,128)(2,1)S(1)}, bf16[272,256]{1,0:T(8,128)(2,1)S(1)}, u32[]{:S(2)}, u32[]{:S(2)}) collective-permute-start(bf16[272,256]{1,0:T(8,128)(2,1)S(1)} %add.9.refs_0_), channel_id=1, source_target_pairs={{0,24},{4,28},{8,0},{12,4},{16,8},{20,12},{24,16},{28,20},{1,25},{... | collective-permute-start | bytes 417800 | tf_op jit(solution)/shard_map/ppermute | solution.py:215
  45.3 8.9 %collective-permute-start.13 = (bf16[272,256]{1,0:T(8,128)(2,1)S(1)}, bf16[272,256]{1,0:T(8,128)(2,1)S(1)}, u32[]{:S(2)}, u32[]{:S(2)}) collective-permute-start(bf16[272,256]{1,0:T(8,128)(2,1)S(1)} %add.9.refs_0_), channel_id=1, source_target_pairs={{0,16},{4,20},{8,24},{12,28},{16,0},{20,4},{24,8},{28,12},{1,17},{... | collective-permute-start | bytes 417800 | tf_op jit(solution)/shard_map/ppermute | solution.py:215
  45.3 8.9 %collective-permute-start.12 = (bf16[272,256]{1,0:T(8,128)(2,1)S(1)}, bf16[272,256]{1,0:T(8,128)(2,1)S(1)}, u32[]{:S(2)}, u32[]{:S(2)}) collective-permute-start(bf16[272,256]{1,0:T(8,128)(2,1)S(1)} %add.9.refs_0_), channel_id=1, source_target_pairs={{0,8},{4,12},{8,16},{12,20},{16,24},{20,28},{24,0},{28,4},{1,9},{5... | collective-permute-start | bytes 417800 | tf_op jit(solution)/shard_map/ppermute | solution.py:215
  46.5 8.9 %collective-permute-start.18 = (s16[528,128]{1,0:T(8,128)(2,1)S(1)}, s16[528,128]{1,0:T(8,128)(2,1)S(1)}, u32[]{:S(2)}, u32[]{:S(2)}) collective-permute-start(s16[528,128]{1,0:T(8,128)(2,1)S(1)} %send_part.10), channel_id=1, source_target_pairs={{0,2},{1,3},{2,0},{3,1},{4,6},{5,7},{6,4},{7,5},{8,10},{9,11},{10,... | collective-permute-start | bytes 405512 | tf_op jit(solution)/shard_map/ppermute | solution.py:222
  49.0 13.5 %collective-permute-start.19 = (s16[1296,128]{1,0:T(8,128)(2,1)S(1)}, s16[1296,128]{1,0:T(8,128)(2,1)S(1)}, u32[]{:S(2)}, u32[]{:S(2)}) collective-permute-start(s16[1296,128]{1,0:T(8,128)(2,1)S(1)} %send_part.11), channel_id=1, source_target_pairs={{0,2},{1,3},{2,0},{3,1},{4,6},{5,7},{6,4},{7,5},{8,10},{9,11},{10,... | collective-permute-start | bytes 995336 | tf_op jit(solution)/shard_map/ppermute | solution.py:222
  56.4 10.5 %collective-permute-start.21 = (s16[1040,128]{1,0:T(8,128)(2,1)S(1)}, s16[1040,128]{1,0:T(8,128)(2,1)S(1)}, u32[]{:S(2)}, u32[]{:S(2)}) collective-permute-start(s16[1040,128]{1,0:T(8,128)(2,1)S(1)} %send_part.12), channel_id=1, source_target_pairs={{0,2},{1,3},{2,0},{3,1},{4,6},{5,7},{6,4},{7,5},{8,10},{9,11},{10,... | collective-permute-start | bytes 798728 | tf_op jit(solution)/shard_map/ppermute | solution.py:222
  62.9 5.7 %collective-permute-start.20 = (s16[272,128]{1,0:T(8,128)(2,1)S(1)}, s16[272,128]{1,0:T(8,128)(2,1)S(1)}, u32[]{:S(2)}, u32[]{:S(2)}) collective-permute-start(s16[272,128]{1,0:T(8,128)(2,1)S(1)} %send_part.13), channel_id=1, source_target_pairs={{0,2},{1,3},{2,0},{3,1},{4,6},{5,7},{6,4},{7,5},{8,10},{9,11},{10,... | collective-permute-start | bytes 208904 | tf_op jit(solution)/shard_map/ppermute | solution.py:222

commit v10 on v9

--- a/solution.py
+++ b/solution.py
@@ -10,8 +10,9 @@
 STEPS = 4
 CORES = 2
 HALVES = 2
-NEAR_CUTS = (0.0, 0.167, 0.583, 1.0)
-FAR_CUTS = (0.0, 0.167, 0.583, 0.917, 1.0)
+NEAR_CUTS = (0.0, 0.2, 0.6, 1.0)
+FAR_CUTS = (0.0, 0.2, 0.6, 1.0)
+WHOLE_CUTS = (0.833, 1.0)
 CODE_TOP = 32767.0
 FRACTION = 8192.0
 META_ROWS = 16
@@ -54,7 +55,7 @@
         piece_ref[pl.ds(share, META_ROWS), :] = info
 
 
-def choose_kernel(col_peers, offsets, peers, plan_ref, *refs):
+def choose_kernel(col_peers, offsets, peers, owner_ref, *refs):
     piece_refs, out_refs = refs[:peers], list(refs[peers:])
     share, tile_width = piece_refs[0].shape[0] - META_ROWS, piece_refs[0].shape[1]
     half_width = tile_width // HALVES
@@ -63,16 +64,15 @@
     core = lax.rem(lax.axis_index("col"), CORES)
     sign = 1 - 2 * core
     for offset in offsets:
+        targets = [(out_refs.pop(0), pl.ds(0, tile_width))]
         if offset:
             spots = [pl.multiple_of(part * half_width, half_width) for part in (half, 1 - half)]
-            targets = [(out_refs.pop(0), pl.ds(spot, half_width)) for spot in spots]
-        else:
-            targets = [(out_refs.pop(0), pl.ds(0, tile_width))]
+            targets += [(out_refs.pop(0), pl.ds(spot, half_width)) for spot in spots]
         for out_ref, _ in targets:
             out_ref[...] = jnp.zeros_like(out_ref)
         for group, shift in enumerate((0, sign)):
             step = lax.rem(CORES * offset - shift + col_peers, col_peers)
-            holder = plan_ref[plan_ref.shape[0] - 1, jnp.minimum(step, STEPS - 1)]
+            holder = owner_ref[0, jnp.minimum(step, STEPS - 1)]
             here = (step < STEPS) & (lax.rem(holder, HALVES) == half)
             back = lax.rem(row // HALVES - holder // HALVES + peers, peers)
             for number, piece_ref in enumerate(piece_refs):
@@ -193,6 +193,31 @@
         copy.wait()
 
 
+def whole_kernel(first, span, height, rows_ref, dense_ref, *refs):
+    prior, (out_ref, done_ref, sem) = refs[:-3], refs[-3:]
+    total = jnp.dot(rows_ref[pl.ds(first * height, span * height), :], dense_ref[...], preferred_element_type=jnp.float32)
+    for number in range(0, len(prior) - 1, 4):
+        plan_ref, part_refs, weights_ref = prior[number], prior[number + 1 : number + 3], prior[number + 3]
+        width, tile_width = part_refs[0].shape[1], weights_ref.shape[1]
+        for group, part_ref in enumerate(part_refs):
+            screened = []
+            for block in range(span):
+                lines = pl.ds(block * height, height)
+                parts = []
+                for tile in range(width // tile_width):
+                    line = group * (width // tile_width) + tile
+                    live = plan_ref[line, first + block].astype(jnp.float32).astype(part_ref.dtype)
+                    parts.append(part_ref[lines, pl.ds(tile * tile_width, tile_width)] * live)
+                screened.append(jnp.concatenate(parts, axis=1))
+            rows = jnp.concatenate(screened, axis=0)
+            weights = weights_ref[pl.ds(group * width, width), :]
+            total = total + jnp.dot(rows, weights, preferred_element_type=jnp.float32)
+    done_ref[...] = total.astype(done_ref.dtype)
+    copy = pltpu.make_async_copy(done_ref, out_ref.at[pl.ds(first * height, span * height), :], sem)
+    copy.start()
+    copy.wait()
+
+
 def after(value, *earlier):
     return lax.optimization_barrier((value, *earlier))[0]
 
@@ -208,8 +233,10 @@
     share = slots * tile_width // peers
     offsets = pair_offsets(col_peers)
     remote = [offset for offset in offsets if offset]
-    near_chunks, far_chunks = row_chunks(block_count, NEAR_CUTS), row_chunks(block_count, FAR_CUTS)
-    chunks = row_chunks(block_count, NEAR_CUTS + FAR_CUTS)
+    whole_chunks = row_chunks(block_count, WHOLE_CUTS)
+    coded_count = whole_chunks[0][0]
+    near_chunks, far_chunks = row_chunks(coded_count, NEAR_CUTS), row_chunks(coded_count, FAR_CUTS)
+    chunks = row_chunks(coded_count, NEAR_CUTS + FAR_CUTS)
 
     def along(value, shift):
         return lax.ppermute(value, "row", [(r, (r + HALVES * shift) % row_peers) for r in range(row_peers)])
@@ -223,12 +250,14 @@
 
     swap = [(c, c ^ 1) for c in range(col_peers)]
     other = lax.ppermute(amplitudes, "col", swap)
-    other_mask = lax.ppermute(pair_mask.T, "col", swap)
-    length = max(block_count, STEPS)
-    plan = jnp.concatenate(
-        [jnp.pad(part, ((0, 0), (0, length - part.shape[1]))) for part in (pair_mask.T, other_mask, owner.T)]
-    )
     in_hbm = partial(pltpu.with_memory_space_constraint, memory_space=pltpu.HBM)
+
+    def whole_rows(first, span, *earlier):
+        part = amplitudes[first * block_rows : (first + span) * block_rows]
+        part = after(part, *earlier) if earlier else part
+        return [across(part, 0, -offset) for offset in remote]
+
+    whole = [whole_rows(*whole_chunks[0])]
 
     pieces = pl.pallas_call(
         pack_kernel,
@@ -243,7 +272,7 @@
     height = CORES * share + META_ROWS
     widths = []
     for offset in offsets:
-        widths += [half_width] * HALVES if offset else [tile_width]
+        widths += [tile_width] + [half_width] * HALVES * (offset > 0)
     chosen = list(
         pl.pallas_call(
             partial(choose_kernel, col_peers, offsets, peers),
@@ -252,8 +281,11 @@
             out_shape=[jax.ShapeDtypeStruct((height, width), integrals.dtype) for width in widths],
             compiler_params=PARAMS,
             name="choose",
-        )(plan, *pieces)
+        )(after(owner.T, other), *pieces)
     )
+
+    other_mask = lax.ppermute(after(pair_mask.T, chosen[0]), "col", swap)
+    plan = jnp.concatenate([pair_mask.T, other_mask])
 
     def fill(held):
         return pl.pallas_call(
@@ -282,14 +314,19 @@
 
     own = chosen.pop(0)
     own = own + across(own, 1, 0)
+    plans = [across(plan, 0, -offset) for offset in remote]
+    distant = []
     near_weights, far_weights, screened = {}, {}, None
     for offset in remote:
-        near, far = chosen.pop(0), chosen.pop(0)
+        full, near, far = chosen.pop(0), chosen.pop(0), chosen.pop(0)
+        distant.append(full + across(full, 1, 0))
         data = across(near, 0, offset) + across(far, 1, offset)
         held = [data] + [along(data, shift) for shift in range(1, peers)]
         if screened is None:
+            whole = [[(part, lax.ppermute(after(part, data), "col", swap)) for part in parts] for parts in whole]
+            siblings = [sibling for parts in whole for _, sibling in parts]
             screened = screen(held[-1], own)
-        near_weights[offset] = fill([after(held[0], screened)] + held[1:])
+        near_weights[offset] = fill([after(held[0], screened, *siblings)] + held[1:])
         far_weights[offset] = across(near_weights[offset], 1, 0)
 
     def cost(span, width):
@@ -333,10 +370,14 @@
             sent.append(code)
         if number == 0:
             own = after(own, *arrived[half, first])
-            own_weights = fill([own] + [along(own, shift) for shift in range(1, peers)])
-
-    out = None
-    for first, span in chunks:
+            own_held = [own] + [along(own, shift) for shift in range(1, peers)]
+            own_weights = fill(own_held)
+            distant_weights = []
+            for data in distant:
+                data = after(data, own_held[-1])
+                distant_weights.append(fill([data] + [along(data, shift) for shift in range(1, peers)]))
+
+    def joined(out, first, span):
         near_first = max(start for start, _ in near_chunks if start <= first)
         far_first = max(start for start, _ in far_chunks if start <= first)
         received = [part for pair in zip(arrived[0, near_first], arrived[1, far_first]) for part in pair]
@@ -348,7 +389,7 @@
             aliases = {len(operands): 0}
             operands.append(out)
             specs.append(HBM)
-        out = pl.pallas_call(
+        return pl.pallas_call(
             partial(join_kernel, first, span, block_rows, skips),
             in_specs=specs,
             out_specs=HBM,
@@ -363,6 +404,30 @@
             cost_estimate=cost(span, tile_width),
             name="join_part",
         )(*operands)
+
+    def joined_whole(out, first, span, parts):
+        operands, specs = [screened, own_weights], [VMEM, VMEM]
+        for plan_part, (same, sibling), weights in zip(plans, parts, distant_weights):
+            operands += [plan_part, same, sibling, weights]
+            specs += [SMEM, VMEM, VMEM, VMEM]
+        return pl.pallas_call(
+            partial(whole_kernel, first, span, block_rows),
+            in_specs=specs + [HBM],
+            out_specs=HBM,
+            out_shape=jax.ShapeDtypeStruct((row_count, tile_width), jnp.bfloat16),
+            scratch_shapes=[pltpu.VMEM((span * block_rows, tile_width), jnp.bfloat16), pltpu.SemaphoreType.DMA(())],
+            input_output_aliases={len(operands): 0},
+            compiler_params=PARAMS,
+            cost_estimate=cost(CORES * span, tile_width),
+            name="join_whole",
+        )(*operands, out)
+
+    out = None
+    for first, span in chunks[:-1]:
+        out = joined(out, first, span)
+    for (first, span), parts in zip(whole_chunks, whole):
+        out = joined_whole(out, first, span, parts)
+    out = joined(out, *chunks[-1])
     return out
 
 

time: 69.8 us -> 85.6 us (1.23)
  waiting for transfers between devices: 19.9 us -> 29.6 us
  starting transfers between devices: 29.3 us -> 34.5 us
  local copies, waits for them, and re-layouts: 0 us -> 1.19 us
    ppermute x9 -> x12, waiting for transfers between devices: 8.62 us -> 19.1 us  [along(): lax.ppermute(value, 'row', [(r, (r + HALVES * shift) % row_peers) for r i...]
    ppermute x9 -> x12, starting transfers between devices: 14.5 us -> 18.4 us  [along(): lax.ppermute(value, 'row', [(r, (r + HALVES * shift) % row_peers) for r i...]
    slice x0 -> x1, local copies, waits for them, and re-layouts: none -> 1.18 us  [whole_rows(): part = amplitudes[first * block_rows:(first + span) * block_rows]]
    ppermute x11 -> x13, starting transfers between devices: 14.3 us -> 15.4 us  [across(): return lax.ppermute(value, ('row', 'col'), pairs)]
    pallas_call x4, Pallas kernels: 5.87 us -> 6.91 us  [the longest x3 4.6 us: joined(): pl.pallas_call(partial(join_kernel, first, span, block_rows, skips), in_s...]
    pallas_call x7 -> x6, Pallas kernels: 6.43 us -> 5.4 us  [shards(): pl.pallas_call(partial(send_kernel, first, span, block_rows), in_specs=[V...]
    ppermute x11 -> x13, waiting for transfers between devices: 11.3 us -> 10.5 us  [across(): return lax.ppermute(value, ('row', 'col'), pairs)]
  transfers between devices with their start and end apart: 22 -> 28, of which waited for: 13 -> 12; matrix products, arithmetic and copies ran while one was open for 1% -> 2% of each run, Pallas kernels for 25% -> 20%
where the time goes in v10:
time: 85.6 us; the launch traced here: 85.4 us
  starting transfers between devices  34.5 us (40%)
  waiting for transfers between devices  29.6 us (35%)
  Pallas kernels  19.1 us (22%)
  local copies, waits for them, and re-layouts  1.19 us (1%)
  between operations  0.87 us (1%)
    ppermute x12, waiting for transfers between devices, along(): lax.ppermute(value, 'row', [(r, (r + HALVES * shift) % row_peers) for r i...  19.1 us
    ppermute x12, starting transfers between devices, along(): lax.ppermute(value, 'row', [(r, (r + HALVES * shift) % row_peers) for r i...  18.4 us
    ppermute x13, starting transfers between devices, across(): return lax.ppermute(value, ('row', 'col'), pairs)  15.4 us
    ppermute x13, waiting for transfers between devices, across(): return lax.ppermute(value, ('row', 'col'), pairs)  10.5 us
    pallas_call x6, Pallas kernels, shards(): pl.pallas_call(partial(send_kernel, first, span, block_rows), in_specs=[V...  5.4 us
    pallas_call x3, Pallas kernels, joined(): pl.pallas_call(partial(join_kernel, first, span, block_rows, skips), in_s...  4.6 us
    pallas_call x1, Pallas kernels, screen(): pl.pallas_call(partial(screen_kernel, tile_width, block_rows), in_specs=[...  4.02 us
    pallas_call x1, Pallas kernels, joined_whole(): pl.pallas_call(partial(whole_kernel, first, span, block_rows), in_specs=s...  2.31 us
  transfers between devices with their start and end apart: 28, of which 12 were waited for; matrix products, arithmetic and copies ran while one was open for 2% of the time, Pallas kernels for 20%

profile of v10, /device:TPU:0, one launch (start us, length us, event | category | flops | bytes accessed | tf_op | source)
XLA Modules:
  0.0 85.4 jit_solution(11321499114378573766)
XLA Ops:
  0.0 0.5 collective-permute-start
  0.5 1.2 %slice.3 = bf16[512,768]{1,0:T(8,128)(2,1)S(1)} slice(bf16[3072,768]{1,0:T(8,128)(2,1)} %own_ref.1), slice={[2560:3072], [0:768]} | slice | bytes 1572864 | tf_op jit(solution)/shard_map/slice | solution.py:256
  1.6 2.6 %collective-permute-start.9 = (bf16[512,768]{1,0:T(8,128)(2,1)S(1)}, bf16[512,768]{1,0:T(8,128)(2,1)S(1)}, u32[]{:S(2)}, u32[]{:S(2)}) collective-permute-start(bf16[512,768]{1,0:T(8,128)(2,1)S(1)} %slice.3), channel_id=1, source_target_pairs={{0,2},{1,3},{2,0},{3,1},{4,6},{5,7},{6,4},{7,5},{8,10},{9,11},{10,... | collective-permute-start | bytes 2359304 | tf_op jit(solution)/shard_map/ppermute | solution.py:249
  4.9 1.0 %pack.1 = (bf16[144,256]{1,0:T(8,128)(2,1)S(1)}, bf16[144,256]{1,0:T(8,128)(2,1)S(1)}, bf16[144,256]{1,0:T(8,128)(2,1)S(1)}, bf16[144,256]{1,0:T(8,128)(2,1)S(1)}) custom-call(s32[1,1,2]{2,1,0:T(1,128)} %list_ref.1, s32[1,1]{1,0:T(1,128)S(6)} %copy.13.count_ref, bf16[1,1,2,256,256]{4,3,2,1,0:T(8,128)(2,1)} %panel_ref.1), custom_call_target="tpu_custom_call" | custom-call | tf_op jit(solution)/shard_map/pack/pallas_call | solution.py:262
  5.9 1.6 %collective-permute-start.1 = (bf16[144,256]{1,0:T(8,128)(2,1)S(1)}, bf16[144,256]{1,0:T(8,128)(2,1)S(1)}, u32[]{:S(2)}, u32[]{:S(2)}) collective-permute-start(bf16[144,256]{1,0:T(8,128)(2,1)S(1)} %get-tuple-element.27), channel_id=1, source_target_pairs={{0,8},{4,12},{8,16},{12,20},{16,24},{20,28},{24,0},{28,4},{1,9},{5... | collective-permute-start | bytes 221192 | tf_op jit(solution)/shard_map/ppermute | solution.py:242
  7.5 2.6 %collective-permute-start.2 = (bf16[144,256]{1,0:T(8,128)(2,1)S(1)}, bf16[144,256]{1,0:T(8,128)(2,1)S(1)}, u32[]{:S(2)}, u32[]{:S(2)}) collective-permute-start(bf16[144,256]{1,0:T(8,128)(2,1)S(1)} %get-tuple-element.28), channel_id=1, source_target_pairs={{0,16},{4,20},{8,24},{12,28},{16,0},{20,4},{24,8},{28,12},{1,17},{... | collective-permute-start | bytes 221192 | tf_op jit(solution)/shard_map/ppermute | solution.py:242
  10.1 1.3 %collective-permute-start.3 = (bf16[144,256]{1,0:T(8,128)(2,1)S(1)}, bf16[144,256]{1,0:T(8,128)(2,1)S(1)}, u32[]{:S(2)}, u32[]{:S(2)}) collective-permute-start(bf16[144,256]{1,0:T(8,128)(2,1)S(1)} %get-tuple-element.29), channel_id=1, source_target_pairs={{0,24},{4,28},{8,0},{12,4},{16,8},{20,12},{24,16},{28,20},{1,25},{... | collective-permute-start | bytes 221192 | tf_op jit(solution)/shard_map/ppermute | solution.py:242
  11.5 1.1 %collective-permute-done.1.refs_1_ = bf16[144,256]{1,0:T(8,128)(2,1)S(1)} collective-permute-done((bf16[144,256]{1,0:T(8,128)(2,1)S(1)}, bf16[144,256]{1,0:T(8,128)(2,1)S(1)}, u32[]{:S(2)}, u32[]{:S(2)}) %collective-permute-start.1) | collective-permute-done | bytes 73760 | tf_op jit(solution)/shard_map/ppermute | solution.py:242
  12.6 2.9 %collective-permute-done.2.refs_2_ = bf16[144,256]{1,0:T(8,128)(2,1)S(1)} collective-permute-done((bf16[144,256]{1,0:T(8,128)(2,1)S(1)}, bf16[144,256]{1,0:T(8,128)(2,1)S(1)}, u32[]{:S(2)}, u32[]{:S(2)}) %collective-permute-start.2) | collective-permute-done | bytes 73760 | tf_op jit(solution)/shard_map/ppermute | solution.py:242
  15.7 0.7 choose.1
  16.4 0.6 collective-permute-start.5
  17.0 2.5 %collective-permute-start.6 = (bf16[272,128]{1,0:T(8,128)(2,1)S(1)}, bf16[272,128]{1,0:T(8,128)(2,1)S(1)}, u32[]{:S(2)}, u32[]{:S(2)}) collective-permute-start(bf16[272,128]{1,0:T(8,128)(2,1)S(1)} %get-tuple-element.33), channel_id=1, source_target_pairs={{0,6},{1,7},{2,4},{3,5},{4,2},{5,3},{6,0},{7,1},{8,14},{9,15},{10,... | collective-permute-start | bytes 208904 | tf_op jit(solution)/shard_map/ppermute | solution.py:249
  19.5 4.7 %collective-permute-done.5 = bf16[272,128]{1,0:T(8,128)(2,1)S(1)} collective-permute-done((bf16[272,128]{1,0:T(8,128)(2,1)S(1)}, bf16[272,128]{1,0:T(8,128)(2,1)S(1)}, u32[]{:S(2)}, u32[]{:S(2)}) %collective-permute-start.5) | collective-permute-done | bytes 69664 | tf_op jit(solution)/shard_map/ppermute | solution.py:249
  24.1 2.5 %collective-permute-done.6 = bf16[272,128]{1,0:T(8,128)(2,1)S(1)} collective-permute-done((bf16[272,128]{1,0:T(8,128)(2,1)S(1)}, bf16[272,128]{1,0:T(8,128)(2,1)S(1)}, u32[]{:S(2)}, u32[]{:S(2)}) %collective-permute-start.6) | collective-permute-done | bytes 69664 | tf_op jit(solution)/shard_map/ppermute | solution.py:249
  27.2 2.8 %collective-permute-start.12 = (bf16[272,128]{1,0:T(8,128)(2,1)S(1)}, bf16[272,128]{1,0:T(8,128)(2,1)S(1)}, u32[]{:S(2)}, u32[]{:S(2)}) collective-permute-start(bf16[272,128]{1,0:T(8,128)(2,1)S(1)} %add.9.refs_0_), channel_id=1, source_target_pairs={{0,16},{4,20},{8,24},{12,28},{16,0},{20,4},{24,8},{28,12},{1,17},{... | collective-permute-start | bytes 208904 | tf_op jit(solution)/shard_map/ppermute | solution.py:242
  30.0 1.6 %collective-permute-start.11 = (bf16[272,128]{1,0:T(8,128)(2,1)S(1)}, bf16[272,128]{1,0:T(8,128)(2,1)S(1)}, u32[]{:S(2)}, u32[]{:S(2)}) collective-permute-start(bf16[272,128]{1,0:T(8,128)(2,1)S(1)} %add.9.refs_0_), channel_id=1, source_target_pairs={{0,8},{4,12},{8,16},{12,20},{16,24},{20,28},{24,0},{28,4},{1,9},{5... | collective-permute-start | bytes 208904 | tf_op jit(solution)/shard_map/ppermute | solution.py:242
  31.6 2.2 %collective-permute-start.7 = (bf16[272,128]{1,0:T(8,128)(2,1)S(1)}, bf16[272,128]{1,0:T(8,128)(2,1)S(1)}, u32[]{:S(2)}, u32[]{:S(2)}) collective-permute-start(bf16[272,128]{1,0:T(8,128)(2,1)S(1)} %add.9.refs_0_), channel_id=1, source_target_pairs={{0,24},{4,28},{8,0},{12,4},{16,8},{20,12},{24,16},{28,20},{1,25},{... | collective-permute-start | bytes 208904 | tf_op jit(solution)/shard_map/ppermute | solution.py:242
  33.9 3.3 %collective-permute-done.7.refs_3_ = bf16[272,128]{1,0:T(8,128)(2,1)S(1)} collective-permute-done((bf16[272,128]{1,0:T(8,128)(2,1)S(1)}, bf16[272,128]{1,0:T(8,128)(2,1)S(1)}, u32[]{:S(2)}, u32[]{:S(2)}) %collective-permute-start.7) | collective-permute-done | bytes 69664 | tf_op jit(solution)/shard_map/ppermute | solution.py:242
  37.2 4.0 %screen.1.rows_ref = bf16[3072,1536]{1,0:T(8,128)(2,1)S(1)} custom-call(s32[6,12]{1,0:T(8,128)S(1)} %pad_add_fusion.mask_ref, bf16[3072,768]{1,0:T(8,128)(2,1)} %own_ref.1, bf16[3072,768]{1,0:T(8,128)(2,1)S(1)} %collective-permute-done.other_ref), custom_call_target="tpu_custom_call" | custom-call | flops 4718592 | bytes 18874368 | tf_op jit(solution)/shard_map/screen/pallas_call | solution.py:301
  41.6 1.6 %collective-permute-start.17 = (bf16[1536,128]{1,0:T(8,128)(2,1)S(1)}, bf16[1536,128]{1,0:T(8,128)(2,1)S(1)}, u32[]{:S(2)}, u32[]{:S(2)}) collective-permute-start(bf16[1536,128]{1,0:T(8,128)(2,1)S(1)} %fill.3.dense_ref), channel_id=1, source_target_pairs={{0,4},{1,5},{2,6},{3,7},{4,0},{5,1},{6,2},{7,3},{8,12},{9,13},{10,... | collective-permute-start | bytes 1179656 | tf_op jit(solution)/shard_map/ppermute | solution.py:249
  43.3 0.6 send_part.6
  43.9 1.6 %collective-permute-start.13 = (s16[528,128]{1,0:T(8,128)(2,1)S(1)}, s16[528,128]{1,0:T(8,128)(2,1)S(1)}, u32[]{:S(2)}, u32[]{:S(2)}) collective-permute-start(s16[528,128]{1,0:T(8,128)(2,1)S(1)} %send_part.6), channel_id=1, source_target_pairs={{0,2},{1,3},{2,0},{3,1},{4,6},{5,7},{6,4},{7,5},{8,10},{9,11},{10,... | collective-permute-start | bytes 405512 | tf_op jit(solution)/shard_map/ppermute | solution.py:249
  45.5 1.0 %send_part.7 = s16[1040,128]{1,0:T(8,128)(2,1)S(1)} custom-call(bf16[3072,1536]{1,0:T(8,128)(2,1)S(1)} %screen.1.rows_ref, bf16[1536,128]{1,0:T(8,128)(2,1)S(1)} %fill.3.dense_ref), custom_call_target="tpu_custom_call" | custom-call | flops 402653184 | bytes 3407872 | tf_op jit(solution)/shard_map/send_part/pallas_call | solution.py:359
  46.5 0.6 collective-permute-start.19
  47.1 2.6 %collective-permute-done.13.refs_0_ = s16[528,128]{1,0:T(8,128)(2,1)S(1)} collective-permute-done((s16[528,128]{1,0:T(8,128)(2,1)S(1)}, s16[528,128]{1,0:T(8,128)(2,1)S(1)}, u32[]{:S(2)}, u32[]{:S(2)}) %collective-permute-start.13) | collective-permute-done | bytes 135200 | tf_op jit(solution)/shard_map/ppermute | solution.py:249
  49.6 3.5 %collective-permute-start.16 = (bf16[272,256]{1,0:T(8,128)(2,1)S(1)}, bf16[272,256]{1,0:T(8,128)(2,1)S(1)}, u32[]{:S(2)}, u32[]{:S(2)}) collective-permute-start(bf16[272,256]{1,0:T(8,128)(2,1)S(1)} %add.10.refs_0_), channel_id=1, source_target_pairs={{0,24},{4,28},{8,0},{12,4},{16,8},{20,12},{24,16},{28,20},{1,25},{... | collective-permute-start | bytes 417800 | tf_op jit(solution)/shard_map/ppermute | solution.py:242
  53.2 0.6 collective-permute-start.14
  53.7 1.0 %send_part.8 = s16[1040,128]{1,0:T(8,128)(2,1)S(1)} custom-call(bf16[3072,1536]{1,0:T(8,128)(2,1)S(1)} %screen.1.rows_ref, bf16[1536,128]{1,0:T(8,128)(2,1)S(1)} %fill.3.dense_ref), custom_call_target="tpu_custom_call" | custom-call | flops 402653184 | bytes 3407872 | tf_op jit(solution)/shard_map/send_part/pallas_call | solution.py:359
  54.8 1.6 %collective-permute-start.18 = (s16[1040,128]{1,0:T(8,128)(2,1)S(1)}, s16[1040,128]{1,0:T(8,128)(2,1)S(1)}, u32[]{:S(2)}, u32[]{:S(2)}) collective-permute-start(s16[1040,128]{1,0:T(8,128)(2,1)S(1)} %send_part.8), channel_id=1, source_target_pairs={{0,2},{1,3},{2,0},{3,1},{4,6},{5,7},{6,4},{7,5},{8,10},{9,11},{10,... | collective-permute-start | bytes 798728 | tf_op jit(solution)/shard_map/ppermute | solution.py:249
  56.4 0.5 collective-permute-done.16.refs_3_
  57.0 0.4 collective-permute-start.23
  57.4 0.6 send_part.9
  58.0 4.7 %collective-permute-done.15.refs_2_ = bf16[272,256]{1,0:T(8,128)(2,1)S(1)} collective-permute-done((bf16[272,256]{1,0:T(8,128)(2,1)S(1)}, bf16[272,256]{1,0:T(8,128)(2,1)S(1)}, u32[]{:S(2)}, u32[]{:S(2)}) %collective-permute-start.15) | collective-permute-done | bytes 139296 | tf_op jit(solution)/shard_map/ppermute | solution.py:242
  62.7 1.4 %collective-permute-start.20 = (s16[528,128]{1,0:T(8,128)(2,1)S(1)}, s16[528,128]{1,0:T(8,128)(2,1)S(1)}, u32[]{:S(2)}, u32[]{:S(2)}) collective-permute-start(s16[528,128]{1,0:T(8,128)(2,1)S(1)} %send_part.9), channel_id=1, source_target_pairs={{0,2},{1,3},{2,0},{3,1},{4,6},{5,7},{6,4},{7,5},{8,10},{9,11},{10,... | collective-permute-start | bytes 405512 | tf_op jit(solution)/shard_map/ppermute | solution.py:249
  64.2 0.3 fill.4.dense_ref
  64.6 1.0 %send_part.10 = s16[1040,128]{1,0:T(8,128)(2,1)S(1)} custom-call(bf16[3072,1536]{1,0:T(8,128)(2,1)S(1)} %screen.1.rows_ref, bf16[1536,128]{1,0:T(8,128)(2,1)S(1)} %collective-permute-done.17.dense_ref), custom_call_target="tpu_custom_call" | custom-call | flops 402653184 | bytes 3407872 | tf_op jit(solution)/shard_map/send_part/pallas_call | solution.py:359
  65.6 0.6 collective-permute-start.27
  66.3 0.5 collective-permute-start.26
  66.8 1.6 %collective-permute-start.25 = (bf16[272,256]{1,0:T(8,128)(2,1)S(1)}, bf16[272,256]{1,0:T(8,128)(2,1)S(1)}, u32[]{:S(2)}, u32[]{:S(2)}) collective-permute-start(bf16[272,256]{1,0:T(8,128)(2,1)S(1)} %add.11.refs_0_), channel_id=1, source_target_pairs={{0,16},{4,20},{8,24},{12,28},{16,0},{20,4},{24,8},{28,12},{1,17},{... | collective-permute-start | bytes 417800 | tf_op jit(solution)/shard_map/ppermute | solution.py:242
  68.4 0.8 collective-permute-done.20.refs_1_
  69.2 1.0 %send_part.11 = s16[1040,128]{1,0:T(8,128)(2,1)S(1)} custom-call(bf16[3072,1536]{1,0:T(8,128)(2,1)S(1)} %screen.1.rows_ref, bf16[1536,128]{1,0:T(8,128)(2,1)S(1)} %collective-permute-done.17.dense_ref), custom_call_target="tpu_custom_call" | custom-call | flops 402653184 | bytes 3407872 | tf_op jit(solution)/shard_map/send_part/pallas_call | solution.py:359
  70.3 1.5 %collective-permute-start.21 = (s16[1040,128]{1,0:T(8,128)(2,1)S(1)}, s16[1040,128]{1,0:T(8,128)(2,1)S(1)}, u32[]{:S(2)}, u32[]{:S(2)}) collective-permute-start(s16[1040,128]{1,0:T(8,128)(2,1)S(1)} %send_part.11), channel_id=1, source_target_pairs={{0,2},{1,3},{2,0},{3,1},{4,6},{5,7},{6,4},{7,5},{8,10},{9,11},{10,... | collective-permute-start | bytes 798728 | tf_op jit(solution)/shard_map/ppermute | solution.py:249
  71.8 1.1 %collective-permute-done.26.refs_3_ = bf16[272,256]{1,0:T(8,128)(2,1)S(1)} collective-permute-done((bf16[272,256]{1,0:T(8,128)(2,1)S(1)}, bf16[272,256]{1,0:T(8,128)(2,1)S(1)}, u32[]{:S(2)}, u32[]{:S(2)}) %collective-permute-start.26) | collective-permute-done | bytes 139296 | tf_op jit(solution)/shard_map/ppermute | solution.py:242
  72.8 5.3 %collective-permute-done.25.refs_2_ = bf16[272,256]{1,0:T(8,128)(2,1)S(1)} collective-permute-done((bf16[272,256]{1,0:T(8,128)(2,1)S(1)}, bf16[272,256]{1,0:T(8,128)(2,1)S(1)}, u32[]{:S(2)}, u32[]{:S(2)}) %collective-permute-start.25) | collective-permute-done | bytes 139296 | tf_op jit(solution)/shard_map/ppermute | solution.py:242
  78.5 1.3 %join_part.3.refs_2_ = bf16[3072,256]{1,0:T(8,128)(2,1)} custom-call(bf16[3072,1536]{1,0:T(8,128)(2,1)S(1)} %screen.1.rows_ref, bf16[1536,256]{1,0:T(8,128)(2,1)S(1)} %fill.4.dense_ref, s16[528,128]{1,0:T(8,128)(2,1)S(1)} %collective-permute-done.13.refs_0_, s16[528,128]{1,0:T(8,128)(2,1)S(1)} %collective-permute-done.20.refs_1_), custom_call_target="tpu_custom_call" | custom-call | flops 402653184 | bytes 1835008 | tf_op jit(solution)/shard_map/join_part/pallas_call | solution.py:392
  79.7 1.7 %join_part.4.refs_4_ = bf16[3072,256]{1,0:T(8,128)(2,1)} custom-call(bf16[3072,1536]{1,0:T(8,128)(2,1)S(1)} %screen.1.rows_ref, bf16[1536,256]{1,0:T(8,128)(2,1)S(1)} %fill.4.dense_ref, s16[1040,128]{1,0:T(8,128)(2,1)S(1)} %collective-permute-done.19.refs_0_, s16[1040,128]{1,0:T(8,128)(2,1)S(1)} %collective-permute-done.27.refs_1_, ...), custom_call_target="tpu_custom_call", output_to_operand_aliasing={{}: (4, {})} | custom-call | flops 805306368 | bytes 3670016 | tf_op jit(solution)/shard_map/join_part/pallas_call | solution.py:392
  81.4 2.3 %join_whole.1.refs_2_ = bf16[3072,256]{1,0:T(8,128)(2,1)} custom-call(bf16[3072,1536]{1,0:T(8,128)(2,1)S(1)} %screen.1.rows_ref, bf16[1536,256]{1,0:T(8,128)(2,1)S(1)} %fill.4.dense_ref, s32[6,12]{1,0:T(8,128)S(1)} %collective-permute-done.22.refs_0_, bf16[512,768]{1,0:T(8,128)(2,1)S(1)} %collective-permute-done.9.refs_1_, ...), custom_call_target="tpu_custom_call", output_to_operand_aliasing={{}: (6, {})} | custom-call | flops 805306368 | bytes 3670016 | tf_op jit(solution)/shard_map/join_whole/pallas_call | solution.py:413
  83.7 1.7 %join_part.5 = bf16[3072,256]{1,0:T(8,128)(2,1)} custom-call(bf16[3072,1536]{1,0:T(8,128)(2,1)S(1)} %screen.1.rows_ref, bf16[1536,256]{1,0:T(8,128)(2,1)S(1)} %fill.4.dense_ref, s16[1040,128]{1,0:T(8,128)(2,1)S(1)} %collective-permute-done.18.refs_0_, s16[1040,128]{1,0:T(8,128)(2,1)S(1)} %collective-permute-done.21.refs_1_, ...), custom_call_target="tpu_custom_call", output_to_operand_aliasing={{}: (4, {})} | custom-call | flops 805306368 | bytes 3670016 | tf_op jit(solution)/shard_map/join_part/pallas_call | solution.py:392
  (33 shorter events, 1.6 us)
Async XLA Ops:
  0.0 15.7 %copy-start = (s32[4,1]{0,1:T(1,128)S(1)}, s32[4,1]{0,1:T(1,128)}, u32[]{:S(2)}) copy-start(s32[4,1]{0,1:T(1,128)} %param.11) | copy-start | bytes 52
  0.0 27.0 %copy-start.1 = (s32[12,3]{0,1:T(4,128)S(1)}, s32[12,3]{0,1:T(4,128)}, u32[]{:S(2)}) copy-start(s32[12,3]{0,1:T(4,128)} %param.7) | copy-start | bytes 436
  0.0 11.4 %collective-permute-start = (bf16[3072,768]{1,0:T(8,128)(2,1)}, bf16[3072,768]{1,0:T(8,128)(2,1)S(1)}, u32[]{:S(2)}, u32[]{:S(2)}) collective-permute-start(bf16[3072,768]{1,0:T(8,128)(2,1)} %own_ref.1), channel_id=1, source_target_pairs={{0,1},{1,0},{2,3},{3,2},{4,5},{5,4},{6,7},{7,6},{8,9},{9,8},{10,11... | collective-permute-start | bytes 14155784 | tf_op jit(solution)/shard_map/ppermute | solution.py:252
  1.6 25.0 %collective-permute-start.9 = (bf16[512,768]{1,0:T(8,128)(2,1)S(1)}, bf16[512,768]{1,0:T(8,128)(2,1)S(1)}, u32[]{:S(2)}, u32[]{:S(2)}) collective-permute-start(bf16[512,768]{1,0:T(8,128)(2,1)S(1)} %slice.3), channel_id=1, source_target_pairs={{0,2},{1,3},{2,0},{3,1},{4,6},{5,7},{6,4},{7,5},{8,10},{9,11},{10,... | collective-permute-start | bytes 2359304 | tf_op jit(solution)/shard_map/ppermute | solution.py:249
  5.9 6.6 %collective-permute-start.1 = (bf16[144,256]{1,0:T(8,128)(2,1)S(1)}, bf16[144,256]{1,0:T(8,128)(2,1)S(1)}, u32[]{:S(2)}, u32[]{:S(2)}) collective-permute-start(bf16[144,256]{1,0:T(8,128)(2,1)S(1)} %get-tuple-element.27), channel_id=1, source_target_pairs={{0,8},{4,12},{8,16},{12,20},{16,24},{20,28},{24,0},{28,4},{1,9},{5... | collective-permute-start | bytes 221192 | tf_op jit(solution)/shard_map/ppermute | solution.py:242
  7.5 7.9 %collective-permute-start.2 = (bf16[144,256]{1,0:T(8,128)(2,1)S(1)}, bf16[144,256]{1,0:T(8,128)(2,1)S(1)}, u32[]{:S(2)}, u32[]{:S(2)}) collective-permute-start(bf16[144,256]{1,0:T(8,128)(2,1)S(1)} %get-tuple-element.28), channel_id=1, source_target_pairs={{0,16},{4,20},{8,24},{12,28},{16,0},{20,4},{24,8},{28,12},{1,17},{... | collective-permute-start | bytes 221192 | tf_op jit(solution)/shard_map/ppermute | solution.py:242
  10.1 5.6 %collective-permute-start.3 = (bf16[144,256]{1,0:T(8,128)(2,1)S(1)}, bf16[144,256]{1,0:T(8,128)(2,1)S(1)}, u32[]{:S(2)}, u32[]{:S(2)}) collective-permute-start(bf16[144,256]{1,0:T(8,128)(2,1)S(1)} %get-tuple-element.29), channel_id=1, source_target_pairs={{0,24},{4,28},{8,0},{12,4},{16,8},{20,12},{24,16},{28,20},{1,25},{... | collective-permute-start | bytes 221192 | tf_op jit(solution)/shard_map/ppermute | solution.py:242
  16.4 7.7 %collective-permute-start.5 = (bf16[272,128]{1,0:T(8,128)(2,1)S(1)}, bf16[272,128]{1,0:T(8,128)(2,1)S(1)}, u32[]{:S(2)}, u32[]{:S(2)}) collective-permute-start(bf16[272,128]{1,0:T(8,128)(2,1)S(1)} %get-tuple-element.32), channel_id=1, source_target_pairs={{0,2},{1,3},{2,0},{3,1},{4,6},{5,7},{6,4},{7,5},{8,10},{9,11},{10,... | collective-permute-start | bytes 208904 | tf_op jit(solution)/shard_map/ppermute | solution.py:249
  17.0 9.6 %collective-permute-start.6 = (bf16[272,128]{1,0:T(8,128)(2,1)S(1)}, bf16[272,128]{1,0:T(8,128)(2,1)S(1)}, u32[]{:S(2)}, u32[]{:S(2)}) collective-permute-start(bf16[272,128]{1,0:T(8,128)(2,1)S(1)} %get-tuple-element.33), channel_id=1, source_target_pairs={{0,6},{1,7},{2,4},{3,5},{4,2},{5,3},{6,0},{7,1},{8,14},{9,15},{10,... | collective-permute-start | bytes 208904 | tf_op jit(solution)/shard_map/ppermute | solution.py:249
  26.6 14.6 %collective-permute-start.10 = (bf16[512,768]{1,0:T(8,128)(2,1)S(1)}, bf16[512,768]{1,0:T(8,128)(2,1)S(1)}, u32[]{:S(2)}, u32[]{:S(2)}) collective-permute-start(bf16[512,768]{1,0:T(8,128)(2,1)S(1)} %collective-permute-done.9.refs_1_), channel_id=1, source_target_pairs={{0,1},{1,0},{2,3},{3,2},{4,5},{5,4},{6,7},{7,6},{8,9},{9,8},{10,11... | collective-permute-start | bytes 2359304 | tf_op jit(solution)/shard_map/ppermute | solution.py:326
  26.7 7.2 %collective-permute-start.8 = (bf16[272,256]{1,0:T(8,128)(2,1)S(1)}, bf16[272,256]{1,0:T(8,128)(2,1)S(1)}, u32[]{:S(2)}, u32[]{:S(2)}) collective-permute-start(bf16[272,256]{1,0:T(8,128)(2,1)S(1)} %get-tuple-element.30), channel_id=1, source_target_pairs={{0,4},{1,5},{2,6},{3,7},{4,0},{5,1},{6,2},{7,3},{8,12},{9,13},{10,... | collective-permute-start | bytes 417800 | tf_op jit(solution)/shard_map/ppermute | solution.py:249
  27.0 4.6 %collective-permute-start.4 = (s32[3,12]{1,0:T(4,128)S(1)}, s32[3,12]{1,0:T(4,128)S(1)}, u32[]{:S(2)}, u32[]{:S(2)}) collective-permute-start(s32[3,12]{1,0:T(4,128)S(1)} %bitcast.3), channel_id=1, source_target_pairs={{0,1},{1,0},{2,3},{3,2},{4,5},{5,4},{6,7},{7,6},{8,9},{9,8},{10,11... | collective-permute-start | bytes 440 | tf_op jit(solution)/shard_map/ppermute | solution.py:287
  27.2 14.1 %collective-permute-start.12 = (bf16[272,128]{1,0:T(8,128)(2,1)S(1)}, bf16[272,128]{1,0:T(8,128)(2,1)S(1)}, u32[]{:S(2)}, u32[]{:S(2)}) collective-permute-start(bf16[272,128]{1,0:T(8,128)(2,1)S(1)} %add.9.refs_0_), channel_id=1, source_target_pairs={{0,16},{4,20},{8,24},{12,28},{16,0},{20,4},{24,8},{28,12},{1,17},{... | collective-permute-start | bytes 208904 | tf_op jit(solution)/shard_map/ppermute | solution.py:242
  30.0 11.2 %collective-permute-start.11 = (bf16[272,128]{1,0:T(8,128)(2,1)S(1)}, bf16[272,128]{1,0:T(8,128)(2,1)S(1)}, u32[]{:S(2)}, u32[]{:S(2)}) collective-permute-start(bf16[272,128]{1,0:T(8,128)(2,1)S(1)} %add.9.refs_0_), channel_id=1, source_target_pairs={{0,8},{4,12},{8,16},{12,20},{16,24},{20,28},{24,0},{28,4},{1,9},{5... | collective-permute-start | bytes 208904 | tf_op jit(solution)/shard_map/ppermute | solution.py:242
  31.6 5.6 %collective-permute-start.7 = (bf16[272,128]{1,0:T(8,128)(2,1)S(1)}, bf16[272,128]{1,0:T(8,128)(2,1)S(1)}, u32[]{:S(2)}, u32[]{:S(2)}) collective-permute-start(bf16[272,128]{1,0:T(8,128)(2,1)S(1)} %add.9.refs_0_), channel_id=1, source_target_pairs={{0,24},{4,28},{8,0},{12,4},{16,8},{20,12},{24,16},{28,20},{1,25},{... | collective-permute-start | bytes 208904 | tf_op jit(solution)/shard_map/ppermute | solution.py:242
  41.6 12.1 %collective-permute-start.17 = (bf16[1536,128]{1,0:T(8,128)(2,1)S(1)}, bf16[1536,128]{1,0:T(8,128)(2,1)S(1)}, u32[]{:S(2)}, u32[]{:S(2)}) collective-permute-start(bf16[1536,128]{1,0:T(8,128)(2,1)S(1)} %fill.3.dense_ref), channel_id=1, source_target_pairs={{0,4},{1,5},{2,6},{3,7},{4,0},{5,1},{6,2},{7,3},{8,12},{9,13},{10,... | collective-permute-start | bytes 1179656 | tf_op jit(solution)/shard_map/ppermute | solution.py:249
  43.9 5.7 %collective-permute-start.13 = (s16[528,128]{1,0:T(8,128)(2,1)S(1)}, s16[528,128]{1,0:T(8,128)(2,1)S(1)}, u32[]{:S(2)}, u32[]{:S(2)}) collective-permute-start(s16[528,128]{1,0:T(8,128)(2,1)S(1)} %send_part.6), channel_id=1, source_target_pairs={{0,2},{1,3},{2,0},{3,1},{4,6},{5,7},{6,4},{7,5},{8,10},{9,11},{10,... | collective-permute-start | bytes 405512 | tf_op jit(solution)/shard_map/ppermute | solution.py:249
  46.5 18.1 %collective-permute-start.19 = (s16[1040,128]{1,0:T(8,128)(2,1)S(1)}, s16[1040,128]{1,0:T(8,128)(2,1)S(1)}, u32[]{:S(2)}, u32[]{:S(2)}) collective-permute-start(s16[1040,128]{1,0:T(8,128)(2,1)S(1)} %send_part.7), channel_id=1, source_target_pairs={{0,2},{1,3},{2,0},{3,1},{4,6},{5,7},{6,4},{7,5},{8,10},{9,11},{10,... | collective-permute-start | bytes 798728 | tf_op jit(solution)/shard_map/ppermute | solution.py:249
  49.6 7.3 %collective-permute-start.16 = (bf16[272,256]{1,0:T(8,128)(2,1)S(1)}, bf16[272,256]{1,0:T(8,128)(2,1)S(1)}, u32[]{:S(2)}, u32[]{:S(2)}) collective-permute-start(bf16[272,256]{1,0:T(8,128)(2,1)S(1)} %add.10.refs_0_), channel_id=1, source_target_pairs={{0,24},{4,28},{8,0},{12,4},{16,8},{20,12},{24,16},{28,20},{1,25},{... | collective-permute-start | bytes 417800 | tf_op jit(solution)/shard_map/ppermute | solution.py:242
  53.2 9.6 %collective-permute-start.15 = (bf16[272,256]{1,0:T(8,128)(2,1)S(1)}, bf16[272,256]{1,0:T(8,128)(2,1)S(1)}, u32[]{:S(2)}, u32[]{:S(2)}) collective-permute-start(bf16[272,256]{1,0:T(8,128)(2,1)S(1)} %add.10.refs_0_), channel_id=1, source_target_pairs={{0,16},{4,20},{8,24},{12,28},{16,0},{20,4},{24,8},{28,12},{1,17},{... | collective-permute-start | bytes 417800 | tf_op jit(solution)/shard_map/ppermute | solution.py:242
  53.2 11.0 %collective-permute-start.14 = (bf16[272,256]{1,0:T(8,128)(2,1)S(1)}, bf16[272,256]{1,0:T(8,128)(2,1)S(1)}, u32[]{:S(2)}, u32[]{:S(2)}) collective-permute-start(bf16[272,256]{1,0:T(8,128)(2,1)S(1)} %add.10.refs_0_), channel_id=1, source_target_pairs={{0,8},{4,12},{8,16},{12,20},{16,24},{20,28},{24,0},{28,4},{1,9},{5... | collective-permute-start | bytes 417800 | tf_op jit(solution)/shard_map/ppermute | solution.py:242
  54.8 14.4 %collective-permute-start.18 = (s16[1040,128]{1,0:T(8,128)(2,1)S(1)}, s16[1040,128]{1,0:T(8,128)(2,1)S(1)}, u32[]{:S(2)}, u32[]{:S(2)}) collective-permute-start(s16[1040,128]{1,0:T(8,128)(2,1)S(1)} %send_part.8), channel_id=1, source_target_pairs={{0,2},{1,3},{2,0},{3,1},{4,6},{5,7},{6,4},{7,5},{8,10},{9,11},{10,... | collective-permute-start | bytes 798728 | tf_op jit(solution)/shard_map/ppermute | solution.py:249
  57.0 9.3 %collective-permute-start.23 = (bf16[272,256]{1,0:T(8,128)(2,1)S(1)}, bf16[272,256]{1,0:T(8,128)(2,1)S(1)}, u32[]{:S(2)}, u32[]{:S(2)}) collective-permute-start(bf16[272,256]{1,0:T(8,128)(2,1)S(1)} %get-tuple-element.43), channel_id=1, source_target_pairs={{0,4},{1,5},{2,6},{3,7},{4,0},{5,1},{6,2},{7,3},{8,12},{9,13},{10,... | collective-permute-start | bytes 417800 | tf_op jit(solution)/shard_map/ppermute | solution.py:249
  62.7 6.5 %collective-permute-start.20 = (s16[528,128]{1,0:T(8,128)(2,1)S(1)}, s16[528,128]{1,0:T(8,128)(2,1)S(1)}, u32[]{:S(2)}, u32[]{:S(2)}) collective-permute-start(s16[528,128]{1,0:T(8,128)(2,1)S(1)} %send_part.9), channel_id=1, source_target_pairs={{0,2},{1,3},{2,0},{3,1},{4,6},{5,7},{6,4},{7,5},{8,10},{9,11},{10,... | collective-permute-start | bytes 405512 | tf_op jit(solution)/shard_map/ppermute | solution.py:249
  65.6 14.1 %collective-permute-start.27 = (s16[1040,128]{1,0:T(8,128)(2,1)S(1)}, s16[1040,128]{1,0:T(8,128)(2,1)S(1)}, u32[]{:S(2)}, u32[]{:S(2)}) collective-permute-start(s16[1040,128]{1,0:T(8,128)(2,1)S(1)} %send_part.10), channel_id=1, source_target_pairs={{0,2},{1,3},{2,0},{3,1},{4,6},{5,7},{6,4},{7,5},{8,10},{9,11},{10,... | collective-permute-start | bytes 798728 | tf_op jit(solution)/shard_map/ppermute | solution.py:249
  66.3 6.5 %collective-permute-start.26 = (bf16[272,256]{1,0:T(8,128)(2,1)S(1)}, bf16[272,256]{1,0:T(8,128)(2,1)S(1)}, u32[]{:S(2)}, u32[]{:S(2)}) collective-permute-start(bf16[272,256]{1,0:T(8,128)(2,1)S(1)} %add.11.refs_0_), channel_id=1, source_target_pairs={{0,24},{4,28},{8,0},{12,4},{16,8},{20,12},{24,16},{28,20},{1,25},{... | collective-permute-start | bytes 417800 | tf_op jit(solution)/shard_map/ppermute | solution.py:242
  66.8 11.3 %collective-permute-start.25 = (bf16[272,256]{1,0:T(8,128)(2,1)S(1)}, bf16[272,256]{1,0:T(8,128)(2,1)S(1)}, u32[]{:S(2)}, u32[]{:S(2)}) collective-permute-start(bf16[272,256]{1,0:T(8,128)(2,1)S(1)} %add.11.refs_0_), channel_id=1, source_target_pairs={{0,16},{4,20},{8,24},{12,28},{16,0},{20,4},{24,8},{28,12},{1,17},{... | collective-permute-start | bytes 417800 | tf_op jit(solution)/shard_map/ppermute | solution.py:242
  69.2 8.9 %collective-permute-start.24 = (bf16[272,256]{1,0:T(8,128)(2,1)S(1)}, bf16[272,256]{1,0:T(8,128)(2,1)S(1)}, u32[]{:S(2)}, u32[]{:S(2)}) collective-permute-start(bf16[272,256]{1,0:T(8,128)(2,1)S(1)} %add.11.refs_0_), channel_id=1, source_target_pairs={{0,8},{4,12},{8,16},{12,20},{16,24},{20,28},{24,0},{28,4},{1,9},{5... | collective-permute-start | bytes 417800 | tf_op jit(solution)/shard_map/ppermute | solution.py:242
  70.3 13.5 %collective-permute-start.21 = (s16[1040,128]{1,0:T(8,128)(2,1)S(1)}, s16[1040,128]{1,0:T(8,128)(2,1)S(1)}, u32[]{:S(2)}, u32[]{:S(2)}) collective-permute-start(s16[1040,128]{1,0:T(8,128)(2,1)S(1)} %send_part.11), channel_id=1, source_target_pairs={{0,2},{1,3},{2,0},{3,1},{4,6},{5,7},{6,4},{7,5},{8,10},{9,11},{10,... | collective-permute-start | bytes 798728 | tf_op jit(solution)/shard_map/ppermute | solution.py:249
  72.8 8.6 %collective-permute-start.22 = (s32[6,12]{1,0:T(8,128)S(1)}, s32[6,12]{1,0:T(8,128)S(1)}, u32[]{:S(2)}, u32[]{:S(2)}) collective-permute-start(s32[6,12]{1,0:T(8,128)S(1)} %pad_add_fusion.mask_ref), channel_id=1, source_target_pairs={{0,2},{1,3},{2,0},{3,1},{4,6},{5,7},{6,4},{7,5},{8,10},{9,11},{10,... | collective-permute-start | bytes 872 | tf_op jit(solution)/shard_map/ppermute | solution.py:249

commit v11 on v9

--- a/solution.py
+++ b/solution.py
@@ -15,7 +15,7 @@
 CODE_TOP = 32767.0
 FRACTION = 8192.0
 META_ROWS = 16
-SCREEN_BLOCKS = 3
+SCREEN_PARTS = 4
 PARAMS = pltpu.CompilerParams(vmem_limit_bytes=16 * 1024 * 1024)
 SMEM = pl.BlockSpec(memory_space=pltpu.SMEM)
 VMEM = pl.BlockSpec(memory_space=pltpu.VMEM)
@@ -29,6 +29,10 @@
         for step in range(STEPS):
             offsets.add(-((core - step) // CORES) % pairs)
     return sorted(offsets)
+
+
+def partner(place, number, peers):
+    return place ^ number if peers & (peers - 1) == 0 else lax.rem(place + peers - number, peers)
 
 
 def row_chunks(block_count, cuts):
@@ -48,7 +52,7 @@
         info = jnp.where(lane == slot, jnp.broadcast_to(list_ref[0, :, slot : slot + 1], lane.shape), info)
     info = info.astype(jnp.float32).astype(panel_ref.dtype)
     for shift, piece_ref in enumerate(piece_refs):
-        first = lax.rem(place + shift, peers) * share
+        first = partner(place, shift if peers & (peers - 1) == 0 else peers - shift, peers) * share
         start = pl.multiple_of(lax.rem(first, tile_width), META_ROWS)
         piece_ref[pl.ds(0, share), :] = panel_ref[0, 0, first // tile_width, pl.ds(start, share), :]
         piece_ref[pl.ds(share, META_ROWS), :] = info
@@ -74,10 +78,9 @@
             step = lax.rem(CORES * offset - shift + col_peers, col_peers)
             holder = plan_ref[plan_ref.shape[0] - 1, jnp.minimum(step, STEPS - 1)]
             here = (step < STEPS) & (lax.rem(holder, HALVES) == half)
-            back = lax.rem(row // HALVES - holder // HALVES + peers, peers)
             for number, piece_ref in enumerate(piece_refs):
 
-                @pl.when(here & (back == number))
+                @pl.when(here & (partner(row // HALVES, number, peers) == holder // HALVES))
                 def _():
                     for out_ref, columns in targets:
                         line = lax.broadcasted_iota(jnp.int32, (META_ROWS, out_ref.shape[1]), 0)
@@ -105,7 +108,7 @@
         count = entry(group, slots)
         starts = [group * width + entry(group, slot) * tile_width for slot in range(slots)]
         for shift, piece_ref in enumerate(piece_refs):
-            first = lax.rem(place - shift + peers, peers) * share
+            first = partner(place, shift, peers) * share
             slot = first // tile_width
             start = starts[0]
             for other in range(1, slots):
@@ -117,29 +120,36 @@
                 dense_ref[pl.ds(spot, share), :] = piece_ref[pl.ds(group * share, share), :]
 
 
-def screen_kernel(tile_width, block_rows, mask_ref, own_ref, other_ref, out_ref):
+def screen_kernel(tile_width, block_rows, mask_ref, own_ref, other_ref, out_ref, sems):
     full_width = own_ref.shape[1]
     tiles = full_width // tile_width
-    block_count = own_ref.shape[0] // block_rows
-    together = SCREEN_BLOCKS if block_count % SCREEN_BLOCKS == 0 else 1
-
-    def body(own_block):
-        for number in range(together):
-            block = pl.program_id(0) * together + number
-            lines = pl.ds(pl.multiple_of(block * block_rows, block_rows), block_rows)
-            for tile in range(CORES * tiles):
-                live = mask_ref[tile, block].astype(jnp.float32).astype(own_block.dtype)
-                if tile < tiles:
-                    part = own_block[pl.ds(number * block_rows, block_rows), pl.ds(tile * tile_width, tile_width)]
-                else:
-                    part = other_ref[lines, pl.ds((tile - tiles) * tile_width, tile_width)]
-                out_ref[lines, pl.ds(tile * tile_width, tile_width)] = part * live
-
-    pltpu.emit_pipeline(
-        body,
-        grid=(block_count // together,),
-        in_specs=[pl.BlockSpec((together * block_rows, full_width), lambda i: (i, 0))],
-    )(own_ref)
+    parts = sems.shape[0]
+    blocks = own_ref.shape[0] // block_rows // parts
+    copies = []
+    for part in range(parts):
+        lines = pl.ds(part * blocks * block_rows, blocks * block_rows)
+        copies.append(
+            pltpu.make_async_copy(own_ref.at[lines, :], out_ref.at[lines, pl.ds(0, full_width)], sems.at[part])
+        )
+        copies[-1].start()
+
+    def screen(source_ref, group, block):
+        lines = pl.ds(pl.multiple_of(block * block_rows, block_rows), block_rows)
+        for tile in range(tiles):
+            live = mask_ref[group * tiles + tile, block].astype(jnp.float32).astype(out_ref.dtype)
+            part = source_ref[lines, pl.ds(tile * tile_width, tile_width)]
+            out_ref[lines, pl.ds((group * tiles + tile) * tile_width, tile_width)] = part * live
+
+    @pl.loop(0, parts * blocks)
+    def _(block):
+        screen(other_ref, 1, block)
+
+    for part in range(parts):
+        copies[part].wait()
+
+        @pl.loop(part * blocks, (part + 1) * blocks)
+        def _(block):
+            screen(out_ref, 0, block)
 
 
 def send_kernel(first, span, height, rows_ref, dense_ref, code_ref, scale_ref):
@@ -212,7 +222,11 @@
     chunks = row_chunks(block_count, NEAR_CUTS + FAR_CUTS)
 
     def along(value, shift):
-        return lax.ppermute(value, "row", [(r, (r + HALVES * shift) % row_peers) for r in range(row_peers)])
+        pairs = []
+        for r in range(row_peers):
+            source = r // HALVES ^ shift if peers & (peers - 1) == 0 else (r // HALVES - shift) % peers
+            pairs.append((source * HALVES + r % HALVES, r))
+        return lax.ppermute(value, "row", pairs)
 
     def across(value, flip, down):
         pairs = []
@@ -277,6 +291,7 @@
                 bytes_accessed=4 * CORES * row_count * full_width,
                 transcendentals=0,
             ),
+            scratch_shapes=[pltpu.SemaphoreType.DMA((SCREEN_PARTS if block_count % SCREEN_PARTS == 0 else 1,))],
             name="screen",
         )(after(plan, *earlier), in_hbm(amplitudes), other)
 

time: 69.8 us -> 69.4 us (level)
  waiting for transfers between devices: 19.9 us -> 22.1 us
  starting transfers between devices: 29.3 us -> 27.7 us
  Pallas kernels: 18.8 us -> 17.8 us
    ppermute x11, waiting for transfers between devices: 11.3 us -> 13.2 us  [across(): return lax.ppermute(value, ('row', 'col'), pairs)]
    ppermute x11, starting transfers between devices: 14.3 us -> 12.7 us  [across(): return lax.ppermute(value, ('row', 'col'), pairs)]
    pallas_call x1, Pallas kernels: 4.03 us -> 3.07 us  [screen(): pl.pallas_call(partial(screen_kernel, tile_width, block_rows), in_specs=[...]
  transfers between devices with their start and end apart: 22 -> 22, of which waited for: 13 -> 10; matrix products, arithmetic and copies ran while one was open for 1% -> 1% of each run, Pallas kernels for 25% -> 24%
where the time goes in v11:
time: 69.4 us; the launch traced here: 69.3 us
  starting transfers between devices  27.7 us (40%)
  waiting for transfers between devices  22.1 us (32%)
  Pallas kernels  17.8 us (26%)
  between operations  0.84 us (1%)
  other arithmetic  0.77 us (1%)
    ppermute x9, starting transfers between devices, along(): return lax.ppermute(value, 'row', pairs)  14.5 us
    ppermute x11, waiting for transfers between devices, across(): return lax.ppermute(value, ('row', 'col'), pairs)  13.2 us
    ppermute x11, starting transfers between devices, across(): return lax.ppermute(value, ('row', 'col'), pairs)  12.7 us
    ppermute x9, waiting for transfers between devices, along(): return lax.ppermute(value, 'row', pairs)  8.52 us
    pallas_call x7, Pallas kernels, shards(): pl.pallas_call(partial(send_kernel, first, span, block_rows), in_specs=[V...  6.43 us
    pallas_call x4, Pallas kernels, shards(): pl.pallas_call(partial(join_kernel, first, span, block_rows, skips), in_s...  5.87 us
    pallas_call x1, Pallas kernels, screen(): pl.pallas_call(partial(screen_kernel, tile_width, block_rows), in_specs=[...  3.07 us
  transfers between devices with their start and end apart: 22, of which 10 were waited for; matrix products, arithmetic and copies ran while one was open for 1% of the time, Pallas kernels for 24%

profile of v11, /device:TPU:0, one launch (start us, length us, event | category | flops | bytes accessed | tf_op | source)
XLA Modules:
  0.0 69.3 jit_solution(16051931490541625227)
XLA Ops:
  0.0 0.5 collective-permute-start.8
  0.5 0.1 collective-permute-start
  1.2 1.0 %pack.1 = (bf16[144,256]{1,0:T(8,128)(2,1)S(1)}, bf16[144,256]{1,0:T(8,128)(2,1)S(1)}, bf16[144,256]{1,0:T(8,128)(2,1)S(1)}, bf16[144,256]{1,0:T(8,128)(2,1)S(1)}) custom-call(s32[1,1,2]{2,1,0:T(1,128)} %list_ref.1, s32[1,1]{1,0:T(1,128)S(6)} %copy.13.count_ref, bf16[1,1,2,256,256]{4,3,2,1,0:T(8,128)(2,1)} %panel_ref.1), custom_call_target="tpu_custom_call" | custom-call | tf_op jit(solution)/shard_map/pack/pallas_call | solution.py:247
  2.2 3.0 %collective-permute-start.1 = (bf16[144,256]{1,0:T(8,128)(2,1)S(1)}, bf16[144,256]{1,0:T(8,128)(2,1)S(1)}, u32[]{:S(2)}, u32[]{:S(2)}) collective-permute-start(bf16[144,256]{1,0:T(8,128)(2,1)S(1)} %get-tuple-element.22), channel_id=1, source_target_pairs={{8,0},{12,4},{0,8},{4,12},{24,16},{28,20},{16,24},{20,28},{9,1},{1... | collective-permute-start | bytes 221192 | tf_op jit(solution)/shard_map/ppermute | solution.py:229
  5.3 2.6 %collective-permute-start.2 = (bf16[144,256]{1,0:T(8,128)(2,1)S(1)}, bf16[144,256]{1,0:T(8,128)(2,1)S(1)}, u32[]{:S(2)}, u32[]{:S(2)}) collective-permute-start(bf16[144,256]{1,0:T(8,128)(2,1)S(1)} %get-tuple-element.23), channel_id=1, source_target_pairs={{16,0},{20,4},{24,8},{28,12},{0,16},{4,20},{8,24},{12,28},{17,1},{... | collective-permute-start | bytes 221192 | tf_op jit(solution)/shard_map/ppermute | solution.py:229
  7.8 0.0 collective-permute-start.3
  7.8 0.4 collective-permute-done
  8.2 0.7 %pad_add_fusion.plan_ref.mask_ref = s32[7,12]{1,0:T(8,128)S(1)} fusion(s32[1,4]{1,0:T(1,128)} %bitcast.4, s32[3,12]{1,0:T(4,128)S(1)} %collective-permute-done, s32[3,12]{1,0:T(4,128)} %bitcast.3), kind=kLoop, calls=%fused_computation | loop fusion | flops 168 | bytes 640 | tf_op jit(solution)/shard_map/concatenate | solution.py:242
  8.9 4.3 %collective-permute-done.2.refs_2_ = bf16[144,256]{1,0:T(8,128)(2,1)S(1)} collective-permute-done((bf16[144,256]{1,0:T(8,128)(2,1)S(1)}, bf16[144,256]{1,0:T(8,128)(2,1)S(1)}, u32[]{:S(2)}, u32[]{:S(2)}) %collective-permute-start.2) | collective-permute-done | bytes 73760 | tf_op jit(solution)/shard_map/ppermute | solution.py:229
  13.3 0.8 %collective-permute-done.3.refs_3_ = bf16[144,256]{1,0:T(8,128)(2,1)S(1)} collective-permute-done((bf16[144,256]{1,0:T(8,128)(2,1)S(1)}, bf16[144,256]{1,0:T(8,128)(2,1)S(1)}, u32[]{:S(2)}, u32[]{:S(2)}) %collective-permute-start.3) | collective-permute-done | bytes 73760 | tf_op jit(solution)/shard_map/ppermute | solution.py:229
  14.1 0.8 %choose.1 = (bf16[272,256]{1,0:T(8,128)(2,1)S(1)}, bf16[272,128]{1,0:T(8,128)(2,1)S(1)}, bf16[272,128]{1,0:T(8,128)(2,1)S(1)}) custom-call(s32[7,12]{1,0:T(8,128)S(1)} %pad_add_fusion.plan_ref.mask_ref, bf16[144,256]{1,0:T(8,128)(2,1)S(1)} %get-tuple-element.21.refs_0_, bf16[144,256]{1,0:T(8,128)(2,1)S(1)} %collective-permute-done.1.refs_1_, ...), custom_call_target="tpu_custom_call" | custom-call | tf_op jit(solution)/shard_map/choose/pallas_call | solution.py:262
  14.9 1.5 %collective-permute-start.4 = (bf16[272,128]{1,0:T(8,128)(2,1)S(1)}, bf16[272,128]{1,0:T(8,128)(2,1)S(1)}, u32[]{:S(2)}, u32[]{:S(2)}) collective-permute-start(bf16[272,128]{1,0:T(8,128)(2,1)S(1)} %get-tuple-element.25), channel_id=1, source_target_pairs={{0,2},{1,3},{2,0},{3,1},{4,6},{5,7},{6,4},{7,5},{8,10},{9,11},{10,... | collective-permute-start | bytes 208904 | tf_op jit(solution)/shard_map/ppermute | solution.py:236
  16.4 1.5 %collective-permute-start.5 = (bf16[272,128]{1,0:T(8,128)(2,1)S(1)}, bf16[272,128]{1,0:T(8,128)(2,1)S(1)}, u32[]{:S(2)}, u32[]{:S(2)}) collective-permute-start(bf16[272,128]{1,0:T(8,128)(2,1)S(1)} %get-tuple-element.26), channel_id=1, source_target_pairs={{0,6},{1,7},{2,4},{3,5},{4,2},{5,3},{6,0},{7,1},{8,14},{9,15},{10,... | collective-permute-start | bytes 208904 | tf_op jit(solution)/shard_map/ppermute | solution.py:236
  17.9 0.5 collective-permute-start.7
  18.4 1.0 %collective-permute-done.4 = bf16[272,128]{1,0:T(8,128)(2,1)S(1)} collective-permute-done((bf16[272,128]{1,0:T(8,128)(2,1)S(1)}, bf16[272,128]{1,0:T(8,128)(2,1)S(1)}, u32[]{:S(2)}, u32[]{:S(2)}) %collective-permute-start.4) | collective-permute-done | bytes 69664 | tf_op jit(solution)/shard_map/ppermute | solution.py:236
  19.4 2.3 %collective-permute-done.5 = bf16[272,128]{1,0:T(8,128)(2,1)S(1)} collective-permute-done((bf16[272,128]{1,0:T(8,128)(2,1)S(1)}, bf16[272,128]{1,0:T(8,128)(2,1)S(1)}, u32[]{:S(2)}, u32[]{:S(2)}) %collective-permute-start.5) | collective-permute-done | bytes 69664 | tf_op jit(solution)/shard_map/ppermute | solution.py:236
  21.7 2.4 %collective-permute-start.6 = (bf16[272,128]{1,0:T(8,128)(2,1)S(1)}, bf16[272,128]{1,0:T(8,128)(2,1)S(1)}, u32[]{:S(2)}, u32[]{:S(2)}) collective-permute-start(bf16[272,128]{1,0:T(8,128)(2,1)S(1)} %add.8.refs_0_), channel_id=1, source_target_pairs={{24,0},{28,4},{16,8},{20,12},{8,16},{12,20},{0,24},{4,28},{25,1},{... | collective-permute-start | bytes 208904 | tf_op jit(solution)/shard_map/ppermute | solution.py:229
  24.1 0.4 collective-permute-start.10
  24.5 1.6 %collective-permute-start.9 = (bf16[272,128]{1,0:T(8,128)(2,1)S(1)}, bf16[272,128]{1,0:T(8,128)(2,1)S(1)}, u32[]{:S(2)}, u32[]{:S(2)}) collective-permute-start(bf16[272,128]{1,0:T(8,128)(2,1)S(1)} %add.8.refs_0_), channel_id=1, source_target_pairs={{8,0},{12,4},{0,8},{4,12},{24,16},{28,20},{16,24},{20,28},{9,1},{1... | collective-permute-start | bytes 208904 | tf_op jit(solution)/shard_map/ppermute | solution.py:229
  26.2 1.7 %collective-permute-done.6.refs_3_ = bf16[272,128]{1,0:T(8,128)(2,1)S(1)} collective-permute-done((bf16[272,128]{1,0:T(8,128)(2,1)S(1)}, bf16[272,128]{1,0:T(8,128)(2,1)S(1)}, u32[]{:S(2)}, u32[]{:S(2)}) %collective-permute-start.6) | collective-permute-done | bytes 69664 | tf_op jit(solution)/shard_map/ppermute | solution.py:229
  27.8 3.1 %screen.1.rows_ref = bf16[3072,1536]{1,0:T(8,128)(2,1)S(1)} custom-call(s32[7,12]{1,0:T(8,128)S(1)} %pad_add_fusion.plan_ref.mask_ref, bf16[3072,768]{1,0:T(8,128)(2,1)} %own_ref.1, bf16[3072,768]{1,0:T(8,128)(2,1)S(1)} %collective-permute-done.8.other_ref), custom_call_target="tpu_custom_call" | custom-call | flops 4718592 | bytes 18874368 | tf_op jit(solution)/shard_map/screen/pallas_call | solution.py:283
  30.9 0.3 fill.2.dense_ref
  31.3 1.7 %collective-permute-start.15 = (bf16[1536,128]{1,0:T(8,128)(2,1)S(1)}, bf16[1536,128]{1,0:T(8,128)(2,1)S(1)}, u32[]{:S(2)}, u32[]{:S(2)}) collective-permute-start(bf16[1536,128]{1,0:T(8,128)(2,1)S(1)} %fill.2.dense_ref), channel_id=1, source_target_pairs={{0,4},{1,5},{2,6},{3,7},{4,0},{5,1},{6,2},{7,3},{8,12},{9,13},{10,... | collective-permute-start | bytes 1179656 | tf_op jit(solution)/shard_map/ppermute | solution.py:236
  33.0 0.6 send_part.7
  33.6 0.5 collective-permute-start.11
  34.1 1.2 %send_part.8 = s16[1296,128]{1,0:T(8,128)(2,1)S(1)} custom-call(bf16[3072,1536]{1,0:T(8,128)(2,1)S(1)} %screen.1.rows_ref, bf16[1536,128]{1,0:T(8,128)(2,1)S(1)} %fill.2.dense_ref), custom_call_target="tpu_custom_call" | custom-call | flops 503316480 | bytes 4259840 | tf_op jit(solution)/shard_map/send_part/pallas_call | solution.py:337
  35.4 1.7 %collective-permute-start.17 = (s16[1296,128]{1,0:T(8,128)(2,1)S(1)}, s16[1296,128]{1,0:T(8,128)(2,1)S(1)}, u32[]{:S(2)}, u32[]{:S(2)}) collective-permute-start(s16[1296,128]{1,0:T(8,128)(2,1)S(1)} %send_part.8), channel_id=1, source_target_pairs={{0,2},{1,3},{2,0},{3,1},{4,6},{5,7},{6,4},{7,5},{8,10},{9,11},{10,... | collective-permute-start | bytes 995336 | tf_op jit(solution)/shard_map/ppermute | solution.py:236
  37.0 2.8 %collective-permute-done.11.refs_0_ = s16[528,128]{1,0:T(8,128)(2,1)S(1)} collective-permute-done((s16[528,128]{1,0:T(8,128)(2,1)S(1)}, s16[528,128]{1,0:T(8,128)(2,1)S(1)}, u32[]{:S(2)}, u32[]{:S(2)}) %collective-permute-start.11) | collective-permute-done | bytes 135200 | tf_op jit(solution)/shard_map/ppermute | solution.py:236
  39.8 1.2 %send_part.9 = s16[1296,128]{1,0:T(8,128)(2,1)S(1)} custom-call(bf16[3072,1536]{1,0:T(8,128)(2,1)S(1)} %screen.1.rows_ref, bf16[1536,128]{1,0:T(8,128)(2,1)S(1)} %fill.2.dense_ref), custom_call_target="tpu_custom_call" | custom-call | flops 503316480 | bytes 4259840 | tf_op jit(solution)/shard_map/send_part/pallas_call | solution.py:337
  41.1 0.9 %collective-permute-start.16 = (s16[1296,128]{1,0:T(8,128)(2,1)S(1)}, s16[1296,128]{1,0:T(8,128)(2,1)S(1)}, u32[]{:S(2)}, u32[]{:S(2)}) collective-permute-start(s16[1296,128]{1,0:T(8,128)(2,1)S(1)} %send_part.9), channel_id=1, source_target_pairs={{0,2},{1,3},{2,0},{3,1},{4,6},{5,7},{6,4},{7,5},{8,10},{9,11},{10,... | collective-permute-start | bytes 995336 | tf_op jit(solution)/shard_map/ppermute | solution.py:236
  42.0 2.0 %collective-permute-start.14 = (bf16[272,256]{1,0:T(8,128)(2,1)S(1)}, bf16[272,256]{1,0:T(8,128)(2,1)S(1)}, u32[]{:S(2)}, u32[]{:S(2)}) collective-permute-start(bf16[272,256]{1,0:T(8,128)(2,1)S(1)} %add.9.refs_0_), channel_id=1, source_target_pairs={{24,0},{28,4},{16,8},{20,12},{8,16},{12,20},{0,24},{4,28},{25,1},{... | collective-permute-start | bytes 417800 | tf_op jit(solution)/shard_map/ppermute | solution.py:229
  44.0 2.4 %collective-permute-start.12 = (bf16[272,256]{1,0:T(8,128)(2,1)S(1)}, bf16[272,256]{1,0:T(8,128)(2,1)S(1)}, u32[]{:S(2)}, u32[]{:S(2)}) collective-permute-start(bf16[272,256]{1,0:T(8,128)(2,1)S(1)} %add.9.refs_0_), channel_id=1, source_target_pairs={{8,0},{12,4},{0,8},{4,12},{24,16},{28,20},{16,24},{20,28},{9,1},{1... | collective-permute-start | bytes 417800 | tf_op jit(solution)/shard_map/ppermute | solution.py:229
  46.3 0.6 send_part.10
  47.0 1.3 %collective-permute-start.18 = (s16[528,128]{1,0:T(8,128)(2,1)S(1)}, s16[528,128]{1,0:T(8,128)(2,1)S(1)}, u32[]{:S(2)}, u32[]{:S(2)}) collective-permute-start(s16[528,128]{1,0:T(8,128)(2,1)S(1)} %send_part.10), channel_id=1, source_target_pairs={{0,2},{1,3},{2,0},{3,1},{4,6},{5,7},{6,4},{7,5},{8,10},{9,11},{10,... | collective-permute-start | bytes 405512 | tf_op jit(solution)/shard_map/ppermute | solution.py:236
  48.3 1.2 %send_part.11 = s16[1296,128]{1,0:T(8,128)(2,1)S(1)} custom-call(bf16[3072,1536]{1,0:T(8,128)(2,1)S(1)} %screen.1.rows_ref, bf16[1536,128]{1,0:T(8,128)(2,1)S(1)} %collective-permute-done.15.dense_ref), custom_call_target="tpu_custom_call" | custom-call | flops 503316480 | bytes 4259840 | tf_op jit(solution)/shard_map/send_part/pallas_call | solution.py:337
  49.5 0.9 %collective-permute-start.19 = (s16[1296,128]{1,0:T(8,128)(2,1)S(1)}, s16[1296,128]{1,0:T(8,128)(2,1)S(1)}, u32[]{:S(2)}, u32[]{:S(2)}) collective-permute-start(s16[1296,128]{1,0:T(8,128)(2,1)S(1)} %send_part.11), channel_id=1, source_target_pairs={{0,2},{1,3},{2,0},{3,1},{4,6},{5,7},{6,4},{7,5},{8,10},{9,11},{10,... | collective-permute-start | bytes 995336 | tf_op jit(solution)/shard_map/ppermute | solution.py:236
  50.4 1.6 %collective-permute-done.13.refs_2_ = bf16[272,256]{1,0:T(8,128)(2,1)S(1)} collective-permute-done((bf16[272,256]{1,0:T(8,128)(2,1)S(1)}, bf16[272,256]{1,0:T(8,128)(2,1)S(1)}, u32[]{:S(2)}, u32[]{:S(2)}) %collective-permute-start.13) | collective-permute-done | bytes 139296 | tf_op jit(solution)/shard_map/ppermute | solution.py:229
  52.1 0.3 fill.3.dense_ref
  52.4 4.3 %collective-permute-done.18.refs_1_ = s16[528,128]{1,0:T(8,128)(2,1)S(1)} collective-permute-done((s16[528,128]{1,0:T(8,128)(2,1)S(1)}, s16[528,128]{1,0:T(8,128)(2,1)S(1)}, u32[]{:S(2)}, u32[]{:S(2)}) %collective-permute-start.18) | collective-permute-done | bytes 135200 | tf_op jit(solution)/shard_map/ppermute | solution.py:236
  56.7 1.0 %send_part.12 = s16[1040,128]{1,0:T(8,128)(2,1)S(1)} custom-call(bf16[3072,1536]{1,0:T(8,128)(2,1)S(1)} %screen.1.rows_ref, bf16[1536,128]{1,0:T(8,128)(2,1)S(1)} %collective-permute-done.15.dense_ref), custom_call_target="tpu_custom_call" | custom-call | flops 402653184 | bytes 3407872 | tf_op jit(solution)/shard_map/send_part/pallas_call | solution.py:337
  57.8 1.1 %collective-permute-start.21 = (s16[1040,128]{1,0:T(8,128)(2,1)S(1)}, s16[1040,128]{1,0:T(8,128)(2,1)S(1)}, u32[]{:S(2)}, u32[]{:S(2)}) collective-permute-start(s16[1040,128]{1,0:T(8,128)(2,1)S(1)} %send_part.12), channel_id=1, source_target_pairs={{0,2},{1,3},{2,0},{3,1},{4,6},{5,7},{6,4},{7,5},{8,10},{9,11},{10,... | collective-permute-start | bytes 798728 | tf_op jit(solution)/shard_map/ppermute | solution.py:236
  58.9 1.2 %join_part.4.refs_2_ = bf16[3072,256]{1,0:T(8,128)(2,1)} custom-call(bf16[3072,1536]{1,0:T(8,128)(2,1)S(1)} %screen.1.rows_ref, bf16[1536,256]{1,0:T(8,128)(2,1)S(1)} %fill.3.dense_ref, s16[528,128]{1,0:T(8,128)(2,1)S(1)} %collective-permute-done.11.refs_0_, s16[528,128]{1,0:T(8,128)(2,1)S(1)} %collective-permute-done.18.refs_1_), custom_call_target="tpu_custom_call" | custom-call | flops 402653184 | bytes 1835008 | tf_op jit(solution)/shard_map/join_part/pallas_call | solution.py:366
  60.1 2.8 %collective-permute-done.19.refs_1_ = s16[1296,128]{1,0:T(8,128)(2,1)S(1)} collective-permute-done((s16[1296,128]{1,0:T(8,128)(2,1)S(1)}, s16[1296,128]{1,0:T(8,128)(2,1)S(1)}, u32[]{:S(2)}, u32[]{:S(2)}) %collective-permute-start.19) | collective-permute-done | bytes 331808 | tf_op jit(solution)/shard_map/ppermute | solution.py:236
  63.0 0.4 send_part.13
  63.4 1.2 %collective-permute-start.20 = (s16[272,128]{1,0:T(8,128)(2,1)S(1)}, s16[272,128]{1,0:T(8,128)(2,1)S(1)}, u32[]{:S(2)}, u32[]{:S(2)}) collective-permute-start(s16[272,128]{1,0:T(8,128)(2,1)S(1)} %send_part.13), channel_id=1, source_target_pairs={{0,2},{1,3},{2,0},{3,1},{4,6},{5,7},{6,4},{7,5},{8,10},{9,11},{10,... | collective-permute-start | bytes 208904 | tf_op jit(solution)/shard_map/ppermute | solution.py:236
  64.6 1.9 %join_part.5.refs_2_ = bf16[3072,256]{1,0:T(8,128)(2,1)} custom-call(bf16[3072,1536]{1,0:T(8,128)(2,1)S(1)} %screen.1.rows_ref, bf16[1536,256]{1,0:T(8,128)(2,1)S(1)} %fill.3.dense_ref, s16[1296,128]{1,0:T(8,128)(2,1)S(1)} %collective-permute-done.17.refs_0_, s16[1296,128]{1,0:T(8,128)(2,1)S(1)} %collective-permute-done.19.refs_1_, ...), custom_call_target="tpu_custom_call", output_to_operand_aliasing={{}: (4, {})} | custom-call | flops 1006632960 | bytes 4587520 | tf_op jit(solution)/shard_map/join_part/pallas_call | solution.py:366
  66.5 1.7 %join_part.6.refs_2_ = bf16[3072,256]{1,0:T(8,128)(2,1)} custom-call(bf16[3072,1536]{1,0:T(8,128)(2,1)S(1)} %screen.1.rows_ref, bf16[1536,256]{1,0:T(8,128)(2,1)S(1)} %fill.3.dense_ref, s16[1296,128]{1,0:T(8,128)(2,1)S(1)} %collective-permute-done.16.refs_0_, s16[1040,128]{1,0:T(8,128)(2,1)S(1)} %collective-permute-done.21.refs_1_, ...), custom_call_target="tpu_custom_call", output_to_operand_aliasing={{}: (4, {})} | custom-call | flops 805306368 | bytes 3670016 | tf_op jit(solution)/shard_map/join_part/pallas_call | solution.py:366
  68.2 1.0 %join_part.7 = bf16[3072,256]{1,0:T(8,128)(2,1)} custom-call(bf16[3072,1536]{1,0:T(8,128)(2,1)S(1)} %screen.1.rows_ref, bf16[1536,256]{1,0:T(8,128)(2,1)S(1)} %fill.3.dense_ref, s16[1296,128]{1,0:T(8,128)(2,1)S(1)} %collective-permute-done.16.refs_0_, s16[272,128]{1,0:T(8,128)(2,1)S(1)} %collective-permute-done.20.refs_1_, ...), custom_call_target="tpu_custom_call", output_to_operand_aliasing={{}: (4, {})} | custom-call | flops 201326592 | bytes 917504 | tf_op jit(solution)/shard_map/join_part/pallas_call | solution.py:366
  (15 shorter events, 0.1 us)
Async XLA Ops:
  0.0 27.8 %collective-permute-start.8 = (bf16[3072,768]{1,0:T(8,128)(2,1)}, bf16[3072,768]{1,0:T(8,128)(2,1)S(1)}, u32[]{:S(2)}, u32[]{:S(2)}) collective-permute-start(bf16[3072,768]{1,0:T(8,128)(2,1)} %own_ref.1), channel_id=1, source_target_pairs={{0,1},{1,0},{2,3},{3,2},{4,5},{5,4},{6,7},{7,6},{8,9},{9,8},{10,11... | collective-permute-start | bytes 14155784 | tf_op jit(solution)/shard_map/ppermute | solution.py:239
  0.5 7.7 %collective-permute-start = (s32[3,12]{1,0:T(4,128)}, s32[3,12]{1,0:T(4,128)S(1)}, u32[]{:S(2)}, u32[]{:S(2)}) collective-permute-start(s32[3,12]{1,0:T(4,128)} %bitcast.2), channel_id=1, source_target_pairs={{0,1},{1,0},{2,3},{3,2},{4,5},{5,4},{6,7},{7,6},{8,9},{9,8},{10,11... | collective-permute-start | bytes 440 | tf_op jit(solution)/shard_map/ppermute | solution.py:240
  2.2 6.7 %collective-permute-start.1 = (bf16[144,256]{1,0:T(8,128)(2,1)S(1)}, bf16[144,256]{1,0:T(8,128)(2,1)S(1)}, u32[]{:S(2)}, u32[]{:S(2)}) collective-permute-start(bf16[144,256]{1,0:T(8,128)(2,1)S(1)} %get-tuple-element.22), channel_id=1, source_target_pairs={{8,0},{12,4},{0,8},{4,12},{24,16},{28,20},{16,24},{20,28},{9,1},{1... | collective-permute-start | bytes 221192 | tf_op jit(solution)/shard_map/ppermute | solution.py:229
  5.3 8.0 %collective-permute-start.2 = (bf16[144,256]{1,0:T(8,128)(2,1)S(1)}, bf16[144,256]{1,0:T(8,128)(2,1)S(1)}, u32[]{:S(2)}, u32[]{:S(2)}) collective-permute-start(bf16[144,256]{1,0:T(8,128)(2,1)S(1)} %get-tuple-element.23), channel_id=1, source_target_pairs={{16,0},{20,4},{24,8},{28,12},{0,16},{4,20},{8,24},{12,28},{17,1},{... | collective-permute-start | bytes 221192 | tf_op jit(solution)/shard_map/ppermute | solution.py:229
  7.8 6.3 %collective-permute-start.3 = (bf16[144,256]{1,0:T(8,128)(2,1)S(1)}, bf16[144,256]{1,0:T(8,128)(2,1)S(1)}, u32[]{:S(2)}, u32[]{:S(2)}) collective-permute-start(bf16[144,256]{1,0:T(8,128)(2,1)S(1)} %get-tuple-element.24), channel_id=1, source_target_pairs={{24,0},{28,4},{16,8},{20,12},{8,16},{12,20},{0,24},{4,28},{25,1},{... | collective-permute-start | bytes 221192 | tf_op jit(solution)/shard_map/ppermute | solution.py:229
  14.9 4.5 %collective-permute-start.4 = (bf16[272,128]{1,0:T(8,128)(2,1)S(1)}, bf16[272,128]{1,0:T(8,128)(2,1)S(1)}, u32[]{:S(2)}, u32[]{:S(2)}) collective-permute-start(bf16[272,128]{1,0:T(8,128)(2,1)S(1)} %get-tuple-element.25), channel_id=1, source_target_pairs={{0,2},{1,3},{2,0},{3,1},{4,6},{5,7},{6,4},{7,5},{8,10},{9,11},{10,... | collective-permute-start | bytes 208904 | tf_op jit(solution)/shard_map/ppermute | solution.py:236
  16.4 5.2 %collective-permute-start.5 = (bf16[272,128]{1,0:T(8,128)(2,1)S(1)}, bf16[272,128]{1,0:T(8,128)(2,1)S(1)}, u32[]{:S(2)}, u32[]{:S(2)}) collective-permute-start(bf16[272,128]{1,0:T(8,128)(2,1)S(1)} %get-tuple-element.26), channel_id=1, source_target_pairs={{0,6},{1,7},{2,4},{3,5},{4,2},{5,3},{6,0},{7,1},{8,14},{9,15},{10,... | collective-permute-start | bytes 208904 | tf_op jit(solution)/shard_map/ppermute | solution.py:236
  17.9 8.2 %collective-permute-start.7 = (bf16[272,256]{1,0:T(8,128)(2,1)S(1)}, bf16[272,256]{1,0:T(8,128)(2,1)S(1)}, u32[]{:S(2)}, u32[]{:S(2)}) collective-permute-start(bf16[272,256]{1,0:T(8,128)(2,1)S(1)} %get-tuple-element.27), channel_id=1, source_target_pairs={{0,4},{1,5},{2,6},{3,7},{4,0},{5,1},{6,2},{7,3},{8,12},{9,13},{10,... | collective-permute-start | bytes 417800 | tf_op jit(solution)/shard_map/ppermute | solution.py:236
  21.7 6.2 %collective-permute-start.6 = (bf16[272,128]{1,0:T(8,128)(2,1)S(1)}, bf16[272,128]{1,0:T(8,128)(2,1)S(1)}, u32[]{:S(2)}, u32[]{:S(2)}) collective-permute-start(bf16[272,128]{1,0:T(8,128)(2,1)S(1)} %add.8.refs_0_), channel_id=1, source_target_pairs={{24,0},{28,4},{16,8},{20,12},{8,16},{12,20},{0,24},{4,28},{25,1},{... | collective-permute-start | bytes 208904 | tf_op jit(solution)/shard_map/ppermute | solution.py:229
  24.1 6.8 %collective-permute-start.10 = (bf16[272,128]{1,0:T(8,128)(2,1)S(1)}, bf16[272,128]{1,0:T(8,128)(2,1)S(1)}, u32[]{:S(2)}, u32[]{:S(2)}) collective-permute-start(bf16[272,128]{1,0:T(8,128)(2,1)S(1)} %add.8.refs_0_), channel_id=1, source_target_pairs={{16,0},{20,4},{24,8},{28,12},{0,16},{4,20},{8,24},{12,28},{17,1},{... | collective-permute-start | bytes 208904 | tf_op jit(solution)/shard_map/ppermute | solution.py:229
  24.5 6.4 %collective-permute-start.9 = (bf16[272,128]{1,0:T(8,128)(2,1)S(1)}, bf16[272,128]{1,0:T(8,128)(2,1)S(1)}, u32[]{:S(2)}, u32[]{:S(2)}) collective-permute-start(bf16[272,128]{1,0:T(8,128)(2,1)S(1)} %add.8.refs_0_), channel_id=1, source_target_pairs={{8,0},{12,4},{0,8},{4,12},{24,16},{28,20},{16,24},{20,28},{9,1},{1... | collective-permute-start | bytes 208904 | tf_op jit(solution)/shard_map/ppermute | solution.py:229
  31.3 8.6 %collective-permute-start.15 = (bf16[1536,128]{1,0:T(8,128)(2,1)S(1)}, bf16[1536,128]{1,0:T(8,128)(2,1)S(1)}, u32[]{:S(2)}, u32[]{:S(2)}) collective-permute-start(bf16[1536,128]{1,0:T(8,128)(2,1)S(1)} %fill.2.dense_ref), channel_id=1, source_target_pairs={{0,4},{1,5},{2,6},{3,7},{4,0},{5,1},{6,2},{7,3},{8,12},{9,13},{10,... | collective-permute-start | bytes 1179656 | tf_op jit(solution)/shard_map/ppermute | solution.py:236
  33.6 6.2 %collective-permute-start.11 = (s16[528,128]{1,0:T(8,128)(2,1)S(1)}, s16[528,128]{1,0:T(8,128)(2,1)S(1)}, u32[]{:S(2)}, u32[]{:S(2)}) collective-permute-start(s16[528,128]{1,0:T(8,128)(2,1)S(1)} %send_part.7), channel_id=1, source_target_pairs={{0,2},{1,3},{2,0},{3,1},{4,6},{5,7},{6,4},{7,5},{8,10},{9,11},{10,... | collective-permute-start | bytes 405512 | tf_op jit(solution)/shard_map/ppermute | solution.py:236
  35.4 11.6 %collective-permute-start.17 = (s16[1296,128]{1,0:T(8,128)(2,1)S(1)}, s16[1296,128]{1,0:T(8,128)(2,1)S(1)}, u32[]{:S(2)}, u32[]{:S(2)}) collective-permute-start(s16[1296,128]{1,0:T(8,128)(2,1)S(1)} %send_part.8), channel_id=1, source_target_pairs={{0,2},{1,3},{2,0},{3,1},{4,6},{5,7},{6,4},{7,5},{8,10},{9,11},{10,... | collective-permute-start | bytes 995336 | tf_op jit(solution)/shard_map/ppermute | solution.py:236
  41.1 15.7 %collective-permute-start.16 = (s16[1296,128]{1,0:T(8,128)(2,1)S(1)}, s16[1296,128]{1,0:T(8,128)(2,1)S(1)}, u32[]{:S(2)}, u32[]{:S(2)}) collective-permute-start(s16[1296,128]{1,0:T(8,128)(2,1)S(1)} %send_part.9), channel_id=1, source_target_pairs={{0,2},{1,3},{2,0},{3,1},{4,6},{5,7},{6,4},{7,5},{8,10},{9,11},{10,... | collective-permute-start | bytes 995336 | tf_op jit(solution)/shard_map/ppermute | solution.py:236
  42.0 7.6 %collective-permute-start.14 = (bf16[272,256]{1,0:T(8,128)(2,1)S(1)}, bf16[272,256]{1,0:T(8,128)(2,1)S(1)}, u32[]{:S(2)}, u32[]{:S(2)}) collective-permute-start(bf16[272,256]{1,0:T(8,128)(2,1)S(1)} %add.9.refs_0_), channel_id=1, source_target_pairs={{24,0},{28,4},{16,8},{20,12},{8,16},{12,20},{0,24},{4,28},{25,1},{... | collective-permute-start | bytes 417800 | tf_op jit(solution)/shard_map/ppermute | solution.py:229
  44.0 8.1 %collective-permute-start.13 = (bf16[272,256]{1,0:T(8,128)(2,1)S(1)}, bf16[272,256]{1,0:T(8,128)(2,1)S(1)}, u32[]{:S(2)}, u32[]{:S(2)}) collective-permute-start(bf16[272,256]{1,0:T(8,128)(2,1)S(1)} %add.9.refs_0_), channel_id=1, source_target_pairs={{16,0},{20,4},{24,8},{28,12},{0,16},{4,20},{8,24},{12,28},{17,1},{... | collective-permute-start | bytes 417800 | tf_op jit(solution)/shard_map/ppermute | solution.py:229
  44.0 8.1 %collective-permute-start.12 = (bf16[272,256]{1,0:T(8,128)(2,1)S(1)}, bf16[272,256]{1,0:T(8,128)(2,1)S(1)}, u32[]{:S(2)}, u32[]{:S(2)}) collective-permute-start(bf16[272,256]{1,0:T(8,128)(2,1)S(1)} %add.9.refs_0_), channel_id=1, source_target_pairs={{8,0},{12,4},{0,8},{4,12},{24,16},{28,20},{16,24},{20,28},{9,1},{1... | collective-permute-start | bytes 417800 | tf_op jit(solution)/shard_map/ppermute | solution.py:229
  47.0 9.7 %collective-permute-start.18 = (s16[528,128]{1,0:T(8,128)(2,1)S(1)}, s16[528,128]{1,0:T(8,128)(2,1)S(1)}, u32[]{:S(2)}, u32[]{:S(2)}) collective-permute-start(s16[528,128]{1,0:T(8,128)(2,1)S(1)} %send_part.10), channel_id=1, source_target_pairs={{0,2},{1,3},{2,0},{3,1},{4,6},{5,7},{6,4},{7,5},{8,10},{9,11},{10,... | collective-permute-start | bytes 405512 | tf_op jit(solution)/shard_map/ppermute | solution.py:236
  49.5 13.4 %collective-permute-start.19 = (s16[1296,128]{1,0:T(8,128)(2,1)S(1)}, s16[1296,128]{1,0:T(8,128)(2,1)S(1)}, u32[]{:S(2)}, u32[]{:S(2)}) collective-permute-start(s16[1296,128]{1,0:T(8,128)(2,1)S(1)} %send_part.11), channel_id=1, source_target_pairs={{0,2},{1,3},{2,0},{3,1},{4,6},{5,7},{6,4},{7,5},{8,10},{9,11},{10,... | collective-permute-start | bytes 995336 | tf_op jit(solution)/shard_map/ppermute | solution.py:236
  57.8 8.7 %collective-permute-start.21 = (s16[1040,128]{1,0:T(8,128)(2,1)S(1)}, s16[1040,128]{1,0:T(8,128)(2,1)S(1)}, u32[]{:S(2)}, u32[]{:S(2)}) collective-permute-start(s16[1040,128]{1,0:T(8,128)(2,1)S(1)} %send_part.12), channel_id=1, source_target_pairs={{0,2},{1,3},{2,0},{3,1},{4,6},{5,7},{6,4},{7,5},{8,10},{9,11},{10,... | collective-permute-start | bytes 798728 | tf_op jit(solution)/shard_map/ppermute | solution.py:236
  63.4 4.8 %collective-permute-start.20 = (s16[272,128]{1,0:T(8,128)(2,1)S(1)}, s16[272,128]{1,0:T(8,128)(2,1)S(1)}, u32[]{:S(2)}, u32[]{:S(2)}) collective-permute-start(s16[272,128]{1,0:T(8,128)(2,1)S(1)} %send_part.13), channel_id=1, source_target_pairs={{0,2},{1,3},{2,0},{3,1},{4,6},{5,7},{6,4},{7,5},{8,10},{9,11},{10,... | collective-permute-start | bytes 208904 | tf_op jit(solution)/shard_map/ppermute | solution.py:236

commit v12 on v11

--- a/solution.py
+++ b/solution.py
@@ -303,7 +303,7 @@
         data = across(near, 0, offset) + across(far, 1, offset)
         held = [data] + [along(data, shift) for shift in range(1, peers)]
         if screened is None:
-            screened = screen(held[-1], own)
+            screened = screen(held[1], own)
         near_weights[offset] = fill([after(held[0], screened)] + held[1:])
         far_weights[offset] = across(near_weights[offset], 1, 0)
 

time: 69.4 us -> 69.7 us (level)
    ppermute x11, starting transfers between devices: 12.7 us -> 13.7 us  [across(): return lax.ppermute(value, ('row', 'col'), pairs)]
  transfers between devices with their start and end apart: 22 -> 22, of which waited for: 10 -> 11; matrix products, arithmetic and copies ran while one was open for 1% -> 1% of each run, Pallas kernels for 24% -> 24%
where the time goes in v12:
time: 69.7 us; the launch traced here: 69.5 us
  starting transfers between devices  28 us (40%)
  waiting for transfers between devices  22.1 us (32%)
  Pallas kernels  17.8 us (26%)
  between operations  0.83 us (1%)
  other arithmetic  0.77 us (1%)
    ppermute x9, starting transfers between devices, along(): return lax.ppermute(value, 'row', pairs)  13.8 us
    ppermute x11, starting transfers between devices, across(): return lax.ppermute(value, ('row', 'col'), pairs)  13.7 us
    ppermute x11, waiting for transfers between devices, across(): return lax.ppermute(value, ('row', 'col'), pairs)  13.1 us
    ppermute x9, waiting for transfers between devices, along(): return lax.ppermute(value, 'row', pairs)  8.65 us
    pallas_call x7, Pallas kernels, shards(): pl.pallas_call(partial(send_kernel, first, span, block_rows), in_specs=[V...  6.43 us
    pallas_call x4, Pallas kernels, shards(): pl.pallas_call(partial(join_kernel, first, span, block_rows, skips), in_s...  5.87 us
    pallas_call x1, Pallas kernels, screen(): pl.pallas_call(partial(screen_kernel, tile_width, block_rows), in_specs=[...  3.07 us
  transfers between devices with their start and end apart: 22, of which 11 were waited for; matrix products, arithmetic and copies ran while one was open for 1% of the time, Pallas kernels for 24%

profile of v12, /device:TPU:0, one launch (start us, length us, event | category | flops | bytes accessed | tf_op | source)
XLA Modules:
  0.0 69.5 jit_solution(1803595498495088432)
XLA Ops:
  0.0 0.5 collective-permute-start.8
  0.5 0.1 collective-permute-start
  1.2 1.0 %pack.1 = (bf16[144,256]{1,0:T(8,128)(2,1)S(1)}, bf16[144,256]{1,0:T(8,128)(2,1)S(1)}, bf16[144,256]{1,0:T(8,128)(2,1)S(1)}, bf16[144,256]{1,0:T(8,128)(2,1)S(1)}) custom-call(s32[1,1,2]{2,1,0:T(1,128)} %list_ref.1, s32[1,1]{1,0:T(1,128)S(6)} %copy.13.count_ref, bf16[1,1,2,256,256]{4,3,2,1,0:T(8,128)(2,1)} %panel_ref.1), custom_call_target="tpu_custom_call" | custom-call | tf_op jit(solution)/shard_map/pack/pallas_call | solution.py:247
  2.2 3.0 %collective-permute-start.1 = (bf16[144,256]{1,0:T(8,128)(2,1)S(1)}, bf16[144,256]{1,0:T(8,128)(2,1)S(1)}, u32[]{:S(2)}, u32[]{:S(2)}) collective-permute-start(bf16[144,256]{1,0:T(8,128)(2,1)S(1)} %get-tuple-element.22), channel_id=1, source_target_pairs={{8,0},{12,4},{0,8},{4,12},{24,16},{28,20},{16,24},{20,28},{9,1},{1... | collective-permute-start | bytes 221192 | tf_op jit(solution)/shard_map/ppermute | solution.py:229
  5.3 2.6 %collective-permute-start.2 = (bf16[144,256]{1,0:T(8,128)(2,1)S(1)}, bf16[144,256]{1,0:T(8,128)(2,1)S(1)}, u32[]{:S(2)}, u32[]{:S(2)}) collective-permute-start(bf16[144,256]{1,0:T(8,128)(2,1)S(1)} %get-tuple-element.23), channel_id=1, source_target_pairs={{16,0},{20,4},{24,8},{28,12},{0,16},{4,20},{8,24},{12,28},{17,1},{... | collective-permute-start | bytes 221192 | tf_op jit(solution)/shard_map/ppermute | solution.py:229
  7.8 0.0 collective-permute-start.3
  7.8 0.4 collective-permute-done
  8.2 0.7 %pad_add_fusion.plan_ref.mask_ref = s32[7,12]{1,0:T(8,128)S(1)} fusion(s32[1,4]{1,0:T(1,128)} %bitcast.4, s32[3,12]{1,0:T(4,128)S(1)} %collective-permute-done, s32[3,12]{1,0:T(4,128)} %bitcast.3), kind=kLoop, calls=%fused_computation | loop fusion | flops 168 | bytes 640 | tf_op jit(solution)/shard_map/concatenate | solution.py:242
  8.9 4.3 %collective-permute-done.2.refs_2_ = bf16[144,256]{1,0:T(8,128)(2,1)S(1)} collective-permute-done((bf16[144,256]{1,0:T(8,128)(2,1)S(1)}, bf16[144,256]{1,0:T(8,128)(2,1)S(1)}, u32[]{:S(2)}, u32[]{:S(2)}) %collective-permute-start.2) | collective-permute-done | bytes 73760 | tf_op jit(solution)/shard_map/ppermute | solution.py:229
  13.3 0.8 %collective-permute-done.3.refs_3_ = bf16[144,256]{1,0:T(8,128)(2,1)S(1)} collective-permute-done((bf16[144,256]{1,0:T(8,128)(2,1)S(1)}, bf16[144,256]{1,0:T(8,128)(2,1)S(1)}, u32[]{:S(2)}, u32[]{:S(2)}) %collective-permute-start.3) | collective-permute-done | bytes 73760 | tf_op jit(solution)/shard_map/ppermute | solution.py:229
  14.1 0.8 %choose.1 = (bf16[272,256]{1,0:T(8,128)(2,1)S(1)}, bf16[272,128]{1,0:T(8,128)(2,1)S(1)}, bf16[272,128]{1,0:T(8,128)(2,1)S(1)}) custom-call(s32[7,12]{1,0:T(8,128)S(1)} %pad_add_fusion.plan_ref.mask_ref, bf16[144,256]{1,0:T(8,128)(2,1)S(1)} %get-tuple-element.21.refs_0_, bf16[144,256]{1,0:T(8,128)(2,1)S(1)} %collective-permute-done.1.refs_1_, ...), custom_call_target="tpu_custom_call" | custom-call | tf_op jit(solution)/shard_map/choose/pallas_call | solution.py:262
  14.9 1.6 %collective-permute-start.4 = (bf16[272,128]{1,0:T(8,128)(2,1)S(1)}, bf16[272,128]{1,0:T(8,128)(2,1)S(1)}, u32[]{:S(2)}, u32[]{:S(2)}) collective-permute-start(bf16[272,128]{1,0:T(8,128)(2,1)S(1)} %get-tuple-element.25), channel_id=1, source_target_pairs={{0,2},{1,3},{2,0},{3,1},{4,6},{5,7},{6,4},{7,5},{8,10},{9,11},{10,... | collective-permute-start | bytes 208904 | tf_op jit(solution)/shard_map/ppermute | solution.py:236
  16.4 1.5 %collective-permute-start.5 = (bf16[272,128]{1,0:T(8,128)(2,1)S(1)}, bf16[272,128]{1,0:T(8,128)(2,1)S(1)}, u32[]{:S(2)}, u32[]{:S(2)}) collective-permute-start(bf16[272,128]{1,0:T(8,128)(2,1)S(1)} %get-tuple-element.26), channel_id=1, source_target_pairs={{0,6},{1,7},{2,4},{3,5},{4,2},{5,3},{6,0},{7,1},{8,14},{9,15},{10,... | collective-permute-start | bytes 208904 | tf_op jit(solution)/shard_map/ppermute | solution.py:236
  17.9 0.5 collective-permute-start.7
  18.4 1.0 %collective-permute-done.4 = bf16[272,128]{1,0:T(8,128)(2,1)S(1)} collective-permute-done((bf16[272,128]{1,0:T(8,128)(2,1)S(1)}, bf16[272,128]{1,0:T(8,128)(2,1)S(1)}, u32[]{:S(2)}, u32[]{:S(2)}) %collective-permute-start.4) | collective-permute-done | bytes 69664 | tf_op jit(solution)/shard_map/ppermute | solution.py:236
  19.4 2.3 %collective-permute-done.5 = bf16[272,128]{1,0:T(8,128)(2,1)S(1)} collective-permute-done((bf16[272,128]{1,0:T(8,128)(2,1)S(1)}, bf16[272,128]{1,0:T(8,128)(2,1)S(1)}, u32[]{:S(2)}, u32[]{:S(2)}) %collective-permute-start.5) | collective-permute-done | bytes 69664 | tf_op jit(solution)/shard_map/ppermute | solution.py:236
  21.7 1.4 %collective-permute-start.6 = (bf16[272,128]{1,0:T(8,128)(2,1)S(1)}, bf16[272,128]{1,0:T(8,128)(2,1)S(1)}, u32[]{:S(2)}, u32[]{:S(2)}) collective-permute-start(bf16[272,128]{1,0:T(8,128)(2,1)S(1)} %add.8.refs_0_), channel_id=1, source_target_pairs={{8,0},{12,4},{0,8},{4,12},{24,16},{28,20},{16,24},{20,28},{9,1},{1... | collective-permute-start | bytes 208904 | tf_op jit(solution)/shard_map/ppermute | solution.py:229
  23.1 2.4 %collective-permute-start.10 = (bf16[272,128]{1,0:T(8,128)(2,1)S(1)}, bf16[272,128]{1,0:T(8,128)(2,1)S(1)}, u32[]{:S(2)}, u32[]{:S(2)}) collective-permute-start(bf16[272,128]{1,0:T(8,128)(2,1)S(1)} %add.8.refs_0_), channel_id=1, source_target_pairs={{24,0},{28,4},{16,8},{20,12},{8,16},{12,20},{0,24},{4,28},{25,1},{... | collective-permute-start | bytes 208904 | tf_op jit(solution)/shard_map/ppermute | solution.py:229
  25.5 1.3 %collective-permute-done.6.refs_1_ = bf16[272,128]{1,0:T(8,128)(2,1)S(1)} collective-permute-done((bf16[272,128]{1,0:T(8,128)(2,1)S(1)}, bf16[272,128]{1,0:T(8,128)(2,1)S(1)}, u32[]{:S(2)}, u32[]{:S(2)}) %collective-permute-start.6) | collective-permute-done | bytes 69664 | tf_op jit(solution)/shard_map/ppermute | solution.py:229
  26.8 3.1 %screen.1.rows_ref = bf16[3072,1536]{1,0:T(8,128)(2,1)S(1)} custom-call(s32[7,12]{1,0:T(8,128)S(1)} %pad_add_fusion.plan_ref.mask_ref, bf16[3072,768]{1,0:T(8,128)(2,1)} %own_ref.1, bf16[3072,768]{1,0:T(8,128)(2,1)S(1)} %collective-permute-done.8.other_ref), custom_call_target="tpu_custom_call" | custom-call | flops 4718592 | bytes 18874368 | tf_op jit(solution)/shard_map/screen/pallas_call | solution.py:283
  29.9 0.8 %collective-permute-done.9.refs_2_ = bf16[272,128]{1,0:T(8,128)(2,1)S(1)} collective-permute-done((bf16[272,128]{1,0:T(8,128)(2,1)S(1)}, bf16[272,128]{1,0:T(8,128)(2,1)S(1)}, u32[]{:S(2)}, u32[]{:S(2)}) %collective-permute-start.9) | collective-permute-done | bytes 69664 | tf_op jit(solution)/shard_map/ppermute | solution.py:229
  30.7 0.3 fill.2.dense_ref
  31.0 1.7 %collective-permute-start.15 = (bf16[1536,128]{1,0:T(8,128)(2,1)S(1)}, bf16[1536,128]{1,0:T(8,128)(2,1)S(1)}, u32[]{:S(2)}, u32[]{:S(2)}) collective-permute-start(bf16[1536,128]{1,0:T(8,128)(2,1)S(1)} %fill.2.dense_ref), channel_id=1, source_target_pairs={{0,4},{1,5},{2,6},{3,7},{4,0},{5,1},{6,2},{7,3},{8,12},{9,13},{10,... | collective-permute-start | bytes 1179656 | tf_op jit(solution)/shard_map/ppermute | solution.py:236
  32.7 0.6 send_part.7
  33.3 0.5 collective-permute-start.11
  33.8 1.2 %send_part.8 = s16[1296,128]{1,0:T(8,128)(2,1)S(1)} custom-call(bf16[3072,1536]{1,0:T(8,128)(2,1)S(1)} %screen.1.rows_ref, bf16[1536,128]{1,0:T(8,128)(2,1)S(1)} %fill.2.dense_ref), custom_call_target="tpu_custom_call" | custom-call | flops 503316480 | bytes 4259840 | tf_op jit(solution)/shard_map/send_part/pallas_call | solution.py:337
  35.1 1.6 %collective-permute-start.17 = (s16[1296,128]{1,0:T(8,128)(2,1)S(1)}, s16[1296,128]{1,0:T(8,128)(2,1)S(1)}, u32[]{:S(2)}, u32[]{:S(2)}) collective-permute-start(s16[1296,128]{1,0:T(8,128)(2,1)S(1)} %send_part.8), channel_id=1, source_target_pairs={{0,2},{1,3},{2,0},{3,1},{4,6},{5,7},{6,4},{7,5},{8,10},{9,11},{10,... | collective-permute-start | bytes 995336 | tf_op jit(solution)/shard_map/ppermute | solution.py:236
  36.7 2.5 %collective-permute-done.11.refs_0_ = s16[528,128]{1,0:T(8,128)(2,1)S(1)} collective-permute-done((s16[528,128]{1,0:T(8,128)(2,1)S(1)}, s16[528,128]{1,0:T(8,128)(2,1)S(1)}, u32[]{:S(2)}, u32[]{:S(2)}) %collective-permute-start.11) | collective-permute-done | bytes 135200 | tf_op jit(solution)/shard_map/ppermute | solution.py:236
  39.2 1.2 %send_part.9 = s16[1296,128]{1,0:T(8,128)(2,1)S(1)} custom-call(bf16[3072,1536]{1,0:T(8,128)(2,1)S(1)} %screen.1.rows_ref, bf16[1536,128]{1,0:T(8,128)(2,1)S(1)} %fill.2.dense_ref), custom_call_target="tpu_custom_call" | custom-call | flops 503316480 | bytes 4259840 | tf_op jit(solution)/shard_map/send_part/pallas_call | solution.py:337
  40.4 1.2 %collective-permute-start.16 = (s16[1296,128]{1,0:T(8,128)(2,1)S(1)}, s16[1296,128]{1,0:T(8,128)(2,1)S(1)}, u32[]{:S(2)}, u32[]{:S(2)}) collective-permute-start(s16[1296,128]{1,0:T(8,128)(2,1)S(1)} %send_part.9), channel_id=1, source_target_pairs={{0,2},{1,3},{2,0},{3,1},{4,6},{5,7},{6,4},{7,5},{8,10},{9,11},{10,... | collective-permute-start | bytes 995336 | tf_op jit(solution)/shard_map/ppermute | solution.py:236
  41.7 2.4 %collective-permute-start.14 = (bf16[272,256]{1,0:T(8,128)(2,1)S(1)}, bf16[272,256]{1,0:T(8,128)(2,1)S(1)}, u32[]{:S(2)}, u32[]{:S(2)}) collective-permute-start(bf16[272,256]{1,0:T(8,128)(2,1)S(1)} %add.9.refs_0_), channel_id=1, source_target_pairs={{24,0},{28,4},{16,8},{20,12},{8,16},{12,20},{0,24},{4,28},{25,1},{... | collective-permute-start | bytes 417800 | tf_op jit(solution)/shard_map/ppermute | solution.py:229
  44.1 2.0 %collective-permute-start.12 = (bf16[272,256]{1,0:T(8,128)(2,1)S(1)}, bf16[272,256]{1,0:T(8,128)(2,1)S(1)}, u32[]{:S(2)}, u32[]{:S(2)}) collective-permute-start(bf16[272,256]{1,0:T(8,128)(2,1)S(1)} %add.9.refs_0_), channel_id=1, source_target_pairs={{8,0},{12,4},{0,8},{4,12},{24,16},{28,20},{16,24},{20,28},{9,1},{1... | collective-permute-start | bytes 417800 | tf_op jit(solution)/shard_map/ppermute | solution.py:229
  46.1 0.6 send_part.10
  46.7 0.9 %collective-permute-start.18 = (s16[528,128]{1,0:T(8,128)(2,1)S(1)}, s16[528,128]{1,0:T(8,128)(2,1)S(1)}, u32[]{:S(2)}, u32[]{:S(2)}) collective-permute-start(s16[528,128]{1,0:T(8,128)(2,1)S(1)} %send_part.10), channel_id=1, source_target_pairs={{0,2},{1,3},{2,0},{3,1},{4,6},{5,7},{6,4},{7,5},{8,10},{9,11},{10,... | collective-permute-start | bytes 405512 | tf_op jit(solution)/shard_map/ppermute | solution.py:236
  47.6 1.2 %send_part.11 = s16[1296,128]{1,0:T(8,128)(2,1)S(1)} custom-call(bf16[3072,1536]{1,0:T(8,128)(2,1)S(1)} %screen.1.rows_ref, bf16[1536,128]{1,0:T(8,128)(2,1)S(1)} %collective-permute-done.15.dense_ref), custom_call_target="tpu_custom_call" | custom-call | flops 503316480 | bytes 4259840 | tf_op jit(solution)/shard_map/send_part/pallas_call | solution.py:337
  48.9 1.2 %collective-permute-start.19 = (s16[1296,128]{1,0:T(8,128)(2,1)S(1)}, s16[1296,128]{1,0:T(8,128)(2,1)S(1)}, u32[]{:S(2)}, u32[]{:S(2)}) collective-permute-start(s16[1296,128]{1,0:T(8,128)(2,1)S(1)} %send_part.11), channel_id=1, source_target_pairs={{0,2},{1,3},{2,0},{3,1},{4,6},{5,7},{6,4},{7,5},{8,10},{9,11},{10,... | collective-permute-start | bytes 995336 | tf_op jit(solution)/shard_map/ppermute | solution.py:236
  50.1 1.4 %collective-permute-done.13.refs_2_ = bf16[272,256]{1,0:T(8,128)(2,1)S(1)} collective-permute-done((bf16[272,256]{1,0:T(8,128)(2,1)S(1)}, bf16[272,256]{1,0:T(8,128)(2,1)S(1)}, u32[]{:S(2)}, u32[]{:S(2)}) %collective-permute-start.13) | collective-permute-done | bytes 139296 | tf_op jit(solution)/shard_map/ppermute | solution.py:229
  51.5 0.3 fill.3.dense_ref
  51.9 4.4 %collective-permute-done.18.refs_1_ = s16[528,128]{1,0:T(8,128)(2,1)S(1)} collective-permute-done((s16[528,128]{1,0:T(8,128)(2,1)S(1)}, s16[528,128]{1,0:T(8,128)(2,1)S(1)}, u32[]{:S(2)}, u32[]{:S(2)}) %collective-permute-start.18) | collective-permute-done | bytes 135200 | tf_op jit(solution)/shard_map/ppermute | solution.py:236
  56.3 1.0 %send_part.12 = s16[1040,128]{1,0:T(8,128)(2,1)S(1)} custom-call(bf16[3072,1536]{1,0:T(8,128)(2,1)S(1)} %screen.1.rows_ref, bf16[1536,128]{1,0:T(8,128)(2,1)S(1)} %collective-permute-done.15.dense_ref), custom_call_target="tpu_custom_call" | custom-call | flops 402653184 | bytes 3407872 | tf_op jit(solution)/shard_map/send_part/pallas_call | solution.py:337
  57.3 1.2 %collective-permute-start.21 = (s16[1040,128]{1,0:T(8,128)(2,1)S(1)}, s16[1040,128]{1,0:T(8,128)(2,1)S(1)}, u32[]{:S(2)}, u32[]{:S(2)}) collective-permute-start(s16[1040,128]{1,0:T(8,128)(2,1)S(1)} %send_part.12), channel_id=1, source_target_pairs={{0,2},{1,3},{2,0},{3,1},{4,6},{5,7},{6,4},{7,5},{8,10},{9,11},{10,... | collective-permute-start | bytes 798728 | tf_op jit(solution)/shard_map/ppermute | solution.py:236
  58.6 1.2 %join_part.4.refs_2_ = bf16[3072,256]{1,0:T(8,128)(2,1)} custom-call(bf16[3072,1536]{1,0:T(8,128)(2,1)S(1)} %screen.1.rows_ref, bf16[1536,256]{1,0:T(8,128)(2,1)S(1)} %fill.3.dense_ref, s16[528,128]{1,0:T(8,128)(2,1)S(1)} %collective-permute-done.11.refs_0_, s16[528,128]{1,0:T(8,128)(2,1)S(1)} %collective-permute-done.18.refs_1_), custom_call_target="tpu_custom_call" | custom-call | flops 402653184 | bytes 1835008 | tf_op jit(solution)/shard_map/join_part/pallas_call | solution.py:366
  59.9 2.9 %collective-permute-done.19.refs_1_ = s16[1296,128]{1,0:T(8,128)(2,1)S(1)} collective-permute-done((s16[1296,128]{1,0:T(8,128)(2,1)S(1)}, s16[1296,128]{1,0:T(8,128)(2,1)S(1)}, u32[]{:S(2)}, u32[]{:S(2)}) %collective-permute-start.19) | collective-permute-done | bytes 331808 | tf_op jit(solution)/shard_map/ppermute | solution.py:236
  62.8 0.4 send_part.13
  63.2 1.7 %collective-permute-start.20 = (s16[272,128]{1,0:T(8,128)(2,1)S(1)}, s16[272,128]{1,0:T(8,128)(2,1)S(1)}, u32[]{:S(2)}, u32[]{:S(2)}) collective-permute-start(s16[272,128]{1,0:T(8,128)(2,1)S(1)} %send_part.13), channel_id=1, source_target_pairs={{0,2},{1,3},{2,0},{3,1},{4,6},{5,7},{6,4},{7,5},{8,10},{9,11},{10,... | collective-permute-start | bytes 208904 | tf_op jit(solution)/shard_map/ppermute | solution.py:236
  64.9 1.9 %join_part.5.refs_2_ = bf16[3072,256]{1,0:T(8,128)(2,1)} custom-call(bf16[3072,1536]{1,0:T(8,128)(2,1)S(1)} %screen.1.rows_ref, bf16[1536,256]{1,0:T(8,128)(2,1)S(1)} %fill.3.dense_ref, s16[1296,128]{1,0:T(8,128)(2,1)S(1)} %collective-permute-done.17.refs_0_, s16[1296,128]{1,0:T(8,128)(2,1)S(1)} %collective-permute-done.19.refs_1_, ...), custom_call_target="tpu_custom_call", output_to_operand_aliasing={{}: (4, {})} | custom-call | flops 1006632960 | bytes 4587520 | tf_op jit(solution)/shard_map/join_part/pallas_call | solution.py:366
  66.8 1.7 %join_part.6.refs_2_ = bf16[3072,256]{1,0:T(8,128)(2,1)} custom-call(bf16[3072,1536]{1,0:T(8,128)(2,1)S(1)} %screen.1.rows_ref, bf16[1536,256]{1,0:T(8,128)(2,1)S(1)} %fill.3.dense_ref, s16[1296,128]{1,0:T(8,128)(2,1)S(1)} %collective-permute-done.16.refs_0_, s16[1040,128]{1,0:T(8,128)(2,1)S(1)} %collective-permute-done.21.refs_1_, ...), custom_call_target="tpu_custom_call", output_to_operand_aliasing={{}: (4, {})} | custom-call | flops 805306368 | bytes 3670016 | tf_op jit(solution)/shard_map/join_part/pallas_call | solution.py:366
  68.5 1.0 %join_part.7 = bf16[3072,256]{1,0:T(8,128)(2,1)} custom-call(bf16[3072,1536]{1,0:T(8,128)(2,1)S(1)} %screen.1.rows_ref, bf16[1536,256]{1,0:T(8,128)(2,1)S(1)} %fill.3.dense_ref, s16[1296,128]{1,0:T(8,128)(2,1)S(1)} %collective-permute-done.16.refs_0_, s16[272,128]{1,0:T(8,128)(2,1)S(1)} %collective-permute-done.20.refs_1_, ...), custom_call_target="tpu_custom_call", output_to_operand_aliasing={{}: (4, {})} | custom-call | flops 201326592 | bytes 917504 | tf_op jit(solution)/shard_map/join_part/pallas_call | solution.py:366
  (15 shorter events, 0.1 us)
Async XLA Ops:
  0.0 26.8 %collective-permute-start.8 = (bf16[3072,768]{1,0:T(8,128)(2,1)}, bf16[3072,768]{1,0:T(8,128)(2,1)S(1)}, u32[]{:S(2)}, u32[]{:S(2)}) collective-permute-start(bf16[3072,768]{1,0:T(8,128)(2,1)} %own_ref.1), channel_id=1, source_target_pairs={{0,1},{1,0},{2,3},{3,2},{4,5},{5,4},{6,7},{7,6},{8,9},{9,8},{10,11... | collective-permute-start | bytes 14155784 | tf_op jit(solution)/shard_map/ppermute | solution.py:239
  0.5 7.7 %collective-permute-start = (s32[3,12]{1,0:T(4,128)}, s32[3,12]{1,0:T(4,128)S(1)}, u32[]{:S(2)}, u32[]{:S(2)}) collective-permute-start(s32[3,12]{1,0:T(4,128)} %bitcast.2), channel_id=1, source_target_pairs={{0,1},{1,0},{2,3},{3,2},{4,5},{5,4},{6,7},{7,6},{8,9},{9,8},{10,11... | collective-permute-start | bytes 440 | tf_op jit(solution)/shard_map/ppermute | solution.py:240
  2.2 6.7 %collective-permute-start.1 = (bf16[144,256]{1,0:T(8,128)(2,1)S(1)}, bf16[144,256]{1,0:T(8,128)(2,1)S(1)}, u32[]{:S(2)}, u32[]{:S(2)}) collective-permute-start(bf16[144,256]{1,0:T(8,128)(2,1)S(1)} %get-tuple-element.22), channel_id=1, source_target_pairs={{8,0},{12,4},{0,8},{4,12},{24,16},{28,20},{16,24},{20,28},{9,1},{1... | collective-permute-start | bytes 221192 | tf_op jit(solution)/shard_map/ppermute | solution.py:229
  5.3 8.0 %collective-permute-start.2 = (bf16[144,256]{1,0:T(8,128)(2,1)S(1)}, bf16[144,256]{1,0:T(8,128)(2,1)S(1)}, u32[]{:S(2)}, u32[]{:S(2)}) collective-permute-start(bf16[144,256]{1,0:T(8,128)(2,1)S(1)} %get-tuple-element.23), channel_id=1, source_target_pairs={{16,0},{20,4},{24,8},{28,12},{0,16},{4,20},{8,24},{12,28},{17,1},{... | collective-permute-start | bytes 221192 | tf_op jit(solution)/shard_map/ppermute | solution.py:229
  7.8 6.3 %collective-permute-start.3 = (bf16[144,256]{1,0:T(8,128)(2,1)S(1)}, bf16[144,256]{1,0:T(8,128)(2,1)S(1)}, u32[]{:S(2)}, u32[]{:S(2)}) collective-permute-start(bf16[144,256]{1,0:T(8,128)(2,1)S(1)} %get-tuple-element.24), channel_id=1, source_target_pairs={{24,0},{28,4},{16,8},{20,12},{8,16},{12,20},{0,24},{4,28},{25,1},{... | collective-permute-start | bytes 221192 | tf_op jit(solution)/shard_map/ppermute | solution.py:229
  14.9 4.5 %collective-permute-start.4 = (bf16[272,128]{1,0:T(8,128)(2,1)S(1)}, bf16[272,128]{1,0:T(8,128)(2,1)S(1)}, u32[]{:S(2)}, u32[]{:S(2)}) collective-permute-start(bf16[272,128]{1,0:T(8,128)(2,1)S(1)} %get-tuple-element.25), channel_id=1, source_target_pairs={{0,2},{1,3},{2,0},{3,1},{4,6},{5,7},{6,4},{7,5},{8,10},{9,11},{10,... | collective-permute-start | bytes 208904 | tf_op jit(solution)/shard_map/ppermute | solution.py:236
  16.4 5.2 %collective-permute-start.5 = (bf16[272,128]{1,0:T(8,128)(2,1)S(1)}, bf16[272,128]{1,0:T(8,128)(2,1)S(1)}, u32[]{:S(2)}, u32[]{:S(2)}) collective-permute-start(bf16[272,128]{1,0:T(8,128)(2,1)S(1)} %get-tuple-element.26), channel_id=1, source_target_pairs={{0,6},{1,7},{2,4},{3,5},{4,2},{5,3},{6,0},{7,1},{8,14},{9,15},{10,... | collective-permute-start | bytes 208904 | tf_op jit(solution)/shard_map/ppermute | solution.py:236
  17.9 7.5 %collective-permute-start.7 = (bf16[272,256]{1,0:T(8,128)(2,1)S(1)}, bf16[272,256]{1,0:T(8,128)(2,1)S(1)}, u32[]{:S(2)}, u32[]{:S(2)}) collective-permute-start(bf16[272,256]{1,0:T(8,128)(2,1)S(1)} %get-tuple-element.27), channel_id=1, source_target_pairs={{0,4},{1,5},{2,6},{3,7},{4,0},{5,1},{6,2},{7,3},{8,12},{9,13},{10,... | collective-permute-start | bytes 417800 | tf_op jit(solution)/shard_map/ppermute | solution.py:236
  21.7 5.1 %collective-permute-start.6 = (bf16[272,128]{1,0:T(8,128)(2,1)S(1)}, bf16[272,128]{1,0:T(8,128)(2,1)S(1)}, u32[]{:S(2)}, u32[]{:S(2)}) collective-permute-start(bf16[272,128]{1,0:T(8,128)(2,1)S(1)} %add.8.refs_0_), channel_id=1, source_target_pairs={{8,0},{12,4},{0,8},{4,12},{24,16},{28,20},{16,24},{20,28},{9,1},{1... | collective-permute-start | bytes 208904 | tf_op jit(solution)/shard_map/ppermute | solution.py:229
  23.1 6.8 %collective-permute-start.10 = (bf16[272,128]{1,0:T(8,128)(2,1)S(1)}, bf16[272,128]{1,0:T(8,128)(2,1)S(1)}, u32[]{:S(2)}, u32[]{:S(2)}) collective-permute-start(bf16[272,128]{1,0:T(8,128)(2,1)S(1)} %add.8.refs_0_), channel_id=1, source_target_pairs={{24,0},{28,4},{16,8},{20,12},{8,16},{12,20},{0,24},{4,28},{25,1},{... | collective-permute-start | bytes 208904 | tf_op jit(solution)/shard_map/ppermute | solution.py:229
  25.5 5.2 %collective-permute-start.9 = (bf16[272,128]{1,0:T(8,128)(2,1)S(1)}, bf16[272,128]{1,0:T(8,128)(2,1)S(1)}, u32[]{:S(2)}, u32[]{:S(2)}) collective-permute-start(bf16[272,128]{1,0:T(8,128)(2,1)S(1)} %add.8.refs_0_), channel_id=1, source_target_pairs={{16,0},{20,4},{24,8},{28,12},{0,16},{4,20},{8,24},{12,28},{17,1},{... | collective-permute-start | bytes 208904 | tf_op jit(solution)/shard_map/ppermute | solution.py:229
  31.0 8.2 %collective-permute-start.15 = (bf16[1536,128]{1,0:T(8,128)(2,1)S(1)}, bf16[1536,128]{1,0:T(8,128)(2,1)S(1)}, u32[]{:S(2)}, u32[]{:S(2)}) collective-permute-start(bf16[1536,128]{1,0:T(8,128)(2,1)S(1)} %fill.2.dense_ref), channel_id=1, source_target_pairs={{0,4},{1,5},{2,6},{3,7},{4,0},{5,1},{6,2},{7,3},{8,12},{9,13},{10,... | collective-permute-start | bytes 1179656 | tf_op jit(solution)/shard_map/ppermute | solution.py:236
  33.3 5.9 %collective-permute-start.11 = (s16[528,128]{1,0:T(8,128)(2,1)S(1)}, s16[528,128]{1,0:T(8,128)(2,1)S(1)}, u32[]{:S(2)}, u32[]{:S(2)}) collective-permute-start(s16[528,128]{1,0:T(8,128)(2,1)S(1)} %send_part.7), channel_id=1, source_target_pairs={{0,2},{1,3},{2,0},{3,1},{4,6},{5,7},{6,4},{7,5},{8,10},{9,11},{10,... | collective-permute-start | bytes 405512 | tf_op jit(solution)/shard_map/ppermute | solution.py:236
  35.1 11.6 %collective-permute-start.17 = (s16[1296,128]{1,0:T(8,128)(2,1)S(1)}, s16[1296,128]{1,0:T(8,128)(2,1)S(1)}, u32[]{:S(2)}, u32[]{:S(2)}) collective-permute-start(s16[1296,128]{1,0:T(8,128)(2,1)S(1)} %send_part.8), channel_id=1, source_target_pairs={{0,2},{1,3},{2,0},{3,1},{4,6},{5,7},{6,4},{7,5},{8,10},{9,11},{10,... | collective-permute-start | bytes 995336 | tf_op jit(solution)/shard_map/ppermute | solution.py:236
  40.4 15.9 %collective-permute-start.16 = (s16[1296,128]{1,0:T(8,128)(2,1)S(1)}, s16[1296,128]{1,0:T(8,128)(2,1)S(1)}, u32[]{:S(2)}, u32[]{:S(2)}) collective-permute-start(s16[1296,128]{1,0:T(8,128)(2,1)S(1)} %send_part.9), channel_id=1, source_target_pairs={{0,2},{1,3},{2,0},{3,1},{4,6},{5,7},{6,4},{7,5},{8,10},{9,11},{10,... | collective-permute-start | bytes 995336 | tf_op jit(solution)/shard_map/ppermute | solution.py:236
  41.7 7.2 %collective-permute-start.14 = (bf16[272,256]{1,0:T(8,128)(2,1)S(1)}, bf16[272,256]{1,0:T(8,128)(2,1)S(1)}, u32[]{:S(2)}, u32[]{:S(2)}) collective-permute-start(bf16[272,256]{1,0:T(8,128)(2,1)S(1)} %add.9.refs_0_), channel_id=1, source_target_pairs={{24,0},{28,4},{16,8},{20,12},{8,16},{12,20},{0,24},{4,28},{25,1},{... | collective-permute-start | bytes 417800 | tf_op jit(solution)/shard_map/ppermute | solution.py:229
  44.1 7.4 %collective-permute-start.13 = (bf16[272,256]{1,0:T(8,128)(2,1)S(1)}, bf16[272,256]{1,0:T(8,128)(2,1)S(1)}, u32[]{:S(2)}, u32[]{:S(2)}) collective-permute-start(bf16[272,256]{1,0:T(8,128)(2,1)S(1)} %add.9.refs_0_), channel_id=1, source_target_pairs={{16,0},{20,4},{24,8},{28,12},{0,16},{4,20},{8,24},{12,28},{17,1},{... | collective-permute-start | bytes 417800 | tf_op jit(solution)/shard_map/ppermute | solution.py:229
  44.1 7.4 %collective-permute-start.12 = (bf16[272,256]{1,0:T(8,128)(2,1)S(1)}, bf16[272,256]{1,0:T(8,128)(2,1)S(1)}, u32[]{:S(2)}, u32[]{:S(2)}) collective-permute-start(bf16[272,256]{1,0:T(8,128)(2,1)S(1)} %add.9.refs_0_), channel_id=1, source_target_pairs={{8,0},{12,4},{0,8},{4,12},{24,16},{28,20},{16,24},{20,28},{9,1},{1... | collective-permute-start | bytes 417800 | tf_op jit(solution)/shard_map/ppermute | solution.py:229
  46.7 9.6 %collective-permute-start.18 = (s16[528,128]{1,0:T(8,128)(2,1)S(1)}, s16[528,128]{1,0:T(8,128)(2,1)S(1)}, u32[]{:S(2)}, u32[]{:S(2)}) collective-permute-start(s16[528,128]{1,0:T(8,128)(2,1)S(1)} %send_part.10), channel_id=1, source_target_pairs={{0,2},{1,3},{2,0},{3,1},{4,6},{5,7},{6,4},{7,5},{8,10},{9,11},{10,... | collective-permute-start | bytes 405512 | tf_op jit(solution)/shard_map/ppermute | solution.py:236
  48.9 13.9 %collective-permute-start.19 = (s16[1296,128]{1,0:T(8,128)(2,1)S(1)}, s16[1296,128]{1,0:T(8,128)(2,1)S(1)}, u32[]{:S(2)}, u32[]{:S(2)}) collective-permute-start(s16[1296,128]{1,0:T(8,128)(2,1)S(1)} %send_part.11), channel_id=1, source_target_pairs={{0,2},{1,3},{2,0},{3,1},{4,6},{5,7},{6,4},{7,5},{8,10},{9,11},{10,... | collective-permute-start | bytes 995336 | tf_op jit(solution)/shard_map/ppermute | solution.py:236
  57.3 9.4 %collective-permute-start.21 = (s16[1040,128]{1,0:T(8,128)(2,1)S(1)}, s16[1040,128]{1,0:T(8,128)(2,1)S(1)}, u32[]{:S(2)}, u32[]{:S(2)}) collective-permute-start(s16[1040,128]{1,0:T(8,128)(2,1)S(1)} %send_part.12), channel_id=1, source_target_pairs={{0,2},{1,3},{2,0},{3,1},{4,6},{5,7},{6,4},{7,5},{8,10},{9,11},{10,... | collective-permute-start | bytes 798728 | tf_op jit(solution)/shard_map/ppermute | solution.py:236
  63.2 5.3 %collective-permute-start.20 = (s16[272,128]{1,0:T(8,128)(2,1)S(1)}, s16[272,128]{1,0:T(8,128)(2,1)S(1)}, u32[]{:S(2)}, u32[]{:S(2)}) collective-permute-start(s16[272,128]{1,0:T(8,128)(2,1)S(1)} %send_part.13), channel_id=1, source_target_pairs={{0,2},{1,3},{2,0},{3,1},{4,6},{5,7},{6,4},{7,5},{8,10},{9,11},{10,... | collective-permute-start | bytes 208904 | tf_op jit(solution)/shard_map/ppermute | solution.py:236

commit v13 on v12

--- a/solution.py
+++ b/solution.py
@@ -10,11 +10,12 @@
 STEPS = 4
 CORES = 2
 HALVES = 2
-NEAR_CUTS = (0.0, 0.167, 0.583, 1.0)
+NEAR_CUTS = (0.0, 0.25, 0.667, 1.0)
 FAR_CUTS = (0.0, 0.167, 0.583, 0.917, 1.0)
 CODE_TOP = 32767.0
 FRACTION = 8192.0
-META_ROWS = 16
+META_ROWS = 8
+TILE_ROWS = 16
 SCREEN_PARTS = 4
 PARAMS = pltpu.CompilerParams(vmem_limit_bytes=16 * 1024 * 1024)
 SMEM = pl.BlockSpec(memory_space=pltpu.SMEM)
@@ -53,7 +54,7 @@
     info = info.astype(jnp.float32).astype(panel_ref.dtype)
     for shift, piece_ref in enumerate(piece_refs):
         first = partner(place, shift if peers & (peers - 1) == 0 else peers - shift, peers) * share
-        start = pl.multiple_of(lax.rem(first, tile_width), META_ROWS)
+        start = pl.multiple_of(lax.rem(first, tile_width), TILE_ROWS)
         piece_ref[pl.ds(0, share), :] = panel_ref[0, 0, first // tile_width, pl.ds(start, share), :]
         piece_ref[pl.ds(share, META_ROWS), :] = info
 
@@ -116,7 +117,7 @@
 
             @pl.when(slot < count)
             def _():
-                spot = pl.multiple_of(start + lax.rem(first, tile_width), META_ROWS)
+                spot = pl.multiple_of(start + lax.rem(first, tile_width), TILE_ROWS)
                 dense_ref[pl.ds(spot, share), :] = piece_ref[pl.ds(group * share, share), :]
 
 
@@ -305,7 +306,6 @@
         if screened is None:
             screened = screen(held[1], own)
         near_weights[offset] = fill([after(held[0], screened)] + held[1:])
-        far_weights[offset] = across(near_weights[offset], 1, 0)
 
     def cost(span, width):
         return pl.CostEstimate(
@@ -315,7 +315,7 @@
         )
 
     def code_shape(span):
-        return (span * block_rows + -(-2 * span // META_ROWS) * META_ROWS, half_width)
+        return (span * block_rows + -(-2 * span // TILE_ROWS) * TILE_ROWS, half_width)
 
     def scratch_rows(span):
         return code_shape(span)[0] - span * block_rows
@@ -324,10 +324,8 @@
     arrived, sent = {}, []
     order = []
     for number, (half, first, span) in enumerate(rounds):
-        ahead = 2 if number in (3, 4) else 1
+        ahead = 1
         earlier = sent[-1:] + [part for key in order[:-ahead] for part in arrived[key]]
-        if number == len(near_chunks) - 1:
-            earlier += list(far_weights.values())
         if number == len(rounds) - 2:
             earlier.append(own_weights)
         arrived[half, first] = []
@@ -346,6 +344,9 @@
             )(screened, after(weights, *earlier))
             arrived[half, first].append(across(code, 0, -offset))
             sent.append(code)
+        if number == 1:
+            for offset, code in zip(remote, sent[-len(remote) :]):
+                far_weights[offset] = across(after(near_weights[offset], code), 1, 0)
         if number == 0:
             own = after(own, *arrived[half, first])
             own_weights = fill([own] + [along(own, shift) for shift in range(1, peers)])

time: 69.7 us -> 70.3 us (level)
  starting transfers between devices: 28 us -> 25.6 us
  Pallas kernels: 17.8 us -> 19.5 us
  waiting for transfers between devices: 22.1 us -> 23.5 us
    ppermute x11, waiting for transfers between devices: 13.1 us -> 16 us  [across(): return lax.ppermute(value, ('row', 'col'), pairs)]
    ppermute x9, starting transfers between devices: 13.8 us -> 11.5 us  [along(): return lax.ppermute(value, 'row', pairs)]
    pallas_call x4 -> x6, Pallas kernels: 5.87 us -> 7.51 us  [shards(): pl.pallas_call(partial(join_kernel, first, span, block_rows, skips), in_s...]
    ppermute x9, waiting for transfers between devices: 8.65 us -> 7.14 us  [along(): return lax.ppermute(value, 'row', pairs)]
  transfers between devices with their start and end apart: 22 -> 22, of which waited for: 11 -> 12; matrix products, arithmetic and copies ran while one was open for 1% -> 1% of each run, Pallas kernels for 24% -> 25%
where the time goes in v13:
time: 70.3 us; the launch traced here: 70.1 us
  starting transfers between devices  25.6 us (36%)
  waiting for transfers between devices  23.5 us (33%)
  Pallas kernels  19.5 us (28%)
  between operations  0.84 us (1%)
  other arithmetic  0.76 us (1%)
    ppermute x11, waiting for transfers between devices, across(): return lax.ppermute(value, ('row', 'col'), pairs)  16 us
    ppermute x11, starting transfers between devices, across(): return lax.ppermute(value, ('row', 'col'), pairs)  13.6 us
    ppermute x9, starting transfers between devices, along(): return lax.ppermute(value, 'row', pairs)  11.5 us
    pallas_call x6, Pallas kernels, shards(): pl.pallas_call(partial(join_kernel, first, span, block_rows, skips), in_s...  7.51 us
    ppermute x9, waiting for transfers between devices, along(): return lax.ppermute(value, 'row', pairs)  7.14 us
    pallas_call x7, Pallas kernels, shards(): pl.pallas_call(partial(send_kernel, first, span, block_rows), in_specs=[V...  6.43 us
    pallas_call x1, Pallas kernels, screen(): pl.pallas_call(partial(screen_kernel, tile_width, block_rows), in_specs=[...  3.07 us
  transfers between devices with their start and end apart: 22, of which 12 were waited for; matrix products, arithmetic and copies ran while one was open for 1% of the time, Pallas kernels for 25%

profile of v13, /device:TPU:0, one launch (start us, length us, event | category | flops | bytes accessed | tf_op | source)
XLA Modules:
  0.0 70.1 jit_solution(7167453001090595513)
XLA Ops:
  0.0 0.5 collective-permute-start.8
  1.2 1.0 %pack.1 = (bf16[136,256]{1,0:T(8,128)(2,1)S(1)}, bf16[136,256]{1,0:T(8,128)(2,1)S(1)}, bf16[136,256]{1,0:T(8,128)(2,1)S(1)}, bf16[136,256]{1,0:T(8,128)(2,1)S(1)}) custom-call(s32[1,1,2]{2,1,0:T(1,128)} %list_ref.1, s32[1,1]{1,0:T(1,128)S(6)} %copy.17.count_ref, bf16[1,1,2,256,256]{4,3,2,1,0:T(8,128)(2,1)} %panel_ref.1), custom_call_target="tpu_custom_call" | custom-call | tf_op jit(solution)/shard_map/pack/pallas_call | solution.py:248
  2.2 3.0 %collective-permute-start.1 = (bf16[136,256]{1,0:T(8,128)(2,1)S(1)}, bf16[136,256]{1,0:T(8,128)(2,1)S(1)}, u32[]{:S(2)}, u32[]{:S(2)}) collective-permute-start(bf16[136,256]{1,0:T(8,128)(2,1)S(1)} %get-tuple-element.23), channel_id=1, source_target_pairs={{8,0},{12,4},{0,8},{4,12},{24,16},{28,20},{16,24},{20,28},{9,1},{1... | collective-permute-start | bytes 208904 | tf_op jit(solution)/shard_map/ppermute | solution.py:230
  5.3 2.6 %collective-permute-start.2 = (bf16[136,256]{1,0:T(8,128)(2,1)S(1)}, bf16[136,256]{1,0:T(8,128)(2,1)S(1)}, u32[]{:S(2)}, u32[]{:S(2)}) collective-permute-start(bf16[136,256]{1,0:T(8,128)(2,1)S(1)} %get-tuple-element.24), channel_id=1, source_target_pairs={{16,0},{20,4},{24,8},{28,12},{0,16},{4,20},{8,24},{12,28},{17,1},{... | collective-permute-start | bytes 208904 | tf_op jit(solution)/shard_map/ppermute | solution.py:230
  7.8 0.4 collective-permute-done
  8.2 0.7 %pad_add_fusion.plan_ref.mask_ref = s32[7,12]{1,0:T(8,128)S(1)} fusion(s32[1,4]{1,0:T(1,128)} %bitcast.4, s32[3,12]{1,0:T(4,128)S(1)} %collective-permute-done, s32[3,12]{1,0:T(4,128)} %bitcast.3), kind=kLoop, calls=%fused_computation | loop fusion | flops 168 | bytes 640 | tf_op jit(solution)/shard_map/concatenate | solution.py:243
  8.9 4.1 %collective-permute-done.2.refs_2_ = bf16[136,256]{1,0:T(8,128)(2,1)S(1)} collective-permute-done((bf16[136,256]{1,0:T(8,128)(2,1)S(1)}, bf16[136,256]{1,0:T(8,128)(2,1)S(1)}, u32[]{:S(2)}, u32[]{:S(2)}) %collective-permute-start.2) | collective-permute-done | bytes 69664 | tf_op jit(solution)/shard_map/ppermute | solution.py:230
  13.0 1.1 %collective-permute-done.3.refs_3_ = bf16[136,256]{1,0:T(8,128)(2,1)S(1)} collective-permute-done((bf16[136,256]{1,0:T(8,128)(2,1)S(1)}, bf16[136,256]{1,0:T(8,128)(2,1)S(1)}, u32[]{:S(2)}, u32[]{:S(2)}) %collective-permute-start.3) | collective-permute-done | bytes 69664 | tf_op jit(solution)/shard_map/ppermute | solution.py:230
  14.1 0.8 %choose.1 = (bf16[264,256]{1,0:T(8,128)(2,1)S(1)}, bf16[264,128]{1,0:T(8,128)(2,1)S(1)}, bf16[264,128]{1,0:T(8,128)(2,1)S(1)}) custom-call(s32[7,12]{1,0:T(8,128)S(1)} %pad_add_fusion.plan_ref.mask_ref, bf16[136,256]{1,0:T(8,128)(2,1)S(1)} %get-tuple-element.22.refs_0_, bf16[136,256]{1,0:T(8,128)(2,1)S(1)} %collective-permute-done.1.refs_1_, ...), custom_call_target="tpu_custom_call" | custom-call | tf_op jit(solution)/shard_map/choose/pallas_call | solution.py:263
  14.8 1.6 %collective-permute-start.4 = (bf16[264,128]{1,0:T(8,128)(2,1)S(1)}, bf16[264,128]{1,0:T(8,128)(2,1)S(1)}, u32[]{:S(2)}, u32[]{:S(2)}) collective-permute-start(bf16[264,128]{1,0:T(8,128)(2,1)S(1)} %get-tuple-element.26), channel_id=1, source_target_pairs={{0,2},{1,3},{2,0},{3,1},{4,6},{5,7},{6,4},{7,5},{8,10},{9,11},{10,... | collective-permute-start | bytes 202760 | tf_op jit(solution)/shard_map/ppermute | solution.py:237
  16.4 1.5 %collective-permute-start.5 = (bf16[264,128]{1,0:T(8,128)(2,1)S(1)}, bf16[264,128]{1,0:T(8,128)(2,1)S(1)}, u32[]{:S(2)}, u32[]{:S(2)}) collective-permute-start(bf16[264,128]{1,0:T(8,128)(2,1)S(1)} %get-tuple-element.27), channel_id=1, source_target_pairs={{0,6},{1,7},{2,4},{3,5},{4,2},{5,3},{6,0},{7,1},{8,14},{9,15},{10,... | collective-permute-start | bytes 202760 | tf_op jit(solution)/shard_map/ppermute | solution.py:237
  17.9 0.5 collective-permute-start.7
  18.4 0.9 %collective-permute-done.4 = bf16[264,128]{1,0:T(8,128)(2,1)S(1)} collective-permute-done((bf16[264,128]{1,0:T(8,128)(2,1)S(1)}, bf16[264,128]{1,0:T(8,128)(2,1)S(1)}, u32[]{:S(2)}, u32[]{:S(2)}) %collective-permute-start.4) | collective-permute-done | bytes 67616 | tf_op jit(solution)/shard_map/ppermute | solution.py:237
  19.3 2.3 %collective-permute-done.5 = bf16[264,128]{1,0:T(8,128)(2,1)S(1)} collective-permute-done((bf16[264,128]{1,0:T(8,128)(2,1)S(1)}, bf16[264,128]{1,0:T(8,128)(2,1)S(1)}, u32[]{:S(2)}, u32[]{:S(2)}) %collective-permute-start.5) | collective-permute-done | bytes 67616 | tf_op jit(solution)/shard_map/ppermute | solution.py:237
  21.6 1.1 %collective-permute-start.6 = (bf16[264,128]{1,0:T(8,128)(2,1)S(1)}, bf16[264,128]{1,0:T(8,128)(2,1)S(1)}, u32[]{:S(2)}, u32[]{:S(2)}) collective-permute-start(bf16[264,128]{1,0:T(8,128)(2,1)S(1)} %add.8.refs_0_), channel_id=1, source_target_pairs={{8,0},{12,4},{0,8},{4,12},{24,16},{28,20},{16,24},{20,28},{9,1},{1... | collective-permute-start | bytes 202760 | tf_op jit(solution)/shard_map/ppermute | solution.py:230
  22.7 2.4 %collective-permute-start.10 = (bf16[264,128]{1,0:T(8,128)(2,1)S(1)}, bf16[264,128]{1,0:T(8,128)(2,1)S(1)}, u32[]{:S(2)}, u32[]{:S(2)}) collective-permute-start(bf16[264,128]{1,0:T(8,128)(2,1)S(1)} %add.8.refs_0_), channel_id=1, source_target_pairs={{24,0},{28,4},{16,8},{20,12},{8,16},{12,20},{0,24},{4,28},{25,1},{... | collective-permute-start | bytes 202760 | tf_op jit(solution)/shard_map/ppermute | solution.py:230
  25.2 1.5 %collective-permute-done.6.refs_1_ = bf16[264,128]{1,0:T(8,128)(2,1)S(1)} collective-permute-done((bf16[264,128]{1,0:T(8,128)(2,1)S(1)}, bf16[264,128]{1,0:T(8,128)(2,1)S(1)}, u32[]{:S(2)}, u32[]{:S(2)}) %collective-permute-start.6) | collective-permute-done | bytes 67616 | tf_op jit(solution)/shard_map/ppermute | solution.py:230
  26.7 3.1 %screen.1.rows_ref = bf16[3072,1536]{1,0:T(8,128)(2,1)S(1)} custom-call(s32[7,12]{1,0:T(8,128)S(1)} %pad_add_fusion.plan_ref.mask_ref, bf16[3072,768]{1,0:T(8,128)(2,1)} %own_ref.1, bf16[3072,768]{1,0:T(8,128)(2,1)S(1)} %collective-permute-done.8.other_ref), custom_call_target="tpu_custom_call" | custom-call | flops 4718592 | bytes 18874368 | tf_op jit(solution)/shard_map/screen/pallas_call | solution.py:284
  29.8 0.5 collective-permute-done.9.refs_2_
  30.3 0.3 fill.2.dense_ref
  30.6 0.8 %send_part.7 = s16[784,128]{1,0:T(8,128)(2,1)S(1)} custom-call(bf16[3072,1536]{1,0:T(8,128)(2,1)S(1)} %screen.1.rows_ref, bf16[1536,128]{1,0:T(8,128)(2,1)S(1)} %fill.2.dense_ref), custom_call_target="tpu_custom_call" | custom-call | flops 301989888 | bytes 2555904 | tf_op jit(solution)/shard_map/send_part/pallas_call | solution.py:335
  31.4 0.9 %collective-permute-start.11 = (s16[784,128]{1,0:T(8,128)(2,1)S(1)}, s16[784,128]{1,0:T(8,128)(2,1)S(1)}, u32[]{:S(2)}, u32[]{:S(2)}) collective-permute-start(s16[784,128]{1,0:T(8,128)(2,1)S(1)} %send_part.7), channel_id=1, source_target_pairs={{0,2},{1,3},{2,0},{3,1},{4,6},{5,7},{6,4},{7,5},{8,10},{9,11},{10,... | collective-permute-start | bytes 602120 | tf_op jit(solution)/shard_map/ppermute | solution.py:237
  32.3 1.2 %send_part.8 = s16[1296,128]{1,0:T(8,128)(2,1)S(1)} custom-call(bf16[3072,1536]{1,0:T(8,128)(2,1)S(1)} %screen.1.rows_ref, bf16[1536,128]{1,0:T(8,128)(2,1)S(1)} %fill.2.dense_ref), custom_call_target="tpu_custom_call" | custom-call | flops 503316480 | bytes 4259840 | tf_op jit(solution)/shard_map/send_part/pallas_call | solution.py:335
  33.5 1.4 %collective-permute-start.16 = (bf16[1536,128]{1,0:T(8,128)(2,1)S(1)}, bf16[1536,128]{1,0:T(8,128)(2,1)S(1)}, u32[]{:S(2)}, u32[]{:S(2)}) collective-permute-start(bf16[1536,128]{1,0:T(8,128)(2,1)S(1)} %fill.2.dense_ref), channel_id=1, source_target_pairs={{0,4},{1,5},{2,6},{3,7},{4,0},{5,1},{6,2},{7,3},{8,12},{9,13},{10,... | collective-permute-start | bytes 1179656 | tf_op jit(solution)/shard_map/ppermute | solution.py:237
  34.9 1.6 %collective-permute-start.17 = (s16[1296,128]{1,0:T(8,128)(2,1)S(1)}, s16[1296,128]{1,0:T(8,128)(2,1)S(1)}, u32[]{:S(2)}, u32[]{:S(2)}) collective-permute-start(s16[1296,128]{1,0:T(8,128)(2,1)S(1)} %send_part.8), channel_id=1, source_target_pairs={{0,2},{1,3},{2,0},{3,1},{4,6},{5,7},{6,4},{7,5},{8,10},{9,11},{10,... | collective-permute-start | bytes 995336 | tf_op jit(solution)/shard_map/ppermute | solution.py:237
  36.5 2.9 %collective-permute-done.11.refs_0_ = s16[784,128]{1,0:T(8,128)(2,1)S(1)} collective-permute-done((s16[784,128]{1,0:T(8,128)(2,1)S(1)}, s16[784,128]{1,0:T(8,128)(2,1)S(1)}, u32[]{:S(2)}, u32[]{:S(2)}) %collective-permute-start.11) | collective-permute-done | bytes 200736 | tf_op jit(solution)/shard_map/ppermute | solution.py:237
  39.4 1.0 %send_part.9 = s16[1040,128]{1,0:T(8,128)(2,1)S(1)} custom-call(bf16[3072,1536]{1,0:T(8,128)(2,1)S(1)} %screen.1.rows_ref, bf16[1536,128]{1,0:T(8,128)(2,1)S(1)} %fill.2.dense_ref), custom_call_target="tpu_custom_call" | custom-call | flops 402653184 | bytes 3407872 | tf_op jit(solution)/shard_map/send_part/pallas_call | solution.py:335
  40.5 0.8 %collective-permute-start.15 = (s16[1040,128]{1,0:T(8,128)(2,1)S(1)}, s16[1040,128]{1,0:T(8,128)(2,1)S(1)}, u32[]{:S(2)}, u32[]{:S(2)}) collective-permute-start(s16[1040,128]{1,0:T(8,128)(2,1)S(1)} %send_part.9), channel_id=1, source_target_pairs={{0,2},{1,3},{2,0},{3,1},{4,6},{5,7},{6,4},{7,5},{8,10},{9,11},{10,... | collective-permute-start | bytes 798728 | tf_op jit(solution)/shard_map/ppermute | solution.py:237
  41.3 2.3 %collective-permute-start.14 = (bf16[264,256]{1,0:T(8,128)(2,1)S(1)}, bf16[264,256]{1,0:T(8,128)(2,1)S(1)}, u32[]{:S(2)}, u32[]{:S(2)}) collective-permute-start(bf16[264,256]{1,0:T(8,128)(2,1)S(1)} %add.9.refs_0_), channel_id=1, source_target_pairs={{24,0},{28,4},{16,8},{20,12},{8,16},{12,20},{0,24},{4,28},{25,1},{... | collective-permute-start | bytes 405512 | tf_op jit(solution)/shard_map/ppermute | solution.py:230
  43.6 3.0 %collective-permute-done.17.refs_0_ = s16[1296,128]{1,0:T(8,128)(2,1)S(1)} collective-permute-done((s16[1296,128]{1,0:T(8,128)(2,1)S(1)}, s16[1296,128]{1,0:T(8,128)(2,1)S(1)}, u32[]{:S(2)}, u32[]{:S(2)}) %collective-permute-start.17) | collective-permute-done | bytes 331808 | tf_op jit(solution)/shard_map/ppermute | solution.py:237
  46.5 0.6 send_part.10
  47.2 0.9 %collective-permute-start.18 = (s16[528,128]{1,0:T(8,128)(2,1)S(1)}, s16[528,128]{1,0:T(8,128)(2,1)S(1)}, u32[]{:S(2)}, u32[]{:S(2)}) collective-permute-start(s16[528,128]{1,0:T(8,128)(2,1)S(1)} %send_part.10), channel_id=1, source_target_pairs={{0,2},{1,3},{2,0},{3,1},{4,6},{5,7},{6,4},{7,5},{8,10},{9,11},{10,... | collective-permute-start | bytes 405512 | tf_op jit(solution)/shard_map/ppermute | solution.py:237
  48.1 2.0 %collective-permute-done.15.refs_0_ = s16[1040,128]{1,0:T(8,128)(2,1)S(1)} collective-permute-done((s16[1040,128]{1,0:T(8,128)(2,1)S(1)}, s16[1040,128]{1,0:T(8,128)(2,1)S(1)}, u32[]{:S(2)}, u32[]{:S(2)}) %collective-permute-start.15) | collective-permute-done | bytes 266272 | tf_op jit(solution)/shard_map/ppermute | solution.py:237
  50.1 1.2 %send_part.11 = s16[1296,128]{1,0:T(8,128)(2,1)S(1)} custom-call(bf16[3072,1536]{1,0:T(8,128)(2,1)S(1)} %screen.1.rows_ref, bf16[1536,128]{1,0:T(8,128)(2,1)S(1)} %collective-permute-done.16.dense_ref), custom_call_target="tpu_custom_call" | custom-call | flops 503316480 | bytes 4259840 | tf_op jit(solution)/shard_map/send_part/pallas_call | solution.py:335
  51.3 1.8 %collective-permute-start.19 = (s16[1296,128]{1,0:T(8,128)(2,1)S(1)}, s16[1296,128]{1,0:T(8,128)(2,1)S(1)}, u32[]{:S(2)}, u32[]{:S(2)}) collective-permute-start(s16[1296,128]{1,0:T(8,128)(2,1)S(1)} %send_part.11), channel_id=1, source_target_pairs={{0,2},{1,3},{2,0},{3,1},{4,6},{5,7},{6,4},{7,5},{8,10},{9,11},{10,... | collective-permute-start | bytes 995336 | tf_op jit(solution)/shard_map/ppermute | solution.py:237
  53.1 0.3 fill.3.dense_ref
  53.5 0.3 collective-permute-done.18.refs_1_
  53.8 1.0 %send_part.12 = s16[1040,128]{1,0:T(8,128)(2,1)S(1)} custom-call(bf16[3072,1536]{1,0:T(8,128)(2,1)S(1)} %screen.1.rows_ref, bf16[1536,128]{1,0:T(8,128)(2,1)S(1)} %collective-permute-done.16.dense_ref), custom_call_target="tpu_custom_call" | custom-call | flops 402653184 | bytes 3407872 | tf_op jit(solution)/shard_map/send_part/pallas_call | solution.py:335
  54.8 1.0 %collective-permute-start.21 = (s16[1040,128]{1,0:T(8,128)(2,1)S(1)}, s16[1040,128]{1,0:T(8,128)(2,1)S(1)}, u32[]{:S(2)}, u32[]{:S(2)}) collective-permute-start(s16[1040,128]{1,0:T(8,128)(2,1)S(1)} %send_part.12), channel_id=1, source_target_pairs={{0,2},{1,3},{2,0},{3,1},{4,6},{5,7},{6,4},{7,5},{8,10},{9,11},{10,... | collective-permute-start | bytes 798728 | tf_op jit(solution)/shard_map/ppermute | solution.py:237
  55.8 1.2 %join_part.6.refs_2_ = bf16[3072,256]{1,0:T(8,128)(2,1)} custom-call(bf16[3072,1536]{1,0:T(8,128)(2,1)S(1)} %screen.1.rows_ref, bf16[1536,256]{1,0:T(8,128)(2,1)S(1)} %fill.3.dense_ref, s16[784,128]{1,0:T(8,128)(2,1)S(1)} %collective-permute-done.11.refs_0_, s16[528,128]{1,0:T(8,128)(2,1)S(1)} %collective-permute-done.18.refs_1_), custom_call_target="tpu_custom_call" | custom-call | flops 402653184 | bytes 1835008 | tf_op jit(solution)/shard_map/join_part/pallas_call | solution.py:367
  57.0 4.5 %collective-permute-done.19.refs_1_ = s16[1296,128]{1,0:T(8,128)(2,1)S(1)} collective-permute-done((s16[1296,128]{1,0:T(8,128)(2,1)S(1)}, s16[1296,128]{1,0:T(8,128)(2,1)S(1)}, u32[]{:S(2)}, u32[]{:S(2)}) %collective-permute-start.19) | collective-permute-done | bytes 331808 | tf_op jit(solution)/shard_map/ppermute | solution.py:237
  61.6 0.4 send_part.13
  62.0 1.8 %collective-permute-start.20 = (s16[272,128]{1,0:T(8,128)(2,1)S(1)}, s16[272,128]{1,0:T(8,128)(2,1)S(1)}, u32[]{:S(2)}, u32[]{:S(2)}) collective-permute-start(s16[272,128]{1,0:T(8,128)(2,1)S(1)} %send_part.13), channel_id=1, source_target_pairs={{0,2},{1,3},{2,0},{3,1},{4,6},{5,7},{6,4},{7,5},{8,10},{9,11},{10,... | collective-permute-start | bytes 208904 | tf_op jit(solution)/shard_map/ppermute | solution.py:237
  63.8 1.0 %join_part.7.refs_2_ = bf16[3072,256]{1,0:T(8,128)(2,1)} custom-call(bf16[3072,1536]{1,0:T(8,128)(2,1)S(1)} %screen.1.rows_ref, bf16[1536,256]{1,0:T(8,128)(2,1)S(1)} %fill.3.dense_ref, s16[784,128]{1,0:T(8,128)(2,1)S(1)} %collective-permute-done.11.refs_0_, s16[1296,128]{1,0:T(8,128)(2,1)S(1)} %collective-permute-done.19.refs_1_, ...), custom_call_target="tpu_custom_call", output_to_operand_aliasing={{}: (4, {})} | custom-call | flops 201326592 | bytes 917504 | tf_op jit(solution)/shard_map/join_part/pallas_call | solution.py:367
  64.8 1.7 %join_part.8.refs_2_ = bf16[3072,256]{1,0:T(8,128)(2,1)} custom-call(bf16[3072,1536]{1,0:T(8,128)(2,1)S(1)} %screen.1.rows_ref, bf16[1536,256]{1,0:T(8,128)(2,1)S(1)} %fill.3.dense_ref, s16[1296,128]{1,0:T(8,128)(2,1)S(1)} %collective-permute-done.17.refs_0_, s16[1296,128]{1,0:T(8,128)(2,1)S(1)} %collective-permute-done.19.refs_1_, ...), custom_call_target="tpu_custom_call", output_to_operand_aliasing={{}: (4, {})} | custom-call | flops 805306368 | bytes 3670016 | tf_op jit(solution)/shard_map/join_part/pallas_call | solution.py:367
  66.5 1.0 %join_part.9.refs_2_ = bf16[3072,256]{1,0:T(8,128)(2,1)} custom-call(bf16[3072,1536]{1,0:T(8,128)(2,1)S(1)} %screen.1.rows_ref, bf16[1536,256]{1,0:T(8,128)(2,1)S(1)} %fill.3.dense_ref, s16[1296,128]{1,0:T(8,128)(2,1)S(1)} %collective-permute-done.17.refs_0_, s16[1040,128]{1,0:T(8,128)(2,1)S(1)} %collective-permute-done.21.refs_1_, ...), custom_call_target="tpu_custom_call", output_to_operand_aliasing={{}: (4, {})} | custom-call | flops 201326592 | bytes 917504 | tf_op jit(solution)/shard_map/join_part/pallas_call | solution.py:367
  67.6 1.5 %join_part.10.refs_2_ = bf16[3072,256]{1,0:T(8,128)(2,1)} custom-call(bf16[3072,1536]{1,0:T(8,128)(2,1)S(1)} %screen.1.rows_ref, bf16[1536,256]{1,0:T(8,128)(2,1)S(1)} %fill.3.dense_ref, s16[1040,128]{1,0:T(8,128)(2,1)S(1)} %collective-permute-done.15.refs_0_, s16[1040,128]{1,0:T(8,128)(2,1)S(1)} %collective-permute-done.21.refs_1_, ...), custom_call_target="tpu_custom_call", output_to_operand_aliasing={{}: (4, {})} | custom-call | flops 603979776 | bytes 2752512 | tf_op jit(solution)/shard_map/join_part/pallas_call | solution.py:367
  69.1 1.0 %join_part.11 = bf16[3072,256]{1,0:T(8,128)(2,1)} custom-call(bf16[3072,1536]{1,0:T(8,128)(2,1)S(1)} %screen.1.rows_ref, bf16[1536,256]{1,0:T(8,128)(2,1)S(1)} %fill.3.dense_ref, s16[1040,128]{1,0:T(8,128)(2,1)S(1)} %collective-permute-done.15.refs_0_, s16[272,128]{1,0:T(8,128)(2,1)S(1)} %collective-permute-done.20.refs_1_, ...), custom_call_target="tpu_custom_call", output_to_operand_aliasing={{}: (4, {})} | custom-call | flops 201326592 | bytes 917504 | tf_op jit(solution)/shard_map/join_part/pallas_call | solution.py:367
  (17 shorter events, 0.2 us)
Async XLA Ops:
  0.0 26.7 %collective-permute-start.8 = (bf16[3072,768]{1,0:T(8,128)(2,1)}, bf16[3072,768]{1,0:T(8,128)(2,1)S(1)}, u32[]{:S(2)}, u32[]{:S(2)}) collective-permute-start(bf16[3072,768]{1,0:T(8,128)(2,1)} %own_ref.1), channel_id=1, source_target_pairs={{0,1},{1,0},{2,3},{3,2},{4,5},{5,4},{6,7},{7,6},{8,9},{9,8},{10,11... | collective-permute-start | bytes 14155784 | tf_op jit(solution)/shard_map/ppermute | solution.py:240
  0.5 7.7 %collective-permute-start = (s32[3,12]{1,0:T(4,128)}, s32[3,12]{1,0:T(4,128)S(1)}, u32[]{:S(2)}, u32[]{:S(2)}) collective-permute-start(s32[3,12]{1,0:T(4,128)} %bitcast.2), channel_id=1, source_target_pairs={{0,1},{1,0},{2,3},{3,2},{4,5},{5,4},{6,7},{7,6},{8,9},{9,8},{10,11... | collective-permute-start | bytes 440 | tf_op jit(solution)/shard_map/ppermute | solution.py:241
  2.2 6.7 %collective-permute-start.1 = (bf16[136,256]{1,0:T(8,128)(2,1)S(1)}, bf16[136,256]{1,0:T(8,128)(2,1)S(1)}, u32[]{:S(2)}, u32[]{:S(2)}) collective-permute-start(bf16[136,256]{1,0:T(8,128)(2,1)S(1)} %get-tuple-element.23), channel_id=1, source_target_pairs={{8,0},{12,4},{0,8},{4,12},{24,16},{28,20},{16,24},{20,28},{9,1},{1... | collective-permute-start | bytes 208904 | tf_op jit(solution)/shard_map/ppermute | solution.py:230
  5.3 7.7 %collective-permute-start.2 = (bf16[136,256]{1,0:T(8,128)(2,1)S(1)}, bf16[136,256]{1,0:T(8,128)(2,1)S(1)}, u32[]{:S(2)}, u32[]{:S(2)}) collective-permute-start(bf16[136,256]{1,0:T(8,128)(2,1)S(1)} %get-tuple-element.24), channel_id=1, source_target_pairs={{16,0},{20,4},{24,8},{28,12},{0,16},{4,20},{8,24},{12,28},{17,1},{... | collective-permute-start | bytes 208904 | tf_op jit(solution)/shard_map/ppermute | solution.py:230
  7.8 6.2 %collective-permute-start.3 = (bf16[136,256]{1,0:T(8,128)(2,1)S(1)}, bf16[136,256]{1,0:T(8,128)(2,1)S(1)}, u32[]{:S(2)}, u32[]{:S(2)}) collective-permute-start(bf16[136,256]{1,0:T(8,128)(2,1)S(1)} %get-tuple-element.25), channel_id=1, source_target_pairs={{24,0},{28,4},{16,8},{20,12},{8,16},{12,20},{0,24},{4,28},{25,1},{... | collective-permute-start | bytes 208904 | tf_op jit(solution)/shard_map/ppermute | solution.py:230
  14.8 4.5 %collective-permute-start.4 = (bf16[264,128]{1,0:T(8,128)(2,1)S(1)}, bf16[264,128]{1,0:T(8,128)(2,1)S(1)}, u32[]{:S(2)}, u32[]{:S(2)}) collective-permute-start(bf16[264,128]{1,0:T(8,128)(2,1)S(1)} %get-tuple-element.26), channel_id=1, source_target_pairs={{0,2},{1,3},{2,0},{3,1},{4,6},{5,7},{6,4},{7,5},{8,10},{9,11},{10,... | collective-permute-start | bytes 202760 | tf_op jit(solution)/shard_map/ppermute | solution.py:237
  16.4 5.2 %collective-permute-start.5 = (bf16[264,128]{1,0:T(8,128)(2,1)S(1)}, bf16[264,128]{1,0:T(8,128)(2,1)S(1)}, u32[]{:S(2)}, u32[]{:S(2)}) collective-permute-start(bf16[264,128]{1,0:T(8,128)(2,1)S(1)} %get-tuple-element.27), channel_id=1, source_target_pairs={{0,6},{1,7},{2,4},{3,5},{4,2},{5,3},{6,0},{7,1},{8,14},{9,15},{10,... | collective-permute-start | bytes 202760 | tf_op jit(solution)/shard_map/ppermute | solution.py:237
  17.9 7.3 %collective-permute-start.7 = (bf16[264,256]{1,0:T(8,128)(2,1)S(1)}, bf16[264,256]{1,0:T(8,128)(2,1)S(1)}, u32[]{:S(2)}, u32[]{:S(2)}) collective-permute-start(bf16[264,256]{1,0:T(8,128)(2,1)S(1)} %get-tuple-element.28), channel_id=1, source_target_pairs={{0,4},{1,5},{2,6},{3,7},{4,0},{5,1},{6,2},{7,3},{8,12},{9,13},{10,... | collective-permute-start | bytes 405512 | tf_op jit(solution)/shard_map/ppermute | solution.py:237
  21.6 5.1 %collective-permute-start.6 = (bf16[264,128]{1,0:T(8,128)(2,1)S(1)}, bf16[264,128]{1,0:T(8,128)(2,1)S(1)}, u32[]{:S(2)}, u32[]{:S(2)}) collective-permute-start(bf16[264,128]{1,0:T(8,128)(2,1)S(1)} %add.8.refs_0_), channel_id=1, source_target_pairs={{8,0},{12,4},{0,8},{4,12},{24,16},{28,20},{16,24},{20,28},{9,1},{1... | collective-permute-start | bytes 202760 | tf_op jit(solution)/shard_map/ppermute | solution.py:230
  22.7 7.1 %collective-permute-start.10 = (bf16[264,128]{1,0:T(8,128)(2,1)S(1)}, bf16[264,128]{1,0:T(8,128)(2,1)S(1)}, u32[]{:S(2)}, u32[]{:S(2)}) collective-permute-start(bf16[264,128]{1,0:T(8,128)(2,1)S(1)} %add.8.refs_0_), channel_id=1, source_target_pairs={{24,0},{28,4},{16,8},{20,12},{8,16},{12,20},{0,24},{4,28},{25,1},{... | collective-permute-start | bytes 202760 | tf_op jit(solution)/shard_map/ppermute | solution.py:230
  25.1 5.2 %collective-permute-start.9 = (bf16[264,128]{1,0:T(8,128)(2,1)S(1)}, bf16[264,128]{1,0:T(8,128)(2,1)S(1)}, u32[]{:S(2)}, u32[]{:S(2)}) collective-permute-start(bf16[264,128]{1,0:T(8,128)(2,1)S(1)} %add.8.refs_0_), channel_id=1, source_target_pairs={{16,0},{20,4},{24,8},{28,12},{0,16},{4,20},{8,24},{12,28},{17,1},{... | collective-permute-start | bytes 202760 | tf_op jit(solution)/shard_map/ppermute | solution.py:230
  31.4 8.0 %collective-permute-start.11 = (s16[784,128]{1,0:T(8,128)(2,1)S(1)}, s16[784,128]{1,0:T(8,128)(2,1)S(1)}, u32[]{:S(2)}, u32[]{:S(2)}) collective-permute-start(s16[784,128]{1,0:T(8,128)(2,1)S(1)} %send_part.7), channel_id=1, source_target_pairs={{0,2},{1,3},{2,0},{3,1},{4,6},{5,7},{6,4},{7,5},{8,10},{9,11},{10,... | collective-permute-start | bytes 602120 | tf_op jit(solution)/shard_map/ppermute | solution.py:237
  33.5 13.0 %collective-permute-start.16 = (bf16[1536,128]{1,0:T(8,128)(2,1)S(1)}, bf16[1536,128]{1,0:T(8,128)(2,1)S(1)}, u32[]{:S(2)}, u32[]{:S(2)}) collective-permute-start(bf16[1536,128]{1,0:T(8,128)(2,1)S(1)} %fill.2.dense_ref), channel_id=1, source_target_pairs={{0,4},{1,5},{2,6},{3,7},{4,0},{5,1},{6,2},{7,3},{8,12},{9,13},{10,... | collective-permute-start | bytes 1179656 | tf_op jit(solution)/shard_map/ppermute | solution.py:237
  34.9 11.6 %collective-permute-start.17 = (s16[1296,128]{1,0:T(8,128)(2,1)S(1)}, s16[1296,128]{1,0:T(8,128)(2,1)S(1)}, u32[]{:S(2)}, u32[]{:S(2)}) collective-permute-start(s16[1296,128]{1,0:T(8,128)(2,1)S(1)} %send_part.8), channel_id=1, source_target_pairs={{0,2},{1,3},{2,0},{3,1},{4,6},{5,7},{6,4},{7,5},{8,10},{9,11},{10,... | collective-permute-start | bytes 995336 | tf_op jit(solution)/shard_map/ppermute | solution.py:237
  40.5 9.6 %collective-permute-start.15 = (s16[1040,128]{1,0:T(8,128)(2,1)S(1)}, s16[1040,128]{1,0:T(8,128)(2,1)S(1)}, u32[]{:S(2)}, u32[]{:S(2)}) collective-permute-start(s16[1040,128]{1,0:T(8,128)(2,1)S(1)} %send_part.9), channel_id=1, source_target_pairs={{0,2},{1,3},{2,0},{3,1},{4,6},{5,7},{6,4},{7,5},{8,10},{9,11},{10,... | collective-permute-start | bytes 798728 | tf_op jit(solution)/shard_map/ppermute | solution.py:237
  41.3 11.8 %collective-permute-start.14 = (bf16[264,256]{1,0:T(8,128)(2,1)S(1)}, bf16[264,256]{1,0:T(8,128)(2,1)S(1)}, u32[]{:S(2)}, u32[]{:S(2)}) collective-permute-start(bf16[264,256]{1,0:T(8,128)(2,1)S(1)} %add.9.refs_0_), channel_id=1, source_target_pairs={{24,0},{28,4},{16,8},{20,12},{8,16},{12,20},{0,24},{4,28},{25,1},{... | collective-permute-start | bytes 405512 | tf_op jit(solution)/shard_map/ppermute | solution.py:230
  43.6 9.5 %collective-permute-start.13 = (bf16[264,256]{1,0:T(8,128)(2,1)S(1)}, bf16[264,256]{1,0:T(8,128)(2,1)S(1)}, u32[]{:S(2)}, u32[]{:S(2)}) collective-permute-start(bf16[264,256]{1,0:T(8,128)(2,1)S(1)} %add.9.refs_0_), channel_id=1, source_target_pairs={{16,0},{20,4},{24,8},{28,12},{0,16},{4,20},{8,24},{12,28},{17,1},{... | collective-permute-start | bytes 405512 | tf_op jit(solution)/shard_map/ppermute | solution.py:230
  46.5 6.6 %collective-permute-start.12 = (bf16[264,256]{1,0:T(8,128)(2,1)S(1)}, bf16[264,256]{1,0:T(8,128)(2,1)S(1)}, u32[]{:S(2)}, u32[]{:S(2)}) collective-permute-start(bf16[264,256]{1,0:T(8,128)(2,1)S(1)} %add.9.refs_0_), channel_id=1, source_target_pairs={{8,0},{12,4},{0,8},{4,12},{24,16},{28,20},{16,24},{20,28},{9,1},{1... | collective-permute-start | bytes 405512 | tf_op jit(solution)/shard_map/ppermute | solution.py:230
  47.2 6.6 %collective-permute-start.18 = (s16[528,128]{1,0:T(8,128)(2,1)S(1)}, s16[528,128]{1,0:T(8,128)(2,1)S(1)}, u32[]{:S(2)}, u32[]{:S(2)}) collective-permute-start(s16[528,128]{1,0:T(8,128)(2,1)S(1)} %send_part.10), channel_id=1, source_target_pairs={{0,2},{1,3},{2,0},{3,1},{4,6},{5,7},{6,4},{7,5},{8,10},{9,11},{10,... | collective-permute-start | bytes 405512 | tf_op jit(solution)/shard_map/ppermute | solution.py:237
  51.3 10.3 %collective-permute-start.19 = (s16[1296,128]{1,0:T(8,128)(2,1)S(1)}, s16[1296,128]{1,0:T(8,128)(2,1)S(1)}, u32[]{:S(2)}, u32[]{:S(2)}) collective-permute-start(s16[1296,128]{1,0:T(8,128)(2,1)S(1)} %send_part.11), channel_id=1, source_target_pairs={{0,2},{1,3},{2,0},{3,1},{4,6},{5,7},{6,4},{7,5},{8,10},{9,11},{10,... | collective-permute-start | bytes 995336 | tf_op jit(solution)/shard_map/ppermute | solution.py:237
  54.8 11.7 %collective-permute-start.21 = (s16[1040,128]{1,0:T(8,128)(2,1)S(1)}, s16[1040,128]{1,0:T(8,128)(2,1)S(1)}, u32[]{:S(2)}, u32[]{:S(2)}) collective-permute-start(s16[1040,128]{1,0:T(8,128)(2,1)S(1)} %send_part.12), channel_id=1, source_target_pairs={{0,2},{1,3},{2,0},{3,1},{4,6},{5,7},{6,4},{7,5},{8,10},{9,11},{10,... | collective-permute-start | bytes 798728 | tf_op jit(solution)/shard_map/ppermute | solution.py:237
  62.0 7.1 %collective-permute-start.20 = (s16[272,128]{1,0:T(8,128)(2,1)S(1)}, s16[272,128]{1,0:T(8,128)(2,1)S(1)}, u32[]{:S(2)}, u32[]{:S(2)}) collective-permute-start(s16[272,128]{1,0:T(8,128)(2,1)S(1)} %send_part.13), channel_id=1, source_target_pairs={{0,2},{1,3},{2,0},{3,1},{4,6},{5,7},{6,4},{7,5},{8,10},{9,11},{10,... | collective-permute-start | bytes 208904 | tf_op jit(solution)/shard_map/ppermute | solution.py:237

commit v14 on v12

--- a/solution.py
+++ b/solution.py
@@ -14,7 +14,8 @@
 FAR_CUTS = (0.0, 0.167, 0.583, 0.917, 1.0)
 CODE_TOP = 32767.0
 FRACTION = 8192.0
-META_ROWS = 16
+META_ROWS = 8
+TILE_ROWS = 16
 SCREEN_PARTS = 4
 PARAMS = pltpu.CompilerParams(vmem_limit_bytes=16 * 1024 * 1024)
 SMEM = pl.BlockSpec(memory_space=pltpu.SMEM)
@@ -53,7 +54,7 @@
     info = info.astype(jnp.float32).astype(panel_ref.dtype)
     for shift, piece_ref in enumerate(piece_refs):
         first = partner(place, shift if peers & (peers - 1) == 0 else peers - shift, peers) * share
-        start = pl.multiple_of(lax.rem(first, tile_width), META_ROWS)
+        start = pl.multiple_of(lax.rem(first, tile_width), TILE_ROWS)
         piece_ref[pl.ds(0, share), :] = panel_ref[0, 0, first // tile_width, pl.ds(start, share), :]
         piece_ref[pl.ds(share, META_ROWS), :] = info
 
@@ -116,7 +117,7 @@
 
             @pl.when(slot < count)
             def _():
-                spot = pl.multiple_of(start + lax.rem(first, tile_width), META_ROWS)
+                spot = pl.multiple_of(start + lax.rem(first, tile_width), TILE_ROWS)
                 dense_ref[pl.ds(spot, share), :] = piece_ref[pl.ds(group * share, share), :]
 
 
@@ -315,7 +316,7 @@
         )
 
     def code_shape(span):
-        return (span * block_rows + -(-2 * span // META_ROWS) * META_ROWS, half_width)
+        return (span * block_rows + -(-2 * span // TILE_ROWS) * TILE_ROWS, half_width)
 
     def scratch_rows(span):
         return code_shape(span)[0] - span * block_rows

time: 69.7 us -> 69.2 us (level)
  no operation moved by 1% of the time
where the time goes in v14:
time: 69.2 us; the launch traced here: 69 us
  starting transfers between devices  27.9 us (40%)
  waiting for transfers between devices  21.7 us (31%)
  Pallas kernels  17.8 us (26%)
  between operations  0.83 us (1%)
  other arithmetic  0.76 us (1%)
    ppermute x11, starting transfers between devices, across(): return lax.ppermute(value, ('row', 'col'), pairs)  13.8 us
    ppermute x9, starting transfers between devices, along(): return lax.ppermute(value, 'row', pairs)  13.6 us
    ppermute x11, waiting for transfers between devices, across(): return lax.ppermute(value, ('row', 'col'), pairs)  13 us
    ppermute x9, waiting for transfers between devices, along(): return lax.ppermute(value, 'row', pairs)  8.38 us
    pallas_call x7, Pallas kernels, shards(): pl.pallas_call(partial(send_kernel, first, span, block_rows), in_specs=[V...  6.43 us
    pallas_call x4, Pallas kernels, shards(): pl.pallas_call(partial(join_kernel, first, span, block_rows, skips), in_s...  5.87 us
    pallas_call x1, Pallas kernels, screen(): pl.pallas_call(partial(screen_kernel, tile_width, block_rows), in_specs=[...  3.07 us
  transfers between devices with their start and end apart: 22, of which 11 were waited for; matrix products, arithmetic and copies ran while one was open for 1% of the time, Pallas kernels for 24%

profile of v14, /device:TPU:0, one launch (start us, length us, event | category | flops | bytes accessed | tf_op | source)
XLA Modules:
  0.0 69.0 jit_solution(13737521072873810602)
XLA Ops:
  0.0 0.5 collective-permute-start.8
  0.5 0.1 collective-permute-start
  1.2 1.0 %pack.1 = (bf16[136,256]{1,0:T(8,128)(2,1)S(1)}, bf16[136,256]{1,0:T(8,128)(2,1)S(1)}, bf16[136,256]{1,0:T(8,128)(2,1)S(1)}, bf16[136,256]{1,0:T(8,128)(2,1)S(1)}) custom-call(s32[1,1,2]{2,1,0:T(1,128)} %list_ref.1, s32[1,1]{1,0:T(1,128)S(6)} %copy.13.count_ref, bf16[1,1,2,256,256]{4,3,2,1,0:T(8,128)(2,1)} %panel_ref.1), custom_call_target="tpu_custom_call" | custom-call | tf_op jit(solution)/shard_map/pack/pallas_call | solution.py:248
  2.2 3.0 %collective-permute-start.1 = (bf16[136,256]{1,0:T(8,128)(2,1)S(1)}, bf16[136,256]{1,0:T(8,128)(2,1)S(1)}, u32[]{:S(2)}, u32[]{:S(2)}) collective-permute-start(bf16[136,256]{1,0:T(8,128)(2,1)S(1)} %get-tuple-element.22), channel_id=1, source_target_pairs={{8,0},{12,4},{0,8},{4,12},{24,16},{28,20},{16,24},{20,28},{9,1},{1... | collective-permute-start | bytes 208904 | tf_op jit(solution)/shard_map/ppermute | solution.py:230
  5.3 2.6 %collective-permute-start.2 = (bf16[136,256]{1,0:T(8,128)(2,1)S(1)}, bf16[136,256]{1,0:T(8,128)(2,1)S(1)}, u32[]{:S(2)}, u32[]{:S(2)}) collective-permute-start(bf16[136,256]{1,0:T(8,128)(2,1)S(1)} %get-tuple-element.23), channel_id=1, source_target_pairs={{16,0},{20,4},{24,8},{28,12},{0,16},{4,20},{8,24},{12,28},{17,1},{... | collective-permute-start | bytes 208904 | tf_op jit(solution)/shard_map/ppermute | solution.py:230
  7.8 0.4 collective-permute-done
  8.2 0.7 %pad_add_fusion.plan_ref.mask_ref = s32[7,12]{1,0:T(8,128)S(1)} fusion(s32[1,4]{1,0:T(1,128)} %bitcast.4, s32[3,12]{1,0:T(4,128)S(1)} %collective-permute-done, s32[3,12]{1,0:T(4,128)} %bitcast.3), kind=kLoop, calls=%fused_computation | loop fusion | flops 168 | bytes 640 | tf_op jit(solution)/shard_map/concatenate | solution.py:243
  8.9 4.1 %collective-permute-done.2.refs_2_ = bf16[136,256]{1,0:T(8,128)(2,1)S(1)} collective-permute-done((bf16[136,256]{1,0:T(8,128)(2,1)S(1)}, bf16[136,256]{1,0:T(8,128)(2,1)S(1)}, u32[]{:S(2)}, u32[]{:S(2)}) %collective-permute-start.2) | collective-permute-done | bytes 69664 | tf_op jit(solution)/shard_map/ppermute | solution.py:230
  13.0 1.1 %collective-permute-done.3.refs_3_ = bf16[136,256]{1,0:T(8,128)(2,1)S(1)} collective-permute-done((bf16[136,256]{1,0:T(8,128)(2,1)S(1)}, bf16[136,256]{1,0:T(8,128)(2,1)S(1)}, u32[]{:S(2)}, u32[]{:S(2)}) %collective-permute-start.3) | collective-permute-done | bytes 69664 | tf_op jit(solution)/shard_map/ppermute | solution.py:230
  14.1 0.8 %choose.1 = (bf16[264,256]{1,0:T(8,128)(2,1)S(1)}, bf16[264,128]{1,0:T(8,128)(2,1)S(1)}, bf16[264,128]{1,0:T(8,128)(2,1)S(1)}) custom-call(s32[7,12]{1,0:T(8,128)S(1)} %pad_add_fusion.plan_ref.mask_ref, bf16[136,256]{1,0:T(8,128)(2,1)S(1)} %get-tuple-element.21.refs_0_, bf16[136,256]{1,0:T(8,128)(2,1)S(1)} %collective-permute-done.1.refs_1_, ...), custom_call_target="tpu_custom_call" | custom-call | tf_op jit(solution)/shard_map/choose/pallas_call | solution.py:263
  14.8 1.5 %collective-permute-start.4 = (bf16[264,128]{1,0:T(8,128)(2,1)S(1)}, bf16[264,128]{1,0:T(8,128)(2,1)S(1)}, u32[]{:S(2)}, u32[]{:S(2)}) collective-permute-start(bf16[264,128]{1,0:T(8,128)(2,1)S(1)} %get-tuple-element.25), channel_id=1, source_target_pairs={{0,2},{1,3},{2,0},{3,1},{4,6},{5,7},{6,4},{7,5},{8,10},{9,11},{10,... | collective-permute-start | bytes 202760 | tf_op jit(solution)/shard_map/ppermute | solution.py:237
  16.4 1.5 %collective-permute-start.5 = (bf16[264,128]{1,0:T(8,128)(2,1)S(1)}, bf16[264,128]{1,0:T(8,128)(2,1)S(1)}, u32[]{:S(2)}, u32[]{:S(2)}) collective-permute-start(bf16[264,128]{1,0:T(8,128)(2,1)S(1)} %get-tuple-element.26), channel_id=1, source_target_pairs={{0,6},{1,7},{2,4},{3,5},{4,2},{5,3},{6,0},{7,1},{8,14},{9,15},{10,... | collective-permute-start | bytes 202760 | tf_op jit(solution)/shard_map/ppermute | solution.py:237
  17.9 0.5 collective-permute-start.7
  18.4 0.9 %collective-permute-done.4 = bf16[264,128]{1,0:T(8,128)(2,1)S(1)} collective-permute-done((bf16[264,128]{1,0:T(8,128)(2,1)S(1)}, bf16[264,128]{1,0:T(8,128)(2,1)S(1)}, u32[]{:S(2)}, u32[]{:S(2)}) %collective-permute-start.4) | collective-permute-done | bytes 67616 | tf_op jit(solution)/shard_map/ppermute | solution.py:237
  19.3 2.3 %collective-permute-done.5 = bf16[264,128]{1,0:T(8,128)(2,1)S(1)} collective-permute-done((bf16[264,128]{1,0:T(8,128)(2,1)S(1)}, bf16[264,128]{1,0:T(8,128)(2,1)S(1)}, u32[]{:S(2)}, u32[]{:S(2)}) %collective-permute-start.5) | collective-permute-done | bytes 67616 | tf_op jit(solution)/shard_map/ppermute | solution.py:237
  21.6 1.1 %collective-permute-start.6 = (bf16[264,128]{1,0:T(8,128)(2,1)S(1)}, bf16[264,128]{1,0:T(8,128)(2,1)S(1)}, u32[]{:S(2)}, u32[]{:S(2)}) collective-permute-start(bf16[264,128]{1,0:T(8,128)(2,1)S(1)} %add.8.refs_0_), channel_id=1, source_target_pairs={{8,0},{12,4},{0,8},{4,12},{24,16},{28,20},{16,24},{20,28},{9,1},{1... | collective-permute-start | bytes 202760 | tf_op jit(solution)/shard_map/ppermute | solution.py:230
  22.7 2.4 %collective-permute-start.10 = (bf16[264,128]{1,0:T(8,128)(2,1)S(1)}, bf16[264,128]{1,0:T(8,128)(2,1)S(1)}, u32[]{:S(2)}, u32[]{:S(2)}) collective-permute-start(bf16[264,128]{1,0:T(8,128)(2,1)S(1)} %add.8.refs_0_), channel_id=1, source_target_pairs={{24,0},{28,4},{16,8},{20,12},{8,16},{12,20},{0,24},{4,28},{25,1},{... | collective-permute-start | bytes 202760 | tf_op jit(solution)/shard_map/ppermute | solution.py:230
  25.1 0.1 collective-permute-start.9
  25.2 1.5 %collective-permute-done.6.refs_1_ = bf16[264,128]{1,0:T(8,128)(2,1)S(1)} collective-permute-done((bf16[264,128]{1,0:T(8,128)(2,1)S(1)}, bf16[264,128]{1,0:T(8,128)(2,1)S(1)}, u32[]{:S(2)}, u32[]{:S(2)}) %collective-permute-start.6) | collective-permute-done | bytes 67616 | tf_op jit(solution)/shard_map/ppermute | solution.py:230
  26.7 3.1 %screen.1.rows_ref = bf16[3072,1536]{1,0:T(8,128)(2,1)S(1)} custom-call(s32[7,12]{1,0:T(8,128)S(1)} %pad_add_fusion.plan_ref.mask_ref, bf16[3072,768]{1,0:T(8,128)(2,1)} %own_ref.1, bf16[3072,768]{1,0:T(8,128)(2,1)S(1)} %collective-permute-done.8.other_ref), custom_call_target="tpu_custom_call" | custom-call | flops 4718592 | bytes 18874368 | tf_op jit(solution)/shard_map/screen/pallas_call | solution.py:284
  29.8 0.5 collective-permute-done.9.refs_2_
  30.3 0.3 fill.2.dense_ref
  30.6 1.7 %collective-permute-start.15 = (bf16[1536,128]{1,0:T(8,128)(2,1)S(1)}, bf16[1536,128]{1,0:T(8,128)(2,1)S(1)}, u32[]{:S(2)}, u32[]{:S(2)}) collective-permute-start(bf16[1536,128]{1,0:T(8,128)(2,1)S(1)} %fill.2.dense_ref), channel_id=1, source_target_pairs={{0,4},{1,5},{2,6},{3,7},{4,0},{5,1},{6,2},{7,3},{8,12},{9,13},{10,... | collective-permute-start | bytes 1179656 | tf_op jit(solution)/shard_map/ppermute | solution.py:237
  32.3 0.6 send_part.7
  32.9 0.5 collective-permute-start.11
  33.4 1.2 %send_part.8 = s16[1296,128]{1,0:T(8,128)(2,1)S(1)} custom-call(bf16[3072,1536]{1,0:T(8,128)(2,1)S(1)} %screen.1.rows_ref, bf16[1536,128]{1,0:T(8,128)(2,1)S(1)} %fill.2.dense_ref), custom_call_target="tpu_custom_call" | custom-call | flops 503316480 | bytes 4259840 | tf_op jit(solution)/shard_map/send_part/pallas_call | solution.py:338
  34.7 1.7 %collective-permute-start.17 = (s16[1296,128]{1,0:T(8,128)(2,1)S(1)}, s16[1296,128]{1,0:T(8,128)(2,1)S(1)}, u32[]{:S(2)}, u32[]{:S(2)}) collective-permute-start(s16[1296,128]{1,0:T(8,128)(2,1)S(1)} %send_part.8), channel_id=1, source_target_pairs={{0,2},{1,3},{2,0},{3,1},{4,6},{5,7},{6,4},{7,5},{8,10},{9,11},{10,... | collective-permute-start | bytes 995336 | tf_op jit(solution)/shard_map/ppermute | solution.py:237
  36.3 2.4 %collective-permute-done.11.refs_0_ = s16[528,128]{1,0:T(8,128)(2,1)S(1)} collective-permute-done((s16[528,128]{1,0:T(8,128)(2,1)S(1)}, s16[528,128]{1,0:T(8,128)(2,1)S(1)}, u32[]{:S(2)}, u32[]{:S(2)}) %collective-permute-start.11) | collective-permute-done | bytes 135200 | tf_op jit(solution)/shard_map/ppermute | solution.py:237
  38.7 1.2 %send_part.9 = s16[1296,128]{1,0:T(8,128)(2,1)S(1)} custom-call(bf16[3072,1536]{1,0:T(8,128)(2,1)S(1)} %screen.1.rows_ref, bf16[1536,128]{1,0:T(8,128)(2,1)S(1)} %fill.2.dense_ref), custom_call_target="tpu_custom_call" | custom-call | flops 503316480 | bytes 4259840 | tf_op jit(solution)/shard_map/send_part/pallas_call | solution.py:338
  40.0 1.3 %collective-permute-start.16 = (s16[1296,128]{1,0:T(8,128)(2,1)S(1)}, s16[1296,128]{1,0:T(8,128)(2,1)S(1)}, u32[]{:S(2)}, u32[]{:S(2)}) collective-permute-start(s16[1296,128]{1,0:T(8,128)(2,1)S(1)} %send_part.9), channel_id=1, source_target_pairs={{0,2},{1,3},{2,0},{3,1},{4,6},{5,7},{6,4},{7,5},{8,10},{9,11},{10,... | collective-permute-start | bytes 995336 | tf_op jit(solution)/shard_map/ppermute | solution.py:237
  41.3 2.3 %collective-permute-start.14 = (bf16[264,256]{1,0:T(8,128)(2,1)S(1)}, bf16[264,256]{1,0:T(8,128)(2,1)S(1)}, u32[]{:S(2)}, u32[]{:S(2)}) collective-permute-start(bf16[264,256]{1,0:T(8,128)(2,1)S(1)} %add.9.refs_0_), channel_id=1, source_target_pairs={{24,0},{28,4},{16,8},{20,12},{8,16},{12,20},{0,24},{4,28},{25,1},{... | collective-permute-start | bytes 405512 | tf_op jit(solution)/shard_map/ppermute | solution.py:230
  43.6 2.0 %collective-permute-start.12 = (bf16[264,256]{1,0:T(8,128)(2,1)S(1)}, bf16[264,256]{1,0:T(8,128)(2,1)S(1)}, u32[]{:S(2)}, u32[]{:S(2)}) collective-permute-start(bf16[264,256]{1,0:T(8,128)(2,1)S(1)} %add.9.refs_0_), channel_id=1, source_target_pairs={{8,0},{12,4},{0,8},{4,12},{24,16},{28,20},{16,24},{20,28},{9,1},{1... | collective-permute-start | bytes 405512 | tf_op jit(solution)/shard_map/ppermute | solution.py:230
  45.7 0.6 send_part.10
  46.3 0.9 %collective-permute-start.18 = (s16[528,128]{1,0:T(8,128)(2,1)S(1)}, s16[528,128]{1,0:T(8,128)(2,1)S(1)}, u32[]{:S(2)}, u32[]{:S(2)}) collective-permute-start(s16[528,128]{1,0:T(8,128)(2,1)S(1)} %send_part.10), channel_id=1, source_target_pairs={{0,2},{1,3},{2,0},{3,1},{4,6},{5,7},{6,4},{7,5},{8,10},{9,11},{10,... | collective-permute-start | bytes 405512 | tf_op jit(solution)/shard_map/ppermute | solution.py:237
  47.2 1.2 %send_part.11 = s16[1296,128]{1,0:T(8,128)(2,1)S(1)} custom-call(bf16[3072,1536]{1,0:T(8,128)(2,1)S(1)} %screen.1.rows_ref, bf16[1536,128]{1,0:T(8,128)(2,1)S(1)} %collective-permute-done.15.dense_ref), custom_call_target="tpu_custom_call" | custom-call | flops 503316480 | bytes 4259840 | tf_op jit(solution)/shard_map/send_part/pallas_call | solution.py:338
  48.4 1.3 %collective-permute-start.19 = (s16[1296,128]{1,0:T(8,128)(2,1)S(1)}, s16[1296,128]{1,0:T(8,128)(2,1)S(1)}, u32[]{:S(2)}, u32[]{:S(2)}) collective-permute-start(s16[1296,128]{1,0:T(8,128)(2,1)S(1)} %send_part.11), channel_id=1, source_target_pairs={{0,2},{1,3},{2,0},{3,1},{4,6},{5,7},{6,4},{7,5},{8,10},{9,11},{10,... | collective-permute-start | bytes 995336 | tf_op jit(solution)/shard_map/ppermute | solution.py:237
  49.7 1.2 %collective-permute-done.13.refs_2_ = bf16[264,256]{1,0:T(8,128)(2,1)S(1)} collective-permute-done((bf16[264,256]{1,0:T(8,128)(2,1)S(1)}, bf16[264,256]{1,0:T(8,128)(2,1)S(1)}, u32[]{:S(2)}, u32[]{:S(2)}) %collective-permute-start.13) | collective-permute-done | bytes 135200 | tf_op jit(solution)/shard_map/ppermute | solution.py:230
  51.0 0.3 fill.3.dense_ref
  51.3 4.5 %collective-permute-done.18.refs_1_ = s16[528,128]{1,0:T(8,128)(2,1)S(1)} collective-permute-done((s16[528,128]{1,0:T(8,128)(2,1)S(1)}, s16[528,128]{1,0:T(8,128)(2,1)S(1)}, u32[]{:S(2)}, u32[]{:S(2)}) %collective-permute-start.18) | collective-permute-done | bytes 135200 | tf_op jit(solution)/shard_map/ppermute | solution.py:237
  55.9 1.0 %send_part.12 = s16[1040,128]{1,0:T(8,128)(2,1)S(1)} custom-call(bf16[3072,1536]{1,0:T(8,128)(2,1)S(1)} %screen.1.rows_ref, bf16[1536,128]{1,0:T(8,128)(2,1)S(1)} %collective-permute-done.15.dense_ref), custom_call_target="tpu_custom_call" | custom-call | flops 402653184 | bytes 3407872 | tf_op jit(solution)/shard_map/send_part/pallas_call | solution.py:338
  56.9 1.3 %collective-permute-start.21 = (s16[1040,128]{1,0:T(8,128)(2,1)S(1)}, s16[1040,128]{1,0:T(8,128)(2,1)S(1)}, u32[]{:S(2)}, u32[]{:S(2)}) collective-permute-start(s16[1040,128]{1,0:T(8,128)(2,1)S(1)} %send_part.12), channel_id=1, source_target_pairs={{0,2},{1,3},{2,0},{3,1},{4,6},{5,7},{6,4},{7,5},{8,10},{9,11},{10,... | collective-permute-start | bytes 798728 | tf_op jit(solution)/shard_map/ppermute | solution.py:237
  58.2 1.2 %join_part.4.refs_2_ = bf16[3072,256]{1,0:T(8,128)(2,1)} custom-call(bf16[3072,1536]{1,0:T(8,128)(2,1)S(1)} %screen.1.rows_ref, bf16[1536,256]{1,0:T(8,128)(2,1)S(1)} %fill.3.dense_ref, s16[528,128]{1,0:T(8,128)(2,1)S(1)} %collective-permute-done.11.refs_0_, s16[528,128]{1,0:T(8,128)(2,1)S(1)} %collective-permute-done.18.refs_1_), custom_call_target="tpu_custom_call" | custom-call | flops 402653184 | bytes 1835008 | tf_op jit(solution)/shard_map/join_part/pallas_call | solution.py:367
  59.4 2.9 %collective-permute-done.19.refs_1_ = s16[1296,128]{1,0:T(8,128)(2,1)S(1)} collective-permute-done((s16[1296,128]{1,0:T(8,128)(2,1)S(1)}, s16[1296,128]{1,0:T(8,128)(2,1)S(1)}, u32[]{:S(2)}, u32[]{:S(2)}) %collective-permute-start.19) | collective-permute-done | bytes 331808 | tf_op jit(solution)/shard_map/ppermute | solution.py:237
  62.3 0.4 send_part.13
  62.7 1.7 %collective-permute-start.20 = (s16[272,128]{1,0:T(8,128)(2,1)S(1)}, s16[272,128]{1,0:T(8,128)(2,1)S(1)}, u32[]{:S(2)}, u32[]{:S(2)}) collective-permute-start(s16[272,128]{1,0:T(8,128)(2,1)S(1)} %send_part.13), channel_id=1, source_target_pairs={{0,2},{1,3},{2,0},{3,1},{4,6},{5,7},{6,4},{7,5},{8,10},{9,11},{10,... | collective-permute-start | bytes 208904 | tf_op jit(solution)/shard_map/ppermute | solution.py:237
  64.4 1.9 %join_part.5.refs_2_ = bf16[3072,256]{1,0:T(8,128)(2,1)} custom-call(bf16[3072,1536]{1,0:T(8,128)(2,1)S(1)} %screen.1.rows_ref, bf16[1536,256]{1,0:T(8,128)(2,1)S(1)} %fill.3.dense_ref, s16[1296,128]{1,0:T(8,128)(2,1)S(1)} %collective-permute-done.17.refs_0_, s16[1296,128]{1,0:T(8,128)(2,1)S(1)} %collective-permute-done.19.refs_1_, ...), custom_call_target="tpu_custom_call", output_to_operand_aliasing={{}: (4, {})} | custom-call | flops 1006632960 | bytes 4587520 | tf_op jit(solution)/shard_map/join_part/pallas_call | solution.py:367
  66.3 1.7 %join_part.6.refs_2_ = bf16[3072,256]{1,0:T(8,128)(2,1)} custom-call(bf16[3072,1536]{1,0:T(8,128)(2,1)S(1)} %screen.1.rows_ref, bf16[1536,256]{1,0:T(8,128)(2,1)S(1)} %fill.3.dense_ref, s16[1296,128]{1,0:T(8,128)(2,1)S(1)} %collective-permute-done.16.refs_0_, s16[1040,128]{1,0:T(8,128)(2,1)S(1)} %collective-permute-done.21.refs_1_, ...), custom_call_target="tpu_custom_call", output_to_operand_aliasing={{}: (4, {})} | custom-call | flops 805306368 | bytes 3670016 | tf_op jit(solution)/shard_map/join_part/pallas_call | solution.py:367
  68.0 1.0 %join_part.7 = bf16[3072,256]{1,0:T(8,128)(2,1)} custom-call(bf16[3072,1536]{1,0:T(8,128)(2,1)S(1)} %screen.1.rows_ref, bf16[1536,256]{1,0:T(8,128)(2,1)S(1)} %fill.3.dense_ref, s16[1296,128]{1,0:T(8,128)(2,1)S(1)} %collective-permute-done.16.refs_0_, s16[272,128]{1,0:T(8,128)(2,1)S(1)} %collective-permute-done.20.refs_1_, ...), custom_call_target="tpu_custom_call", output_to_operand_aliasing={{}: (4, {})} | custom-call | flops 201326592 | bytes 917504 | tf_op jit(solution)/shard_map/join_part/pallas_call | solution.py:367
  (15 shorter events, 0.1 us)
Async XLA Ops:
  0.0 26.7 %collective-permute-start.8 = (bf16[3072,768]{1,0:T(8,128)(2,1)}, bf16[3072,768]{1,0:T(8,128)(2,1)S(1)}, u32[]{:S(2)}, u32[]{:S(2)}) collective-permute-start(bf16[3072,768]{1,0:T(8,128)(2,1)} %own_ref.1), channel_id=1, source_target_pairs={{0,1},{1,0},{2,3},{3,2},{4,5},{5,4},{6,7},{7,6},{8,9},{9,8},{10,11... | collective-permute-start | bytes 14155784 | tf_op jit(solution)/shard_map/ppermute | solution.py:240
  0.5 7.7 %collective-permute-start = (s32[3,12]{1,0:T(4,128)}, s32[3,12]{1,0:T(4,128)S(1)}, u32[]{:S(2)}, u32[]{:S(2)}) collective-permute-start(s32[3,12]{1,0:T(4,128)} %bitcast.2), channel_id=1, source_target_pairs={{0,1},{1,0},{2,3},{3,2},{4,5},{5,4},{6,7},{7,6},{8,9},{9,8},{10,11... | collective-permute-start | bytes 440 | tf_op jit(solution)/shard_map/ppermute | solution.py:241
  2.2 6.7 %collective-permute-start.1 = (bf16[136,256]{1,0:T(8,128)(2,1)S(1)}, bf16[136,256]{1,0:T(8,128)(2,1)S(1)}, u32[]{:S(2)}, u32[]{:S(2)}) collective-permute-start(bf16[136,256]{1,0:T(8,128)(2,1)S(1)} %get-tuple-element.22), channel_id=1, source_target_pairs={{8,0},{12,4},{0,8},{4,12},{24,16},{28,20},{16,24},{20,28},{9,1},{1... | collective-permute-start | bytes 208904 | tf_op jit(solution)/shard_map/ppermute | solution.py:230
  5.3 7.7 %collective-permute-start.2 = (bf16[136,256]{1,0:T(8,128)(2,1)S(1)}, bf16[136,256]{1,0:T(8,128)(2,1)S(1)}, u32[]{:S(2)}, u32[]{:S(2)}) collective-permute-start(bf16[136,256]{1,0:T(8,128)(2,1)S(1)} %get-tuple-element.23), channel_id=1, source_target_pairs={{16,0},{20,4},{24,8},{28,12},{0,16},{4,20},{8,24},{12,28},{17,1},{... | collective-permute-start | bytes 208904 | tf_op jit(solution)/shard_map/ppermute | solution.py:230
  7.8 6.2 %collective-permute-start.3 = (bf16[136,256]{1,0:T(8,128)(2,1)S(1)}, bf16[136,256]{1,0:T(8,128)(2,1)S(1)}, u32[]{:S(2)}, u32[]{:S(2)}) collective-permute-start(bf16[136,256]{1,0:T(8,128)(2,1)S(1)} %get-tuple-element.24), channel_id=1, source_target_pairs={{24,0},{28,4},{16,8},{20,12},{8,16},{12,20},{0,24},{4,28},{25,1},{... | collective-permute-start | bytes 208904 | tf_op jit(solution)/shard_map/ppermute | solution.py:230
  14.8 4.4 %collective-permute-start.4 = (bf16[264,128]{1,0:T(8,128)(2,1)S(1)}, bf16[264,128]{1,0:T(8,128)(2,1)S(1)}, u32[]{:S(2)}, u32[]{:S(2)}) collective-permute-start(bf16[264,128]{1,0:T(8,128)(2,1)S(1)} %get-tuple-element.25), channel_id=1, source_target_pairs={{0,2},{1,3},{2,0},{3,1},{4,6},{5,7},{6,4},{7,5},{8,10},{9,11},{10,... | collective-permute-start | bytes 202760 | tf_op jit(solution)/shard_map/ppermute | solution.py:237
  16.4 5.2 %collective-permute-start.5 = (bf16[264,128]{1,0:T(8,128)(2,1)S(1)}, bf16[264,128]{1,0:T(8,128)(2,1)S(1)}, u32[]{:S(2)}, u32[]{:S(2)}) collective-permute-start(bf16[264,128]{1,0:T(8,128)(2,1)S(1)} %get-tuple-element.26), channel_id=1, source_target_pairs={{0,6},{1,7},{2,4},{3,5},{4,2},{5,3},{6,0},{7,1},{8,14},{9,15},{10,... | collective-permute-start | bytes 202760 | tf_op jit(solution)/shard_map/ppermute | solution.py:237
  17.9 7.3 %collective-permute-start.7 = (bf16[264,256]{1,0:T(8,128)(2,1)S(1)}, bf16[264,256]{1,0:T(8,128)(2,1)S(1)}, u32[]{:S(2)}, u32[]{:S(2)}) collective-permute-start(bf16[264,256]{1,0:T(8,128)(2,1)S(1)} %get-tuple-element.27), channel_id=1, source_target_pairs={{0,4},{1,5},{2,6},{3,7},{4,0},{5,1},{6,2},{7,3},{8,12},{9,13},{10,... | collective-permute-start | bytes 405512 | tf_op jit(solution)/shard_map/ppermute | solution.py:237
  21.6 5.1 %collective-permute-start.6 = (bf16[264,128]{1,0:T(8,128)(2,1)S(1)}, bf16[264,128]{1,0:T(8,128)(2,1)S(1)}, u32[]{:S(2)}, u32[]{:S(2)}) collective-permute-start(bf16[264,128]{1,0:T(8,128)(2,1)S(1)} %add.8.refs_0_), channel_id=1, source_target_pairs={{8,0},{12,4},{0,8},{4,12},{24,16},{28,20},{16,24},{20,28},{9,1},{1... | collective-permute-start | bytes 202760 | tf_op jit(solution)/shard_map/ppermute | solution.py:230
  22.7 7.1 %collective-permute-start.10 = (bf16[264,128]{1,0:T(8,128)(2,1)S(1)}, bf16[264,128]{1,0:T(8,128)(2,1)S(1)}, u32[]{:S(2)}, u32[]{:S(2)}) collective-permute-start(bf16[264,128]{1,0:T(8,128)(2,1)S(1)} %add.8.refs_0_), channel_id=1, source_target_pairs={{24,0},{28,4},{16,8},{20,12},{8,16},{12,20},{0,24},{4,28},{25,1},{... | collective-permute-start | bytes 202760 | tf_op jit(solution)/shard_map/ppermute | solution.py:230
  25.1 5.2 %collective-permute-start.9 = (bf16[264,128]{1,0:T(8,128)(2,1)S(1)}, bf16[264,128]{1,0:T(8,128)(2,1)S(1)}, u32[]{:S(2)}, u32[]{:S(2)}) collective-permute-start(bf16[264,128]{1,0:T(8,128)(2,1)S(1)} %add.8.refs_0_), channel_id=1, source_target_pairs={{16,0},{20,4},{24,8},{28,12},{0,16},{4,20},{8,24},{12,28},{17,1},{... | collective-permute-start | bytes 202760 | tf_op jit(solution)/shard_map/ppermute | solution.py:230
  30.6 8.1 %collective-permute-start.15 = (bf16[1536,128]{1,0:T(8,128)(2,1)S(1)}, bf16[1536,128]{1,0:T(8,128)(2,1)S(1)}, u32[]{:S(2)}, u32[]{:S(2)}) collective-permute-start(bf16[1536,128]{1,0:T(8,128)(2,1)S(1)} %fill.2.dense_ref), channel_id=1, source_target_pairs={{0,4},{1,5},{2,6},{3,7},{4,0},{5,1},{6,2},{7,3},{8,12},{9,13},{10,... | collective-permute-start | bytes 1179656 | tf_op jit(solution)/shard_map/ppermute | solution.py:237
  32.9 5.8 %collective-permute-start.11 = (s16[528,128]{1,0:T(8,128)(2,1)S(1)}, s16[528,128]{1,0:T(8,128)(2,1)S(1)}, u32[]{:S(2)}, u32[]{:S(2)}) collective-permute-start(s16[528,128]{1,0:T(8,128)(2,1)S(1)} %send_part.7), channel_id=1, source_target_pairs={{0,2},{1,3},{2,0},{3,1},{4,6},{5,7},{6,4},{7,5},{8,10},{9,11},{10,... | collective-permute-start | bytes 405512 | tf_op jit(solution)/shard_map/ppermute | solution.py:237
  34.7 11.6 %collective-permute-start.17 = (s16[1296,128]{1,0:T(8,128)(2,1)S(1)}, s16[1296,128]{1,0:T(8,128)(2,1)S(1)}, u32[]{:S(2)}, u32[]{:S(2)}) collective-permute-start(s16[1296,128]{1,0:T(8,128)(2,1)S(1)} %send_part.8), channel_id=1, source_target_pairs={{0,2},{1,3},{2,0},{3,1},{4,6},{5,7},{6,4},{7,5},{8,10},{9,11},{10,... | collective-permute-start | bytes 995336 | tf_op jit(solution)/shard_map/ppermute | solution.py:237
  40.0 15.9 %collective-permute-start.16 = (s16[1296,128]{1,0:T(8,128)(2,1)S(1)}, s16[1296,128]{1,0:T(8,128)(2,1)S(1)}, u32[]{:S(2)}, u32[]{:S(2)}) collective-permute-start(s16[1296,128]{1,0:T(8,128)(2,1)S(1)} %send_part.9), channel_id=1, source_target_pairs={{0,2},{1,3},{2,0},{3,1},{4,6},{5,7},{6,4},{7,5},{8,10},{9,11},{10,... | collective-permute-start | bytes 995336 | tf_op jit(solution)/shard_map/ppermute | solution.py:237
  41.3 7.2 %collective-permute-start.14 = (bf16[264,256]{1,0:T(8,128)(2,1)S(1)}, bf16[264,256]{1,0:T(8,128)(2,1)S(1)}, u32[]{:S(2)}, u32[]{:S(2)}) collective-permute-start(bf16[264,256]{1,0:T(8,128)(2,1)S(1)} %add.9.refs_0_), channel_id=1, source_target_pairs={{24,0},{28,4},{16,8},{20,12},{8,16},{12,20},{0,24},{4,28},{25,1},{... | collective-permute-start | bytes 405512 | tf_op jit(solution)/shard_map/ppermute | solution.py:230
  43.6 7.4 %collective-permute-start.13 = (bf16[264,256]{1,0:T(8,128)(2,1)S(1)}, bf16[264,256]{1,0:T(8,128)(2,1)S(1)}, u32[]{:S(2)}, u32[]{:S(2)}) collective-permute-start(bf16[264,256]{1,0:T(8,128)(2,1)S(1)} %add.9.refs_0_), channel_id=1, source_target_pairs={{16,0},{20,4},{24,8},{28,12},{0,16},{4,20},{8,24},{12,28},{17,1},{... | collective-permute-start | bytes 405512 | tf_op jit(solution)/shard_map/ppermute | solution.py:230
  43.6 7.4 %collective-permute-start.12 = (bf16[264,256]{1,0:T(8,128)(2,1)S(1)}, bf16[264,256]{1,0:T(8,128)(2,1)S(1)}, u32[]{:S(2)}, u32[]{:S(2)}) collective-permute-start(bf16[264,256]{1,0:T(8,128)(2,1)S(1)} %add.9.refs_0_), channel_id=1, source_target_pairs={{8,0},{12,4},{0,8},{4,12},{24,16},{28,20},{16,24},{20,28},{9,1},{1... | collective-permute-start | bytes 405512 | tf_op jit(solution)/shard_map/ppermute | solution.py:230
  46.3 9.5 %collective-permute-start.18 = (s16[528,128]{1,0:T(8,128)(2,1)S(1)}, s16[528,128]{1,0:T(8,128)(2,1)S(1)}, u32[]{:S(2)}, u32[]{:S(2)}) collective-permute-start(s16[528,128]{1,0:T(8,128)(2,1)S(1)} %send_part.10), channel_id=1, source_target_pairs={{0,2},{1,3},{2,0},{3,1},{4,6},{5,7},{6,4},{7,5},{8,10},{9,11},{10,... | collective-permute-start | bytes 405512 | tf_op jit(solution)/shard_map/ppermute | solution.py:237
  48.4 13.8 %collective-permute-start.19 = (s16[1296,128]{1,0:T(8,128)(2,1)S(1)}, s16[1296,128]{1,0:T(8,128)(2,1)S(1)}, u32[]{:S(2)}, u32[]{:S(2)}) collective-permute-start(s16[1296,128]{1,0:T(8,128)(2,1)S(1)} %send_part.11), channel_id=1, source_target_pairs={{0,2},{1,3},{2,0},{3,1},{4,6},{5,7},{6,4},{7,5},{8,10},{9,11},{10,... | collective-permute-start | bytes 995336 | tf_op jit(solution)/shard_map/ppermute | solution.py:237
  56.9 9.4 %collective-permute-start.21 = (s16[1040,128]{1,0:T(8,128)(2,1)S(1)}, s16[1040,128]{1,0:T(8,128)(2,1)S(1)}, u32[]{:S(2)}, u32[]{:S(2)}) collective-permute-start(s16[1040,128]{1,0:T(8,128)(2,1)S(1)} %send_part.12), channel_id=1, source_target_pairs={{0,2},{1,3},{2,0},{3,1},{4,6},{5,7},{6,4},{7,5},{8,10},{9,11},{10,... | collective-permute-start | bytes 798728 | tf_op jit(solution)/shard_map/ppermute | solution.py:237
  62.7 5.3 %collective-permute-start.20 = (s16[272,128]{1,0:T(8,128)(2,1)S(1)}, s16[272,128]{1,0:T(8,128)(2,1)S(1)}, u32[]{:S(2)}, u32[]{:S(2)}) collective-permute-start(s16[272,128]{1,0:T(8,128)(2,1)S(1)} %send_part.13), channel_id=1, source_target_pairs={{0,2},{1,3},{2,0},{3,1},{4,6},{5,7},{6,4},{7,5},{8,10},{9,11},{10,... | collective-permute-start | bytes 208904 | tf_op jit(solution)/shard_map/ppermute | solution.py:237

commit v15 on v13

--- a/solution.py
+++ b/solution.py
@@ -10,8 +10,8 @@
 STEPS = 4
 CORES = 2
 HALVES = 2
-NEAR_CUTS = (0.0, 0.25, 0.667, 1.0)
-FAR_CUTS = (0.0, 0.167, 0.583, 0.917, 1.0)
+NEAR_CUTS = (0.0, 0.25, 0.583, 1.0)
+FAR_CUTS = (0.0, 0.25, 0.583, 0.917, 1.0)
 CODE_TOP = 32767.0
 FRACTION = 8192.0
 META_ROWS = 8
@@ -324,7 +324,7 @@
     arrived, sent = {}, []
     order = []
     for number, (half, first, span) in enumerate(rounds):
-        ahead = 1
+        ahead = 2 if number in (4, 5) else 1
         earlier = sent[-1:] + [part for key in order[:-ahead] for part in arrived[key]]
         if number == len(rounds) - 2:
             earlier.append(own_weights)

time: 70.3 us -> 69.6 us (0.990)
  Pallas kernels: 19.5 us -> 17.8 us
  waiting for transfers between devices: 23.5 us -> 24.4 us
    pallas_call x6 -> x4, Pallas kernels: 7.51 us -> 5.85 us  [shards(): pl.pallas_call(partial(join_kernel, first, span, block_rows, skips), in_s...]
    ppermute x9, waiting for transfers between devices: 7.14 us -> 8.79 us  [along(): return lax.ppermute(value, 'row', pairs)]
    ppermute x11, starting transfers between devices: 13.6 us -> 12.8 us  [across(): return lax.ppermute(value, ('row', 'col'), pairs)]
    ppermute x9, starting transfers between devices: 11.5 us -> 12.3 us  [along(): return lax.ppermute(value, 'row', pairs)]
  transfers between devices with their start and end apart: 22 -> 22, of which waited for: 12 -> 13; matrix products, arithmetic and copies ran while one was open for 1% -> 1% of each run, Pallas kernels for 25% -> 22%
where the time goes in v15:
time: 69.6 us; the launch traced here: 69.4 us
  starting transfers between devices  25.6 us (37%)
  waiting for transfers between devices  24.4 us (35%)
  Pallas kernels  17.8 us (26%)
  between operations  0.82 us (1%)
  other arithmetic  0.76 us (1%)
    ppermute x11, waiting for transfers between devices, across(): return lax.ppermute(value, ('row', 'col'), pairs)  15.3 us
    ppermute x11, starting transfers between devices, across(): return lax.ppermute(value, ('row', 'col'), pairs)  12.8 us
    ppermute x9, starting transfers between devices, along(): return lax.ppermute(value, 'row', pairs)  12.3 us
    ppermute x9, waiting for transfers between devices, along(): return lax.ppermute(value, 'row', pairs)  8.79 us
    pallas_call x7, Pallas kernels, shards(): pl.pallas_call(partial(send_kernel, first, span, block_rows), in_specs=[V...  6.43 us
    pallas_call x4, Pallas kernels, shards(): pl.pallas_call(partial(join_kernel, first, span, block_rows, skips), in_s...  5.85 us
    pallas_call x1, Pallas kernels, screen(): pl.pallas_call(partial(screen_kernel, tile_width, block_rows), in_specs=[...  3.07 us
  transfers between devices with their start and end apart: 22, of which 13 were waited for; matrix products, arithmetic and copies ran while one was open for 1% of the time, Pallas kernels for 22%

profile of v15, /device:TPU:0, one launch (start us, length us, event | category | flops | bytes accessed | tf_op | source)
XLA Modules:
  0.0 69.4 jit_solution(9485720793115312590)
XLA Ops:
  0.0 0.5 collective-permute-start.8
  1.2 1.0 %pack.1 = (bf16[136,256]{1,0:T(8,128)(2,1)S(1)}, bf16[136,256]{1,0:T(8,128)(2,1)S(1)}, bf16[136,256]{1,0:T(8,128)(2,1)S(1)}, bf16[136,256]{1,0:T(8,128)(2,1)S(1)}) custom-call(s32[1,1,2]{2,1,0:T(1,128)} %list_ref.1, s32[1,1]{1,0:T(1,128)S(6)} %copy.13.count_ref, bf16[1,1,2,256,256]{4,3,2,1,0:T(8,128)(2,1)} %panel_ref.1), custom_call_target="tpu_custom_call" | custom-call | tf_op jit(solution)/shard_map/pack/pallas_call | solution.py:248
  2.2 3.0 %collective-permute-start.1 = (bf16[136,256]{1,0:T(8,128)(2,1)S(1)}, bf16[136,256]{1,0:T(8,128)(2,1)S(1)}, u32[]{:S(2)}, u32[]{:S(2)}) collective-permute-start(bf16[136,256]{1,0:T(8,128)(2,1)S(1)} %get-tuple-element.23), channel_id=1, source_target_pairs={{8,0},{12,4},{0,8},{4,12},{24,16},{28,20},{16,24},{20,28},{9,1},{1... | collective-permute-start | bytes 208904 | tf_op jit(solution)/shard_map/ppermute | solution.py:230
  5.3 2.6 %collective-permute-start.2 = (bf16[136,256]{1,0:T(8,128)(2,1)S(1)}, bf16[136,256]{1,0:T(8,128)(2,1)S(1)}, u32[]{:S(2)}, u32[]{:S(2)}) collective-permute-start(bf16[136,256]{1,0:T(8,128)(2,1)S(1)} %get-tuple-element.24), channel_id=1, source_target_pairs={{16,0},{20,4},{24,8},{28,12},{0,16},{4,20},{8,24},{12,28},{17,1},{... | collective-permute-start | bytes 208904 | tf_op jit(solution)/shard_map/ppermute | solution.py:230
  7.8 0.4 collective-permute-done
  8.2 0.7 %pad_add_fusion.plan_ref.mask_ref = s32[7,12]{1,0:T(8,128)S(1)} fusion(s32[1,4]{1,0:T(1,128)} %bitcast.4, s32[3,12]{1,0:T(4,128)S(1)} %collective-permute-done, s32[3,12]{1,0:T(4,128)} %bitcast.3), kind=kLoop, calls=%fused_computation | loop fusion | flops 168 | bytes 640 | tf_op jit(solution)/shard_map/concatenate | solution.py:243
  8.9 4.1 %collective-permute-done.2.refs_2_ = bf16[136,256]{1,0:T(8,128)(2,1)S(1)} collective-permute-done((bf16[136,256]{1,0:T(8,128)(2,1)S(1)}, bf16[136,256]{1,0:T(8,128)(2,1)S(1)}, u32[]{:S(2)}, u32[]{:S(2)}) %collective-permute-start.2) | collective-permute-done | bytes 69664 | tf_op jit(solution)/shard_map/ppermute | solution.py:230
  13.0 1.1 %collective-permute-done.3.refs_3_ = bf16[136,256]{1,0:T(8,128)(2,1)S(1)} collective-permute-done((bf16[136,256]{1,0:T(8,128)(2,1)S(1)}, bf16[136,256]{1,0:T(8,128)(2,1)S(1)}, u32[]{:S(2)}, u32[]{:S(2)}) %collective-permute-start.3) | collective-permute-done | bytes 69664 | tf_op jit(solution)/shard_map/ppermute | solution.py:230
  14.1 0.8 %choose.1 = (bf16[264,256]{1,0:T(8,128)(2,1)S(1)}, bf16[264,128]{1,0:T(8,128)(2,1)S(1)}, bf16[264,128]{1,0:T(8,128)(2,1)S(1)}) custom-call(s32[7,12]{1,0:T(8,128)S(1)} %pad_add_fusion.plan_ref.mask_ref, bf16[136,256]{1,0:T(8,128)(2,1)S(1)} %get-tuple-element.22.refs_0_, bf16[136,256]{1,0:T(8,128)(2,1)S(1)} %collective-permute-done.1.refs_1_, ...), custom_call_target="tpu_custom_call" | custom-call | tf_op jit(solution)/shard_map/choose/pallas_call | solution.py:263
  14.8 1.6 %collective-permute-start.4 = (bf16[264,128]{1,0:T(8,128)(2,1)S(1)}, bf16[264,128]{1,0:T(8,128)(2,1)S(1)}, u32[]{:S(2)}, u32[]{:S(2)}) collective-permute-start(bf16[264,128]{1,0:T(8,128)(2,1)S(1)} %get-tuple-element.26), channel_id=1, source_target_pairs={{0,2},{1,3},{2,0},{3,1},{4,6},{5,7},{6,4},{7,5},{8,10},{9,11},{10,... | collective-permute-start | bytes 202760 | tf_op jit(solution)/shard_map/ppermute | solution.py:237
  16.4 1.5 %collective-permute-start.5 = (bf16[264,128]{1,0:T(8,128)(2,1)S(1)}, bf16[264,128]{1,0:T(8,128)(2,1)S(1)}, u32[]{:S(2)}, u32[]{:S(2)}) collective-permute-start(bf16[264,128]{1,0:T(8,128)(2,1)S(1)} %get-tuple-element.27), channel_id=1, source_target_pairs={{0,6},{1,7},{2,4},{3,5},{4,2},{5,3},{6,0},{7,1},{8,14},{9,15},{10,... | collective-permute-start | bytes 202760 | tf_op jit(solution)/shard_map/ppermute | solution.py:237
  17.9 0.5 collective-permute-start.7
  18.4 0.9 %collective-permute-done.4 = bf16[264,128]{1,0:T(8,128)(2,1)S(1)} collective-permute-done((bf16[264,128]{1,0:T(8,128)(2,1)S(1)}, bf16[264,128]{1,0:T(8,128)(2,1)S(1)}, u32[]{:S(2)}, u32[]{:S(2)}) %collective-permute-start.4) | collective-permute-done | bytes 67616 | tf_op jit(solution)/shard_map/ppermute | solution.py:237
  19.3 2.3 %collective-permute-done.5 = bf16[264,128]{1,0:T(8,128)(2,1)S(1)} collective-permute-done((bf16[264,128]{1,0:T(8,128)(2,1)S(1)}, bf16[264,128]{1,0:T(8,128)(2,1)S(1)}, u32[]{:S(2)}, u32[]{:S(2)}) %collective-permute-start.5) | collective-permute-done | bytes 67616 | tf_op jit(solution)/shard_map/ppermute | solution.py:237
  21.6 1.1 %collective-permute-start.6 = (bf16[264,128]{1,0:T(8,128)(2,1)S(1)}, bf16[264,128]{1,0:T(8,128)(2,1)S(1)}, u32[]{:S(2)}, u32[]{:S(2)}) collective-permute-start(bf16[264,128]{1,0:T(8,128)(2,1)S(1)} %add.8.refs_0_), channel_id=1, source_target_pairs={{8,0},{12,4},{0,8},{4,12},{24,16},{28,20},{16,24},{20,28},{9,1},{1... | collective-permute-start | bytes 202760 | tf_op jit(solution)/shard_map/ppermute | solution.py:230
  22.7 2.4 %collective-permute-start.10 = (bf16[264,128]{1,0:T(8,128)(2,1)S(1)}, bf16[264,128]{1,0:T(8,128)(2,1)S(1)}, u32[]{:S(2)}, u32[]{:S(2)}) collective-permute-start(bf16[264,128]{1,0:T(8,128)(2,1)S(1)} %add.8.refs_0_), channel_id=1, source_target_pairs={{24,0},{28,4},{16,8},{20,12},{8,16},{12,20},{0,24},{4,28},{25,1},{... | collective-permute-start | bytes 202760 | tf_op jit(solution)/shard_map/ppermute | solution.py:230
  25.2 1.5 %collective-permute-done.6.refs_1_ = bf16[264,128]{1,0:T(8,128)(2,1)S(1)} collective-permute-done((bf16[264,128]{1,0:T(8,128)(2,1)S(1)}, bf16[264,128]{1,0:T(8,128)(2,1)S(1)}, u32[]{:S(2)}, u32[]{:S(2)}) %collective-permute-start.6) | collective-permute-done | bytes 67616 | tf_op jit(solution)/shard_map/ppermute | solution.py:230
  26.7 3.1 %screen.1.rows_ref = bf16[3072,1536]{1,0:T(8,128)(2,1)S(1)} custom-call(s32[7,12]{1,0:T(8,128)S(1)} %pad_add_fusion.plan_ref.mask_ref, bf16[3072,768]{1,0:T(8,128)(2,1)} %own_ref.1, bf16[3072,768]{1,0:T(8,128)(2,1)S(1)} %collective-permute-done.8.other_ref), custom_call_target="tpu_custom_call" | custom-call | flops 4718592 | bytes 18874368 | tf_op jit(solution)/shard_map/screen/pallas_call | solution.py:284
  29.8 0.5 collective-permute-done.9.refs_2_
  30.3 0.3 fill.2.dense_ref
  30.6 0.8 %send_part.7 = s16[784,128]{1,0:T(8,128)(2,1)S(1)} custom-call(bf16[3072,1536]{1,0:T(8,128)(2,1)S(1)} %screen.1.rows_ref, bf16[1536,128]{1,0:T(8,128)(2,1)S(1)} %fill.2.dense_ref), custom_call_target="tpu_custom_call" | custom-call | flops 301989888 | bytes 2555904 | tf_op jit(solution)/shard_map/send_part/pallas_call | solution.py:335
  31.4 0.9 %collective-permute-start.11 = (s16[784,128]{1,0:T(8,128)(2,1)S(1)}, s16[784,128]{1,0:T(8,128)(2,1)S(1)}, u32[]{:S(2)}, u32[]{:S(2)}) collective-permute-start(s16[784,128]{1,0:T(8,128)(2,1)S(1)} %send_part.7), channel_id=1, source_target_pairs={{0,2},{1,3},{2,0},{3,1},{4,6},{5,7},{6,4},{7,5},{8,10},{9,11},{10,... | collective-permute-start | bytes 602120 | tf_op jit(solution)/shard_map/ppermute | solution.py:237
  32.3 1.0 %send_part.8 = s16[1040,128]{1,0:T(8,128)(2,1)S(1)} custom-call(bf16[3072,1536]{1,0:T(8,128)(2,1)S(1)} %screen.1.rows_ref, bf16[1536,128]{1,0:T(8,128)(2,1)S(1)} %fill.2.dense_ref), custom_call_target="tpu_custom_call" | custom-call | flops 402653184 | bytes 3407872 | tf_op jit(solution)/shard_map/send_part/pallas_call | solution.py:335
  33.3 1.3 %collective-permute-start.16 = (bf16[1536,128]{1,0:T(8,128)(2,1)S(1)}, bf16[1536,128]{1,0:T(8,128)(2,1)S(1)}, u32[]{:S(2)}, u32[]{:S(2)}) collective-permute-start(bf16[1536,128]{1,0:T(8,128)(2,1)S(1)} %fill.2.dense_ref), channel_id=1, source_target_pairs={{0,4},{1,5},{2,6},{3,7},{4,0},{5,1},{6,2},{7,3},{8,12},{9,13},{10,... | collective-permute-start | bytes 1179656 | tf_op jit(solution)/shard_map/ppermute | solution.py:237
  34.7 1.6 %collective-permute-start.17 = (s16[1040,128]{1,0:T(8,128)(2,1)S(1)}, s16[1040,128]{1,0:T(8,128)(2,1)S(1)}, u32[]{:S(2)}, u32[]{:S(2)}) collective-permute-start(s16[1040,128]{1,0:T(8,128)(2,1)S(1)} %send_part.8), channel_id=1, source_target_pairs={{0,2},{1,3},{2,0},{3,1},{4,6},{5,7},{6,4},{7,5},{8,10},{9,11},{10,... | collective-permute-start | bytes 798728 | tf_op jit(solution)/shard_map/ppermute | solution.py:237
  36.3 3.2 %collective-permute-done.11.refs_0_ = s16[784,128]{1,0:T(8,128)(2,1)S(1)} collective-permute-done((s16[784,128]{1,0:T(8,128)(2,1)S(1)}, s16[784,128]{1,0:T(8,128)(2,1)S(1)}, u32[]{:S(2)}, u32[]{:S(2)}) %collective-permute-start.11) | collective-permute-done | bytes 200736 | tf_op jit(solution)/shard_map/ppermute | solution.py:237
  39.4 1.3 %send_part.9 = s16[1296,128]{1,0:T(8,128)(2,1)S(1)} custom-call(bf16[3072,1536]{1,0:T(8,128)(2,1)S(1)} %screen.1.rows_ref, bf16[1536,128]{1,0:T(8,128)(2,1)S(1)} %fill.2.dense_ref), custom_call_target="tpu_custom_call" | custom-call | flops 503316480 | bytes 4259840 | tf_op jit(solution)/shard_map/send_part/pallas_call | solution.py:335
  40.7 0.8 %collective-permute-start.15 = (s16[1296,128]{1,0:T(8,128)(2,1)S(1)}, s16[1296,128]{1,0:T(8,128)(2,1)S(1)}, u32[]{:S(2)}, u32[]{:S(2)}) collective-permute-start(s16[1296,128]{1,0:T(8,128)(2,1)S(1)} %send_part.9), channel_id=1, source_target_pairs={{0,2},{1,3},{2,0},{3,1},{4,6},{5,7},{6,4},{7,5},{8,10},{9,11},{10,... | collective-permute-start | bytes 995336 | tf_op jit(solution)/shard_map/ppermute | solution.py:237
  41.5 2.3 %collective-permute-start.14 = (bf16[264,256]{1,0:T(8,128)(2,1)S(1)}, bf16[264,256]{1,0:T(8,128)(2,1)S(1)}, u32[]{:S(2)}, u32[]{:S(2)}) collective-permute-start(bf16[264,256]{1,0:T(8,128)(2,1)S(1)} %add.9.refs_0_), channel_id=1, source_target_pairs={{24,0},{28,4},{16,8},{20,12},{8,16},{12,20},{0,24},{4,28},{25,1},{... | collective-permute-start | bytes 405512 | tf_op jit(solution)/shard_map/ppermute | solution.py:230
  43.8 1.3 %collective-permute-done.17.refs_0_ = s16[1040,128]{1,0:T(8,128)(2,1)S(1)} collective-permute-done((s16[1040,128]{1,0:T(8,128)(2,1)S(1)}, s16[1040,128]{1,0:T(8,128)(2,1)S(1)}, u32[]{:S(2)}, u32[]{:S(2)}) %collective-permute-start.17) | collective-permute-done | bytes 266272 | tf_op jit(solution)/shard_map/ppermute | solution.py:237
  45.1 0.8 %collective-permute-start.12 = (bf16[264,256]{1,0:T(8,128)(2,1)S(1)}, bf16[264,256]{1,0:T(8,128)(2,1)S(1)}, u32[]{:S(2)}, u32[]{:S(2)}) collective-permute-start(bf16[264,256]{1,0:T(8,128)(2,1)S(1)} %add.9.refs_0_), channel_id=1, source_target_pairs={{8,0},{12,4},{0,8},{4,12},{24,16},{28,20},{16,24},{20,28},{9,1},{1... | collective-permute-start | bytes 405512 | tf_op jit(solution)/shard_map/ppermute | solution.py:230
  45.9 0.8 %send_part.10 = s16[784,128]{1,0:T(8,128)(2,1)S(1)} custom-call(bf16[3072,1536]{1,0:T(8,128)(2,1)S(1)} %screen.1.rows_ref, bf16[1536,128]{1,0:T(8,128)(2,1)S(1)} %collective-permute-done.16.dense_ref), custom_call_target="tpu_custom_call" | custom-call | flops 301989888 | bytes 2555904 | tf_op jit(solution)/shard_map/send_part/pallas_call | solution.py:335
  46.8 1.0 %send_part.11 = s16[1040,128]{1,0:T(8,128)(2,1)S(1)} custom-call(bf16[3072,1536]{1,0:T(8,128)(2,1)S(1)} %screen.1.rows_ref, bf16[1536,128]{1,0:T(8,128)(2,1)S(1)} %collective-permute-done.16.dense_ref), custom_call_target="tpu_custom_call" | custom-call | flops 402653184 | bytes 3407872 | tf_op jit(solution)/shard_map/send_part/pallas_call | solution.py:335
  47.8 1.3 %collective-permute-start.19 = (s16[1040,128]{1,0:T(8,128)(2,1)S(1)}, s16[1040,128]{1,0:T(8,128)(2,1)S(1)}, u32[]{:S(2)}, u32[]{:S(2)}) collective-permute-start(s16[1040,128]{1,0:T(8,128)(2,1)S(1)} %send_part.11), channel_id=1, source_target_pairs={{0,2},{1,3},{2,0},{3,1},{4,6},{5,7},{6,4},{7,5},{8,10},{9,11},{10,... | collective-permute-start | bytes 798728 | tf_op jit(solution)/shard_map/ppermute | solution.py:237
  49.1 0.8 %collective-permute-start.18 = (s16[784,128]{1,0:T(8,128)(2,1)S(1)}, s16[784,128]{1,0:T(8,128)(2,1)S(1)}, u32[]{:S(2)}, u32[]{:S(2)}) collective-permute-start(s16[784,128]{1,0:T(8,128)(2,1)S(1)} %send_part.10), channel_id=1, source_target_pairs={{0,2},{1,3},{2,0},{3,1},{4,6},{5,7},{6,4},{7,5},{8,10},{9,11},{10,... | collective-permute-start | bytes 602120 | tf_op jit(solution)/shard_map/ppermute | solution.py:237
  49.9 1.4 %collective-permute-done.13.refs_2_ = bf16[264,256]{1,0:T(8,128)(2,1)S(1)} collective-permute-done((bf16[264,256]{1,0:T(8,128)(2,1)S(1)}, bf16[264,256]{1,0:T(8,128)(2,1)S(1)}, u32[]{:S(2)}, u32[]{:S(2)}) %collective-permute-start.13) | collective-permute-done | bytes 135200 | tf_op jit(solution)/shard_map/ppermute | solution.py:230
  51.3 0.2 collective-permute-done.12.refs_1_
  51.6 0.3 fill.3.dense_ref
  51.9 0.3 collective-permute-done.15.refs_0_
  52.2 1.0 %send_part.12 = s16[1040,128]{1,0:T(8,128)(2,1)S(1)} custom-call(bf16[3072,1536]{1,0:T(8,128)(2,1)S(1)} %screen.1.rows_ref, bf16[1536,128]{1,0:T(8,128)(2,1)S(1)} %collective-permute-done.16.dense_ref), custom_call_target="tpu_custom_call" | custom-call | flops 402653184 | bytes 3407872 | tf_op jit(solution)/shard_map/send_part/pallas_call | solution.py:335
  53.3 0.8 %collective-permute-start.21 = (s16[1040,128]{1,0:T(8,128)(2,1)S(1)}, s16[1040,128]{1,0:T(8,128)(2,1)S(1)}, u32[]{:S(2)}, u32[]{:S(2)}) collective-permute-start(s16[1040,128]{1,0:T(8,128)(2,1)S(1)} %send_part.12), channel_id=1, source_target_pairs={{0,2},{1,3},{2,0},{3,1},{4,6},{5,7},{6,4},{7,5},{8,10},{9,11},{10,... | collective-permute-start | bytes 798728 | tf_op jit(solution)/shard_map/ppermute | solution.py:237
  54.1 7.3 %collective-permute-done.18.refs_1_ = s16[784,128]{1,0:T(8,128)(2,1)S(1)} collective-permute-done((s16[784,128]{1,0:T(8,128)(2,1)S(1)}, s16[784,128]{1,0:T(8,128)(2,1)S(1)}, u32[]{:S(2)}, u32[]{:S(2)}) %collective-permute-start.18) | collective-permute-done | bytes 200736 | tf_op jit(solution)/shard_map/ppermute | solution.py:237
  61.4 1.5 %join_part.4.refs_2_ = bf16[3072,256]{1,0:T(8,128)(2,1)} custom-call(bf16[3072,1536]{1,0:T(8,128)(2,1)S(1)} %screen.1.rows_ref, bf16[1536,256]{1,0:T(8,128)(2,1)S(1)} %fill.3.dense_ref, s16[784,128]{1,0:T(8,128)(2,1)S(1)} %collective-permute-done.11.refs_0_, s16[784,128]{1,0:T(8,128)(2,1)S(1)} %collective-permute-done.18.refs_1_), custom_call_target="tpu_custom_call" | custom-call | flops 603979776 | bytes 2752512 | tf_op jit(solution)/shard_map/join_part/pallas_call | solution.py:367
  62.8 0.4 send_part.13
  63.3 1.7 %collective-permute-start.20 = (s16[272,128]{1,0:T(8,128)(2,1)S(1)}, s16[272,128]{1,0:T(8,128)(2,1)S(1)}, u32[]{:S(2)}, u32[]{:S(2)}) collective-permute-start(s16[272,128]{1,0:T(8,128)(2,1)S(1)} %send_part.13), channel_id=1, source_target_pairs={{0,2},{1,3},{2,0},{3,1},{4,6},{5,7},{6,4},{7,5},{8,10},{9,11},{10,... | collective-permute-start | bytes 208904 | tf_op jit(solution)/shard_map/ppermute | solution.py:237
  65.0 1.7 %join_part.5.refs_2_ = bf16[3072,256]{1,0:T(8,128)(2,1)} custom-call(bf16[3072,1536]{1,0:T(8,128)(2,1)S(1)} %screen.1.rows_ref, bf16[1536,256]{1,0:T(8,128)(2,1)S(1)} %fill.3.dense_ref, s16[1040,128]{1,0:T(8,128)(2,1)S(1)} %collective-permute-done.17.refs_0_, s16[1040,128]{1,0:T(8,128)(2,1)S(1)} %collective-permute-done.19.refs_1_, ...), custom_call_target="tpu_custom_call", output_to_operand_aliasing={{}: (4, {})} | custom-call | flops 805306368 | bytes 3670016 | tf_op jit(solution)/shard_map/join_part/pallas_call | solution.py:367
  66.7 1.7 %join_part.6.refs_2_ = bf16[3072,256]{1,0:T(8,128)(2,1)} custom-call(bf16[3072,1536]{1,0:T(8,128)(2,1)S(1)} %screen.1.rows_ref, bf16[1536,256]{1,0:T(8,128)(2,1)S(1)} %fill.3.dense_ref, s16[1296,128]{1,0:T(8,128)(2,1)S(1)} %collective-permute-done.15.refs_0_, s16[1040,128]{1,0:T(8,128)(2,1)S(1)} %collective-permute-done.21.refs_1_, ...), custom_call_target="tpu_custom_call", output_to_operand_aliasing={{}: (4, {})} | custom-call | flops 805306368 | bytes 3670016 | tf_op jit(solution)/shard_map/join_part/pallas_call | solution.py:367
  68.4 1.0 %join_part.7 = bf16[3072,256]{1,0:T(8,128)(2,1)} custom-call(bf16[3072,1536]{1,0:T(8,128)(2,1)S(1)} %screen.1.rows_ref, bf16[1536,256]{1,0:T(8,128)(2,1)S(1)} %fill.3.dense_ref, s16[1296,128]{1,0:T(8,128)(2,1)S(1)} %collective-permute-done.15.refs_0_, s16[272,128]{1,0:T(8,128)(2,1)S(1)} %collective-permute-done.20.refs_1_, ...), custom_call_target="tpu_custom_call", output_to_operand_aliasing={{}: (4, {})} | custom-call | flops 201326592 | bytes 917504 | tf_op jit(solution)/shard_map/join_part/pallas_call | solution.py:367
  (15 shorter events, 0.2 us)
Async XLA Ops:
  0.0 26.7 %collective-permute-start.8 = (bf16[3072,768]{1,0:T(8,128)(2,1)}, bf16[3072,768]{1,0:T(8,128)(2,1)S(1)}, u32[]{:S(2)}, u32[]{:S(2)}) collective-permute-start(bf16[3072,768]{1,0:T(8,128)(2,1)} %own_ref.1), channel_id=1, source_target_pairs={{0,1},{1,0},{2,3},{3,2},{4,5},{5,4},{6,7},{7,6},{8,9},{9,8},{10,11... | collective-permute-start | bytes 14155784 | tf_op jit(solution)/shard_map/ppermute | solution.py:240
  0.5 7.7 %collective-permute-start = (s32[3,12]{1,0:T(4,128)}, s32[3,12]{1,0:T(4,128)S(1)}, u32[]{:S(2)}, u32[]{:S(2)}) collective-permute-start(s32[3,12]{1,0:T(4,128)} %bitcast.2), channel_id=1, source_target_pairs={{0,1},{1,0},{2,3},{3,2},{4,5},{5,4},{6,7},{7,6},{8,9},{9,8},{10,11... | collective-permute-start | bytes 440 | tf_op jit(solution)/shard_map/ppermute | solution.py:241
  2.2 6.7 %collective-permute-start.1 = (bf16[136,256]{1,0:T(8,128)(2,1)S(1)}, bf16[136,256]{1,0:T(8,128)(2,1)S(1)}, u32[]{:S(2)}, u32[]{:S(2)}) collective-permute-start(bf16[136,256]{1,0:T(8,128)(2,1)S(1)} %get-tuple-element.23), channel_id=1, source_target_pairs={{8,0},{12,4},{0,8},{4,12},{24,16},{28,20},{16,24},{20,28},{9,1},{1... | collective-permute-start | bytes 208904 | tf_op jit(solution)/shard_map/ppermute | solution.py:230
  5.3 7.7 %collective-permute-start.2 = (bf16[136,256]{1,0:T(8,128)(2,1)S(1)}, bf16[136,256]{1,0:T(8,128)(2,1)S(1)}, u32[]{:S(2)}, u32[]{:S(2)}) collective-permute-start(bf16[136,256]{1,0:T(8,128)(2,1)S(1)} %get-tuple-element.24), channel_id=1, source_target_pairs={{16,0},{20,4},{24,8},{28,12},{0,16},{4,20},{8,24},{12,28},{17,1},{... | collective-permute-start | bytes 208904 | tf_op jit(solution)/shard_map/ppermute | solution.py:230
  7.8 6.2 %collective-permute-start.3 = (bf16[136,256]{1,0:T(8,128)(2,1)S(1)}, bf16[136,256]{1,0:T(8,128)(2,1)S(1)}, u32[]{:S(2)}, u32[]{:S(2)}) collective-permute-start(bf16[136,256]{1,0:T(8,128)(2,1)S(1)} %get-tuple-element.25), channel_id=1, source_target_pairs={{24,0},{28,4},{16,8},{20,12},{8,16},{12,20},{0,24},{4,28},{25,1},{... | collective-permute-start | bytes 208904 | tf_op jit(solution)/shard_map/ppermute | solution.py:230
  14.8 4.5 %collective-permute-start.4 = (bf16[264,128]{1,0:T(8,128)(2,1)S(1)}, bf16[264,128]{1,0:T(8,128)(2,1)S(1)}, u32[]{:S(2)}, u32[]{:S(2)}) collective-permute-start(bf16[264,128]{1,0:T(8,128)(2,1)S(1)} %get-tuple-element.26), channel_id=1, source_target_pairs={{0,2},{1,3},{2,0},{3,1},{4,6},{5,7},{6,4},{7,5},{8,10},{9,11},{10,... | collective-permute-start | bytes 202760 | tf_op jit(solution)/shard_map/ppermute | solution.py:237
  16.4 5.2 %collective-permute-start.5 = (bf16[264,128]{1,0:T(8,128)(2,1)S(1)}, bf16[264,128]{1,0:T(8,128)(2,1)S(1)}, u32[]{:S(2)}, u32[]{:S(2)}) collective-permute-start(bf16[264,128]{1,0:T(8,128)(2,1)S(1)} %get-tuple-element.27), channel_id=1, source_target_pairs={{0,6},{1,7},{2,4},{3,5},{4,2},{5,3},{6,0},{7,1},{8,14},{9,15},{10,... | collective-permute-start | bytes 202760 | tf_op jit(solution)/shard_map/ppermute | solution.py:237
  17.9 7.3 %collective-permute-start.7 = (bf16[264,256]{1,0:T(8,128)(2,1)S(1)}, bf16[264,256]{1,0:T(8,128)(2,1)S(1)}, u32[]{:S(2)}, u32[]{:S(2)}) collective-permute-start(bf16[264,256]{1,0:T(8,128)(2,1)S(1)} %get-tuple-element.28), channel_id=1, source_target_pairs={{0,4},{1,5},{2,6},{3,7},{4,0},{5,1},{6,2},{7,3},{8,12},{9,13},{10,... | collective-permute-start | bytes 405512 | tf_op jit(solution)/shard_map/ppermute | solution.py:237
  21.6 5.1 %collective-permute-start.6 = (bf16[264,128]{1,0:T(8,128)(2,1)S(1)}, bf16[264,128]{1,0:T(8,128)(2,1)S(1)}, u32[]{:S(2)}, u32[]{:S(2)}) collective-permute-start(bf16[264,128]{1,0:T(8,128)(2,1)S(1)} %add.8.refs_0_), channel_id=1, source_target_pairs={{8,0},{12,4},{0,8},{4,12},{24,16},{28,20},{16,24},{20,28},{9,1},{1... | collective-permute-start | bytes 202760 | tf_op jit(solution)/shard_map/ppermute | solution.py:230
  22.7 7.1 %collective-permute-start.10 = (bf16[264,128]{1,0:T(8,128)(2,1)S(1)}, bf16[264,128]{1,0:T(8,128)(2,1)S(1)}, u32[]{:S(2)}, u32[]{:S(2)}) collective-permute-start(bf16[264,128]{1,0:T(8,128)(2,1)S(1)} %add.8.refs_0_), channel_id=1, source_target_pairs={{24,0},{28,4},{16,8},{20,12},{8,16},{12,20},{0,24},{4,28},{25,1},{... | collective-permute-start | bytes 202760 | tf_op jit(solution)/shard_map/ppermute | solution.py:230
  25.1 5.2 %collective-permute-start.9 = (bf16[264,128]{1,0:T(8,128)(2,1)S(1)}, bf16[264,128]{1,0:T(8,128)(2,1)S(1)}, u32[]{:S(2)}, u32[]{:S(2)}) collective-permute-start(bf16[264,128]{1,0:T(8,128)(2,1)S(1)} %add.8.refs_0_), channel_id=1, source_target_pairs={{16,0},{20,4},{24,8},{28,12},{0,16},{4,20},{8,24},{12,28},{17,1},{... | collective-permute-start | bytes 202760 | tf_op jit(solution)/shard_map/ppermute | solution.py:230
  31.4 8.0 %collective-permute-start.11 = (s16[784,128]{1,0:T(8,128)(2,1)S(1)}, s16[784,128]{1,0:T(8,128)(2,1)S(1)}, u32[]{:S(2)}, u32[]{:S(2)}) collective-permute-start(s16[784,128]{1,0:T(8,128)(2,1)S(1)} %send_part.7), channel_id=1, source_target_pairs={{0,2},{1,3},{2,0},{3,1},{4,6},{5,7},{6,4},{7,5},{8,10},{9,11},{10,... | collective-permute-start | bytes 602120 | tf_op jit(solution)/shard_map/ppermute | solution.py:237
  33.3 12.6 %collective-permute-start.16 = (bf16[1536,128]{1,0:T(8,128)(2,1)S(1)}, bf16[1536,128]{1,0:T(8,128)(2,1)S(1)}, u32[]{:S(2)}, u32[]{:S(2)}) collective-permute-start(bf16[1536,128]{1,0:T(8,128)(2,1)S(1)} %fill.2.dense_ref), channel_id=1, source_target_pairs={{0,4},{1,5},{2,6},{3,7},{4,0},{5,1},{6,2},{7,3},{8,12},{9,13},{10,... | collective-permute-start | bytes 1179656 | tf_op jit(solution)/shard_map/ppermute | solution.py:237
  34.7 10.5 %collective-permute-start.17 = (s16[1040,128]{1,0:T(8,128)(2,1)S(1)}, s16[1040,128]{1,0:T(8,128)(2,1)S(1)}, u32[]{:S(2)}, u32[]{:S(2)}) collective-permute-start(s16[1040,128]{1,0:T(8,128)(2,1)S(1)} %send_part.8), channel_id=1, source_target_pairs={{0,2},{1,3},{2,0},{3,1},{4,6},{5,7},{6,4},{7,5},{8,10},{9,11},{10,... | collective-permute-start | bytes 798728 | tf_op jit(solution)/shard_map/ppermute | solution.py:237
  40.7 11.6 %collective-permute-start.15 = (s16[1296,128]{1,0:T(8,128)(2,1)S(1)}, s16[1296,128]{1,0:T(8,128)(2,1)S(1)}, u32[]{:S(2)}, u32[]{:S(2)}) collective-permute-start(s16[1296,128]{1,0:T(8,128)(2,1)S(1)} %send_part.9), channel_id=1, source_target_pairs={{0,2},{1,3},{2,0},{3,1},{4,6},{5,7},{6,4},{7,5},{8,10},{9,11},{10,... | collective-permute-start | bytes 995336 | tf_op jit(solution)/shard_map/ppermute | solution.py:237
  41.5 7.6 %collective-permute-start.14 = (bf16[264,256]{1,0:T(8,128)(2,1)S(1)}, bf16[264,256]{1,0:T(8,128)(2,1)S(1)}, u32[]{:S(2)}, u32[]{:S(2)}) collective-permute-start(bf16[264,256]{1,0:T(8,128)(2,1)S(1)} %add.9.refs_0_), channel_id=1, source_target_pairs={{24,0},{28,4},{16,8},{20,12},{8,16},{12,20},{0,24},{4,28},{25,1},{... | collective-permute-start | bytes 405512 | tf_op jit(solution)/shard_map/ppermute | solution.py:230
  43.8 7.5 %collective-permute-start.13 = (bf16[264,256]{1,0:T(8,128)(2,1)S(1)}, bf16[264,256]{1,0:T(8,128)(2,1)S(1)}, u32[]{:S(2)}, u32[]{:S(2)}) collective-permute-start(bf16[264,256]{1,0:T(8,128)(2,1)S(1)} %add.9.refs_0_), channel_id=1, source_target_pairs={{16,0},{20,4},{24,8},{28,12},{0,16},{4,20},{8,24},{12,28},{17,1},{... | collective-permute-start | bytes 405512 | tf_op jit(solution)/shard_map/ppermute | solution.py:230
  45.1 6.4 %collective-permute-start.12 = (bf16[264,256]{1,0:T(8,128)(2,1)S(1)}, bf16[264,256]{1,0:T(8,128)(2,1)S(1)}, u32[]{:S(2)}, u32[]{:S(2)}) collective-permute-start(bf16[264,256]{1,0:T(8,128)(2,1)S(1)} %add.9.refs_0_), channel_id=1, source_target_pairs={{8,0},{12,4},{0,8},{4,12},{24,16},{28,20},{16,24},{20,28},{9,1},{1... | collective-permute-start | bytes 405512 | tf_op jit(solution)/shard_map/ppermute | solution.py:230
  47.8 15.0 %collective-permute-start.19 = (s16[1040,128]{1,0:T(8,128)(2,1)S(1)}, s16[1040,128]{1,0:T(8,128)(2,1)S(1)}, u32[]{:S(2)}, u32[]{:S(2)}) collective-permute-start(s16[1040,128]{1,0:T(8,128)(2,1)S(1)} %send_part.11), channel_id=1, source_target_pairs={{0,2},{1,3},{2,0},{3,1},{4,6},{5,7},{6,4},{7,5},{8,10},{9,11},{10,... | collective-permute-start | bytes 798728 | tf_op jit(solution)/shard_map/ppermute | solution.py:237
  49.1 12.2 %collective-permute-start.18 = (s16[784,128]{1,0:T(8,128)(2,1)S(1)}, s16[784,128]{1,0:T(8,128)(2,1)S(1)}, u32[]{:S(2)}, u32[]{:S(2)}) collective-permute-start(s16[784,128]{1,0:T(8,128)(2,1)S(1)} %send_part.10), channel_id=1, source_target_pairs={{0,2},{1,3},{2,0},{3,1},{4,6},{5,7},{6,4},{7,5},{8,10},{9,11},{10,... | collective-permute-start | bytes 602120 | tf_op jit(solution)/shard_map/ppermute | solution.py:237
  53.3 13.4 %collective-permute-start.21 = (s16[1040,128]{1,0:T(8,128)(2,1)S(1)}, s16[1040,128]{1,0:T(8,128)(2,1)S(1)}, u32[]{:S(2)}, u32[]{:S(2)}) collective-permute-start(s16[1040,128]{1,0:T(8,128)(2,1)S(1)} %send_part.12), channel_id=1, source_target_pairs={{0,2},{1,3},{2,0},{3,1},{4,6},{5,7},{6,4},{7,5},{8,10},{9,11},{10,... | collective-permute-start | bytes 798728 | tf_op jit(solution)/shard_map/ppermute | solution.py:237
  63.3 5.1 %collective-permute-start.20 = (s16[272,128]{1,0:T(8,128)(2,1)S(1)}, s16[272,128]{1,0:T(8,128)(2,1)S(1)}, u32[]{:S(2)}, u32[]{:S(2)}) collective-permute-start(s16[272,128]{1,0:T(8,128)(2,1)S(1)} %send_part.13), channel_id=1, source_target_pairs={{0,2},{1,3},{2,0},{3,1},{4,6},{5,7},{6,4},{7,5},{8,10},{9,11},{10,... | collective-permute-start | bytes 208904 | tf_op jit(solution)/shard_map/ppermute | solution.py:237

commit v16 on v14

--- a/solution.py
+++ b/solution.py
@@ -14,6 +14,7 @@
 FAR_CUTS = (0.0, 0.167, 0.583, 0.917, 1.0)
 CODE_TOP = 32767.0
 FRACTION = 8192.0
+SMALLEST_UNIT = 2.0**-100
 META_ROWS = 8
 TILE_ROWS = 16
 SCREEN_PARTS = 4
@@ -159,7 +160,7 @@
     for step in range(span):
         total = sums[step * height : (step + 1) * height]
         top = jnp.max(jnp.abs(total), axis=0, keepdims=True)
-        unit = jnp.where(top > 0, top, 1.0) * (1.0 / CODE_TOP)
+        unit = jnp.maximum(jnp.where(top > 0, top, 1.0) * (1.0 / CODE_TOP), SMALLEST_UNIT)
         power = jnp.floor(jnp.log2(unit))
         fraction = jnp.ceil(unit * jnp.exp2(-power) * FRACTION)
         unit = fraction * jnp.exp2(power) * (1.0 / FRACTION)

time: 69.2 us -> 69.2 us (level)
  no operation moved by 1% of the time
where the time goes in v16:
time: 69.2 us; the launch traced here: 69 us
  starting transfers between devices  27.9 us (40%)
  waiting for transfers between devices  21.7 us (31%)
  Pallas kernels  17.8 us (26%)
  between operations  0.83 us (1%)
  other arithmetic  0.76 us (1%)
    ppermute x11, starting transfers between devices, across(): return lax.ppermute(value, ('row', 'col'), pairs)  13.8 us
    ppermute x9, starting transfers between devices, along(): return lax.ppermute(value, 'row', pairs)  13.6 us
    ppermute x11, waiting for transfers between devices, across(): return lax.ppermute(value, ('row', 'col'), pairs)  13 us
    ppermute x9, waiting for transfers between devices, along(): return lax.ppermute(value, 'row', pairs)  8.39 us
    pallas_call x7, Pallas kernels, shards(): pl.pallas_call(partial(send_kernel, first, span, block_rows), in_specs=[V...  6.43 us
    pallas_call x4, Pallas kernels, shards(): pl.pallas_call(partial(join_kernel, first, span, block_rows, skips), in_s...  5.87 us
    pallas_call x1, Pallas kernels, screen(): pl.pallas_call(partial(screen_kernel, tile_width, block_rows), in_specs=[...  3.07 us
  transfers between devices with their start and end apart: 22, of which 11 were waited for; matrix products, arithmetic and copies ran while one was open for 1% of the time, Pallas kernels for 24%

profile of v16, /device:TPU:0, one launch (start us, length us, event | category | flops | bytes accessed | tf_op | source)
XLA Modules:
  0.0 69.0 jit_solution(7536404476869280692)
XLA Ops:
  0.0 0.5 collective-permute-start.8
  0.5 0.1 collective-permute-start
  1.2 1.0 %pack.1 = (bf16[136,256]{1,0:T(8,128)(2,1)S(1)}, bf16[136,256]{1,0:T(8,128)(2,1)S(1)}, bf16[136,256]{1,0:T(8,128)(2,1)S(1)}, bf16[136,256]{1,0:T(8,128)(2,1)S(1)}) custom-call(s32[1,1,2]{2,1,0:T(1,128)} %list_ref.1, s32[1,1]{1,0:T(1,128)S(6)} %copy.13.count_ref, bf16[1,1,2,256,256]{4,3,2,1,0:T(8,128)(2,1)} %panel_ref.1), custom_call_target="tpu_custom_call" | custom-call | tf_op jit(solution)/shard_map/pack/pallas_call | solution.py:249
  2.2 3.0 %collective-permute-start.1 = (bf16[136,256]{1,0:T(8,128)(2,1)S(1)}, bf16[136,256]{1,0:T(8,128)(2,1)S(1)}, u32[]{:S(2)}, u32[]{:S(2)}) collective-permute-start(bf16[136,256]{1,0:T(8,128)(2,1)S(1)} %get-tuple-element.22), channel_id=1, source_target_pairs={{8,0},{12,4},{0,8},{4,12},{24,16},{28,20},{16,24},{20,28},{9,1},{1... | collective-permute-start | bytes 208904 | tf_op jit(solution)/shard_map/ppermute | solution.py:231
  5.3 2.6 %collective-permute-start.2 = (bf16[136,256]{1,0:T(8,128)(2,1)S(1)}, bf16[136,256]{1,0:T(8,128)(2,1)S(1)}, u32[]{:S(2)}, u32[]{:S(2)}) collective-permute-start(bf16[136,256]{1,0:T(8,128)(2,1)S(1)} %get-tuple-element.23), channel_id=1, source_target_pairs={{16,0},{20,4},{24,8},{28,12},{0,16},{4,20},{8,24},{12,28},{17,1},{... | collective-permute-start | bytes 208904 | tf_op jit(solution)/shard_map/ppermute | solution.py:231
  7.8 0.4 collective-permute-done
  8.2 0.7 %pad_add_fusion.plan_ref.mask_ref = s32[7,12]{1,0:T(8,128)S(1)} fusion(s32[1,4]{1,0:T(1,128)} %bitcast.4, s32[3,12]{1,0:T(4,128)S(1)} %collective-permute-done, s32[3,12]{1,0:T(4,128)} %bitcast.3), kind=kLoop, calls=%fused_computation | loop fusion | flops 168 | bytes 640 | tf_op jit(solution)/shard_map/concatenate | solution.py:244
  8.9 4.1 %collective-permute-done.2.refs_2_ = bf16[136,256]{1,0:T(8,128)(2,1)S(1)} collective-permute-done((bf16[136,256]{1,0:T(8,128)(2,1)S(1)}, bf16[136,256]{1,0:T(8,128)(2,1)S(1)}, u32[]{:S(2)}, u32[]{:S(2)}) %collective-permute-start.2) | collective-permute-done | bytes 69664 | tf_op jit(solution)/shard_map/ppermute | solution.py:231
  13.0 1.1 %collective-permute-done.3.refs_3_ = bf16[136,256]{1,0:T(8,128)(2,1)S(1)} collective-permute-done((bf16[136,256]{1,0:T(8,128)(2,1)S(1)}, bf16[136,256]{1,0:T(8,128)(2,1)S(1)}, u32[]{:S(2)}, u32[]{:S(2)}) %collective-permute-start.3) | collective-permute-done | bytes 69664 | tf_op jit(solution)/shard_map/ppermute | solution.py:231
  14.1 0.8 %choose.1 = (bf16[264,256]{1,0:T(8,128)(2,1)S(1)}, bf16[264,128]{1,0:T(8,128)(2,1)S(1)}, bf16[264,128]{1,0:T(8,128)(2,1)S(1)}) custom-call(s32[7,12]{1,0:T(8,128)S(1)} %pad_add_fusion.plan_ref.mask_ref, bf16[136,256]{1,0:T(8,128)(2,1)S(1)} %get-tuple-element.21.refs_0_, bf16[136,256]{1,0:T(8,128)(2,1)S(1)} %collective-permute-done.1.refs_1_, ...), custom_call_target="tpu_custom_call" | custom-call | tf_op jit(solution)/shard_map/choose/pallas_call | solution.py:264
  14.8 1.6 %collective-permute-start.4 = (bf16[264,128]{1,0:T(8,128)(2,1)S(1)}, bf16[264,128]{1,0:T(8,128)(2,1)S(1)}, u32[]{:S(2)}, u32[]{:S(2)}) collective-permute-start(bf16[264,128]{1,0:T(8,128)(2,1)S(1)} %get-tuple-element.25), channel_id=1, source_target_pairs={{0,2},{1,3},{2,0},{3,1},{4,6},{5,7},{6,4},{7,5},{8,10},{9,11},{10,... | collective-permute-start | bytes 202760 | tf_op jit(solution)/shard_map/ppermute | solution.py:238
  16.4 1.5 %collective-permute-start.5 = (bf16[264,128]{1,0:T(8,128)(2,1)S(1)}, bf16[264,128]{1,0:T(8,128)(2,1)S(1)}, u32[]{:S(2)}, u32[]{:S(2)}) collective-permute-start(bf16[264,128]{1,0:T(8,128)(2,1)S(1)} %get-tuple-element.26), channel_id=1, source_target_pairs={{0,6},{1,7},{2,4},{3,5},{4,2},{5,3},{6,0},{7,1},{8,14},{9,15},{10,... | collective-permute-start | bytes 202760 | tf_op jit(solution)/shard_map/ppermute | solution.py:238
  17.9 0.5 collective-permute-start.7
  18.4 0.9 %collective-permute-done.4 = bf16[264,128]{1,0:T(8,128)(2,1)S(1)} collective-permute-done((bf16[264,128]{1,0:T(8,128)(2,1)S(1)}, bf16[264,128]{1,0:T(8,128)(2,1)S(1)}, u32[]{:S(2)}, u32[]{:S(2)}) %collective-permute-start.4) | collective-permute-done | bytes 67616 | tf_op jit(solution)/shard_map/ppermute | solution.py:238
  19.3 2.3 %collective-permute-done.5 = bf16[264,128]{1,0:T(8,128)(2,1)S(1)} collective-permute-done((bf16[264,128]{1,0:T(8,128)(2,1)S(1)}, bf16[264,128]{1,0:T(8,128)(2,1)S(1)}, u32[]{:S(2)}, u32[]{:S(2)}) %collective-permute-start.5) | collective-permute-done | bytes 67616 | tf_op jit(solution)/shard_map/ppermute | solution.py:238
  21.6 1.1 %collective-permute-start.6 = (bf16[264,128]{1,0:T(8,128)(2,1)S(1)}, bf16[264,128]{1,0:T(8,128)(2,1)S(1)}, u32[]{:S(2)}, u32[]{:S(2)}) collective-permute-start(bf16[264,128]{1,0:T(8,128)(2,1)S(1)} %add.8.refs_0_), channel_id=1, source_target_pairs={{8,0},{12,4},{0,8},{4,12},{24,16},{28,20},{16,24},{20,28},{9,1},{1... | collective-permute-start | bytes 202760 | tf_op jit(solution)/shard_map/ppermute | solution.py:231
  22.7 2.4 %collective-permute-start.10 = (bf16[264,128]{1,0:T(8,128)(2,1)S(1)}, bf16[264,128]{1,0:T(8,128)(2,1)S(1)}, u32[]{:S(2)}, u32[]{:S(2)}) collective-permute-start(bf16[264,128]{1,0:T(8,128)(2,1)S(1)} %add.8.refs_0_), channel_id=1, source_target_pairs={{24,0},{28,4},{16,8},{20,12},{8,16},{12,20},{0,24},{4,28},{25,1},{... | collective-permute-start | bytes 202760 | tf_op jit(solution)/shard_map/ppermute | solution.py:231
  25.1 0.1 collective-permute-start.9
  25.2 1.5 %collective-permute-done.6.refs_1_ = bf16[264,128]{1,0:T(8,128)(2,1)S(1)} collective-permute-done((bf16[264,128]{1,0:T(8,128)(2,1)S(1)}, bf16[264,128]{1,0:T(8,128)(2,1)S(1)}, u32[]{:S(2)}, u32[]{:S(2)}) %collective-permute-start.6) | collective-permute-done | bytes 67616 | tf_op jit(solution)/shard_map/ppermute | solution.py:231
  26.7 3.1 %screen.1.rows_ref = bf16[3072,1536]{1,0:T(8,128)(2,1)S(1)} custom-call(s32[7,12]{1,0:T(8,128)S(1)} %pad_add_fusion.plan_ref.mask_ref, bf16[3072,768]{1,0:T(8,128)(2,1)} %own_ref.1, bf16[3072,768]{1,0:T(8,128)(2,1)S(1)} %collective-permute-done.8.other_ref), custom_call_target="tpu_custom_call" | custom-call | flops 4718592 | bytes 18874368 | tf_op jit(solution)/shard_map/screen/pallas_call | solution.py:285
  29.8 0.5 collective-permute-done.9.refs_2_
  30.3 0.3 fill.2.dense_ref
  30.6 1.7 %collective-permute-start.15 = (bf16[1536,128]{1,0:T(8,128)(2,1)S(1)}, bf16[1536,128]{1,0:T(8,128)(2,1)S(1)}, u32[]{:S(2)}, u32[]{:S(2)}) collective-permute-start(bf16[1536,128]{1,0:T(8,128)(2,1)S(1)} %fill.2.dense_ref), channel_id=1, source_target_pairs={{0,4},{1,5},{2,6},{3,7},{4,0},{5,1},{6,2},{7,3},{8,12},{9,13},{10,... | collective-permute-start | bytes 1179656 | tf_op jit(solution)/shard_map/ppermute | solution.py:238
  32.3 0.6 send_part.7
  32.9 0.5 collective-permute-start.11
  33.4 1.2 %send_part.8 = s16[1296,128]{1,0:T(8,128)(2,1)S(1)} custom-call(bf16[3072,1536]{1,0:T(8,128)(2,1)S(1)} %screen.1.rows_ref, bf16[1536,128]{1,0:T(8,128)(2,1)S(1)} %fill.2.dense_ref), custom_call_target="tpu_custom_call" | custom-call | flops 503316480 | bytes 4259840 | tf_op jit(solution)/shard_map/send_part/pallas_call | solution.py:339
  34.7 1.6 %collective-permute-start.17 = (s16[1296,128]{1,0:T(8,128)(2,1)S(1)}, s16[1296,128]{1,0:T(8,128)(2,1)S(1)}, u32[]{:S(2)}, u32[]{:S(2)}) collective-permute-start(s16[1296,128]{1,0:T(8,128)(2,1)S(1)} %send_part.8), channel_id=1, source_target_pairs={{0,2},{1,3},{2,0},{3,1},{4,6},{5,7},{6,4},{7,5},{8,10},{9,11},{10,... | collective-permute-start | bytes 995336 | tf_op jit(solution)/shard_map/ppermute | solution.py:238
  36.3 2.4 %collective-permute-done.11.refs_0_ = s16[528,128]{1,0:T(8,128)(2,1)S(1)} collective-permute-done((s16[528,128]{1,0:T(8,128)(2,1)S(1)}, s16[528,128]{1,0:T(8,128)(2,1)S(1)}, u32[]{:S(2)}, u32[]{:S(2)}) %collective-permute-start.11) | collective-permute-done | bytes 135200 | tf_op jit(solution)/shard_map/ppermute | solution.py:238
  38.7 1.2 %send_part.9 = s16[1296,128]{1,0:T(8,128)(2,1)S(1)} custom-call(bf16[3072,1536]{1,0:T(8,128)(2,1)S(1)} %screen.1.rows_ref, bf16[1536,128]{1,0:T(8,128)(2,1)S(1)} %fill.2.dense_ref), custom_call_target="tpu_custom_call" | custom-call | flops 503316480 | bytes 4259840 | tf_op jit(solution)/shard_map/send_part/pallas_call | solution.py:339
  40.0 1.3 %collective-permute-start.16 = (s16[1296,128]{1,0:T(8,128)(2,1)S(1)}, s16[1296,128]{1,0:T(8,128)(2,1)S(1)}, u32[]{:S(2)}, u32[]{:S(2)}) collective-permute-start(s16[1296,128]{1,0:T(8,128)(2,1)S(1)} %send_part.9), channel_id=1, source_target_pairs={{0,2},{1,3},{2,0},{3,1},{4,6},{5,7},{6,4},{7,5},{8,10},{9,11},{10,... | collective-permute-start | bytes 995336 | tf_op jit(solution)/shard_map/ppermute | solution.py:238
  41.3 2.3 %collective-permute-start.14 = (bf16[264,256]{1,0:T(8,128)(2,1)S(1)}, bf16[264,256]{1,0:T(8,128)(2,1)S(1)}, u32[]{:S(2)}, u32[]{:S(2)}) collective-permute-start(bf16[264,256]{1,0:T(8,128)(2,1)S(1)} %add.9.refs_0_), channel_id=1, source_target_pairs={{24,0},{28,4},{16,8},{20,12},{8,16},{12,20},{0,24},{4,28},{25,1},{... | collective-permute-start | bytes 405512 | tf_op jit(solution)/shard_map/ppermute | solution.py:231
  43.6 2.0 %collective-permute-start.12 = (bf16[264,256]{1,0:T(8,128)(2,1)S(1)}, bf16[264,256]{1,0:T(8,128)(2,1)S(1)}, u32[]{:S(2)}, u32[]{:S(2)}) collective-permute-start(bf16[264,256]{1,0:T(8,128)(2,1)S(1)} %add.9.refs_0_), channel_id=1, source_target_pairs={{8,0},{12,4},{0,8},{4,12},{24,16},{28,20},{16,24},{20,28},{9,1},{1... | collective-permute-start | bytes 405512 | tf_op jit(solution)/shard_map/ppermute | solution.py:231
  45.7 0.6 send_part.10
  46.3 0.9 %collective-permute-start.18 = (s16[528,128]{1,0:T(8,128)(2,1)S(1)}, s16[528,128]{1,0:T(8,128)(2,1)S(1)}, u32[]{:S(2)}, u32[]{:S(2)}) collective-permute-start(s16[528,128]{1,0:T(8,128)(2,1)S(1)} %send_part.10), channel_id=1, source_target_pairs={{0,2},{1,3},{2,0},{3,1},{4,6},{5,7},{6,4},{7,5},{8,10},{9,11},{10,... | collective-permute-start | bytes 405512 | tf_op jit(solution)/shard_map/ppermute | solution.py:238
  47.2 1.2 %send_part.11 = s16[1296,128]{1,0:T(8,128)(2,1)S(1)} custom-call(bf16[3072,1536]{1,0:T(8,128)(2,1)S(1)} %screen.1.rows_ref, bf16[1536,128]{1,0:T(8,128)(2,1)S(1)} %collective-permute-done.15.dense_ref), custom_call_target="tpu_custom_call" | custom-call | flops 503316480 | bytes 4259840 | tf_op jit(solution)/shard_map/send_part/pallas_call | solution.py:339
  48.4 1.3 %collective-permute-start.19 = (s16[1296,128]{1,0:T(8,128)(2,1)S(1)}, s16[1296,128]{1,0:T(8,128)(2,1)S(1)}, u32[]{:S(2)}, u32[]{:S(2)}) collective-permute-start(s16[1296,128]{1,0:T(8,128)(2,1)S(1)} %send_part.11), channel_id=1, source_target_pairs={{0,2},{1,3},{2,0},{3,1},{4,6},{5,7},{6,4},{7,5},{8,10},{9,11},{10,... | collective-permute-start | bytes 995336 | tf_op jit(solution)/shard_map/ppermute | solution.py:238
  49.7 1.3 %collective-permute-done.13.refs_2_ = bf16[264,256]{1,0:T(8,128)(2,1)S(1)} collective-permute-done((bf16[264,256]{1,0:T(8,128)(2,1)S(1)}, bf16[264,256]{1,0:T(8,128)(2,1)S(1)}, u32[]{:S(2)}, u32[]{:S(2)}) %collective-permute-start.13) | collective-permute-done | bytes 135200 | tf_op jit(solution)/shard_map/ppermute | solution.py:231
  51.0 0.3 fill.3.dense_ref
  51.3 4.5 %collective-permute-done.18.refs_1_ = s16[528,128]{1,0:T(8,128)(2,1)S(1)} collective-permute-done((s16[528,128]{1,0:T(8,128)(2,1)S(1)}, s16[528,128]{1,0:T(8,128)(2,1)S(1)}, u32[]{:S(2)}, u32[]{:S(2)}) %collective-permute-start.18) | collective-permute-done | bytes 135200 | tf_op jit(solution)/shard_map/ppermute | solution.py:238
  55.8 1.0 %send_part.12 = s16[1040,128]{1,0:T(8,128)(2,1)S(1)} custom-call(bf16[3072,1536]{1,0:T(8,128)(2,1)S(1)} %screen.1.rows_ref, bf16[1536,128]{1,0:T(8,128)(2,1)S(1)} %collective-permute-done.15.dense_ref), custom_call_target="tpu_custom_call" | custom-call | flops 402653184 | bytes 3407872 | tf_op jit(solution)/shard_map/send_part/pallas_call | solution.py:339
  56.9 1.3 %collective-permute-start.21 = (s16[1040,128]{1,0:T(8,128)(2,1)S(1)}, s16[1040,128]{1,0:T(8,128)(2,1)S(1)}, u32[]{:S(2)}, u32[]{:S(2)}) collective-permute-start(s16[1040,128]{1,0:T(8,128)(2,1)S(1)} %send_part.12), channel_id=1, source_target_pairs={{0,2},{1,3},{2,0},{3,1},{4,6},{5,7},{6,4},{7,5},{8,10},{9,11},{10,... | collective-permute-start | bytes 798728 | tf_op jit(solution)/shard_map/ppermute | solution.py:238
  58.2 1.2 %join_part.4.refs_2_ = bf16[3072,256]{1,0:T(8,128)(2,1)} custom-call(bf16[3072,1536]{1,0:T(8,128)(2,1)S(1)} %screen.1.rows_ref, bf16[1536,256]{1,0:T(8,128)(2,1)S(1)} %fill.3.dense_ref, s16[528,128]{1,0:T(8,128)(2,1)S(1)} %collective-permute-done.11.refs_0_, s16[528,128]{1,0:T(8,128)(2,1)S(1)} %collective-permute-done.18.refs_1_), custom_call_target="tpu_custom_call" | custom-call | flops 402653184 | bytes 1835008 | tf_op jit(solution)/shard_map/join_part/pallas_call | solution.py:368
  59.4 2.8 %collective-permute-done.19.refs_1_ = s16[1296,128]{1,0:T(8,128)(2,1)S(1)} collective-permute-done((s16[1296,128]{1,0:T(8,128)(2,1)S(1)}, s16[1296,128]{1,0:T(8,128)(2,1)S(1)}, u32[]{:S(2)}, u32[]{:S(2)}) %collective-permute-start.19) | collective-permute-done | bytes 331808 | tf_op jit(solution)/shard_map/ppermute | solution.py:238
  62.3 0.4 send_part.13
  62.7 1.7 %collective-permute-start.20 = (s16[272,128]{1,0:T(8,128)(2,1)S(1)}, s16[272,128]{1,0:T(8,128)(2,1)S(1)}, u32[]{:S(2)}, u32[]{:S(2)}) collective-permute-start(s16[272,128]{1,0:T(8,128)(2,1)S(1)} %send_part.13), channel_id=1, source_target_pairs={{0,2},{1,3},{2,0},{3,1},{4,6},{5,7},{6,4},{7,5},{8,10},{9,11},{10,... | collective-permute-start | bytes 208904 | tf_op jit(solution)/shard_map/ppermute | solution.py:238
  64.3 1.9 %join_part.5.refs_2_ = bf16[3072,256]{1,0:T(8,128)(2,1)} custom-call(bf16[3072,1536]{1,0:T(8,128)(2,1)S(1)} %screen.1.rows_ref, bf16[1536,256]{1,0:T(8,128)(2,1)S(1)} %fill.3.dense_ref, s16[1296,128]{1,0:T(8,128)(2,1)S(1)} %collective-permute-done.17.refs_0_, s16[1296,128]{1,0:T(8,128)(2,1)S(1)} %collective-permute-done.19.refs_1_, ...), custom_call_target="tpu_custom_call", output_to_operand_aliasing={{}: (4, {})} | custom-call | flops 1006632960 | bytes 4587520 | tf_op jit(solution)/shard_map/join_part/pallas_call | solution.py:368
  66.3 1.7 %join_part.6.refs_2_ = bf16[3072,256]{1,0:T(8,128)(2,1)} custom-call(bf16[3072,1536]{1,0:T(8,128)(2,1)S(1)} %screen.1.rows_ref, bf16[1536,256]{1,0:T(8,128)(2,1)S(1)} %fill.3.dense_ref, s16[1296,128]{1,0:T(8,128)(2,1)S(1)} %collective-permute-done.16.refs_0_, s16[1040,128]{1,0:T(8,128)(2,1)S(1)} %collective-permute-done.21.refs_1_, ...), custom_call_target="tpu_custom_call", output_to_operand_aliasing={{}: (4, {})} | custom-call | flops 805306368 | bytes 3670016 | tf_op jit(solution)/shard_map/join_part/pallas_call | solution.py:368
  68.0 1.0 %join_part.7 = bf16[3072,256]{1,0:T(8,128)(2,1)} custom-call(bf16[3072,1536]{1,0:T(8,128)(2,1)S(1)} %screen.1.rows_ref, bf16[1536,256]{1,0:T(8,128)(2,1)S(1)} %fill.3.dense_ref, s16[1296,128]{1,0:T(8,128)(2,1)S(1)} %collective-permute-done.16.refs_0_, s16[272,128]{1,0:T(8,128)(2,1)S(1)} %collective-permute-done.20.refs_1_, ...), custom_call_target="tpu_custom_call", output_to_operand_aliasing={{}: (4, {})} | custom-call | flops 201326592 | bytes 917504 | tf_op jit(solution)/shard_map/join_part/pallas_call | solution.py:368
  (15 shorter events, 0.1 us)
Async XLA Ops:
  0.0 26.7 %collective-permute-start.8 = (bf16[3072,768]{1,0:T(8,128)(2,1)}, bf16[3072,768]{1,0:T(8,128)(2,1)S(1)}, u32[]{:S(2)}, u32[]{:S(2)}) collective-permute-start(bf16[3072,768]{1,0:T(8,128)(2,1)} %own_ref.1), channel_id=1, source_target_pairs={{0,1},{1,0},{2,3},{3,2},{4,5},{5,4},{6,7},{7,6},{8,9},{9,8},{10,11... | collective-permute-start | bytes 14155784 | tf_op jit(solution)/shard_map/ppermute | solution.py:241
  0.5 7.7 %collective-permute-start = (s32[3,12]{1,0:T(4,128)}, s32[3,12]{1,0:T(4,128)S(1)}, u32[]{:S(2)}, u32[]{:S(2)}) collective-permute-start(s32[3,12]{1,0:T(4,128)} %bitcast.2), channel_id=1, source_target_pairs={{0,1},{1,0},{2,3},{3,2},{4,5},{5,4},{6,7},{7,6},{8,9},{9,8},{10,11... | collective-permute-start | bytes 440 | tf_op jit(solution)/shard_map/ppermute | solution.py:242
  2.2 6.7 %collective-permute-start.1 = (bf16[136,256]{1,0:T(8,128)(2,1)S(1)}, bf16[136,256]{1,0:T(8,128)(2,1)S(1)}, u32[]{:S(2)}, u32[]{:S(2)}) collective-permute-start(bf16[136,256]{1,0:T(8,128)(2,1)S(1)} %get-tuple-element.22), channel_id=1, source_target_pairs={{8,0},{12,4},{0,8},{4,12},{24,16},{28,20},{16,24},{20,28},{9,1},{1... | collective-permute-start | bytes 208904 | tf_op jit(solution)/shard_map/ppermute | solution.py:231
  5.3 7.7 %collective-permute-start.2 = (bf16[136,256]{1,0:T(8,128)(2,1)S(1)}, bf16[136,256]{1,0:T(8,128)(2,1)S(1)}, u32[]{:S(2)}, u32[]{:S(2)}) collective-permute-start(bf16[136,256]{1,0:T(8,128)(2,1)S(1)} %get-tuple-element.23), channel_id=1, source_target_pairs={{16,0},{20,4},{24,8},{28,12},{0,16},{4,20},{8,24},{12,28},{17,1},{... | collective-permute-start | bytes 208904 | tf_op jit(solution)/shard_map/ppermute | solution.py:231
  7.8 6.2 %collective-permute-start.3 = (bf16[136,256]{1,0:T(8,128)(2,1)S(1)}, bf16[136,256]{1,0:T(8,128)(2,1)S(1)}, u32[]{:S(2)}, u32[]{:S(2)}) collective-permute-start(bf16[136,256]{1,0:T(8,128)(2,1)S(1)} %get-tuple-element.24), channel_id=1, source_target_pairs={{24,0},{28,4},{16,8},{20,12},{8,16},{12,20},{0,24},{4,28},{25,1},{... | collective-permute-start | bytes 208904 | tf_op jit(solution)/shard_map/ppermute | solution.py:231
  14.8 4.5 %collective-permute-start.4 = (bf16[264,128]{1,0:T(8,128)(2,1)S(1)}, bf16[264,128]{1,0:T(8,128)(2,1)S(1)}, u32[]{:S(2)}, u32[]{:S(2)}) collective-permute-start(bf16[264,128]{1,0:T(8,128)(2,1)S(1)} %get-tuple-element.25), channel_id=1, source_target_pairs={{0,2},{1,3},{2,0},{3,1},{4,6},{5,7},{6,4},{7,5},{8,10},{9,11},{10,... | collective-permute-start | bytes 202760 | tf_op jit(solution)/shard_map/ppermute | solution.py:238
  16.4 5.2 %collective-permute-start.5 = (bf16[264,128]{1,0:T(8,128)(2,1)S(1)}, bf16[264,128]{1,0:T(8,128)(2,1)S(1)}, u32[]{:S(2)}, u32[]{:S(2)}) collective-permute-start(bf16[264,128]{1,0:T(8,128)(2,1)S(1)} %get-tuple-element.26), channel_id=1, source_target_pairs={{0,6},{1,7},{2,4},{3,5},{4,2},{5,3},{6,0},{7,1},{8,14},{9,15},{10,... | collective-permute-start | bytes 202760 | tf_op jit(solution)/shard_map/ppermute | solution.py:238
  17.9 7.3 %collective-permute-start.7 = (bf16[264,256]{1,0:T(8,128)(2,1)S(1)}, bf16[264,256]{1,0:T(8,128)(2,1)S(1)}, u32[]{:S(2)}, u32[]{:S(2)}) collective-permute-start(bf16[264,256]{1,0:T(8,128)(2,1)S(1)} %get-tuple-element.27), channel_id=1, source_target_pairs={{0,4},{1,5},{2,6},{3,7},{4,0},{5,1},{6,2},{7,3},{8,12},{9,13},{10,... | collective-permute-start | bytes 405512 | tf_op jit(solution)/shard_map/ppermute | solution.py:238
  21.6 5.1 %collective-permute-start.6 = (bf16[264,128]{1,0:T(8,128)(2,1)S(1)}, bf16[264,128]{1,0:T(8,128)(2,1)S(1)}, u32[]{:S(2)}, u32[]{:S(2)}) collective-permute-start(bf16[264,128]{1,0:T(8,128)(2,1)S(1)} %add.8.refs_0_), channel_id=1, source_target_pairs={{8,0},{12,4},{0,8},{4,12},{24,16},{28,20},{16,24},{20,28},{9,1},{1... | collective-permute-start | bytes 202760 | tf_op jit(solution)/shard_map/ppermute | solution.py:231
  22.7 7.1 %collective-permute-start.10 = (bf16[264,128]{1,0:T(8,128)(2,1)S(1)}, bf16[264,128]{1,0:T(8,128)(2,1)S(1)}, u32[]{:S(2)}, u32[]{:S(2)}) collective-permute-start(bf16[264,128]{1,0:T(8,128)(2,1)S(1)} %add.8.refs_0_), channel_id=1, source_target_pairs={{24,0},{28,4},{16,8},{20,12},{8,16},{12,20},{0,24},{4,28},{25,1},{... | collective-permute-start | bytes 202760 | tf_op jit(solution)/shard_map/ppermute | solution.py:231
  25.1 5.2 %collective-permute-start.9 = (bf16[264,128]{1,0:T(8,128)(2,1)S(1)}, bf16[264,128]{1,0:T(8,128)(2,1)S(1)}, u32[]{:S(2)}, u32[]{:S(2)}) collective-permute-start(bf16[264,128]{1,0:T(8,128)(2,1)S(1)} %add.8.refs_0_), channel_id=1, source_target_pairs={{16,0},{20,4},{24,8},{28,12},{0,16},{4,20},{8,24},{12,28},{17,1},{... | collective-permute-start | bytes 202760 | tf_op jit(solution)/shard_map/ppermute | solution.py:231
  30.6 8.1 %collective-permute-start.15 = (bf16[1536,128]{1,0:T(8,128)(2,1)S(1)}, bf16[1536,128]{1,0:T(8,128)(2,1)S(1)}, u32[]{:S(2)}, u32[]{:S(2)}) collective-permute-start(bf16[1536,128]{1,0:T(8,128)(2,1)S(1)} %fill.2.dense_ref), channel_id=1, source_target_pairs={{0,4},{1,5},{2,6},{3,7},{4,0},{5,1},{6,2},{7,3},{8,12},{9,13},{10,... | collective-permute-start | bytes 1179656 | tf_op jit(solution)/shard_map/ppermute | solution.py:238
  32.9 5.8 %collective-permute-start.11 = (s16[528,128]{1,0:T(8,128)(2,1)S(1)}, s16[528,128]{1,0:T(8,128)(2,1)S(1)}, u32[]{:S(2)}, u32[]{:S(2)}) collective-permute-start(s16[528,128]{1,0:T(8,128)(2,1)S(1)} %send_part.7), channel_id=1, source_target_pairs={{0,2},{1,3},{2,0},{3,1},{4,6},{5,7},{6,4},{7,5},{8,10},{9,11},{10,... | collective-permute-start | bytes 405512 | tf_op jit(solution)/shard_map/ppermute | solution.py:238
  34.7 11.6 %collective-permute-start.17 = (s16[1296,128]{1,0:T(8,128)(2,1)S(1)}, s16[1296,128]{1,0:T(8,128)(2,1)S(1)}, u32[]{:S(2)}, u32[]{:S(2)}) collective-permute-start(s16[1296,128]{1,0:T(8,128)(2,1)S(1)} %send_part.8), channel_id=1, source_target_pairs={{0,2},{1,3},{2,0},{3,1},{4,6},{5,7},{6,4},{7,5},{8,10},{9,11},{10,... | collective-permute-start | bytes 995336 | tf_op jit(solution)/shard_map/ppermute | solution.py:238
  40.0 15.9 %collective-permute-start.16 = (s16[1296,128]{1,0:T(8,128)(2,1)S(1)}, s16[1296,128]{1,0:T(8,128)(2,1)S(1)}, u32[]{:S(2)}, u32[]{:S(2)}) collective-permute-start(s16[1296,128]{1,0:T(8,128)(2,1)S(1)} %send_part.9), channel_id=1, source_target_pairs={{0,2},{1,3},{2,0},{3,1},{4,6},{5,7},{6,4},{7,5},{8,10},{9,11},{10,... | collective-permute-start | bytes 995336 | tf_op jit(solution)/shard_map/ppermute | solution.py:238
  41.3 7.2 %collective-permute-start.14 = (bf16[264,256]{1,0:T(8,128)(2,1)S(1)}, bf16[264,256]{1,0:T(8,128)(2,1)S(1)}, u32[]{:S(2)}, u32[]{:S(2)}) collective-permute-start(bf16[264,256]{1,0:T(8,128)(2,1)S(1)} %add.9.refs_0_), channel_id=1, source_target_pairs={{24,0},{28,4},{16,8},{20,12},{8,16},{12,20},{0,24},{4,28},{25,1},{... | collective-permute-start | bytes 405512 | tf_op jit(solution)/shard_map/ppermute | solution.py:231
  43.6 7.4 %collective-permute-start.13 = (bf16[264,256]{1,0:T(8,128)(2,1)S(1)}, bf16[264,256]{1,0:T(8,128)(2,1)S(1)}, u32[]{:S(2)}, u32[]{:S(2)}) collective-permute-start(bf16[264,256]{1,0:T(8,128)(2,1)S(1)} %add.9.refs_0_), channel_id=1, source_target_pairs={{16,0},{20,4},{24,8},{28,12},{0,16},{4,20},{8,24},{12,28},{17,1},{... | collective-permute-start | bytes 405512 | tf_op jit(solution)/shard_map/ppermute | solution.py:231
  43.6 7.4 %collective-permute-start.12 = (bf16[264,256]{1,0:T(8,128)(2,1)S(1)}, bf16[264,256]{1,0:T(8,128)(2,1)S(1)}, u32[]{:S(2)}, u32[]{:S(2)}) collective-permute-start(bf16[264,256]{1,0:T(8,128)(2,1)S(1)} %add.9.refs_0_), channel_id=1, source_target_pairs={{8,0},{12,4},{0,8},{4,12},{24,16},{28,20},{16,24},{20,28},{9,1},{1... | collective-permute-start | bytes 405512 | tf_op jit(solution)/shard_map/ppermute | solution.py:231
  46.3 9.5 %collective-permute-start.18 = (s16[528,128]{1,0:T(8,128)(2,1)S(1)}, s16[528,128]{1,0:T(8,128)(2,1)S(1)}, u32[]{:S(2)}, u32[]{:S(2)}) collective-permute-start(s16[528,128]{1,0:T(8,128)(2,1)S(1)} %send_part.10), channel_id=1, source_target_pairs={{0,2},{1,3},{2,0},{3,1},{4,6},{5,7},{6,4},{7,5},{8,10},{9,11},{10,... | collective-permute-start | bytes 405512 | tf_op jit(solution)/shard_map/ppermute | solution.py:238
  48.4 13.8 %collective-permute-start.19 = (s16[1296,128]{1,0:T(8,128)(2,1)S(1)}, s16[1296,128]{1,0:T(8,128)(2,1)S(1)}, u32[]{:S(2)}, u32[]{:S(2)}) collective-permute-start(s16[1296,128]{1,0:T(8,128)(2,1)S(1)} %send_part.11), channel_id=1, source_target_pairs={{0,2},{1,3},{2,0},{3,1},{4,6},{5,7},{6,4},{7,5},{8,10},{9,11},{10,... | collective-permute-start | bytes 995336 | tf_op jit(solution)/shard_map/ppermute | solution.py:238
  56.9 9.4 %collective-permute-start.21 = (s16[1040,128]{1,0:T(8,128)(2,1)S(1)}, s16[1040,128]{1,0:T(8,128)(2,1)S(1)}, u32[]{:S(2)}, u32[]{:S(2)}) collective-permute-start(s16[1040,128]{1,0:T(8,128)(2,1)S(1)} %send_part.12), channel_id=1, source_target_pairs={{0,2},{1,3},{2,0},{3,1},{4,6},{5,7},{6,4},{7,5},{8,10},{9,11},{10,... | collective-permute-start | bytes 798728 | tf_op jit(solution)/shard_map/ppermute | solution.py:238
  62.7 5.3 %collective-permute-start.20 = (s16[272,128]{1,0:T(8,128)(2,1)S(1)}, s16[272,128]{1,0:T(8,128)(2,1)S(1)}, u32[]{:S(2)}, u32[]{:S(2)}) collective-permute-start(s16[272,128]{1,0:T(8,128)(2,1)S(1)} %send_part.13), channel_id=1, source_target_pairs={{0,2},{1,3},{2,0},{3,1},{4,6},{5,7},{6,4},{7,5},{8,10},{9,11},{10,... | collective-permute-start | bytes 208904 | tf_op jit(solution)/shard_map/ppermute | solution.py:238

commit v17 on v16

--- a/solution.py
+++ b/solution.py
@@ -326,7 +326,7 @@
     arrived, sent = {}, []
     order = []
     for number, (half, first, span) in enumerate(rounds):
-        ahead = 2 if number in (3, 4) else 1
+        ahead = 2 if number in (3, 4, 6) else 1
         earlier = sent[-1:] + [part for key in order[:-ahead] for part in arrived[key]]
         if number == len(near_chunks) - 1:
             earlier += list(far_weights.values())

time: 69.2 us -> 68 us (0.983)
  starting transfers between devices: 27.9 us -> 27.1 us
    ppermute x11, starting transfers between devices: 13.8 us -> 13 us  [across(): return lax.ppermute(value, ('row', 'col'), pairs)]
  transfers between devices with their start and end apart: 22 -> 22, of which waited for: 11 -> 12; matrix products, arithmetic and copies ran while one was open for 1% -> 1% of each run, Pallas kernels for 24% -> 24%
where the time goes in v17:
time: 68 us; the launch traced here: 67.9 us
  starting transfers between devices  27.1 us (40%)
  waiting for transfers between devices  21.4 us (31%)
  Pallas kernels  17.8 us (26%)
  between operations  0.82 us (1%)
  other arithmetic  0.76 us (1%)
    ppermute x9, starting transfers between devices, along(): return lax.ppermute(value, 'row', pairs)  13.6 us
    ppermute x11, starting transfers between devices, across(): return lax.ppermute(value, ('row', 'col'), pairs)  13 us
    ppermute x11, waiting for transfers between devices, across(): return lax.ppermute(value, ('row', 'col'), pairs)  12.6 us
    ppermute x9, waiting for transfers between devices, along(): return lax.ppermute(value, 'row', pairs)  8.39 us
    pallas_call x7, Pallas kernels, shards(): pl.pallas_call(partial(send_kernel, first, span, block_rows), in_specs=[V...  6.43 us
    pallas_call x4, Pallas kernels, shards(): pl.pallas_call(partial(join_kernel, first, span, block_rows, skips), in_s...  5.86 us
    pallas_call x1, Pallas kernels, screen(): pl.pallas_call(partial(screen_kernel, tile_width, block_rows), in_specs=[...  3.07 us
  transfers between devices with their start and end apart: 22, of which 12 were waited for; matrix products, arithmetic and copies ran while one was open for 1% of the time, Pallas kernels for 24%

profile of v17, /device:TPU:0, one launch (start us, length us, event | category | flops | bytes accessed | tf_op | source)
XLA Modules:
  0.0 67.9 jit_solution(12842942095085750304)
XLA Ops:
  0.0 0.5 collective-permute-start.8
  1.2 1.0 %pack.1 = (bf16[136,256]{1,0:T(8,128)(2,1)S(1)}, bf16[136,256]{1,0:T(8,128)(2,1)S(1)}, bf16[136,256]{1,0:T(8,128)(2,1)S(1)}, bf16[136,256]{1,0:T(8,128)(2,1)S(1)}) custom-call(s32[1,1,2]{2,1,0:T(1,128)} %list_ref.1, s32[1,1]{1,0:T(1,128)S(6)} %copy.13.count_ref, bf16[1,1,2,256,256]{4,3,2,1,0:T(8,128)(2,1)} %panel_ref.1), custom_call_target="tpu_custom_call" | custom-call | tf_op jit(solution)/shard_map/pack/pallas_call | solution.py:249
  2.2 3.0 %collective-permute-start.1 = (bf16[136,256]{1,0:T(8,128)(2,1)S(1)}, bf16[136,256]{1,0:T(8,128)(2,1)S(1)}, u32[]{:S(2)}, u32[]{:S(2)}) collective-permute-start(bf16[136,256]{1,0:T(8,128)(2,1)S(1)} %get-tuple-element.22), channel_id=1, source_target_pairs={{8,0},{12,4},{0,8},{4,12},{24,16},{28,20},{16,24},{20,28},{9,1},{1... | collective-permute-start | bytes 208904 | tf_op jit(solution)/shard_map/ppermute | solution.py:231
  5.3 2.6 %collective-permute-start.2 = (bf16[136,256]{1,0:T(8,128)(2,1)S(1)}, bf16[136,256]{1,0:T(8,128)(2,1)S(1)}, u32[]{:S(2)}, u32[]{:S(2)}) collective-permute-start(bf16[136,256]{1,0:T(8,128)(2,1)S(1)} %get-tuple-element.23), channel_id=1, source_target_pairs={{16,0},{20,4},{24,8},{28,12},{0,16},{4,20},{8,24},{12,28},{17,1},{... | collective-permute-start | bytes 208904 | tf_op jit(solution)/shard_map/ppermute | solution.py:231
  7.8 0.4 collective-permute-done
  8.2 0.7 %pad_add_fusion.plan_ref.mask_ref = s32[7,12]{1,0:T(8,128)S(1)} fusion(s32[1,4]{1,0:T(1,128)} %bitcast.4, s32[3,12]{1,0:T(4,128)S(1)} %collective-permute-done, s32[3,12]{1,0:T(4,128)} %bitcast.3), kind=kLoop, calls=%fused_computation | loop fusion | flops 168 | bytes 640 | tf_op jit(solution)/shard_map/concatenate | solution.py:244
  8.9 4.1 %collective-permute-done.2.refs_2_ = bf16[136,256]{1,0:T(8,128)(2,1)S(1)} collective-permute-done((bf16[136,256]{1,0:T(8,128)(2,1)S(1)}, bf16[136,256]{1,0:T(8,128)(2,1)S(1)}, u32[]{:S(2)}, u32[]{:S(2)}) %collective-permute-start.2) | collective-permute-done | bytes 69664 | tf_op jit(solution)/shard_map/ppermute | solution.py:231
  13.0 1.1 %collective-permute-done.3.refs_3_ = bf16[136,256]{1,0:T(8,128)(2,1)S(1)} collective-permute-done((bf16[136,256]{1,0:T(8,128)(2,1)S(1)}, bf16[136,256]{1,0:T(8,128)(2,1)S(1)}, u32[]{:S(2)}, u32[]{:S(2)}) %collective-permute-start.3) | collective-permute-done | bytes 69664 | tf_op jit(solution)/shard_map/ppermute | solution.py:231
  14.1 0.8 %choose.1 = (bf16[264,256]{1,0:T(8,128)(2,1)S(1)}, bf16[264,128]{1,0:T(8,128)(2,1)S(1)}, bf16[264,128]{1,0:T(8,128)(2,1)S(1)}) custom-call(s32[7,12]{1,0:T(8,128)S(1)} %pad_add_fusion.plan_ref.mask_ref, bf16[136,256]{1,0:T(8,128)(2,1)S(1)} %get-tuple-element.21.refs_0_, bf16[136,256]{1,0:T(8,128)(2,1)S(1)} %collective-permute-done.1.refs_1_, ...), custom_call_target="tpu_custom_call" | custom-call | tf_op jit(solution)/shard_map/choose/pallas_call | solution.py:264
  14.8 1.6 %collective-permute-start.4 = (bf16[264,128]{1,0:T(8,128)(2,1)S(1)}, bf16[264,128]{1,0:T(8,128)(2,1)S(1)}, u32[]{:S(2)}, u32[]{:S(2)}) collective-permute-start(bf16[264,128]{1,0:T(8,128)(2,1)S(1)} %get-tuple-element.25), channel_id=1, source_target_pairs={{0,2},{1,3},{2,0},{3,1},{4,6},{5,7},{6,4},{7,5},{8,10},{9,11},{10,... | collective-permute-start | bytes 202760 | tf_op jit(solution)/shard_map/ppermute | solution.py:238
  16.4 1.5 %collective-permute-start.5 = (bf16[264,128]{1,0:T(8,128)(2,1)S(1)}, bf16[264,128]{1,0:T(8,128)(2,1)S(1)}, u32[]{:S(2)}, u32[]{:S(2)}) collective-permute-start(bf16[264,128]{1,0:T(8,128)(2,1)S(1)} %get-tuple-element.26), channel_id=1, source_target_pairs={{0,6},{1,7},{2,4},{3,5},{4,2},{5,3},{6,0},{7,1},{8,14},{9,15},{10,... | collective-permute-start | bytes 202760 | tf_op jit(solution)/shard_map/ppermute | solution.py:238
  17.9 0.5 collective-permute-start.7
  18.4 0.9 %collective-permute-done.4 = bf16[264,128]{1,0:T(8,128)(2,1)S(1)} collective-permute-done((bf16[264,128]{1,0:T(8,128)(2,1)S(1)}, bf16[264,128]{1,0:T(8,128)(2,1)S(1)}, u32[]{:S(2)}, u32[]{:S(2)}) %collective-permute-start.4) | collective-permute-done | bytes 67616 | tf_op jit(solution)/shard_map/ppermute | solution.py:238
  19.3 2.3 %collective-permute-done.5 = bf16[264,128]{1,0:T(8,128)(2,1)S(1)} collective-permute-done((bf16[264,128]{1,0:T(8,128)(2,1)S(1)}, bf16[264,128]{1,0:T(8,128)(2,1)S(1)}, u32[]{:S(2)}, u32[]{:S(2)}) %collective-permute-start.5) | collective-permute-done | bytes 67616 | tf_op jit(solution)/shard_map/ppermute | solution.py:238
  21.6 1.1 %collective-permute-start.6 = (bf16[264,128]{1,0:T(8,128)(2,1)S(1)}, bf16[264,128]{1,0:T(8,128)(2,1)S(1)}, u32[]{:S(2)}, u32[]{:S(2)}) collective-permute-start(bf16[264,128]{1,0:T(8,128)(2,1)S(1)} %add.8.refs_0_), channel_id=1, source_target_pairs={{8,0},{12,4},{0,8},{4,12},{24,16},{28,20},{16,24},{20,28},{9,1},{1... | collective-permute-start | bytes 202760 | tf_op jit(solution)/shard_map/ppermute | solution.py:231
  22.7 2.4 %collective-permute-start.10 = (bf16[264,128]{1,0:T(8,128)(2,1)S(1)}, bf16[264,128]{1,0:T(8,128)(2,1)S(1)}, u32[]{:S(2)}, u32[]{:S(2)}) collective-permute-start(bf16[264,128]{1,0:T(8,128)(2,1)S(1)} %add.8.refs_0_), channel_id=1, source_target_pairs={{24,0},{28,4},{16,8},{20,12},{8,16},{12,20},{0,24},{4,28},{25,1},{... | collective-permute-start | bytes 202760 | tf_op jit(solution)/shard_map/ppermute | solution.py:231
  25.1 0.1 collective-permute-start.9
  25.2 1.5 %collective-permute-done.6.refs_1_ = bf16[264,128]{1,0:T(8,128)(2,1)S(1)} collective-permute-done((bf16[264,128]{1,0:T(8,128)(2,1)S(1)}, bf16[264,128]{1,0:T(8,128)(2,1)S(1)}, u32[]{:S(2)}, u32[]{:S(2)}) %collective-permute-start.6) | collective-permute-done | bytes 67616 | tf_op jit(solution)/shard_map/ppermute | solution.py:231
  26.7 3.1 %screen.1.rows_ref = bf16[3072,1536]{1,0:T(8,128)(2,1)S(1)} custom-call(s32[7,12]{1,0:T(8,128)S(1)} %pad_add_fusion.plan_ref.mask_ref, bf16[3072,768]{1,0:T(8,128)(2,1)} %own_ref.1, bf16[3072,768]{1,0:T(8,128)(2,1)S(1)} %collective-permute-done.8.other_ref), custom_call_target="tpu_custom_call" | custom-call | flops 4718592 | bytes 18874368 | tf_op jit(solution)/shard_map/screen/pallas_call | solution.py:285
  29.8 0.5 collective-permute-done.9.refs_2_
  30.3 0.3 fill.2.dense_ref
  30.6 1.7 %collective-permute-start.15 = (bf16[1536,128]{1,0:T(8,128)(2,1)S(1)}, bf16[1536,128]{1,0:T(8,128)(2,1)S(1)}, u32[]{:S(2)}, u32[]{:S(2)}) collective-permute-start(bf16[1536,128]{1,0:T(8,128)(2,1)S(1)} %fill.2.dense_ref), channel_id=1, source_target_pairs={{0,4},{1,5},{2,6},{3,7},{4,0},{5,1},{6,2},{7,3},{8,12},{9,13},{10,... | collective-permute-start | bytes 1179656 | tf_op jit(solution)/shard_map/ppermute | solution.py:238
  32.3 0.6 send_part.7
  32.9 0.5 collective-permute-start.11
  33.4 1.2 %send_part.8 = s16[1296,128]{1,0:T(8,128)(2,1)S(1)} custom-call(bf16[3072,1536]{1,0:T(8,128)(2,1)S(1)} %screen.1.rows_ref, bf16[1536,128]{1,0:T(8,128)(2,1)S(1)} %fill.2.dense_ref), custom_call_target="tpu_custom_call" | custom-call | flops 503316480 | bytes 4259840 | tf_op jit(solution)/shard_map/send_part/pallas_call | solution.py:339
  34.7 1.6 %collective-permute-start.17 = (s16[1296,128]{1,0:T(8,128)(2,1)S(1)}, s16[1296,128]{1,0:T(8,128)(2,1)S(1)}, u32[]{:S(2)}, u32[]{:S(2)}) collective-permute-start(s16[1296,128]{1,0:T(8,128)(2,1)S(1)} %send_part.8), channel_id=1, source_target_pairs={{0,2},{1,3},{2,0},{3,1},{4,6},{5,7},{6,4},{7,5},{8,10},{9,11},{10,... | collective-permute-start | bytes 995336 | tf_op jit(solution)/shard_map/ppermute | solution.py:238
  36.3 2.4 %collective-permute-done.11.refs_0_ = s16[528,128]{1,0:T(8,128)(2,1)S(1)} collective-permute-done((s16[528,128]{1,0:T(8,128)(2,1)S(1)}, s16[528,128]{1,0:T(8,128)(2,1)S(1)}, u32[]{:S(2)}, u32[]{:S(2)}) %collective-permute-start.11) | collective-permute-done | bytes 135200 | tf_op jit(solution)/shard_map/ppermute | solution.py:238
  38.7 1.2 %send_part.9 = s16[1296,128]{1,0:T(8,128)(2,1)S(1)} custom-call(bf16[3072,1536]{1,0:T(8,128)(2,1)S(1)} %screen.1.rows_ref, bf16[1536,128]{1,0:T(8,128)(2,1)S(1)} %fill.2.dense_ref), custom_call_target="tpu_custom_call" | custom-call | flops 503316480 | bytes 4259840 | tf_op jit(solution)/shard_map/send_part/pallas_call | solution.py:339
  40.0 1.3 %collective-permute-start.16 = (s16[1296,128]{1,0:T(8,128)(2,1)S(1)}, s16[1296,128]{1,0:T(8,128)(2,1)S(1)}, u32[]{:S(2)}, u32[]{:S(2)}) collective-permute-start(s16[1296,128]{1,0:T(8,128)(2,1)S(1)} %send_part.9), channel_id=1, source_target_pairs={{0,2},{1,3},{2,0},{3,1},{4,6},{5,7},{6,4},{7,5},{8,10},{9,11},{10,... | collective-permute-start | bytes 995336 | tf_op jit(solution)/shard_map/ppermute | solution.py:238
  41.3 2.3 %collective-permute-start.14 = (bf16[264,256]{1,0:T(8,128)(2,1)S(1)}, bf16[264,256]{1,0:T(8,128)(2,1)S(1)}, u32[]{:S(2)}, u32[]{:S(2)}) collective-permute-start(bf16[264,256]{1,0:T(8,128)(2,1)S(1)} %add.9.refs_0_), channel_id=1, source_target_pairs={{24,0},{28,4},{16,8},{20,12},{8,16},{12,20},{0,24},{4,28},{25,1},{... | collective-permute-start | bytes 405512 | tf_op jit(solution)/shard_map/ppermute | solution.py:231
  43.6 2.0 %collective-permute-start.12 = (bf16[264,256]{1,0:T(8,128)(2,1)S(1)}, bf16[264,256]{1,0:T(8,128)(2,1)S(1)}, u32[]{:S(2)}, u32[]{:S(2)}) collective-permute-start(bf16[264,256]{1,0:T(8,128)(2,1)S(1)} %add.9.refs_0_), channel_id=1, source_target_pairs={{8,0},{12,4},{0,8},{4,12},{24,16},{28,20},{16,24},{20,28},{9,1},{1... | collective-permute-start | bytes 405512 | tf_op jit(solution)/shard_map/ppermute | solution.py:231
  45.7 0.6 send_part.10
  46.3 0.9 %collective-permute-start.18 = (s16[528,128]{1,0:T(8,128)(2,1)S(1)}, s16[528,128]{1,0:T(8,128)(2,1)S(1)}, u32[]{:S(2)}, u32[]{:S(2)}) collective-permute-start(s16[528,128]{1,0:T(8,128)(2,1)S(1)} %send_part.10), channel_id=1, source_target_pairs={{0,2},{1,3},{2,0},{3,1},{4,6},{5,7},{6,4},{7,5},{8,10},{9,11},{10,... | collective-permute-start | bytes 405512 | tf_op jit(solution)/shard_map/ppermute | solution.py:238
  47.2 1.2 %send_part.11 = s16[1296,128]{1,0:T(8,128)(2,1)S(1)} custom-call(bf16[3072,1536]{1,0:T(8,128)(2,1)S(1)} %screen.1.rows_ref, bf16[1536,128]{1,0:T(8,128)(2,1)S(1)} %collective-permute-done.15.dense_ref), custom_call_target="tpu_custom_call" | custom-call | flops 503316480 | bytes 4259840 | tf_op jit(solution)/shard_map/send_part/pallas_call | solution.py:339
  48.4 1.3 %collective-permute-start.21 = (s16[1296,128]{1,0:T(8,128)(2,1)S(1)}, s16[1296,128]{1,0:T(8,128)(2,1)S(1)}, u32[]{:S(2)}, u32[]{:S(2)}) collective-permute-start(s16[1296,128]{1,0:T(8,128)(2,1)S(1)} %send_part.11), channel_id=1, source_target_pairs={{0,2},{1,3},{2,0},{3,1},{4,6},{5,7},{6,4},{7,5},{8,10},{9,11},{10,... | collective-permute-start | bytes 995336 | tf_op jit(solution)/shard_map/ppermute | solution.py:238
  49.7 1.3 %collective-permute-done.13.refs_2_ = bf16[264,256]{1,0:T(8,128)(2,1)S(1)} collective-permute-done((bf16[264,256]{1,0:T(8,128)(2,1)S(1)}, bf16[264,256]{1,0:T(8,128)(2,1)S(1)}, u32[]{:S(2)}, u32[]{:S(2)}) %collective-permute-start.13) | collective-permute-done | bytes 135200 | tf_op jit(solution)/shard_map/ppermute | solution.py:231
  51.0 0.3 fill.3.dense_ref
  51.3 4.5 %collective-permute-done.18.refs_1_ = s16[528,128]{1,0:T(8,128)(2,1)S(1)} collective-permute-done((s16[528,128]{1,0:T(8,128)(2,1)S(1)}, s16[528,128]{1,0:T(8,128)(2,1)S(1)}, u32[]{:S(2)}, u32[]{:S(2)}) %collective-permute-start.18) | collective-permute-done | bytes 135200 | tf_op jit(solution)/shard_map/ppermute | solution.py:238
  55.8 1.0 %send_part.12 = s16[1040,128]{1,0:T(8,128)(2,1)S(1)} custom-call(bf16[3072,1536]{1,0:T(8,128)(2,1)S(1)} %screen.1.rows_ref, bf16[1536,128]{1,0:T(8,128)(2,1)S(1)} %collective-permute-done.15.dense_ref), custom_call_target="tpu_custom_call" | custom-call | flops 402653184 | bytes 3407872 | tf_op jit(solution)/shard_map/send_part/pallas_call | solution.py:339
  56.9 1.3 %collective-permute-start.20 = (s16[1040,128]{1,0:T(8,128)(2,1)S(1)}, s16[1040,128]{1,0:T(8,128)(2,1)S(1)}, u32[]{:S(2)}, u32[]{:S(2)}) collective-permute-start(s16[1040,128]{1,0:T(8,128)(2,1)S(1)} %send_part.12), channel_id=1, source_target_pairs={{0,2},{1,3},{2,0},{3,1},{4,6},{5,7},{6,4},{7,5},{8,10},{9,11},{10,... | collective-permute-start | bytes 798728 | tf_op jit(solution)/shard_map/ppermute | solution.py:238
  58.2 1.2 %join_part.4.refs_2_ = bf16[3072,256]{1,0:T(8,128)(2,1)} custom-call(bf16[3072,1536]{1,0:T(8,128)(2,1)S(1)} %screen.1.rows_ref, bf16[1536,256]{1,0:T(8,128)(2,1)S(1)} %fill.3.dense_ref, s16[528,128]{1,0:T(8,128)(2,1)S(1)} %collective-permute-done.11.refs_0_, s16[528,128]{1,0:T(8,128)(2,1)S(1)} %collective-permute-done.18.refs_1_), custom_call_target="tpu_custom_call" | custom-call | flops 402653184 | bytes 1835008 | tf_op jit(solution)/shard_map/join_part/pallas_call | solution.py:368
  59.4 0.4 send_part.13
  59.9 0.9 %collective-permute-start.19 = (s16[272,128]{1,0:T(8,128)(2,1)S(1)}, s16[272,128]{1,0:T(8,128)(2,1)S(1)}, u32[]{:S(2)}, u32[]{:S(2)}) collective-permute-start(s16[272,128]{1,0:T(8,128)(2,1)S(1)} %send_part.13), channel_id=1, source_target_pairs={{0,2},{1,3},{2,0},{3,1},{4,6},{5,7},{6,4},{7,5},{8,10},{9,11},{10,... | collective-permute-start | bytes 208904 | tf_op jit(solution)/shard_map/ppermute | solution.py:238
  60.7 1.6 %collective-permute-done.21.refs_1_ = s16[1296,128]{1,0:T(8,128)(2,1)S(1)} collective-permute-done((s16[1296,128]{1,0:T(8,128)(2,1)S(1)}, s16[1296,128]{1,0:T(8,128)(2,1)S(1)}, u32[]{:S(2)}, u32[]{:S(2)}) %collective-permute-start.21) | collective-permute-done | bytes 331808 | tf_op jit(solution)/shard_map/ppermute | solution.py:238
  62.3 1.9 %join_part.5.refs_2_ = bf16[3072,256]{1,0:T(8,128)(2,1)} custom-call(bf16[3072,1536]{1,0:T(8,128)(2,1)S(1)} %screen.1.rows_ref, bf16[1536,256]{1,0:T(8,128)(2,1)S(1)} %fill.3.dense_ref, s16[1296,128]{1,0:T(8,128)(2,1)S(1)} %collective-permute-done.17.refs_0_, s16[1296,128]{1,0:T(8,128)(2,1)S(1)} %collective-permute-done.21.refs_1_, ...), custom_call_target="tpu_custom_call", output_to_operand_aliasing={{}: (4, {})} | custom-call | flops 1006632960 | bytes 4587520 | tf_op jit(solution)/shard_map/join_part/pallas_call | solution.py:368
  64.2 1.0 %collective-permute-done.20.refs_1_ = s16[1040,128]{1,0:T(8,128)(2,1)S(1)} collective-permute-done((s16[1040,128]{1,0:T(8,128)(2,1)S(1)}, s16[1040,128]{1,0:T(8,128)(2,1)S(1)}, u32[]{:S(2)}, u32[]{:S(2)}) %collective-permute-start.20) | collective-permute-done | bytes 266272 | tf_op jit(solution)/shard_map/ppermute | solution.py:238
  65.1 1.7 %join_part.6.refs_2_ = bf16[3072,256]{1,0:T(8,128)(2,1)} custom-call(bf16[3072,1536]{1,0:T(8,128)(2,1)S(1)} %screen.1.rows_ref, bf16[1536,256]{1,0:T(8,128)(2,1)S(1)} %fill.3.dense_ref, s16[1296,128]{1,0:T(8,128)(2,1)S(1)} %collective-permute-done.16.refs_0_, s16[1040,128]{1,0:T(8,128)(2,1)S(1)} %collective-permute-done.20.refs_1_, ...), custom_call_target="tpu_custom_call", output_to_operand_aliasing={{}: (4, {})} | custom-call | flops 805306368 | bytes 3670016 | tf_op jit(solution)/shard_map/join_part/pallas_call | solution.py:368
  66.8 1.0 %join_part.7 = bf16[3072,256]{1,0:T(8,128)(2,1)} custom-call(bf16[3072,1536]{1,0:T(8,128)(2,1)S(1)} %screen.1.rows_ref, bf16[1536,256]{1,0:T(8,128)(2,1)S(1)} %fill.3.dense_ref, s16[1296,128]{1,0:T(8,128)(2,1)S(1)} %collective-permute-done.16.refs_0_, s16[272,128]{1,0:T(8,128)(2,1)S(1)} %collective-permute-done.19.refs_1_, ...), custom_call_target="tpu_custom_call", output_to_operand_aliasing={{}: (4, {})} | custom-call | flops 201326592 | bytes 917504 | tf_op jit(solution)/shard_map/join_part/pallas_call | solution.py:368
  (15 shorter events, 0.1 us)
Async XLA Ops:
  0.0 26.7 %collective-permute-start.8 = (bf16[3072,768]{1,0:T(8,128)(2,1)}, bf16[3072,768]{1,0:T(8,128)(2,1)S(1)}, u32[]{:S(2)}, u32[]{:S(2)}) collective-permute-start(bf16[3072,768]{1,0:T(8,128)(2,1)} %own_ref.1), channel_id=1, source_target_pairs={{0,1},{1,0},{2,3},{3,2},{4,5},{5,4},{6,7},{7,6},{8,9},{9,8},{10,11... | collective-permute-start | bytes 14155784 | tf_op jit(solution)/shard_map/ppermute | solution.py:241
  0.5 7.7 %collective-permute-start = (s32[3,12]{1,0:T(4,128)}, s32[3,12]{1,0:T(4,128)S(1)}, u32[]{:S(2)}, u32[]{:S(2)}) collective-permute-start(s32[3,12]{1,0:T(4,128)} %bitcast.2), channel_id=1, source_target_pairs={{0,1},{1,0},{2,3},{3,2},{4,5},{5,4},{6,7},{7,6},{8,9},{9,8},{10,11... | collective-permute-start | bytes 440 | tf_op jit(solution)/shard_map/ppermute | solution.py:242
  2.2 6.7 %collective-permute-start.1 = (bf16[136,256]{1,0:T(8,128)(2,1)S(1)}, bf16[136,256]{1,0:T(8,128)(2,1)S(1)}, u32[]{:S(2)}, u32[]{:S(2)}) collective-permute-start(bf16[136,256]{1,0:T(8,128)(2,1)S(1)} %get-tuple-element.22), channel_id=1, source_target_pairs={{8,0},{12,4},{0,8},{4,12},{24,16},{28,20},{16,24},{20,28},{9,1},{1... | collective-permute-start | bytes 208904 | tf_op jit(solution)/shard_map/ppermute | solution.py:231
  5.3 7.7 %collective-permute-start.2 = (bf16[136,256]{1,0:T(8,128)(2,1)S(1)}, bf16[136,256]{1,0:T(8,128)(2,1)S(1)}, u32[]{:S(2)}, u32[]{:S(2)}) collective-permute-start(bf16[136,256]{1,0:T(8,128)(2,1)S(1)} %get-tuple-element.23), channel_id=1, source_target_pairs={{16,0},{20,4},{24,8},{28,12},{0,16},{4,20},{8,24},{12,28},{17,1},{... | collective-permute-start | bytes 208904 | tf_op jit(solution)/shard_map/ppermute | solution.py:231
  7.8 6.2 %collective-permute-start.3 = (bf16[136,256]{1,0:T(8,128)(2,1)S(1)}, bf16[136,256]{1,0:T(8,128)(2,1)S(1)}, u32[]{:S(2)}, u32[]{:S(2)}) collective-permute-start(bf16[136,256]{1,0:T(8,128)(2,1)S(1)} %get-tuple-element.24), channel_id=1, source_target_pairs={{24,0},{28,4},{16,8},{20,12},{8,16},{12,20},{0,24},{4,28},{25,1},{... | collective-permute-start | bytes 208904 | tf_op jit(solution)/shard_map/ppermute | solution.py:231
  14.8 4.5 %collective-permute-start.4 = (bf16[264,128]{1,0:T(8,128)(2,1)S(1)}, bf16[264,128]{1,0:T(8,128)(2,1)S(1)}, u32[]{:S(2)}, u32[]{:S(2)}) collective-permute-start(bf16[264,128]{1,0:T(8,128)(2,1)S(1)} %get-tuple-element.25), channel_id=1, source_target_pairs={{0,2},{1,3},{2,0},{3,1},{4,6},{5,7},{6,4},{7,5},{8,10},{9,11},{10,... | collective-permute-start | bytes 202760 | tf_op jit(solution)/shard_map/ppermute | solution.py:238
  16.4 5.2 %collective-permute-start.5 = (bf16[264,128]{1,0:T(8,128)(2,1)S(1)}, bf16[264,128]{1,0:T(8,128)(2,1)S(1)}, u32[]{:S(2)}, u32[]{:S(2)}) collective-permute-start(bf16[264,128]{1,0:T(8,128)(2,1)S(1)} %get-tuple-element.26), channel_id=1, source_target_pairs={{0,6},{1,7},{2,4},{3,5},{4,2},{5,3},{6,0},{7,1},{8,14},{9,15},{10,... | collective-permute-start | bytes 202760 | tf_op jit(solution)/shard_map/ppermute | solution.py:238
  17.9 7.3 %collective-permute-start.7 = (bf16[264,256]{1,0:T(8,128)(2,1)S(1)}, bf16[264,256]{1,0:T(8,128)(2,1)S(1)}, u32[]{:S(2)}, u32[]{:S(2)}) collective-permute-start(bf16[264,256]{1,0:T(8,128)(2,1)S(1)} %get-tuple-element.27), channel_id=1, source_target_pairs={{0,4},{1,5},{2,6},{3,7},{4,0},{5,1},{6,2},{7,3},{8,12},{9,13},{10,... | collective-permute-start | bytes 405512 | tf_op jit(solution)/shard_map/ppermute | solution.py:238
  21.6 5.1 %collective-permute-start.6 = (bf16[264,128]{1,0:T(8,128)(2,1)S(1)}, bf16[264,128]{1,0:T(8,128)(2,1)S(1)}, u32[]{:S(2)}, u32[]{:S(2)}) collective-permute-start(bf16[264,128]{1,0:T(8,128)(2,1)S(1)} %add.8.refs_0_), channel_id=1, source_target_pairs={{8,0},{12,4},{0,8},{4,12},{24,16},{28,20},{16,24},{20,28},{9,1},{1... | collective-permute-start | bytes 202760 | tf_op jit(solution)/shard_map/ppermute | solution.py:231
  22.7 7.1 %collective-permute-start.10 = (bf16[264,128]{1,0:T(8,128)(2,1)S(1)}, bf16[264,128]{1,0:T(8,128)(2,1)S(1)}, u32[]{:S(2)}, u32[]{:S(2)}) collective-permute-start(bf16[264,128]{1,0:T(8,128)(2,1)S(1)} %add.8.refs_0_), channel_id=1, source_target_pairs={{24,0},{28,4},{16,8},{20,12},{8,16},{12,20},{0,24},{4,28},{25,1},{... | collective-permute-start | bytes 202760 | tf_op jit(solution)/shard_map/ppermute | solution.py:231
  25.1 5.2 %collective-permute-start.9 = (bf16[264,128]{1,0:T(8,128)(2,1)S(1)}, bf16[264,128]{1,0:T(8,128)(2,1)S(1)}, u32[]{:S(2)}, u32[]{:S(2)}) collective-permute-start(bf16[264,128]{1,0:T(8,128)(2,1)S(1)} %add.8.refs_0_), channel_id=1, source_target_pairs={{16,0},{20,4},{24,8},{28,12},{0,16},{4,20},{8,24},{12,28},{17,1},{... | collective-permute-start | bytes 202760 | tf_op jit(solution)/shard_map/ppermute | solution.py:231
  30.6 8.1 %collective-permute-start.15 = (bf16[1536,128]{1,0:T(8,128)(2,1)S(1)}, bf16[1536,128]{1,0:T(8,128)(2,1)S(1)}, u32[]{:S(2)}, u32[]{:S(2)}) collective-permute-start(bf16[1536,128]{1,0:T(8,128)(2,1)S(1)} %fill.2.dense_ref), channel_id=1, source_target_pairs={{0,4},{1,5},{2,6},{3,7},{4,0},{5,1},{6,2},{7,3},{8,12},{9,13},{10,... | collective-permute-start | bytes 1179656 | tf_op jit(solution)/shard_map/ppermute | solution.py:238
  32.9 5.8 %collective-permute-start.11 = (s16[528,128]{1,0:T(8,128)(2,1)S(1)}, s16[528,128]{1,0:T(8,128)(2,1)S(1)}, u32[]{:S(2)}, u32[]{:S(2)}) collective-permute-start(s16[528,128]{1,0:T(8,128)(2,1)S(1)} %send_part.7), channel_id=1, source_target_pairs={{0,2},{1,3},{2,0},{3,1},{4,6},{5,7},{6,4},{7,5},{8,10},{9,11},{10,... | collective-permute-start | bytes 405512 | tf_op jit(solution)/shard_map/ppermute | solution.py:238
  34.7 11.6 %collective-permute-start.17 = (s16[1296,128]{1,0:T(8,128)(2,1)S(1)}, s16[1296,128]{1,0:T(8,128)(2,1)S(1)}, u32[]{:S(2)}, u32[]{:S(2)}) collective-permute-start(s16[1296,128]{1,0:T(8,128)(2,1)S(1)} %send_part.8), channel_id=1, source_target_pairs={{0,2},{1,3},{2,0},{3,1},{4,6},{5,7},{6,4},{7,5},{8,10},{9,11},{10,... | collective-permute-start | bytes 995336 | tf_op jit(solution)/shard_map/ppermute | solution.py:238
  40.0 15.9 %collective-permute-start.16 = (s16[1296,128]{1,0:T(8,128)(2,1)S(1)}, s16[1296,128]{1,0:T(8,128)(2,1)S(1)}, u32[]{:S(2)}, u32[]{:S(2)}) collective-permute-start(s16[1296,128]{1,0:T(8,128)(2,1)S(1)} %send_part.9), channel_id=1, source_target_pairs={{0,2},{1,3},{2,0},{3,1},{4,6},{5,7},{6,4},{7,5},{8,10},{9,11},{10,... | collective-permute-start | bytes 995336 | tf_op jit(solution)/shard_map/ppermute | solution.py:238
  41.3 7.2 %collective-permute-start.14 = (bf16[264,256]{1,0:T(8,128)(2,1)S(1)}, bf16[264,256]{1,0:T(8,128)(2,1)S(1)}, u32[]{:S(2)}, u32[]{:S(2)}) collective-permute-start(bf16[264,256]{1,0:T(8,128)(2,1)S(1)} %add.9.refs_0_), channel_id=1, source_target_pairs={{24,0},{28,4},{16,8},{20,12},{8,16},{12,20},{0,24},{4,28},{25,1},{... | collective-permute-start | bytes 405512 | tf_op jit(solution)/shard_map/ppermute | solution.py:231
  43.6 7.4 %collective-permute-start.13 = (bf16[264,256]{1,0:T(8,128)(2,1)S(1)}, bf16[264,256]{1,0:T(8,128)(2,1)S(1)}, u32[]{:S(2)}, u32[]{:S(2)}) collective-permute-start(bf16[264,256]{1,0:T(8,128)(2,1)S(1)} %add.9.refs_0_), channel_id=1, source_target_pairs={{16,0},{20,4},{24,8},{28,12},{0,16},{4,20},{8,24},{12,28},{17,1},{... | collective-permute-start | bytes 405512 | tf_op jit(solution)/shard_map/ppermute | solution.py:231
  43.6 7.4 %collective-permute-start.12 = (bf16[264,256]{1,0:T(8,128)(2,1)S(1)}, bf16[264,256]{1,0:T(8,128)(2,1)S(1)}, u32[]{:S(2)}, u32[]{:S(2)}) collective-permute-start(bf16[264,256]{1,0:T(8,128)(2,1)S(1)} %add.9.refs_0_), channel_id=1, source_target_pairs={{8,0},{12,4},{0,8},{4,12},{24,16},{28,20},{16,24},{20,28},{9,1},{1... | collective-permute-start | bytes 405512 | tf_op jit(solution)/shard_map/ppermute | solution.py:231
  46.3 9.5 %collective-permute-start.18 = (s16[528,128]{1,0:T(8,128)(2,1)S(1)}, s16[528,128]{1,0:T(8,128)(2,1)S(1)}, u32[]{:S(2)}, u32[]{:S(2)}) collective-permute-start(s16[528,128]{1,0:T(8,128)(2,1)S(1)} %send_part.10), channel_id=1, source_target_pairs={{0,2},{1,3},{2,0},{3,1},{4,6},{5,7},{6,4},{7,5},{8,10},{9,11},{10,... | collective-permute-start | bytes 405512 | tf_op jit(solution)/shard_map/ppermute | solution.py:238
  48.4 13.8 %collective-permute-start.21 = (s16[1296,128]{1,0:T(8,128)(2,1)S(1)}, s16[1296,128]{1,0:T(8,128)(2,1)S(1)}, u32[]{:S(2)}, u32[]{:S(2)}) collective-permute-start(s16[1296,128]{1,0:T(8,128)(2,1)S(1)} %send_part.11), channel_id=1, source_target_pairs={{0,2},{1,3},{2,0},{3,1},{4,6},{5,7},{6,4},{7,5},{8,10},{9,11},{10,... | collective-permute-start | bytes 995336 | tf_op jit(solution)/shard_map/ppermute | solution.py:238
  56.9 8.2 %collective-permute-start.20 = (s16[1040,128]{1,0:T(8,128)(2,1)S(1)}, s16[1040,128]{1,0:T(8,128)(2,1)S(1)}, u32[]{:S(2)}, u32[]{:S(2)}) collective-permute-start(s16[1040,128]{1,0:T(8,128)(2,1)S(1)} %send_part.12), channel_id=1, source_target_pairs={{0,2},{1,3},{2,0},{3,1},{4,6},{5,7},{6,4},{7,5},{8,10},{9,11},{10,... | collective-permute-start | bytes 798728 | tf_op jit(solution)/shard_map/ppermute | solution.py:238
  59.9 6.9 %collective-permute-start.19 = (s16[272,128]{1,0:T(8,128)(2,1)S(1)}, s16[272,128]{1,0:T(8,128)(2,1)S(1)}, u32[]{:S(2)}, u32[]{:S(2)}) collective-permute-start(s16[272,128]{1,0:T(8,128)(2,1)S(1)} %send_part.13), channel_id=1, source_target_pairs={{0,2},{1,3},{2,0},{3,1},{4,6},{5,7},{6,4},{7,5},{8,10},{9,11},{10,... | collective-permute-start | bytes 208904 | tf_op jit(solution)/shard_map/ppermute | solution.py:238
